TPU v7x, 32 devices: a whole 2x2x4 slice. The times are simulated.
32 devices in a mesh: pages: 8 (over z, x), mp: 4 (over y, core).
Axes of the slice: x: 2, y: 2, z: 4, core: 2. Of those that a mesh axis runs over, the one named last changes fastest.
Arguments:
- queries: bfloat16 [256, 8192], P('pages', 'mp'), may hold values from -9 to 9
- cached_keys: bfloat16 [128, 128, 8, 128], P('pages', None, 'mp'), may hold values from -8 to 8
- cached_values: bfloat16 [128, 128, 8, 128], P('pages', None, 'mp'), may hold values from -4 to 4
- out_weight: bfloat16 [8192, 8192], P('mp', 'pages'), may hold values from -0.0625 to 0.0625
- select: int32 [2, 24], replicated, may hold values from 0 to 127, as said below
- page_table: int32 [128], replicated, may hold values from 0 to 127, as said below
- block_page: int32 [2], replicated, may hold values from 0 to 127, as said below
Outputs:
- mixed: bfloat16 [256, 8192], P('mp', 'pages')
Inputs may be any that keep to these rules, and one draw needn't show every extreme that they name: A permutation: each logical page has its own cache row, held by index page_table[p] // 16 of pages. `select`: each row holds 24 distinct pages: the block's own page block_page[b] and pages lying wholly before the block. They lie on exactly 4 owners, 6 on each. No owner holds selected pages of more than min(2, 4) blocks, and some owner holds that many. `block_page`: Distinct.
All inputs are finite; a program needn't handle non-finite values.
Results may differ from a plain program's by a relative error of at most 0.0063.
Values may be sent and summed in bfloat16 or wider, within the bound.
No kernel may reach another device: no remote copies, remote signals or barrier semaphores. Data moves between devices by JAX's collectives and lax.ppermute only.
A program may use at most 64 MiB of HBM per device.

v0:
```python
import jax
import jax.numpy as jnp
from jax import lax
from jax.sharding import PartitionSpec as P

PICKED_PAGES = 6


FLOOR = -1e30


def joined(part, axis, combine):
    gathered = jax.tree.map(lambda a: lax.all_gather(a, axis), part)

    def take(source):
        return jax.tree.map(lambda a: lax.dynamic_index_in_dim(a, source, 0, False), gathered)

    return lax.fori_loop(
        1, lax.axis_size(axis), lambda source, state: combine(state, take(source)), take(0)
    )


def hit_table(select, page_table, owner_index, pages_dev):
    owners = page_table[select] // pages_dev
    mine = owners == owner_index
    touched = jnp.any(mine, axis=1)
    order = jnp.argsort(jnp.where(touched, 0, 1).astype(jnp.int32), stable=True)
    count = jnp.sum(touched.astype(jnp.int32))
    return (mine, order, count)


def slot_pages(select, page_table, mine, order, slot_index, owner_index, pages_dev):
    block = order[jnp.minimum(slot_index, order.shape[0] - 1)]
    positions = jnp.argsort(jnp.where(mine[block], 0, 1).astype(jnp.int32), stable=True)[
        :PICKED_PAGES
    ]
    logical = select[block][positions]
    local = jnp.clip(page_table[logical] - owner_index * pages_dev, 0, pages_dev - 1)
    return (block, logical, local)


def attend(queries_all, block_page, block, logical, key_rows, value_rows):
    page = key_rows.shape[1]
    kv_heads = key_rows.shape[2]
    head_dim = key_rows.shape[3]
    width = queries_all.shape[1]
    repeat_heads = width // (kv_heads * head_dim)
    row_list = lax.dynamic_slice_in_dim(queries_all, block * page, page, 0).reshape(
        page, kv_heads, repeat_heads, head_dim
    )
    flat_keys = key_rows.reshape(-1, kv_heads, head_dim)
    flat_values = value_rows.reshape(-1, kv_heads, head_dim)
    scores = jnp.einsum(
        "rgeh,kgh->rgek", row_list, flat_keys, preferred_element_type=jnp.float32
    ) * head_dim ** (-0.5)
    offsets = jnp.arange(page, dtype=jnp.int32)
    key_pos = (logical[:, None] * page + offsets[None, :]).reshape(-1)
    query_pos = block_page[block] * page + offsets
    allowed = key_pos[None, :] <= query_pos[:, None]
    scores = jnp.where(allowed[:, None, None, :], scores, FLOOR)
    peak = jnp.max(scores, axis=-1)
    weights = jnp.exp(scores - peak[..., None])
    total = jnp.sum(weights, axis=-1)
    output = jnp.einsum(
        "rgek,kgh->rgeh",
        weights.astype(jnp.bfloat16),
        flat_values,
        preferred_element_type=jnp.float32,
    )
    return (output.reshape(page, width), peak.reshape(page, -1), total.reshape(page, -1))


def absorb(state, block, output, peak, total):
    outputs, maxima, totals = state
    page, heads = peak.shape
    start = block * page
    old_out = lax.dynamic_slice_in_dim(outputs, start, page, 0)
    old_max = lax.dynamic_slice_in_dim(maxima, start, page, 0)
    old_total = lax.dynamic_slice_in_dim(totals, start, page, 0)
    new_max = jnp.maximum(old_max, peak)
    keep = jnp.exp(old_max - new_max)
    fresh = jnp.exp(peak - new_max)
    new_out = (
        old_out.reshape(page, heads, -1) * keep[..., None]
        + output.reshape(page, heads, -1) * fresh[..., None]
    )
    new_total = old_total * keep + total * fresh
    outputs = lax.dynamic_update_slice_in_dim(outputs, new_out.reshape(page, -1), start, 0)
    maxima = lax.dynamic_update_slice_in_dim(maxima, new_max, start, 0)
    totals = lax.dynamic_update_slice_in_dim(totals, new_total, start, 0)
    return (outputs, maxima, totals)


def combine_stats(first, second):
    peak = jnp.maximum(first[0], second[0])
    return (peak, first[1] * jnp.exp(first[0] - peak) + second[1] * jnp.exp(second[0] - peak))


def per_device(queries, cached_keys, cached_values, out_weight, select, page_table, block_page):
    pages_dev = cached_keys.shape[0]
    owner_index = lax.axis_index("pages")
    queries_all = lax.all_gather(queries, "pages", axis=0, tiled=True)
    rows_all, width = queries_all.shape
    heads = width // cached_keys.shape[3]
    state = (
        jnp.zeros((rows_all, width), jnp.float32),
        jnp.full((rows_all, heads), FLOOR, jnp.float32),
        jnp.zeros((rows_all, heads), jnp.float32),
    )
    mine, order, count = hit_table(select, page_table, owner_index, pages_dev)

    def local_slot(slot_index, carried):
        block, logical, local = slot_pages(
            select, page_table, mine, order, slot_index, owner_index, pages_dev
        )
        return absorb(
            carried,
            block,
            *attend(
                queries_all, block_page, block, logical, cached_keys[local], cached_values[local]
            )
        )

    state = lax.fori_loop(0, count, local_slot, state)
    outputs, maxima, totals = state
    row_max, row_total = joined((maxima, totals), "pages", combine_stats)
    factor = jnp.exp(maxima - row_max) / row_total
    contributions = (
        (outputs.reshape(rows_all, heads, -1) * factor[..., None])
        .reshape(rows_all, width)
        .astype(jnp.bfloat16)
    )
    received = lax.all_to_all(contributions[None], "pages", split_axis=1, concat_axis=0, tiled=True)
    merged = jnp.sum(received, axis=0, dtype=jnp.float32).astype(jnp.bfloat16)
    terms = jnp.dot(
        lax.all_gather(merged, "pages", axis=0, tiled=True),
        out_weight,
        preferred_element_type=jnp.float32,
    )
    return lax.psum_scatter(terms, "mp", scatter_dimension=0, tiled=True).astype(jnp.bfloat16)


def solution(mesh):
    placed = (
        P("pages", "mp"),
        P("pages", None, "mp", None),
        P("pages", None, "mp", None),
        P("mp", "pages"),
        P(),
        P(),
        P(),
    )
    return jax.shard_map(
        per_device, mesh=mesh, in_specs=placed, out_specs=P("mp", "pages"), check_vma=False
    )
```

profile of v0, /device:TPU:0, one launch (start us, length us, event | category | flops | bytes accessed | tf_op | source)
XLA Modules:
  0.0 282.2 jit_solution(476613608024646394)
XLA Ops:
  6.5 0.7 all-gather.5.cloned.1.call-update
  7.3 0.7 compare_select_fusion.3
  8.1 1.4 gather_fusion.4
  9.7 0.7 broadcast_select_fusion
  10.4 0.7 sort.38
  11.1 41.2 %all-gather.5.cloned.1.call-done = bf16[256,2048]{1,0:T(8,128)(2,1)} async-done(((bf16[32,2048]{1,0:T(8,128)(2,1)}), bf16[256,2048]{1,0:T(8,128)(2,1)}) %all-gather.5.cloned.1.call-update) | async-done | bytes 1048592 | tf_op jit(solution)/shard_map/all_gather | solution.py:102
  52.4 1.6 broadcast_in_dim.68.clone
  54.0 57.8 %while.33 = (s32[]{:T(128)}, f32[256,2048]{1,0:T(8,128)}, f32[256,16]{0,1:T(8,128)S(1)}, f32[256,16]{0,1:T(8,128)S(1)}, s32[]{:T(128)}, /*index=5*/s32[2]{0:T(12...) while((s32[]{:T(128)}, f32[256,2048]{1,0:T(8,128)}, ...), condition=%wide.region_7.8_spmd, body=%wide.region_3.7_spmd.sunk | while | flops 823505024 | bytes 70521496 | solution.py:124
  54.7 0.7 dynamic_slice.103
  57.4 0.7 fusion.49
  58.1 1.6 sort.40
  59.7 0.6 gather_fusion
  60.4 1.3 gather_fusion.1
  61.7 2.6 gather_fusion.2
  64.3 1.2 dynamic_slice.104
  67.0 1.1 constant_dynamic-slice_fusion.9
  68.4 1.1 fusion.52
  69.5 2.7 copy-done
  72.1 1.3 fusion.54
  73.5 2.6 gather_fusion.3
  76.0 4.5 %fusion.53 = f32[2,128,128,8]{2,1,3,0:T(8,128)S(1)} fusion(f32[2,768,128,8]{2,1,3,0:T(8,128)} %copy-done, f32[128,2,8]{0,2,1:T(8,128)S(1)} %get-tuple-element.537, pred[128,768]{0,1:T(8,128)(4,1)S(1)} %broadcast_compare_fusion.2, bf16[768,2,128,1]{2,1,0,3:T(2,128)(2,1)S(1)} %bitcast.143), kind=kOutput, calls=%fused_computation.17.clone.1 | convolution fusion | flops 408944640 | bytes 7839744 | tf_op jit(solution)/shard_map/while/body/rgek,kgh->rgeh/dot_general | solution.py:64
  81.4 1.1 constant_dynamic-update-slice_fusion.3
  83.2 0.7 dynamic_slice.103
  86.0 0.7 fusion.49
  86.6 1.6 sort.40
  88.9 1.3 gather_fusion.1
  90.2 2.6 gather_fusion.2
  92.9 1.2 dynamic_slice.104
  95.6 1.1 constant_dynamic-slice_fusion.9
  96.9 1.1 fusion.52
  98.0 2.7 copy-done
  100.7 1.3 fusion.54
  102.0 2.6 gather_fusion.3
  104.6 4.5 %fusion.53 = f32[2,128,128,8]{2,1,3,0:T(8,128)S(1)} fusion(f32[2,768,128,8]{2,1,3,0:T(8,128)} %copy-done, f32[128,2,8]{0,2,1:T(8,128)S(1)} %get-tuple-element.537, pred[128,768]{0,1:T(8,128)(4,1)S(1)} %broadcast_compare_fusion.2, bf16[768,2,128,1]{2,1,0,3:T(2,128)(2,1)S(1)} %bitcast.143), kind=kOutput, calls=%fused_computation.17.clone.1 | convolution fusion | flops 408944640 | bytes 7839744 | tf_op jit(solution)/shard_map/while/body/rgek,kgh->rgeh/dot_general | solution.py:64
  110.0 1.1 constant_dynamic-update-slice_fusion.3
  111.7 30.7 %all-gather = f32[2048,16]{0,1:T(8,128)S(1)} all-gather(f32[256,16]{0,1:T(8,128)S(1)} %get-tuple-element.307), channel_id=2, replica_groups=mesh['pages'=8,'mp'=4] {'pages'}, dimensions={0}, use_global_device_ids=true | all-gather | bytes 147456 | tf_op jit(solution)/shard_map/all_gather | solution.py:13
  142.4 30.7 %all-gather.1 = f32[2048,16]{0,1:T(8,128)S(1)} all-gather(f32[256,16]{0,1:T(8,128)S(1)} %get-tuple-element.308), channel_id=3, replica_groups=mesh['pages'=8,'mp'=4] {'pages'}, dimensions={0}, use_global_device_ids=true | all-gather | bytes 147456 | tf_op jit(solution)/shard_map/all_gather | solution.py:13
  174.5 1.1 fusion.24
  175.6 1.6 copy.78
  177.7 6.8 %reduce.3 = bf16[256,2048]{1,0:T(8,128)(2,1)S(1)} reduce(bf16[256,1,2048]{2,1,0:T(2,128)(2,1)S(1)} %bitcast.146, bf16[]{:T(256)} %broadcast.191), dimensions={1}, to_apply=%bitcast.100.reduce_sub_computation | reduce | bytes 2097154
  184.5 0.8 reshape.199
  185.3 18.4 %all_to_all.12 = bf16[8,2,32768]{2,1,0:T(2,128)(2,1)S(1)} all-to-all(bf16[8,2,32768]{2,1,0:T(2,128)(2,1)S(1)} %reshape.199), channel_id=1, replica_groups=mesh['pages'=8,'mp'=4] {'pages'}, dimensions={0} | all-to-all | bytes 2097152 | tf_op jit(solution)/shard_map/all_to_all | solution.py:133
  203.7 1.0 reshape.200
  205.4 0.8 reduce_sum.33
  206.3 39.2 %all-gather.7.cloned.1.call-done = bf16[256,2048]{1,0:T(8,128)(2,1)} async-done(((bf16[32,2048]{1,0:T(8,128)(2,1)}), bf16[256,2048]{1,0:T(8,128)(2,1)}) %all-gather.7.cloned.1.call-update) | async-done | bytes 1048592 | tf_op jit(solution)/shard_map/all_gather | solution.py:136
  245.5 4.8 %fusion.30 = f32[256,1024]{1,0:T(8,128)} fusion(bf16[256,2048]{1,0:T(8,128)(2,1)} %all-gather.7.cloned.1.call-done, bf16[2048,1024]{1,0:T(8,128)(2,1)} %param.14), kind=kOutput, calls=%fused_computation.70 | convolution fusion | flops 1073741824 | bytes 6291456 | tf_op jit(solution)/shard_map/dot_general | solution.py:135
  250.3 23.8 %reduce-scatter.2.cloned.1.call-done = f32[64,1024]{1,0:T(8,128)} async-done(((f32[256,1024]{1,0:T(8,128)}), f32[64,1024]{1,0:T(8,128)}) %reduce-scatter.2.cloned.1.call-update) | async-done | bytes 262160 | tf_op jit(solution)/shard_map/reduce_scatter | solution.py:140
  274.0 1.6 convert_element_type.18
  (79 shorter events, 6.8 us)
Async XLA Ops:
  6.5 45.8 %all-gather.5.cloned.1.call-start = ((), (), s32[]{:S(2)}) async-start(), calls=%async_computation.2 | async-start | bytes 1179648 | tf_op jit(solution)/shard_map/all_gather | solution.py:102
  7.3 238.2 %all-gather.7.cloned.1.call-start = ((), (), s32[]{:S(2)}) async-start(), calls=%async_computation.3 | async-start | bytes 1179648 | tf_op jit(solution)/shard_map/all_gather | solution.py:136
  69.5 2.7 copy-start
  76.0 4.5 %copy-start.1 = (f32[256,2048]{1,0:T(8,128)S(1)}, f32[256,2048]{1,0:T(8,128)}, u32[]{:S(2)}) copy-start(f32[256,2048]{1,0:T(8,128)} %get-tuple-element.572) | copy-start | bytes 6291460 | tf_op jit(solution)/shard_map/while
  98.0 2.7 copy-start
  104.6 4.5 %copy-start.1 = (f32[256,2048]{1,0:T(8,128)S(1)}, f32[256,2048]{1,0:T(8,128)}, u32[]{:S(2)}) copy-start(f32[256,2048]{1,0:T(8,128)} %get-tuple-element.572) | copy-start | bytes 6291460 | tf_op jit(solution)/shard_map/while
  111.7 62.8 %copy-start.2 = (f32[256,2048]{1,0:T(8,128)S(1)}, f32[256,2048]{1,0:T(8,128)}, u32[]{:S(2)}) copy-start(f32[256,2048]{1,0:T(8,128)} %get-tuple-element.306) | copy-start | bytes 6291460
  206.2 67.8 %reduce-scatter.2.cloned.1.call-start = ((), (), s32[]{:S(2)}) async-start(), calls=%async_computation.4 | async-start | bytes 1310720 | tf_op jit(solution)/shard_map/reduce_scatter | solution.py:140
Sparse Core Ops, SparseCore 0:
  9.5 42.8 all-gather.4
  206.3 39.1 all-gather.6
  250.4 23.6 reduce-scatter.1
where the time goes:
time: 283 us; the launch traced here: 282 us
  waiting for transfers between devices  105 us (37%)
  blocking collectives  79.7 us (28%)
  local copies, waits for them, and re-layouts  38.3 us (14%)
  other arithmetic  20.8 us (7%)
  matrix products  15.8 us (6%)
  between operations  13.2 us (5%)
  loops' own time  9.26 us (3%)
    all_gather x2, blocking collectives, joined(): gathered = jax.tree.map(lambda a: lax.all_gather(a, axis), part)  61.4 us
    all_gather x1, waiting for transfers between devices, per_device(): queries_all = lax.all_gather(queries, 'pages', axis=0, tiled=True)  41.2 us
    all_gather x1, waiting for transfers between devices, per_device(): lax.all_gather(merged, 'pages', axis=0, tiled=True)  39.2 us
    reduce_scatter x1, waiting for transfers between devices, per_device(): lax.psum_scatter(terms, 'mp', scatter_dimension=0, tiled=True)  23.8 us
    all_to_all x1, blocking collectives, per_device(): lax.all_to_all(contributions[None], 'pages', split_axis=1, concat_axis=0,...  18.4 us
    another operation x1, loops' own time, per_device(): state = lax.fori_loop(0, count, local_slot, state)  9.04 us
    dot_general x2, matrix products, attend(): jnp.einsum('rgek,kgh->rgeh', weights.astype(jnp.bfloat16), flat_values, p...  8.96 us
    unnamed x1, other arithmetic  6.79 us
  transfers between devices with their start and end apart: 3, of which 3 were waited for; matrix products, arithmetic and copies ran while one was open for 1% of the time, Pallas kernels for 0%

commit v1 on v0

v1 whole, which is shorter than its diff:
```python
import functools
import math

import jax
import jax.numpy as jnp
from jax import lax
from jax.experimental import pallas as pl
from jax.experimental.pallas import tpu as pltpu
from jax.sharding import PartitionSpec as P

PICKED_PAGES = 6
FLOOR = -1e30
LANES = 128
HEADS_PER_TILE = 2

VMEM = pltpu.VMEM
SMEM = pltpu.SMEM
BF16 = jnp.bfloat16
F32 = jnp.float32


def in_vmem():
    return pl.BlockSpec(memory_space=VMEM)


def in_smem():
    return pl.BlockSpec(memory_space=SMEM)


def params(mib):
    return pltpu.CompilerParams(vmem_limit_bytes=mib * 2**20)


class Plan:
    def __init__(self, n, ways, rows, blocks, page):
        self.n, self.rows, self.blocks, self.page = n, rows, blocks, page
        self.group = n // blocks
        self.halves = blocks == 2 and n == 8 and ways == 4 and rows * self.group == page
        self.cross = n * 3 // 4
        self.chunks = self.group if self.halves else 1

    def block(self, me, lb):
        return (me // self.group) ^ lb if self.halves else lb

    def offsets(self, me, lb, shape):
        row = lax.broadcasted_iota(jnp.int32, shape, 0) % self.page
        if not self.halves:
            return row
        mine = (me ^ (lb * self.cross)) % self.group
        return ((row // self.rows) ^ mine) * self.rows + row % self.rows


def fetch_kernel(plan, pages_dev, select, table, stands, keys, values, k_out, v_out, info, k_buf, v_buf, sems):
    me = lax.axis_index("pages")
    blocks, picked = k_buf.shape[:2]
    span = k_buf.shape[2]
    heads = k_out.shape[1]
    page = span // heads
    low = me * pages_dev
    for lb in range(blocks):
        block = plan.block(me, lb)
        stand = stands[block]
        info[lb, 1] = 0

        def step(i, carry, lb=lb, block=block, stand=stand):
            others, all_ = carry
            logical = select[block, i]
            row = table[logical] - low
            mine = (row >= 0) & (row < pages_dev)
            own = logical == stand
            slot = jnp.where(own, 0, jnp.clip(picked - 1 - others, 0, picked - 1))

            @pl.when(mine)
            def _():
                pltpu.make_async_copy(keys.at[row], k_buf.at[lb, slot], sems.at[lb, slot, 0]).start()
                pltpu.make_async_copy(values.at[row], v_buf.at[lb, slot], sems.at[lb, slot, 1]).start()

                @pl.when(slot == 0)
                def _():
                    info[lb, 1] = logical

            one = mine.astype(jnp.int32)
            return others + jnp.where(own, 0, one), all_ + one

        _, count = lax.fori_loop(0, select.shape[1], step, (jnp.int32(0), jnp.int32(0)))
        info[lb, 0] = count

    row = lax.broadcasted_iota(jnp.int32, (span, span), 0)
    column = lax.broadcasted_iota(jnp.int32, (span, span), 1)
    apart = (column == (row % page) * heads + row // page).astype(F32).astype(BF16)
    for lb in range(blocks):

        @pl.when(info[lb, 0] > 0)
        def _(lb=lb):
            for g in range(heads):
                v_out[lb, g, :, LANES:] = jnp.ones((picked * page, LANES), BF16)
            for slot in range(picked):
                pltpu.make_async_copy(keys.at[0], k_buf.at[lb, slot], sems.at[lb, slot, 0]).wait()
                pltpu.make_async_copy(values.at[0], v_buf.at[lb, slot], sems.at[lb, slot, 1]).wait()
                both = jnp.concatenate([k_buf[lb, slot], v_buf[lb, slot]], axis=1)
                split = jnp.dot(apart, both, preferred_element_type=F32).astype(BF16)
                for g in range(heads):
                    here = slice(slot * page, (slot + 1) * page)
                    k_out[lb, g, here, :] = split[g * page : (g + 1) * page, :LANES]
                    v_out[lb, g, here, :LANES] = split[g * page : (g + 1) * page, LANES:]


def fetch(plan, select, table, stands, keys, values):
    pages_dev, page, heads, size = keys.shape
    blocks, picked = select.shape[0], PICKED_PAGES
    span = page * heads
    return pl.pallas_call(
        functools.partial(fetch_kernel, plan, pages_dev),
        out_shape=(
            jax.ShapeDtypeStruct((blocks, heads, picked * page, size), BF16),
            jax.ShapeDtypeStruct((blocks, heads, picked * page, size + LANES), BF16),
            jax.ShapeDtypeStruct((blocks, 2), jnp.int32),
        ),
        in_specs=[in_smem(), in_smem(), in_smem()] + [pl.BlockSpec(memory_space=pl.ANY)] * 2,
        out_specs=(in_vmem(), in_vmem(), in_smem()),
        scratch_shapes=[
            VMEM((blocks, picked, span, size), BF16),
            VMEM((blocks, picked, span, size), BF16),
            pltpu.SemaphoreType.DMA((blocks, picked, 2)),
        ],
        compiler_params=params(16),
        cost_estimate=pl.CostEstimate(flops=4 * 10**9, bytes_accessed=8 * 2**20, transcendentals=0),
    )(select, table, stands, keys.reshape(pages_dev, span, size), values.reshape(pages_dev, span, size))


def pack_stats(lse, heads):
    lane = lax.broadcasted_iota(jnp.int32, lse.shape, 1)
    high = lse.astype(BF16).astype(F32)
    rest = lse - high
    middle = rest.astype(BF16).astype(F32)
    low = rest - middle
    packed = jnp.where(lane < heads, high, 0.0)
    packed = packed + jnp.where((lane >= heads) & (lane < 2 * heads), pltpu.roll(middle, heads, 1), 0.0)
    packed = packed + jnp.where((lane >= 2 * heads) & (lane < 3 * heads), pltpu.roll(low, 2 * heads, 1), 0.0)
    return packed.astype(BF16)


def unpack_stats(packed, heads):
    wide = packed.astype(F32)
    return wide + pltpu.roll(wide, LANES - heads, 1) + pltpu.roll(wide, LANES - 2 * heads, 1)


def attend_kernel(plan, heads, info, stands, *refs):
    me = lax.axis_index("pages")
    blocks, chunks, page = plan.blocks, plan.chunks, plan.page
    queries = refs[: blocks * chunks]
    k_ref, v_ref = refs[blocks * chunks : blocks * chunks + 2]
    outs = refs[blocks * chunks + 2 :]
    kv_heads, size = k_ref.shape[1], k_ref.shape[3]
    repeat = heads // kv_heads
    width = heads * size
    part = page // chunks
    tile = math.gcd(repeat, HEADS_PER_TILE)
    scale = size**-0.5 * math.log2(math.e)
    lane = lax.broadcasted_iota(jnp.int32, (page, LANES), 1)
    for lb in range(blocks):
        block = plan.block(me, lb)
        mine = queries[lb * chunks : (lb + 1) * chunks]

        def put(c, columns, value, lb=lb):
            outs[c][lb * part : (lb + 1) * part, columns] = value

        @pl.when(info[lb, 0] > 0)
        def _(lb=lb, block=block, mine=mine, put=put):
            shape = (tile * page, page)
            key_pos = info[lb, 1] * page + lax.broadcasted_iota(jnp.int32, shape, 1)
            query_pos = stands[block] * page + plan.offsets(me, lb, shape)
            allowed = key_pos <= query_pos
            stats = jnp.zeros((page, LANES), F32)
            for g in range(kv_heads):
                for t in range(0, repeat, tile):
                    first = g * repeat + t
                    q = jnp.concatenate(
                        [m[:, h * size : (h + 1) * size] for h in range(first, first + tile) for m in mine], axis=0
                    )
                    scores = scale * lax.dot_general(
                        q, k_ref[lb, g], (((1,), (1,)), ((), ())), preferred_element_type=F32
                    )
                    scores = jnp.concatenate(
                        [jnp.where(allowed, scores[:, :page], FLOOR), scores[:, page:]], axis=1
                    )
                    peak = jnp.max(scores, axis=1, keepdims=True)
                    weights = jnp.exp2(scores - peak).astype(BF16)
                    both = jnp.dot(weights, v_ref[lb, g], preferred_element_type=F32)
                    total = both[:, size:]
                    out = (both[:, :size] / total).astype(BF16)
                    lse = peak + jnp.log2(total)
                    for i in range(tile):
                        h = first + i
                        stats = jnp.where(lane == h, lse[i * page : (i + 1) * page], stats)
                        for c in range(chunks):
                            put(c, slice(h * size, (h + 1) * size), out[i * page + c * part : i * page + (c + 1) * part])
            packed = pack_stats(stats, heads)
            for c in range(chunks):
                put(c, slice(width, width + LANES), packed[c * part : (c + 1) * part])

        @pl.when(info[lb, 0] == 0)
        def _(put=put):
            for c in range(chunks):
                put(c, slice(0, width), jnp.zeros((part, width), BF16))
                put(c, slice(width, width + LANES), pack_stats(jnp.full((part, LANES), FLOOR, F32), heads))


def attend(plan, heads, info, stands, queries, keys, values):
    part = plan.page // plan.chunks
    shape = jax.ShapeDtypeStruct((plan.blocks * part, queries[0].shape[1] + LANES), BF16)
    return pl.pallas_call(
        functools.partial(attend_kernel, plan, heads),
        out_shape=(shape,) * plan.chunks,
        in_specs=[in_smem(), in_smem()] + [in_vmem()] * (len(queries) + 2),
        out_specs=(in_vmem(),) * plan.chunks,
        compiler_params=params(32),
    )(info, stands, *queries, keys, values)


def merged(parts, stats, heads, size):
    top = functools.reduce(jnp.maximum, stats)
    shares = [jnp.exp2(s - top) for s in stats]
    total = functools.reduce(jnp.add, shares)
    shares = [s / total for s in shares]

    def head(h):
        return functools.reduce(
            jnp.add, [p(h).astype(F32) * s[:, h : h + 1] for p, s in zip(parts, shares, strict=True)]
        )

    return head, top + jnp.log2(total)


def merge_kernel(heads, *refs):
    sources, out = refs[:-1], refs[-1]
    width = out.shape[1] - LANES
    size = width // heads
    head, lse = merged(
        [lambda h, r=r: r[:, h * size : (h + 1) * size] for r in sources],
        [unpack_stats(r[:, width:], heads) for r in sources],
        heads,
        size,
    )
    for h in range(heads):
        out[:, h * size : (h + 1) * size] = head(h).astype(BF16)
    out[:, width:] = pack_stats(lse, heads)


def merge(heads, *sources):
    return pl.pallas_call(
        functools.partial(merge_kernel, heads),
        out_shape=jax.ShapeDtypeStruct(sources[0].shape, BF16),
        in_specs=[in_vmem()] * len(sources),
        out_specs=in_vmem(),
        compiler_params=params(8),
    )(*sources)


def finish_kernel(heads, near, far, out):
    rows, width = out.shape
    size = width // heads
    part = rows // 2
    for i in range(2):
        here, there = slice(i * part, (i + 1) * part), slice((1 - i) * part, (2 - i) * part)
        head, _ = merged(
            [
                lambda h: near[here, h * size : (h + 1) * size],
                lambda h: far[there, h * size : (h + 1) * size],
            ],
            [unpack_stats(near[here, width:], heads), unpack_stats(far[there, width:], heads)],
            heads,
            size,
        )
        for h in range(heads):
            out[here, h * size : (h + 1) * size] = head(h).astype(BF16)


def finish(heads, near, far):
    return pl.pallas_call(
        functools.partial(finish_kernel, heads),
        out_shape=jax.ShapeDtypeStruct((near.shape[0], near.shape[1] - LANES), BF16),
        in_specs=[in_vmem()] * 2,
        out_specs=in_vmem(),
        compiler_params=params(8),
    )(near, far)


def project_kernel(plan, ways, *refs):
    sources, weight, outs, rows_ref = refs[: plan.group], refs[plan.group], refs[plan.group + 1 : -1], refs[-1]
    me, column = lax.axis_index("pages"), lax.axis_index("mp")
    rows = plan.rows
    holders = plan.n // ways
    for k in range(plan.group):
        for half in range(2):
            device = me ^ k ^ (half * plan.cross)
            place = ((device // holders) ^ column) * holders + device % holders
            rows_ref[pl.ds(pl.multiple_of(place * rows, rows), rows), :] = sources[k][half * rows : (half + 1) * rows, :]
    part = holders * rows
    product = jnp.dot(rows_ref[...], weight[...], preferred_element_type=F32)
    keep, send = outs
    for i, w in enumerate(range(0, ways, 2)):
        keep[i * part : (i + 1) * part, :] = product[w * part : (w + 1) * part]
        send[i * part : (i + 1) * part, :] = product[(w + 1) * part : (w + 2) * part].astype(BF16)


def project(plan, ways, sources, weight):
    total = plan.n * plan.rows
    columns = weight.shape[1]
    return pl.pallas_call(
        functools.partial(project_kernel, plan, ways),
        out_shape=(
            jax.ShapeDtypeStruct((total // 2, columns), F32),
            jax.ShapeDtypeStruct((total // 2, columns), BF16),
        ),
        in_specs=[in_vmem()] * (plan.group + 1),
        out_specs=(in_vmem(), in_vmem()),
        scratch_shapes=[VMEM((total, weight.shape[0]), BF16)],
        compiler_params=params(24),
    )(*sources, weight)


def swap(x, axis, distance):
    n = lax.axis_size(axis)
    return lax.ppermute(x, axis, [(i, i ^ distance) for i in range(n)])


def by_halves(plan, heads, queries, weight, stands, pages):
    keys, values, info = pages
    far = swap(queries, "pages", plan.cross)
    own = [queries] + [swap(queries, "pages", k) for k in range(1, plan.group)]
    other = [far] + [swap(far, "pages", k) for k in range(1, plan.group)]
    outs = attend(plan, heads, info, stands, own + other, keys, values)
    near = merge(heads, outs[0], *(swap(outs[k], "pages", k) for k in range(1, plan.group)))
    rows = finish(heads, near, swap(near, "pages", plan.cross))
    every = [rows] + [swap(rows, "pages", k) for k in range(1, plan.group)]
    keep, send = project(plan, lax.axis_size("mp"), every, weight)
    total = keep + swap(send, "mp", 1).astype(F32)
    part = total.shape[0] // 2
    return (total[:part] + swap(total[part:].astype(BF16), "mp", 2).astype(F32)).astype(BF16)


def by_gathers(plan, heads, queries, weight, stands, pages):
    keys, values, info = pages
    width = queries.shape[1]
    size = width // heads
    gathered = lax.all_gather(queries, "pages", axis=0, tiled=True)
    rows = gathered.shape[0]
    mine = [gathered[i * plan.page : (i + 1) * plan.page] for i in range(plan.blocks)]
    (out,) = attend(plan, heads, info, stands, mine, keys, values)
    packed = out[:, width : width + 3 * heads].astype(F32)
    lse = packed[:, :heads] + packed[:, heads : 2 * heads] + packed[:, 2 * heads :]
    every = lax.all_gather(lse, "pages")
    top = jnp.max(every, axis=0)
    share = jnp.exp2(lse - top) / jnp.sum(jnp.exp2(every - top), axis=0)
    part = (out[:, :width].reshape(rows, heads, size).astype(F32) * share[..., None]).reshape(1, rows, width)
    received = lax.all_to_all(part.astype(BF16), "pages", split_axis=1, concat_axis=0, tiled=True)
    mixed = jnp.sum(received, axis=0, dtype=F32).astype(BF16)
    terms = jnp.dot(lax.all_gather(mixed, "pages", axis=0, tiled=True), weight, preferred_element_type=F32)
    return lax.psum_scatter(terms, "mp", scatter_dimension=0, tiled=True).astype(BF16)


def per_device(queries, cached_keys, cached_values, out_weight, select, page_table, block_page):
    n, ways = lax.axis_size("pages"), lax.axis_size("mp")
    plan = Plan(n, ways, queries.shape[0], select.shape[0], cached_keys.shape[1])
    heads = queries.shape[1] // cached_keys.shape[3]
    pages = fetch(plan, select, page_table, block_page, cached_keys, cached_values)
    way = by_halves if plan.halves else by_gathers
    return way(plan, heads, queries, out_weight, block_page, pages)


def solution(mesh):
    placed = (
        P("pages", "mp"),
        P("pages", None, "mp", None),
        P("pages", None, "mp", None),
        P("mp", "pages"),
        P(),
        P(),
        P(),
    )
    return jax.shard_map(
        per_device, mesh=mesh, in_specs=placed, out_specs=P("mp", "pages"), check_vma=False
    )
```

time: 283 us -> 80.3 us (0.28)
  blocking collectives: 79.7 us -> 0 us
  waiting for transfers between devices: 105 us -> 35.2 us
  local copies, waits for them, and re-layouts: 38.3 us -> 4.47 us
  starting transfers between devices: 0.08 us -> 24.2 us
  other arithmetic: 20.8 us -> 0.73 us
  matrix products: 15.8 us -> 0 us
  Pallas kernels: 0 us -> 15.7 us
  between operations: 13.2 us -> 0.14 us
  loops' own time: 9.26 us -> 0 us
    all_gather x2 -> x0, waiting for transfers between devices: 80.5 us -> none  [the longest x1 41.2 us: per_device(): queries_all = lax.all_gather(queries, 'pages', axis=0, tiled=True)]
    all_gather x2 -> x0, blocking collectives: 61.4 us -> none  [joined(): gathered = jax.tree.map(lambda a: lax.all_gather(a, axis), part)]
    ppermute x0 -> x16, waiting for transfers between devices: none -> 35.2 us  [swap(): return lax.ppermute(x, axis, [(i, i ^ distance) for i in range(n)])]
    ppermute x0 -> x16, starting transfers between devices: none -> 24.2 us  [swap(): return lax.ppermute(x, axis, [(i, i ^ distance) for i in range(n)])]
    reduce_scatter x1 -> x0, waiting for transfers between devices: 23.8 us -> none  [per_device(): lax.psum_scatter(terms, 'mp', scatter_dimension=0, tiled=True)]
    all_to_all x1 -> x0, blocking collectives: 18.4 us -> none  [per_device(): lax.all_to_all(contributions[None], 'pages', split_axis=1, concat_axis=0,...]
    dot_general x5 -> x0, matrix products: 15.8 us -> none  [the longest x2 8.96 us: attend(): jnp.einsum('rgek,kgh->rgeh', weights.astype(jnp.bfloat16), flat_values, p...]
    pallas_call x0 -> x5, Pallas kernels: none -> 15.7 us  [the longest x1 7.21 us: fetch(): pl.pallas_call(functools.partial(fetch_kernel, plan, pages_dev), out_shap...]
  transfers between devices with their start and end apart: 3 -> 16, of which waited for: 3 -> 11; matrix products, arithmetic and copies ran while one was open for 1% -> 0% of each run, Pallas kernels for 0% -> 9%
where the time goes in v1:
time: 80.3 us; the launch traced here: 80.6 us
  waiting for transfers between devices  35.2 us (44%)
  starting transfers between devices  24.2 us (30%)
  Pallas kernels  15.7 us (20%)
  local copies, waits for them, and re-layouts  4.47 us (6%)
    ppermute x16, waiting for transfers between devices, swap(): return lax.ppermute(x, axis, [(i, i ^ distance) for i in range(n)])  35.2 us
    ppermute x16, starting transfers between devices, swap(): return lax.ppermute(x, axis, [(i, i ^ distance) for i in range(n)])  24.2 us
    pallas_call x1, Pallas kernels, fetch(): pl.pallas_call(functools.partial(fetch_kernel, plan, pages_dev), out_shap...  7.21 us
    pallas_call x1, Pallas kernels, attend(): pl.pallas_call(functools.partial(attend_kernel, plan, heads), out_shape=(...  5.79 us
    unnamed x16, local copies, waits for them, and re-layouts  4.45 us
  transfers between devices with their start and end apart: 16, of which 11 were waited for; matrix products, arithmetic and copies ran while one was open for 0% of the time, Pallas kernels for 9%

profile of v1, /device:TPU:0, one launch (start us, length us, event | category | flops | bytes accessed | tf_op | source)
XLA Modules:
  0.0 80.6 jit_solution(17576914275120163976)
XLA Ops:
  0.0 5.0 %collective-permute-start.3 = (bf16[32,2048]{1,0:T(8,128)(2,1)}, bf16[32,2048]{1,0:T(8,128)(2,1)S(1)}, u32[]{:S(2)}, u32[]{:S(2)}) collective-permute-start(bf16[32,2048]{1,0:T(8,128)(2,1)} %refs_0_.1), channel_id=1, source_target_pairs={{0,24},{4,28},{8,16},{12,20},{16,8},{20,12},{24,0},{28,4},{1,25},{... | collective-permute-start | bytes 393224 | tf_op jit(solution)/shard_map/ppermute | solution.py:325
  5.0 0.5 collective-permute-start.2
  5.5 2.5 %collective-permute-start.1 = (bf16[32,2048]{1,0:T(8,128)(2,1)}, bf16[32,2048]{1,0:T(8,128)(2,1)S(1)}, u32[]{:S(2)}, u32[]{:S(2)}) collective-permute-start(bf16[32,2048]{1,0:T(8,128)(2,1)} %refs_0_.1), channel_id=1, source_target_pairs={{0,8},{4,12},{8,0},{12,4},{16,24},{20,28},{24,16},{28,20},{1,9},{5... | collective-permute-start | bytes 393224 | tf_op jit(solution)/shard_map/ppermute | solution.py:325
  8.0 0.5 collective-permute-start
  8.5 1.1 %collective-permute-done.3.refs_4_ = bf16[32,2048]{1,0:T(8,128)(2,1)S(1)} collective-permute-done((bf16[32,2048]{1,0:T(8,128)(2,1)}, bf16[32,2048]{1,0:T(8,128)(2,1)S(1)}, u32[]{:S(2)}, u32[]{:S(2)}) %collective-permute-start.3) | collective-permute-done | bytes 131104 | tf_op jit(solution)/shard_map/ppermute | solution.py:325
  9.6 2.6 %collective-permute-start.6 = (bf16[32,2048]{1,0:T(8,128)(2,1)S(1)}, bf16[32,2048]{1,0:T(8,128)(2,1)S(1)}, u32[]{:S(2)}, u32[]{:S(2)}) collective-permute-start(bf16[32,2048]{1,0:T(8,128)(2,1)S(1)} %collective-permute-done.3.refs_4_), channel_id=1, source_target_pairs={{0,12},{4,8},{8,4},{12,0},{16,28},{20,24},{24,20},{28,16},{1,13},{... | collective-permute-start | bytes 393224 | tf_op jit(solution)/shard_map/ppermute | solution.py:325
  12.2 0.6 collective-permute-start.5
  12.8 0.4 collective-permute-done.2.refs_3_
  13.2 1.0 %collective-permute-start.4 = (bf16[32,2048]{1,0:T(8,128)(2,1)S(1)}, bf16[32,2048]{1,0:T(8,128)(2,1)S(1)}, u32[]{:S(2)}, u32[]{:S(2)}) collective-permute-start(bf16[32,2048]{1,0:T(8,128)(2,1)S(1)} %collective-permute-done.3.refs_4_), channel_id=1, source_target_pairs={{0,4},{4,0},{8,12},{12,8},{16,20},{20,16},{24,28},{28,24},{1,5},{5... | collective-permute-start | bytes 393224 | tf_op jit(solution)/shard_map/ppermute | solution.py:325
  14.1 0.7 copy-done.2
  14.8 1.2 %copy-done.4 = bf16[16,128,2,128]{3,2,1,0:T(2,128)(2,1)S(1)} copy-done((bf16[16,128,2,128]{3,2,1,0:T(2,128)(2,1)S(1)}, bf16[16,128,2,128]{3,2,1,0:T(2,128)(2,1)}, u32[]{:S(2)}) %copy-start.4) | copy-done | bytes 1048600
  16.0 1.2 %copy-done.5 = bf16[16,128,2,128]{3,2,1,0:T(2,128)(2,1)S(1)} copy-done((bf16[16,128,2,128]{3,2,1,0:T(2,128)(2,1)S(1)}, bf16[16,128,2,128]{3,2,1,0:T(2,128)(2,1)}, u32[]{:S(2)}) %copy-start.5) | copy-done | bytes 1048600
  17.2 0.7 copy-done.6
  17.9 0.7 copy-done.7
  18.6 7.2 %shard_map.73 = (bf16[2,2,768,128]{3,2,1,0:T(8,128)(2,1)S(1)}, bf16[2,2,768,256]{3,2,1,0:T(8,128)(2,1)S(1)}, s32[2,2]{1,0:T(2,128)S(1)}) custom-call(s32[2,24]{1,0:T(2,128)S(1)} %copy-done.6, s32[128]{0:T(128)S(1)} %copy-done.7, s32[2]{0:T(128)S(1)} %copy-done.2, bf16[16,256,128]{2,1,0:T(8,128)(2,1)S(1)} %bitcast.2, bf16[16,256,128]{2,1,0:T(8,128)(2,1)S(1)} %bitcast.3), custom_call_target="tpu_custom_call" | custom-call | flops 4000000000 | bytes 8388608 | tf_op jit(solution)/shard_map/pallas_call | solution.py:112
  25.8 0.0 copy-start
  25.8 0.0 collective-permute-done.1.refs_2_
  25.8 0.0 collective-permute-done.refs_1_
  25.8 0.0 collective-permute-done.6.refs_7_
  25.8 0.0 collective-permute-done.5.refs_6_
  25.8 0.0 collective-permute-done.4.refs_5_
  25.8 0.0 copy-done.1
  25.9 0.0 copy-done.3
  25.9 5.8 %shard_map.74 = (bf16[64,2176]{1,0:T(8,128)(2,1)S(1)}, bf16[64,2176]{1,0:T(8,128)(2,1)S(1)}, bf16[64,2176]{1,0:T(8,128)(2,1)S(1)}, bf16[64,2176]{1,0:T(8,128)(2,1)S(1)}) custom-call(s32[2,2]{1,0:T(2,128)S(1)} %get-tuple-element.14.info, s32[2]{0:T(128)S(1)} %copy-done.3, bf16[32,2048]{1,0:T(8,128)(2,1)S(1)} %copy-done.1, ...), custom_call_target="tpu_custom_call" | custom-call | tf_op jit(solution)/shard_map/pallas_call | solution.py:212
  31.7 1.1 %collective-permute-start.7 = (bf16[64,2176]{1,0:T(8,128)(2,1)S(1)}, bf16[64,2176]{1,0:T(8,128)(2,1)S(1)}, u32[]{:S(2)}, u32[]{:S(2)}) collective-permute-start(bf16[64,2176]{1,0:T(8,128)(2,1)S(1)} %get-tuple-element.18), channel_id=1, source_target_pairs={{0,4},{4,0},{8,12},{12,8},{16,20},{20,16},{24,28},{28,24},{1,5},{5... | collective-permute-start | bytes 835592 | tf_op jit(solution)/shard_map/ppermute | solution.py:325
  32.8 0.0 collective-permute-start.8
  32.8 2.4 %collective-permute-start.9 = (bf16[64,2176]{1,0:T(8,128)(2,1)S(1)}, bf16[64,2176]{1,0:T(8,128)(2,1)S(1)}, u32[]{:S(2)}, u32[]{:S(2)}) collective-permute-start(bf16[64,2176]{1,0:T(8,128)(2,1)S(1)} %get-tuple-element.20), channel_id=1, source_target_pairs={{0,12},{4,8},{8,4},{12,0},{16,28},{20,24},{24,20},{28,16},{1,13},{... | collective-permute-start | bytes 835592 | tf_op jit(solution)/shard_map/ppermute | solution.py:325
  35.2 5.2 %collective-permute-done.7.refs_1_ = bf16[64,2176]{1,0:T(8,128)(2,1)S(1)} collective-permute-done((bf16[64,2176]{1,0:T(8,128)(2,1)S(1)}, bf16[64,2176]{1,0:T(8,128)(2,1)S(1)}, u32[]{:S(2)}, u32[]{:S(2)}) %collective-permute-start.7) | collective-permute-done | bytes 278560 | tf_op jit(solution)/shard_map/ppermute | solution.py:325
  40.4 2.0 %collective-permute-done.8.refs_2_ = bf16[64,2176]{1,0:T(8,128)(2,1)S(1)} collective-permute-done((bf16[64,2176]{1,0:T(8,128)(2,1)S(1)}, bf16[64,2176]{1,0:T(8,128)(2,1)S(1)}, u32[]{:S(2)}, u32[]{:S(2)}) %collective-permute-start.8) | collective-permute-done | bytes 278560 | tf_op jit(solution)/shard_map/ppermute | solution.py:325
  42.4 3.3 %collective-permute-done.9.refs_3_ = bf16[64,2176]{1,0:T(8,128)(2,1)S(1)} collective-permute-done((bf16[64,2176]{1,0:T(8,128)(2,1)S(1)}, bf16[64,2176]{1,0:T(8,128)(2,1)S(1)}, u32[]{:S(2)}, u32[]{:S(2)}) %collective-permute-start.9) | collective-permute-done | bytes 278560 | tf_op jit(solution)/shard_map/ppermute | solution.py:325
  45.6 0.8 shard_map.75.near
  46.4 0.3 collective-permute-start.10
  46.8 8.2 %collective-permute-done.10.far = bf16[64,2176]{1,0:T(8,128)(2,1)S(1)} collective-permute-done((bf16[64,2176]{1,0:T(8,128)(2,1)S(1)}, bf16[64,2176]{1,0:T(8,128)(2,1)S(1)}, u32[]{:S(2)}, u32[]{:S(2)}) %collective-permute-start.10) | collective-permute-done | bytes 278560 | tf_op jit(solution)/shard_map/ppermute | solution.py:325
  55.0 0.6 shard_map.76.refs_0_
  55.6 5.4 %collective-permute-start.13 = (bf16[64,2048]{1,0:T(8,128)(2,1)S(1)}, bf16[64,2048]{1,0:T(8,128)(2,1)S(1)}, u32[]{:S(2)}, u32[]{:S(2)}) collective-permute-start(bf16[64,2048]{1,0:T(8,128)(2,1)S(1)} %shard_map.76.refs_0_), channel_id=1, source_target_pairs={{0,12},{4,8},{8,4},{12,0},{16,28},{20,24},{24,20},{28,16},{1,13},{... | collective-permute-start | bytes 786440 | tf_op jit(solution)/shard_map/ppermute | solution.py:325
  61.0 0.0 collective-permute-start.12
  61.0 0.6 collective-permute-start.11
  61.6 6.6 %collective-permute-done.13.refs_3_ = bf16[64,2048]{1,0:T(8,128)(2,1)S(1)} collective-permute-done((bf16[64,2048]{1,0:T(8,128)(2,1)S(1)}, bf16[64,2048]{1,0:T(8,128)(2,1)S(1)}, u32[]{:S(2)}, u32[]{:S(2)}) %collective-permute-start.13) | collective-permute-done | bytes 262176 | tf_op jit(solution)/shard_map/ppermute | solution.py:325
  68.2 2.3 %collective-permute-done.12.refs_2_ = bf16[64,2048]{1,0:T(8,128)(2,1)S(1)} collective-permute-done((bf16[64,2048]{1,0:T(8,128)(2,1)S(1)}, bf16[64,2048]{1,0:T(8,128)(2,1)S(1)}, u32[]{:S(2)}, u32[]{:S(2)}) %collective-permute-start.12) | collective-permute-done | bytes 262176 | tf_op jit(solution)/shard_map/ppermute | solution.py:325
  70.5 0.7 collective-permute-done.11.refs_1_
  71.2 0.0 copy-done
  71.2 1.3 %shard_map.77 = (f32[128,1024]{1,0:T(8,128)S(1)}, bf16[128,1024]{1,0:T(8,128)(2,1)S(1)}) custom-call(bf16[64,2048]{1,0:T(8,128)(2,1)S(1)} %shard_map.76.refs_0_, bf16[64,2048]{1,0:T(8,128)(2,1)S(1)} %collective-permute-done.11.refs_1_, bf16[64,2048]{1,0:T(8,128)(2,1)S(1)} %collective-permute-done.12.refs_2_, ...), custom_call_target="tpu_custom_call" | custom-call | tf_op jit(solution)/shard_map/pallas_call | solution.py:310
  72.6 0.1 collective-permute-start.14
  72.7 1.5 %collective-permute-done.14 = bf16[128,1024]{1,0:T(8,128)(2,1)S(1)} collective-permute-done((bf16[128,1024]{1,0:T(8,128)(2,1)S(1)}, bf16[128,1024]{1,0:T(8,128)(2,1)S(1)}, u32[]{:S(2)}, u32[]{:S(2)}) %collective-permute-start.14) | collective-permute-done | bytes 262176 | tf_op jit(solution)/shard_map/ppermute | solution.py:325
  74.2 0.1 convert_add_fusion
  74.3 1.6 %collective-permute-start.15 = (bf16[64,1024]{1,0:T(8,128)(2,1)S(1)}, bf16[64,1024]{1,0:T(8,128)(2,1)S(1)}, u32[]{:S(2)}, u32[]{:S(2)}) collective-permute-start(bf16[64,1024]{1,0:T(8,128)(2,1)S(1)} %slice.15), channel_id=1, source_target_pairs={{0,2},{1,3},{2,0},{3,1},{4,6},{5,7},{6,4},{7,5},{8,10},{9,11},{10,... | collective-permute-start | bytes 393224 | tf_op jit(solution)/shard_map/ppermute | solution.py:325
  75.9 4.0 %collective-permute-done.15 = bf16[64,1024]{1,0:T(8,128)(2,1)S(1)} collective-permute-done((bf16[64,1024]{1,0:T(8,128)(2,1)S(1)}, bf16[64,1024]{1,0:T(8,128)(2,1)S(1)}, u32[]{:S(2)}, u32[]{:S(2)}) %collective-permute-start.15) | collective-permute-done | bytes 131104 | tf_op jit(solution)/shard_map/ppermute | solution.py:325
  79.9 0.7 fusion
  (8 shorter events, 0.0 us)
Async XLA Ops:
  0.0 9.6 %collective-permute-start.3 = (bf16[32,2048]{1,0:T(8,128)(2,1)}, bf16[32,2048]{1,0:T(8,128)(2,1)S(1)}, u32[]{:S(2)}, u32[]{:S(2)}) collective-permute-start(bf16[32,2048]{1,0:T(8,128)(2,1)} %refs_0_.1), channel_id=1, source_target_pairs={{0,24},{4,28},{8,16},{12,20},{16,8},{20,12},{24,0},{28,4},{1,25},{... | collective-permute-start | bytes 393224 | tf_op jit(solution)/shard_map/ppermute | solution.py:325
  5.0 8.1 %collective-permute-start.2 = (bf16[32,2048]{1,0:T(8,128)(2,1)}, bf16[32,2048]{1,0:T(8,128)(2,1)S(1)}, u32[]{:S(2)}, u32[]{:S(2)}) collective-permute-start(bf16[32,2048]{1,0:T(8,128)(2,1)} %refs_0_.1), channel_id=1, source_target_pairs={{0,12},{4,8},{8,4},{12,0},{16,28},{20,24},{24,20},{28,16},{1,13},{... | collective-permute-start | bytes 393224 | tf_op jit(solution)/shard_map/ppermute | solution.py:325
  5.5 20.3 %collective-permute-start.1 = (bf16[32,2048]{1,0:T(8,128)(2,1)}, bf16[32,2048]{1,0:T(8,128)(2,1)S(1)}, u32[]{:S(2)}, u32[]{:S(2)}) collective-permute-start(bf16[32,2048]{1,0:T(8,128)(2,1)} %refs_0_.1), channel_id=1, source_target_pairs={{0,8},{4,12},{8,0},{12,4},{16,24},{20,28},{24,16},{28,20},{1,9},{5... | collective-permute-start | bytes 393224 | tf_op jit(solution)/shard_map/ppermute | solution.py:325
  8.0 17.8 %collective-permute-start = (bf16[32,2048]{1,0:T(8,128)(2,1)}, bf16[32,2048]{1,0:T(8,128)(2,1)S(1)}, u32[]{:S(2)}, u32[]{:S(2)}) collective-permute-start(bf16[32,2048]{1,0:T(8,128)(2,1)} %refs_0_.1), channel_id=1, source_target_pairs={{0,4},{4,0},{8,12},{12,8},{16,20},{20,16},{24,28},{28,24},{1,5},{5... | collective-permute-start | bytes 393224 | tf_op jit(solution)/shard_map/ppermute | solution.py:325
  9.6 16.2 %collective-permute-start.6 = (bf16[32,2048]{1,0:T(8,128)(2,1)S(1)}, bf16[32,2048]{1,0:T(8,128)(2,1)S(1)}, u32[]{:S(2)}, u32[]{:S(2)}) collective-permute-start(bf16[32,2048]{1,0:T(8,128)(2,1)S(1)} %collective-permute-done.3.refs_4_), channel_id=1, source_target_pairs={{0,12},{4,8},{8,4},{12,0},{16,28},{20,24},{24,20},{28,16},{1,13},{... | collective-permute-start | bytes 393224 | tf_op jit(solution)/shard_map/ppermute | solution.py:325
  12.2 13.6 %collective-permute-start.5 = (bf16[32,2048]{1,0:T(8,128)(2,1)S(1)}, bf16[32,2048]{1,0:T(8,128)(2,1)S(1)}, u32[]{:S(2)}, u32[]{:S(2)}) collective-permute-start(bf16[32,2048]{1,0:T(8,128)(2,1)S(1)} %collective-permute-done.3.refs_4_), channel_id=1, source_target_pairs={{0,8},{4,12},{8,0},{12,4},{16,24},{20,28},{24,16},{28,20},{1,9},{5... | collective-permute-start | bytes 393224 | tf_op jit(solution)/shard_map/ppermute | solution.py:325
  13.2 12.7 %collective-permute-start.4 = (bf16[32,2048]{1,0:T(8,128)(2,1)S(1)}, bf16[32,2048]{1,0:T(8,128)(2,1)S(1)}, u32[]{:S(2)}, u32[]{:S(2)}) collective-permute-start(bf16[32,2048]{1,0:T(8,128)(2,1)S(1)} %collective-permute-done.3.refs_4_), channel_id=1, source_target_pairs={{0,4},{4,0},{8,12},{12,8},{16,20},{20,16},{24,28},{28,24},{1,5},{5... | collective-permute-start | bytes 393224 | tf_op jit(solution)/shard_map/ppermute | solution.py:325
  14.1 0.7 copy-start.2
  14.8 1.2 %copy-start.4 = (bf16[16,128,2,128]{3,2,1,0:T(2,128)(2,1)S(1)}, bf16[16,128,2,128]{3,2,1,0:T(2,128)(2,1)}, u32[]{:S(2)}) copy-start(bf16[16,128,2,128]{3,2,1,0:T(2,128)(2,1)} %param.8) | copy-start | bytes 3145732
  16.0 1.2 %copy-start.5 = (bf16[16,128,2,128]{3,2,1,0:T(2,128)(2,1)S(1)}, bf16[16,128,2,128]{3,2,1,0:T(2,128)(2,1)}, u32[]{:S(2)}) copy-start(bf16[16,128,2,128]{3,2,1,0:T(2,128)(2,1)} %param.9) | copy-start | bytes 3145732
  17.2 0.7 copy-start.6
  17.9 0.7 copy-start.7
  18.6 7.3 %copy-start.1 = (bf16[32,2048]{1,0:T(8,128)(2,1)S(1)}, bf16[32,2048]{1,0:T(8,128)(2,1)}, u32[]{:S(2)}) copy-start(bf16[32,2048]{1,0:T(8,128)(2,1)} %refs_0_.1) | copy-start | bytes 393220
  18.6 7.3 %copy-start.3 = (s32[2]{0:T(128)S(1)}, s32[2]{0:T(128)}, u32[]{:S(2)}) copy-start(s32[2]{0:T(128)} %stands.3) | copy-start | bytes 28
  25.8 45.5 %copy-start = (bf16[2048,1024]{1,0:T(8,128)(2,1)S(1)}, bf16[2048,1024]{1,0:T(8,128)(2,1)}, u32[]{:S(2)}) copy-start(bf16[2048,1024]{1,0:T(8,128)(2,1)} %refs_4_.1) | copy-start | bytes 12582916
  31.7 8.7 %collective-permute-start.7 = (bf16[64,2176]{1,0:T(8,128)(2,1)S(1)}, bf16[64,2176]{1,0:T(8,128)(2,1)S(1)}, u32[]{:S(2)}, u32[]{:S(2)}) collective-permute-start(bf16[64,2176]{1,0:T(8,128)(2,1)S(1)} %get-tuple-element.18), channel_id=1, source_target_pairs={{0,4},{4,0},{8,12},{12,8},{16,20},{20,16},{24,28},{28,24},{1,5},{5... | collective-permute-start | bytes 835592 | tf_op jit(solution)/shard_map/ppermute | solution.py:325
  32.8 9.6 %collective-permute-start.8 = (bf16[64,2176]{1,0:T(8,128)(2,1)S(1)}, bf16[64,2176]{1,0:T(8,128)(2,1)S(1)}, u32[]{:S(2)}, u32[]{:S(2)}) collective-permute-start(bf16[64,2176]{1,0:T(8,128)(2,1)S(1)} %get-tuple-element.19), channel_id=1, source_target_pairs={{0,8},{4,12},{8,0},{12,4},{16,24},{20,28},{24,16},{28,20},{1,9},{5... | collective-permute-start | bytes 835592 | tf_op jit(solution)/shard_map/ppermute | solution.py:325
  32.8 12.9 %collective-permute-start.9 = (bf16[64,2176]{1,0:T(8,128)(2,1)S(1)}, bf16[64,2176]{1,0:T(8,128)(2,1)S(1)}, u32[]{:S(2)}, u32[]{:S(2)}) collective-permute-start(bf16[64,2176]{1,0:T(8,128)(2,1)S(1)} %get-tuple-element.20), channel_id=1, source_target_pairs={{0,12},{4,8},{8,4},{12,0},{16,28},{20,24},{24,20},{28,16},{1,13},{... | collective-permute-start | bytes 835592 | tf_op jit(solution)/shard_map/ppermute | solution.py:325
  46.4 8.5 %collective-permute-start.10 = (bf16[64,2176]{1,0:T(8,128)(2,1)S(1)}, bf16[64,2176]{1,0:T(8,128)(2,1)S(1)}, u32[]{:S(2)}, u32[]{:S(2)}) collective-permute-start(bf16[64,2176]{1,0:T(8,128)(2,1)S(1)} %shard_map.75.near), channel_id=1, source_target_pairs={{0,24},{4,28},{8,16},{12,20},{16,8},{20,12},{24,0},{28,4},{1,25},{... | collective-permute-start | bytes 835592 | tf_op jit(solution)/shard_map/ppermute | solution.py:325
  55.6 12.6 %collective-permute-start.13 = (bf16[64,2048]{1,0:T(8,128)(2,1)S(1)}, bf16[64,2048]{1,0:T(8,128)(2,1)S(1)}, u32[]{:S(2)}, u32[]{:S(2)}) collective-permute-start(bf16[64,2048]{1,0:T(8,128)(2,1)S(1)} %shard_map.76.refs_0_), channel_id=1, source_target_pairs={{0,12},{4,8},{8,4},{12,0},{16,28},{20,24},{24,20},{28,16},{1,13},{... | collective-permute-start | bytes 786440 | tf_op jit(solution)/shard_map/ppermute | solution.py:325
  61.0 9.5 %collective-permute-start.12 = (bf16[64,2048]{1,0:T(8,128)(2,1)S(1)}, bf16[64,2048]{1,0:T(8,128)(2,1)S(1)}, u32[]{:S(2)}, u32[]{:S(2)}) collective-permute-start(bf16[64,2048]{1,0:T(8,128)(2,1)S(1)} %shard_map.76.refs_0_), channel_id=1, source_target_pairs={{0,8},{4,12},{8,0},{12,4},{16,24},{20,28},{24,16},{28,20},{1,9},{5... | collective-permute-start | bytes 786440 | tf_op jit(solution)/shard_map/ppermute | solution.py:325
  61.0 10.2 %collective-permute-start.11 = (bf16[64,2048]{1,0:T(8,128)(2,1)S(1)}, bf16[64,2048]{1,0:T(8,128)(2,1)S(1)}, u32[]{:S(2)}, u32[]{:S(2)}) collective-permute-start(bf16[64,2048]{1,0:T(8,128)(2,1)S(1)} %shard_map.76.refs_0_), channel_id=1, source_target_pairs={{0,4},{4,0},{8,12},{12,8},{16,20},{20,16},{24,28},{28,24},{1,5},{5... | collective-permute-start | bytes 786440 | tf_op jit(solution)/shard_map/ppermute | solution.py:325
  72.6 1.6 %collective-permute-start.14 = (bf16[128,1024]{1,0:T(8,128)(2,1)S(1)}, bf16[128,1024]{1,0:T(8,128)(2,1)S(1)}, u32[]{:S(2)}, u32[]{:S(2)}) collective-permute-start(bf16[128,1024]{1,0:T(8,128)(2,1)S(1)} %get-tuple-element.22), channel_id=1, source_target_pairs={{0,1},{1,0},{2,3},{3,2},{4,5},{5,4},{6,7},{7,6},{8,9},{9,8},{10,11... | collective-permute-start | bytes 786440 | tf_op jit(solution)/shard_map/ppermute | solution.py:325
  74.3 5.6 %collective-permute-start.15 = (bf16[64,1024]{1,0:T(8,128)(2,1)S(1)}, bf16[64,1024]{1,0:T(8,128)(2,1)S(1)}, u32[]{:S(2)}, u32[]{:S(2)}) collective-permute-start(bf16[64,1024]{1,0:T(8,128)(2,1)S(1)} %slice.15), channel_id=1, source_target_pairs={{0,2},{1,3},{2,0},{3,1},{4,6},{5,7},{6,4},{7,5},{8,10},{9,11},{10,... | collective-permute-start | bytes 393224 | tf_op jit(solution)/shard_map/ppermute | solution.py:325

commit v2 on v1

v2 whole, which is shorter than its diff:
```python
import functools
import math

import jax
import jax.numpy as jnp
from jax import lax
from jax.experimental import pallas as pl
from jax.experimental.pallas import tpu as pltpu
from jax.sharding import PartitionSpec as P

PICKED_PAGES = 6
FLOOR = -1e30
LANES = 128
HEADS_PER_TILE = 2

VMEM = pltpu.VMEM
SMEM = pltpu.SMEM
BF16 = jnp.bfloat16
F32 = jnp.float32


def in_vmem():
    return pl.BlockSpec(memory_space=VMEM)


def in_smem():
    return pl.BlockSpec(memory_space=SMEM)


def params(mib):
    return pltpu.CompilerParams(vmem_limit_bytes=mib * 2**20)


class Plan:
    def __init__(self, n, ways, rows, blocks, page):
        self.n, self.rows, self.blocks, self.page = n, rows, blocks, page
        self.group = n // blocks
        self.halves = blocks == 2 and n == 8 and ways == 4 and rows * self.group == page
        self.cross = n * 3 // 4
        self.chunks = self.group if self.halves else 1

    def block(self, me, lb):
        return (me // self.group) ^ lb if self.halves else lb

    def offsets(self, me, lb, shape):
        row = lax.broadcasted_iota(jnp.int32, shape, 0) % self.page
        if not self.halves:
            return row
        mine = (me ^ (lb * self.cross)) % self.group
        return ((row // self.rows) ^ mine) * self.rows + row % self.rows


def fetch_kernel(plan, pages_dev, select_hbm, table_hbm, stands_hbm, keys, values, k_out, v_out, info, select, table, stands, rows, k_buf, v_buf, sems, int_sems):
    me = lax.axis_index("pages")
    blocks, picked = k_buf.shape[:2]
    span = k_buf.shape[2]
    heads = k_out.shape[1]
    page = span // heads
    low = me * pages_dev
    loads = [
        pltpu.make_async_copy(a, b, int_sems.at[i])
        for i, (a, b) in enumerate(((select_hbm, select), (table_hbm, table), (stands_hbm, stands)))
    ]
    for load in loads:
        load.start()
    row = lax.broadcasted_iota(jnp.int32, (span, span), 0)
    column = lax.broadcasted_iota(jnp.int32, (span, span), 1)
    apart = (column == (row % page) * heads + row // page).astype(F32).astype(BF16)
    for load in loads:
        load.wait()
    for lb in range(blocks):
        block = plan.block(me, lb)
        stand = stands[block]
        info[lb, 1] = plan.n * pages_dev
        info[lb, 2] = stand
        others = jnp.int32(0)
        count = jnp.int32(0)
        for i in range(select.shape[1]):
            logical = select[block, i]
            local = table[logical] - low
            mine = (local >= 0) & (local < pages_dev)
            own = logical == stand
            slot = jnp.where(own, 0, jnp.maximum(picked - 1 - others, 0))
            slot = jnp.where(mine, slot, picked)
            rows[lb, slot] = local
            rows[blocks + lb, slot] = logical
            one = mine.astype(jnp.int32)
            others = others + jnp.where(own, 0, one)
            count = count + one
        info[lb, 0] = count
        info[lb, 1] = rows[blocks + lb, 0]

        @pl.when(count > 0)
        def _(lb=lb):
            for slot in range(picked):
                local = jnp.clip(rows[lb, slot], 0, pages_dev - 1)
                pltpu.make_async_copy(keys.at[local], k_buf.at[lb, slot], sems.at[lb, slot, 0]).start()
                pltpu.make_async_copy(values.at[local], v_buf.at[lb, slot], sems.at[lb, slot, 1]).start()

    for lb in range(blocks):

        @pl.when(info[lb, 0] > 0)
        def _(lb=lb):
            for g in range(heads):
                v_out[lb, g, :, LANES:] = jnp.ones((picked * page, LANES), BF16)
            for slot in range(picked):
                pltpu.make_async_copy(keys.at[0], k_buf.at[lb, slot], sems.at[lb, slot, 0]).wait()
                pltpu.make_async_copy(values.at[0], v_buf.at[lb, slot], sems.at[lb, slot, 1]).wait()
            for slot in range(picked):
                both = jnp.concatenate([k_buf[lb, slot], v_buf[lb, slot]], axis=1)
                split = jnp.dot(apart, both, preferred_element_type=F32).astype(BF16)
                for g in range(heads):
                    here = slice(slot * page, (slot + 1) * page)
                    k_out[lb, g, here, :] = split[g * page : (g + 1) * page, :LANES]
                    v_out[lb, g, here, :LANES] = split[g * page : (g + 1) * page, LANES:]


def fetch(plan, select, table, stands, keys, values):
    pages_dev, page, heads, size = keys.shape
    blocks, picked = select.shape[0], PICKED_PAGES
    span = page * heads
    return pl.pallas_call(
        functools.partial(fetch_kernel, plan, pages_dev),
        out_shape=(
            jax.ShapeDtypeStruct((blocks, heads, picked * page, size), BF16),
            jax.ShapeDtypeStruct((blocks, heads, picked * page, size + LANES), BF16),
            jax.ShapeDtypeStruct((blocks, 3), jnp.int32),
        ),
        in_specs=[pl.BlockSpec(memory_space=pltpu.HBM)] * 5,
        out_specs=(in_vmem(), in_vmem(), in_smem()),
        scratch_shapes=[
            SMEM(select.shape, jnp.int32),
            SMEM(table.shape, jnp.int32),
            SMEM(stands.shape, jnp.int32),
            SMEM((2 * blocks, picked + 1), jnp.int32),
            VMEM((blocks, picked, span, size), BF16),
            VMEM((blocks, picked, span, size), BF16),
            pltpu.SemaphoreType.DMA((blocks, picked, 2)),
            pltpu.SemaphoreType.DMA((3,)),
        ],
        compiler_params=params(16),
        cost_estimate=pl.CostEstimate(flops=2 * 10**9, bytes_accessed=8 * 2**20, transcendentals=0),
    )(*(pltpu.with_memory_space_constraint(x, pltpu.HBM) for x in (select, table, stands, keys.reshape(pages_dev, span, size), values.reshape(pages_dev, span, size))))


def pack_stats(lse, heads):
    lane = lax.broadcasted_iota(jnp.int32, lse.shape, 1)
    high = lse.astype(BF16).astype(F32)
    rest = lse - high
    middle = rest.astype(BF16).astype(F32)
    low = rest - middle
    packed = jnp.where(lane < heads, high, 0.0)
    packed = packed + jnp.where((lane >= heads) & (lane < 2 * heads), pltpu.roll(middle, heads, 1), 0.0)
    packed = packed + jnp.where((lane >= 2 * heads) & (lane < 3 * heads), pltpu.roll(low, 2 * heads, 1), 0.0)
    return packed.astype(BF16)


def unpack_stats(packed, heads):
    wide = packed.astype(F32)
    return wide + pltpu.roll(wide, LANES - heads, 1) + pltpu.roll(wide, LANES - 2 * heads, 1)


def attend_kernel(plan, heads, lb, info, *refs):
    me = lax.axis_index("pages")
    chunks, page = plan.chunks, plan.page
    queries, (k_ref, v_ref), outs = refs[:chunks], refs[chunks : chunks + 2], refs[chunks + 2 :]
    kv_heads, size = k_ref.shape[1], k_ref.shape[3]
    repeat = heads // kv_heads
    width = heads * size
    part = page // chunks
    tile = math.gcd(repeat, HEADS_PER_TILE)
    scale = size**-0.5 * math.log2(math.e)
    lane = lax.broadcasted_iota(jnp.int32, (page, LANES), 1)

    @pl.when(info[lb, 0] > 0)
    def _():
        shape = (tile * page, page)
        key_pos = info[lb, 1] * page + lax.broadcasted_iota(jnp.int32, shape, 1)
        query_pos = info[lb, 2] * page + plan.offsets(me, lb, shape)
        allowed = key_pos <= query_pos
        stats = jnp.zeros((page, LANES), F32)
        for g in range(kv_heads):
            for t in range(0, repeat, tile):
                first = g * repeat + t
                q = jnp.concatenate(
                    [m[:, h * size : (h + 1) * size] for h in range(first, first + tile) for m in queries], axis=0
                )
                scores = scale * lax.dot_general(
                    q, k_ref[lb, g], (((1,), (1,)), ((), ())), preferred_element_type=F32
                )
                scores = jnp.concatenate([jnp.where(allowed, scores[:, :page], FLOOR), scores[:, page:]], axis=1)
                peak = jnp.max(scores, axis=1, keepdims=True)
                weights = jnp.exp2(scores - peak).astype(BF16)
                both = jnp.dot(weights, v_ref[lb, g], preferred_element_type=F32)
                total = both[:, size:]
                out = (both[:, :size] / total).astype(BF16)
                lse = peak + jnp.log2(total)
                for i in range(tile):
                    h = first + i
                    stats = jnp.where(lane == h, lse[i * page : (i + 1) * page], stats)
                    for c in range(chunks):
                        outs[c][:, h * size : (h + 1) * size] = out[i * page + c * part : i * page + (c + 1) * part]
        packed = pack_stats(stats, heads)
        for c in range(chunks):
            outs[c][:, width:] = packed[c * part : (c + 1) * part]

    @pl.when(info[lb, 0] == 0)
    def _():
        for c in range(chunks):
            outs[c][:, :width] = jnp.zeros((part, width), BF16)
            outs[c][:, width:] = pack_stats(jnp.full((part, LANES), FLOOR, F32), heads)


def attend(plan, heads, lb, pages, queries):
    keys, values, info = pages
    part = plan.page // plan.chunks
    shape = jax.ShapeDtypeStruct((part, queries[0].shape[1] + LANES), BF16)
    return pl.pallas_call(
        functools.partial(attend_kernel, plan, heads, lb),
        out_shape=(shape,) * plan.chunks,
        in_specs=[in_smem()] + [in_vmem()] * (len(queries) + 2),
        out_specs=(in_vmem(),) * plan.chunks,
        compiler_params=params(32),
        cost_estimate=pl.CostEstimate(flops=2 * 10**9, bytes_accessed=4 * 2**20, transcendentals=10**6),
    )(info, *queries, keys, values)


def merged(parts, stats, heads, size):
    top = functools.reduce(jnp.maximum, stats)
    shares = [jnp.exp2(s - top) for s in stats]
    total = functools.reduce(jnp.add, shares)
    shares = [s / total for s in shares]

    def head(h):
        return functools.reduce(
            jnp.add, [p(h).astype(F32) * s[:, h : h + 1] for p, s in zip(parts, shares, strict=True)]
        )

    return head, top + jnp.log2(total)


def merge_kernel(heads, *refs):
    sources, out = refs[:-1], refs[-1]
    width = out.shape[1] - LANES
    size = width // heads
    head, lse = merged(
        [lambda h, r=r: r[:, h * size : (h + 1) * size] for r in sources],
        [unpack_stats(r[:, width:], heads) for r in sources],
        heads,
        size,
    )
    for h in range(heads):
        out[:, h * size : (h + 1) * size] = head(h).astype(BF16)
    out[:, width:] = pack_stats(lse, heads)


def merge(heads, *sources):
    return pl.pallas_call(
        functools.partial(merge_kernel, heads),
        out_shape=jax.ShapeDtypeStruct(sources[0].shape, BF16),
        in_specs=[in_vmem()] * len(sources),
        out_specs=in_vmem(),
        compiler_params=params(8),
    )(*sources)


def finish_kernel(heads, near, far, out):
    width = out.shape[1]
    size = width // heads
    head, _ = merged(
        [lambda h, r=r: r[:, h * size : (h + 1) * size] for r in (near, far)],
        [unpack_stats(r[:, width:], heads) for r in (near, far)],
        heads,
        size,
    )
    for h in range(heads):
        out[:, h * size : (h + 1) * size] = head(h).astype(BF16)


def finish(heads, near, far):
    return pl.pallas_call(
        functools.partial(finish_kernel, heads),
        out_shape=jax.ShapeDtypeStruct((near.shape[0], near.shape[1] - LANES), BF16),
        in_specs=[in_vmem()] * 2,
        out_specs=in_vmem(),
        compiler_params=params(8),
    )(near, far)


def project_kernel(plan, ways, *refs):
    sources, weight, outs, rows_ref = refs[: plan.n], refs[plan.n], refs[plan.n + 1 : -1], refs[-1]
    me, column = lax.axis_index("pages"), lax.axis_index("mp")
    rows = plan.rows
    holders = plan.n // ways
    for k in range(plan.group):
        for half in range(2):
            device = me ^ k ^ (half * plan.cross)
            place = ((device // holders) ^ column) * holders + device % holders
            rows_ref[pl.ds(pl.multiple_of(place * rows, rows), rows), :] = sources[half * plan.group + k][...]
    part = holders * rows
    product = jnp.dot(rows_ref[...], weight[...], preferred_element_type=F32)
    keep, send = outs
    for i, w in enumerate(range(0, ways, 2)):
        keep[i * part : (i + 1) * part, :] = product[w * part : (w + 1) * part]
        send[i * part : (i + 1) * part, :] = product[(w + 1) * part : (w + 2) * part].astype(BF16)


def project(plan, ways, sources, weight):
    total = plan.n * plan.rows
    columns = weight.shape[1]
    return pl.pallas_call(
        functools.partial(project_kernel, plan, ways),
        out_shape=(
            jax.ShapeDtypeStruct((total // 2, columns), F32),
            jax.ShapeDtypeStruct((total // 2, columns), BF16),
        ),
        in_specs=[in_vmem()] * (plan.n + 1),
        out_specs=(in_vmem(), in_vmem()),
        scratch_shapes=[VMEM((total, weight.shape[0]), BF16)],
        compiler_params=params(24),
    )(*sources, weight)


def swap(x, axis, distance):
    n = lax.axis_size(axis)
    return lax.ppermute(x, axis, [(i, i ^ distance) for i in range(n)])


def spread(x, plan):
    return [x] + [swap(x, "pages", k) for k in range(1, plan.group)]


def by_halves(plan, heads, queries, weight, pages):
    far = swap(queries, "pages", plan.cross)
    chunks = [spread(queries, plan), spread(far, plan)]
    near = []
    for lb in range(plan.blocks):
        outs = attend(plan, heads, lb, pages, chunks[lb])
        near.append(merge(heads, outs[0], *(swap(outs[k], "pages", k) for k in range(1, plan.group))))
    across = [swap(x, "pages", plan.cross) for x in near]
    others = spread(finish(heads, near[1], across[0]), plan)
    mine = spread(finish(heads, near[0], across[1]), plan)
    keep, send = project(plan, lax.axis_size("mp"), mine + others, weight)
    total = keep + swap(send, "mp", 1).astype(F32)
    part = total.shape[0] // 2
    return (total[:part] + swap(total[part:].astype(BF16), "mp", 2).astype(F32)).astype(BF16)


def by_gathers(plan, heads, queries, weight, pages):
    width = queries.shape[1]
    size = width // heads
    gathered = lax.all_gather(queries, "pages", axis=0, tiled=True)
    rows = gathered.shape[0]
    outs = [
        attend(plan, heads, lb, pages, [gathered[lb * plan.page : (lb + 1) * plan.page]])[0]
        for lb in range(plan.blocks)
    ]
    out = jnp.concatenate(outs, axis=0)
    packed = out[:, width : width + 3 * heads].astype(F32)
    lse = packed[:, :heads] + packed[:, heads : 2 * heads] + packed[:, 2 * heads :]
    every = lax.all_gather(lse, "pages")
    top = jnp.max(every, axis=0)
    share = jnp.exp2(lse - top) / jnp.sum(jnp.exp2(every - top), axis=0)
    part = (out[:, :width].reshape(rows, heads, size).astype(F32) * share[..., None]).reshape(1, rows, width)
    received = lax.all_to_all(part.astype(BF16), "pages", split_axis=1, concat_axis=0, tiled=True)
    mixed = jnp.sum(received, axis=0, dtype=F32).astype(BF16)
    terms = jnp.dot(lax.all_gather(mixed, "pages", axis=0, tiled=True), weight, preferred_element_type=F32)
    return lax.psum_scatter(terms, "mp", scatter_dimension=0, tiled=True).astype(BF16)


def per_device(queries, cached_keys, cached_values, out_weight, select, page_table, block_page):
    n, ways = lax.axis_size("pages"), lax.axis_size("mp")
    plan = Plan(n, ways, queries.shape[0], select.shape[0], cached_keys.shape[1])
    heads = queries.shape[1] // cached_keys.shape[3]
    pages = fetch(plan, select, page_table, block_page, cached_keys, cached_values)
    way = by_halves if plan.halves else by_gathers
    return way(plan, heads, queries, out_weight, pages)


def solution(mesh):
    placed = (
        P("pages", "mp"),
        P("pages", None, "mp", None),
        P("pages", None, "mp", None),
        P("mp", "pages"),
        P(),
        P(),
        P(),
    )
    return jax.shard_map(
        per_device, mesh=mesh, in_specs=placed, out_specs=P("mp", "pages"), check_vma=False
    )
```

time: 80.3 us -> 61.9 us (0.77)
  waiting for transfers between devices: 35.2 us -> 16.3 us
  starting transfers between devices: 24.2 us -> 31.6 us
  local copies, waits for them, and re-layouts: 4.47 us -> 0.02 us
  Pallas kernels: 15.7 us -> 12.9 us
    ppermute x16 -> x23, waiting for transfers between devices: 35.2 us -> 16.3 us  [swap(): return lax.ppermute(x, axis, [(i, i ^ distance) for i in range(n)])]
    ppermute x16 -> x23, starting transfers between devices: 24.2 us -> 31.6 us  [swap(): return lax.ppermute(x, axis, [(i, i ^ distance) for i in range(n)])]
    unnamed x16 -> x4, local copies, waits for them, and re-layouts: 4.45 us -> 0.01 us
    pallas_call x1, Pallas kernels: 7.21 us -> 3.7 us  [fetch(): pl.pallas_call(functools.partial(fetch_kernel, plan, pages_dev), out_shap...]
    pallas_call x1 -> x2, Pallas kernels: 5.79 us -> 6.29 us  [attend(): pl.pallas_call(functools.partial(attend_kernel, plan, heads, lb), out_sha...]
  transfers between devices with their start and end apart: 16 -> 23, of which waited for: 11 -> 10; matrix products, arithmetic and copies ran while one was open for 0% -> 0% of each run, Pallas kernels for 9% -> 19%
where the time goes in v2:
time: 61.9 us; the launch traced here: 61.7 us
  starting transfers between devices  31.6 us (51%)
  waiting for transfers between devices  16.3 us (26%)
  Pallas kernels  12.9 us (21%)
  other arithmetic  0.75 us (1%)
    ppermute x23, starting transfers between devices, swap(): return lax.ppermute(x, axis, [(i, i ^ distance) for i in range(n)])  31.6 us
    ppermute x23, waiting for transfers between devices, swap(): return lax.ppermute(x, axis, [(i, i ^ distance) for i in range(n)])  16.3 us
    pallas_call x2, Pallas kernels, attend(): pl.pallas_call(functools.partial(attend_kernel, plan, heads, lb), out_sha...  6.29 us
    pallas_call x1, Pallas kernels, fetch(): pl.pallas_call(functools.partial(fetch_kernel, plan, pages_dev), out_shap...  3.7 us
    pallas_call x1, Pallas kernels, project(): pl.pallas_call(functools.partial(project_kernel, plan, ways), out_shape=(...  1.33 us
  transfers between devices with their start and end apart: 23, of which 10 were waited for; matrix products, arithmetic and copies ran while one was open for 0% of the time, Pallas kernels for 19%

profile of v2, /device:TPU:0, one launch (start us, length us, event | category | flops | bytes accessed | tf_op | source)
XLA Modules:
  0.0 61.7 jit_solution(12914615594692857790)
XLA Ops:
  0.0 5.0 %collective-permute-start.6 = (bf16[32,2048]{1,0:T(8,128)(2,1)}, bf16[32,2048]{1,0:T(8,128)(2,1)S(1)}, u32[]{:S(2)}, u32[]{:S(2)}) collective-permute-start(bf16[32,2048]{1,0:T(8,128)(2,1)} %refs_0_.1), channel_id=1, source_target_pairs={{0,24},{4,28},{8,16},{12,20},{16,8},{20,12},{24,0},{28,4},{1,25},{... | collective-permute-start | bytes 393224 | tf_op jit(solution)/shard_map/ppermute | solution.py:326
  5.1 1.5 %collective-permute-start = (bf16[32,2048]{1,0:T(8,128)(2,1)}, bf16[32,2048]{1,0:T(8,128)(2,1)S(1)}, u32[]{:S(2)}, u32[]{:S(2)}) collective-permute-start(bf16[32,2048]{1,0:T(8,128)(2,1)} %refs_0_.1), channel_id=1, source_target_pairs={{0,4},{4,0},{8,12},{12,8},{16,20},{20,16},{24,28},{28,24},{1,5},{5... | collective-permute-start | bytes 393224 | tf_op jit(solution)/shard_map/ppermute | solution.py:326
  6.5 0.0 collective-permute-start.1
  6.5 2.0 %collective-permute-start.2 = (bf16[32,2048]{1,0:T(8,128)(2,1)}, bf16[32,2048]{1,0:T(8,128)(2,1)S(1)}, u32[]{:S(2)}, u32[]{:S(2)}) collective-permute-start(bf16[32,2048]{1,0:T(8,128)(2,1)} %refs_0_.1), channel_id=1, source_target_pairs={{0,12},{4,8},{8,4},{12,0},{16,28},{20,24},{24,20},{28,16},{1,13},{... | collective-permute-start | bytes 393224 | tf_op jit(solution)/shard_map/ppermute | solution.py:326
  8.5 3.7 %shard_map.73 = (bf16[2,2,768,128]{3,2,1,0:T(8,128)(2,1)S(1)}, bf16[2,2,768,256]{3,2,1,0:T(8,128)(2,1)S(1)}, s32[2,3]{1,0:T(2,128)S(1)}) custom-call(s32[2,24]{1,0:T(2,128)} %select_hbm.1, s32[128]{0:T(128)} %table_hbm.1, s32[2]{0:T(128)} %stands_hbm.1, bf16[16,256,128]{2,1,0:T(8,128)(2,1)} %bitcast.2, bf16[16,256,128]{2,1,0:T(8,128)(2,1)} %bitcast.3), custom_call_target="tpu_custom_call" | custom-call | flops 2000000000 | bytes 8388608 | tf_op jit(solution)/shard_map/pallas_call | solution.py:122
  12.3 0.1 collective-permute-start.7
  12.3 1.5 %collective-permute-start.8 = (bf16[32,2048]{1,0:T(8,128)(2,1)S(1)}, bf16[32,2048]{1,0:T(8,128)(2,1)S(1)}, u32[]{:S(2)}, u32[]{:S(2)}) collective-permute-start(bf16[32,2048]{1,0:T(8,128)(2,1)S(1)} %collective-permute-done.6.refs_0_), channel_id=1, source_target_pairs={{0,8},{4,12},{8,0},{12,4},{16,24},{20,28},{24,16},{28,20},{1,9},{5... | collective-permute-start | bytes 393224 | tf_op jit(solution)/shard_map/ppermute | solution.py:326
  13.8 0.0 collective-permute-done.refs_1_
  13.8 2.0 %collective-permute-start.9 = (bf16[32,2048]{1,0:T(8,128)(2,1)S(1)}, bf16[32,2048]{1,0:T(8,128)(2,1)S(1)}, u32[]{:S(2)}, u32[]{:S(2)}) collective-permute-start(bf16[32,2048]{1,0:T(8,128)(2,1)S(1)} %collective-permute-done.6.refs_0_), channel_id=1, source_target_pairs={{0,12},{4,8},{8,4},{12,0},{16,28},{20,24},{24,20},{28,16},{1,13},{... | collective-permute-start | bytes 393224 | tf_op jit(solution)/shard_map/ppermute | solution.py:326
  15.8 0.2 collective-permute-done.2.refs_3_
  16.1 3.1 %shard_map.74 = (bf16[32,2176]{1,0:T(8,128)(2,1)S(1)}, bf16[32,2176]{1,0:T(8,128)(2,1)S(1)}, bf16[32,2176]{1,0:T(8,128)(2,1)S(1)}, bf16[32,2176]{1,0:T(8,128)(2,1)S(1)}) custom-call(s32[2,3]{1,0:T(2,128)S(1)} %get-tuple-element.18.info, bf16[32,2048]{1,0:T(8,128)(2,1)S(1)} %copy-done.1, bf16[32,2048]{1,0:T(8,128)(2,1)S(1)} %collective-permute-done.refs_1_, ...), custom_call_target="tpu_custom_call" | custom-call | flops 2000000000 | bytes 4194304 | tf_op jit(solution)/shard_map/pallas_call | solution.py:218
  19.2 0.1 collective-permute-start.3
  19.3 2.5 %collective-permute-start.4 = (bf16[32,2176]{1,0:T(8,128)(2,1)S(1)}, bf16[32,2176]{1,0:T(8,128)(2,1)S(1)}, u32[]{:S(2)}, u32[]{:S(2)}) collective-permute-start(bf16[32,2176]{1,0:T(8,128)(2,1)S(1)} %get-tuple-element.23), channel_id=1, source_target_pairs={{0,8},{4,12},{8,0},{12,4},{16,24},{20,28},{24,16},{28,20},{1,9},{5... | collective-permute-start | bytes 417800 | tf_op jit(solution)/shard_map/ppermute | solution.py:326
  21.8 0.0 collective-permute-done.7.refs_1_
  21.8 1.0 %collective-permute-start.5 = (bf16[32,2176]{1,0:T(8,128)(2,1)S(1)}, bf16[32,2176]{1,0:T(8,128)(2,1)S(1)}, u32[]{:S(2)}, u32[]{:S(2)}) collective-permute-start(bf16[32,2176]{1,0:T(8,128)(2,1)S(1)} %get-tuple-element.24), channel_id=1, source_target_pairs={{0,12},{4,8},{8,4},{12,0},{16,28},{20,24},{24,20},{28,16},{1,13},{... | collective-permute-start | bytes 417800 | tf_op jit(solution)/shard_map/ppermute | solution.py:326
  22.8 0.0 collective-permute-done.8.refs_2_
  22.8 0.0 collective-permute-done.9.refs_3_
  22.8 3.1 %shard_map.76 = (bf16[32,2176]{1,0:T(8,128)(2,1)S(1)}, bf16[32,2176]{1,0:T(8,128)(2,1)S(1)}, bf16[32,2176]{1,0:T(8,128)(2,1)S(1)}, bf16[32,2176]{1,0:T(8,128)(2,1)S(1)}) custom-call(s32[2,3]{1,0:T(2,128)S(1)} %get-tuple-element.18.info, bf16[32,2048]{1,0:T(8,128)(2,1)S(1)} %collective-permute-done.6.refs_0_, ...), custom_call_target="tpu_custom_call" | custom-call | flops 2000000000 | bytes 4194304 | tf_op jit(solution)/shard_map/pallas_call | solution.py:218
  25.9 0.1 collective-permute-start.10
  26.0 2.5 %collective-permute-start.11 = (bf16[32,2176]{1,0:T(8,128)(2,1)S(1)}, bf16[32,2176]{1,0:T(8,128)(2,1)S(1)}, u32[]{:S(2)}, u32[]{:S(2)}) collective-permute-start(bf16[32,2176]{1,0:T(8,128)(2,1)S(1)} %get-tuple-element.27), channel_id=1, source_target_pairs={{0,8},{4,12},{8,0},{12,4},{16,24},{20,28},{24,16},{28,20},{1,9},{5... | collective-permute-start | bytes 417800 | tf_op jit(solution)/shard_map/ppermute | solution.py:326
  28.5 0.0 collective-permute-done.3.refs_1_
  28.5 1.0 %collective-permute-start.12 = (bf16[32,2176]{1,0:T(8,128)(2,1)S(1)}, bf16[32,2176]{1,0:T(8,128)(2,1)S(1)}, u32[]{:S(2)}, u32[]{:S(2)}) collective-permute-start(bf16[32,2176]{1,0:T(8,128)(2,1)S(1)} %get-tuple-element.28), channel_id=1, source_target_pairs={{0,12},{4,8},{8,4},{12,0},{16,28},{20,24},{24,20},{28,16},{1,13},{... | collective-permute-start | bytes 417800 | tf_op jit(solution)/shard_map/ppermute | solution.py:326
  29.5 0.5 shard_map.75.near
  30.0 1.7 %collective-permute-start.17 = (bf16[32,2176]{1,0:T(8,128)(2,1)S(1)}, bf16[32,2176]{1,0:T(8,128)(2,1)S(1)}, u32[]{:S(2)}, u32[]{:S(2)}) collective-permute-start(bf16[32,2176]{1,0:T(8,128)(2,1)S(1)} %shard_map.75.near), channel_id=1, source_target_pairs={{0,24},{4,28},{8,16},{12,20},{16,8},{20,12},{24,0},{28,4},{1,25},{... | collective-permute-start | bytes 417800 | tf_op jit(solution)/shard_map/ppermute | solution.py:326
  31.7 0.7 %collective-permute-done.10.refs_1_ = bf16[32,2176]{1,0:T(8,128)(2,1)S(1)} collective-permute-done((bf16[32,2176]{1,0:T(8,128)(2,1)S(1)}, bf16[32,2176]{1,0:T(8,128)(2,1)S(1)}, u32[]{:S(2)}, u32[]{:S(2)}) %collective-permute-start.10) | collective-permute-done | bytes 139296 | tf_op jit(solution)/shard_map/ppermute | solution.py:326
  32.3 3.5 %collective-permute-done.12.refs_3_ = bf16[32,2176]{1,0:T(8,128)(2,1)S(1)} collective-permute-done((bf16[32,2176]{1,0:T(8,128)(2,1)S(1)}, bf16[32,2176]{1,0:T(8,128)(2,1)S(1)}, u32[]{:S(2)}, u32[]{:S(2)}) %collective-permute-start.12) | collective-permute-done | bytes 139296 | tf_op jit(solution)/shard_map/ppermute | solution.py:326
  35.8 0.5 shard_map.77.near
  36.3 1.1 %collective-permute-start.13 = (bf16[32,2176]{1,0:T(8,128)(2,1)S(1)}, bf16[32,2176]{1,0:T(8,128)(2,1)S(1)}, u32[]{:S(2)}, u32[]{:S(2)}) collective-permute-start(bf16[32,2176]{1,0:T(8,128)(2,1)S(1)} %shard_map.77.near), channel_id=1, source_target_pairs={{0,24},{4,28},{8,16},{12,20},{16,8},{20,12},{24,0},{28,4},{1,25},{... | collective-permute-start | bytes 417800 | tf_op jit(solution)/shard_map/ppermute | solution.py:326
  37.4 1.1 %collective-permute-done.17.far = bf16[32,2176]{1,0:T(8,128)(2,1)S(1)} collective-permute-done((bf16[32,2176]{1,0:T(8,128)(2,1)S(1)}, bf16[32,2176]{1,0:T(8,128)(2,1)S(1)}, u32[]{:S(2)}, u32[]{:S(2)}) %collective-permute-start.17) | collective-permute-done | bytes 139296 | tf_op jit(solution)/shard_map/ppermute | solution.py:326
  38.5 0.3 shard_map.79.refs_4_
  38.8 2.4 %collective-permute-start.18 = (bf16[32,2048]{1,0:T(8,128)(2,1)S(1)}, bf16[32,2048]{1,0:T(8,128)(2,1)S(1)}, u32[]{:S(2)}, u32[]{:S(2)}) collective-permute-start(bf16[32,2048]{1,0:T(8,128)(2,1)S(1)} %shard_map.79.refs_4_), channel_id=1, source_target_pairs={{0,4},{4,0},{8,12},{12,8},{16,20},{20,16},{24,28},{28,24},{1,5},{5... | collective-permute-start | bytes 393224 | tf_op jit(solution)/shard_map/ppermute | solution.py:326
  41.2 1.3 %collective-permute-start.19 = (bf16[32,2048]{1,0:T(8,128)(2,1)S(1)}, bf16[32,2048]{1,0:T(8,128)(2,1)S(1)}, u32[]{:S(2)}, u32[]{:S(2)}) collective-permute-start(bf16[32,2048]{1,0:T(8,128)(2,1)S(1)} %shard_map.79.refs_4_), channel_id=1, source_target_pairs={{0,8},{4,12},{8,0},{12,4},{16,24},{20,28},{24,16},{28,20},{1,9},{5... | collective-permute-start | bytes 393224 | tf_op jit(solution)/shard_map/ppermute | solution.py:326
  42.6 0.2 collective-permute-start.20
  42.8 0.4 collective-permute-done.13.far
  43.2 0.3 shard_map.78.refs_0_
  43.5 1.6 %collective-permute-start.14 = (bf16[32,2048]{1,0:T(8,128)(2,1)S(1)}, bf16[32,2048]{1,0:T(8,128)(2,1)S(1)}, u32[]{:S(2)}, u32[]{:S(2)}) collective-permute-start(bf16[32,2048]{1,0:T(8,128)(2,1)S(1)} %shard_map.78.refs_0_), channel_id=1, source_target_pairs={{0,4},{4,0},{8,12},{12,8},{16,20},{20,16},{24,28},{28,24},{1,5},{5... | collective-permute-start | bytes 393224 | tf_op jit(solution)/shard_map/ppermute | solution.py:326
  45.1 1.3 %collective-permute-start.15 = (bf16[32,2048]{1,0:T(8,128)(2,1)S(1)}, bf16[32,2048]{1,0:T(8,128)(2,1)S(1)}, u32[]{:S(2)}, u32[]{:S(2)}) collective-permute-start(bf16[32,2048]{1,0:T(8,128)(2,1)S(1)} %shard_map.78.refs_0_), channel_id=1, source_target_pairs={{0,8},{4,12},{8,0},{12,4},{16,24},{20,28},{24,16},{28,20},{1,9},{5... | collective-permute-start | bytes 393224 | tf_op jit(solution)/shard_map/ppermute | solution.py:326
  46.5 1.0 %collective-permute-start.16 = (bf16[32,2048]{1,0:T(8,128)(2,1)S(1)}, bf16[32,2048]{1,0:T(8,128)(2,1)S(1)}, u32[]{:S(2)}, u32[]{:S(2)}) collective-permute-start(bf16[32,2048]{1,0:T(8,128)(2,1)S(1)} %shard_map.78.refs_0_), channel_id=1, source_target_pairs={{0,12},{4,8},{8,4},{12,0},{16,28},{20,24},{24,20},{28,16},{1,13},{... | collective-permute-start | bytes 393224 | tf_op jit(solution)/shard_map/ppermute | solution.py:326
  47.5 2.0 %collective-permute-done.20.refs_7_ = bf16[32,2048]{1,0:T(8,128)(2,1)S(1)} collective-permute-done((bf16[32,2048]{1,0:T(8,128)(2,1)S(1)}, bf16[32,2048]{1,0:T(8,128)(2,1)S(1)}, u32[]{:S(2)}, u32[]{:S(2)}) %collective-permute-start.20) | collective-permute-done | bytes 131104 | tf_op jit(solution)/shard_map/ppermute | solution.py:326
  49.5 1.3 %collective-permute-done.14.refs_1_ = bf16[32,2048]{1,0:T(8,128)(2,1)S(1)} collective-permute-done((bf16[32,2048]{1,0:T(8,128)(2,1)S(1)}, bf16[32,2048]{1,0:T(8,128)(2,1)S(1)}, u32[]{:S(2)}, u32[]{:S(2)}) %collective-permute-start.14) | collective-permute-done | bytes 131104 | tf_op jit(solution)/shard_map/ppermute | solution.py:326
  50.8 1.5 %collective-permute-done.16.refs_3_ = bf16[32,2048]{1,0:T(8,128)(2,1)S(1)} collective-permute-done((bf16[32,2048]{1,0:T(8,128)(2,1)S(1)}, bf16[32,2048]{1,0:T(8,128)(2,1)S(1)}, u32[]{:S(2)}, u32[]{:S(2)}) %collective-permute-start.16) | collective-permute-done | bytes 131104 | tf_op jit(solution)/shard_map/ppermute | solution.py:326
  52.3 1.3 %shard_map.80 = (f32[128,1024]{1,0:T(8,128)S(1)}, bf16[128,1024]{1,0:T(8,128)(2,1)S(1)}) custom-call(bf16[32,2048]{1,0:T(8,128)(2,1)S(1)} %shard_map.78.refs_0_, bf16[32,2048]{1,0:T(8,128)(2,1)S(1)} %collective-permute-done.14.refs_1_, bf16[32,2048]{1,0:T(8,128)(2,1)S(1)} %collective-permute-done.15.refs_2_, ...), custom_call_target="tpu_custom_call" | custom-call | tf_op jit(solution)/shard_map/pallas_call | solution.py:311
  53.7 0.1 collective-permute-start.21
  53.8 1.5 %collective-permute-done.21 = bf16[128,1024]{1,0:T(8,128)(2,1)S(1)} collective-permute-done((bf16[128,1024]{1,0:T(8,128)(2,1)S(1)}, bf16[128,1024]{1,0:T(8,128)(2,1)S(1)}, u32[]{:S(2)}, u32[]{:S(2)}) %collective-permute-start.21) | collective-permute-done | bytes 262176 | tf_op jit(solution)/shard_map/ppermute | solution.py:326
  55.3 0.1 convert_add_fusion
  55.4 1.6 %collective-permute-start.22 = (bf16[64,1024]{1,0:T(8,128)(2,1)S(1)}, bf16[64,1024]{1,0:T(8,128)(2,1)S(1)}, u32[]{:S(2)}, u32[]{:S(2)}) collective-permute-start(bf16[64,1024]{1,0:T(8,128)(2,1)S(1)} %slice.15), channel_id=1, source_target_pairs={{0,2},{1,3},{2,0},{3,1},{4,6},{5,7},{6,4},{7,5},{8,10},{9,11},{10,... | collective-permute-start | bytes 393224 | tf_op jit(solution)/shard_map/ppermute | solution.py:326
  57.0 4.0 %collective-permute-done.22 = bf16[64,1024]{1,0:T(8,128)(2,1)S(1)} collective-permute-done((bf16[64,1024]{1,0:T(8,128)(2,1)S(1)}, bf16[64,1024]{1,0:T(8,128)(2,1)S(1)}, u32[]{:S(2)}, u32[]{:S(2)}) %collective-permute-start.22) | collective-permute-done | bytes 131104 | tf_op jit(solution)/shard_map/ppermute | solution.py:326
  61.0 0.7 %fusion = bf16[64,1024]{1,0:T(8,128)(2,1)} fusion(f32[128,1024]{1,0:T(8,128)S(1)} %convert_add_fusion, bf16[64,1024]{1,0:T(8,128)(2,1)S(1)} %collective-permute-done.22), kind=kLoop, calls=%fused_computation.3 | loop fusion | flops 196608 | bytes 524288 | tf_op jit(solution)/shard_map/convert_element_type | solution.py:346
  (13 shorter events, 0.0 us)
Async XLA Ops:
  0.0 16.1 %copy-start.1 = (bf16[32,2048]{1,0:T(8,128)(2,1)S(1)}, bf16[32,2048]{1,0:T(8,128)(2,1)}, u32[]{:S(2)}) copy-start(bf16[32,2048]{1,0:T(8,128)(2,1)} %refs_0_.1) | copy-start | bytes 393220
  0.0 12.3 %collective-permute-start.6 = (bf16[32,2048]{1,0:T(8,128)(2,1)}, bf16[32,2048]{1,0:T(8,128)(2,1)S(1)}, u32[]{:S(2)}, u32[]{:S(2)}) collective-permute-start(bf16[32,2048]{1,0:T(8,128)(2,1)} %refs_0_.1), channel_id=1, source_target_pairs={{0,24},{4,28},{8,16},{12,20},{16,8},{20,12},{24,0},{28,4},{1,25},{... | collective-permute-start | bytes 393224 | tf_op jit(solution)/shard_map/ppermute | solution.py:326
  5.1 8.8 %collective-permute-start = (bf16[32,2048]{1,0:T(8,128)(2,1)}, bf16[32,2048]{1,0:T(8,128)(2,1)S(1)}, u32[]{:S(2)}, u32[]{:S(2)}) collective-permute-start(bf16[32,2048]{1,0:T(8,128)(2,1)} %refs_0_.1), channel_id=1, source_target_pairs={{0,4},{4,0},{8,12},{12,8},{16,20},{20,16},{24,28},{28,24},{1,5},{5... | collective-permute-start | bytes 393224 | tf_op jit(solution)/shard_map/ppermute | solution.py:326
  6.5 9.3 %collective-permute-start.1 = (bf16[32,2048]{1,0:T(8,128)(2,1)}, bf16[32,2048]{1,0:T(8,128)(2,1)S(1)}, u32[]{:S(2)}, u32[]{:S(2)}) collective-permute-start(bf16[32,2048]{1,0:T(8,128)(2,1)} %refs_0_.1), channel_id=1, source_target_pairs={{0,8},{4,12},{8,0},{12,4},{16,24},{20,28},{24,16},{28,20},{1,9},{5... | collective-permute-start | bytes 393224 | tf_op jit(solution)/shard_map/ppermute | solution.py:326
  6.5 9.5 %collective-permute-start.2 = (bf16[32,2048]{1,0:T(8,128)(2,1)}, bf16[32,2048]{1,0:T(8,128)(2,1)S(1)}, u32[]{:S(2)}, u32[]{:S(2)}) collective-permute-start(bf16[32,2048]{1,0:T(8,128)(2,1)} %refs_0_.1), channel_id=1, source_target_pairs={{0,12},{4,8},{8,4},{12,0},{16,28},{20,24},{24,20},{28,16},{1,13},{... | collective-permute-start | bytes 393224 | tf_op jit(solution)/shard_map/ppermute | solution.py:326
  12.3 9.6 %collective-permute-start.7 = (bf16[32,2048]{1,0:T(8,128)(2,1)S(1)}, bf16[32,2048]{1,0:T(8,128)(2,1)S(1)}, u32[]{:S(2)}, u32[]{:S(2)}) collective-permute-start(bf16[32,2048]{1,0:T(8,128)(2,1)S(1)} %collective-permute-done.6.refs_0_), channel_id=1, source_target_pairs={{0,4},{4,0},{8,12},{12,8},{16,20},{20,16},{24,28},{28,24},{1,5},{5... | collective-permute-start | bytes 393224 | tf_op jit(solution)/shard_map/ppermute | solution.py:326
  12.3 10.4 %collective-permute-start.8 = (bf16[32,2048]{1,0:T(8,128)(2,1)S(1)}, bf16[32,2048]{1,0:T(8,128)(2,1)S(1)}, u32[]{:S(2)}, u32[]{:S(2)}) collective-permute-start(bf16[32,2048]{1,0:T(8,128)(2,1)S(1)} %collective-permute-done.6.refs_0_), channel_id=1, source_target_pairs={{0,8},{4,12},{8,0},{12,4},{16,24},{20,28},{24,16},{28,20},{1,9},{5... | collective-permute-start | bytes 393224 | tf_op jit(solution)/shard_map/ppermute | solution.py:326
  13.8 9.0 %collective-permute-start.9 = (bf16[32,2048]{1,0:T(8,128)(2,1)S(1)}, bf16[32,2048]{1,0:T(8,128)(2,1)S(1)}, u32[]{:S(2)}, u32[]{:S(2)}) collective-permute-start(bf16[32,2048]{1,0:T(8,128)(2,1)S(1)} %collective-permute-done.6.refs_0_), channel_id=1, source_target_pairs={{0,12},{4,8},{8,4},{12,0},{16,28},{20,24},{24,20},{28,16},{1,13},{... | collective-permute-start | bytes 393224 | tf_op jit(solution)/shard_map/ppermute | solution.py:326
  19.2 9.3 %collective-permute-start.3 = (bf16[32,2176]{1,0:T(8,128)(2,1)S(1)}, bf16[32,2176]{1,0:T(8,128)(2,1)S(1)}, u32[]{:S(2)}, u32[]{:S(2)}) collective-permute-start(bf16[32,2176]{1,0:T(8,128)(2,1)S(1)} %get-tuple-element.22), channel_id=1, source_target_pairs={{0,4},{4,0},{8,12},{12,8},{16,20},{20,16},{24,28},{28,24},{1,5},{5... | collective-permute-start | bytes 417800 | tf_op jit(solution)/shard_map/ppermute | solution.py:326
  19.3 10.2 %collective-permute-start.4 = (bf16[32,2176]{1,0:T(8,128)(2,1)S(1)}, bf16[32,2176]{1,0:T(8,128)(2,1)S(1)}, u32[]{:S(2)}, u32[]{:S(2)}) collective-permute-start(bf16[32,2176]{1,0:T(8,128)(2,1)S(1)} %get-tuple-element.23), channel_id=1, source_target_pairs={{0,8},{4,12},{8,0},{12,4},{16,24},{20,28},{24,16},{28,20},{1,9},{5... | collective-permute-start | bytes 417800 | tf_op jit(solution)/shard_map/ppermute | solution.py:326
  21.8 30.5 %copy-start = (bf16[2048,1024]{1,0:T(8,128)(2,1)S(1)}, bf16[2048,1024]{1,0:T(8,128)(2,1)}, u32[]{:S(2)}) copy-start(bf16[2048,1024]{1,0:T(8,128)(2,1)} %refs_8_.1) | copy-start | bytes 12582916
  21.8 7.7 %collective-permute-start.5 = (bf16[32,2176]{1,0:T(8,128)(2,1)S(1)}, bf16[32,2176]{1,0:T(8,128)(2,1)S(1)}, u32[]{:S(2)}, u32[]{:S(2)}) collective-permute-start(bf16[32,2176]{1,0:T(8,128)(2,1)S(1)} %get-tuple-element.24), channel_id=1, source_target_pairs={{0,12},{4,8},{8,4},{12,0},{16,28},{20,24},{24,20},{28,16},{1,13},{... | collective-permute-start | bytes 417800 | tf_op jit(solution)/shard_map/ppermute | solution.py:326
  25.9 6.4 %collective-permute-start.10 = (bf16[32,2176]{1,0:T(8,128)(2,1)S(1)}, bf16[32,2176]{1,0:T(8,128)(2,1)S(1)}, u32[]{:S(2)}, u32[]{:S(2)}) collective-permute-start(bf16[32,2176]{1,0:T(8,128)(2,1)S(1)} %get-tuple-element.26), channel_id=1, source_target_pairs={{0,4},{4,0},{8,12},{12,8},{16,20},{20,16},{24,28},{28,24},{1,5},{5... | collective-permute-start | bytes 417800 | tf_op jit(solution)/shard_map/ppermute | solution.py:326
  26.0 6.3 %collective-permute-start.11 = (bf16[32,2176]{1,0:T(8,128)(2,1)S(1)}, bf16[32,2176]{1,0:T(8,128)(2,1)S(1)}, u32[]{:S(2)}, u32[]{:S(2)}) collective-permute-start(bf16[32,2176]{1,0:T(8,128)(2,1)S(1)} %get-tuple-element.27), channel_id=1, source_target_pairs={{0,8},{4,12},{8,0},{12,4},{16,24},{20,28},{24,16},{28,20},{1,9},{5... | collective-permute-start | bytes 417800 | tf_op jit(solution)/shard_map/ppermute | solution.py:326
  28.5 7.3 %collective-permute-start.12 = (bf16[32,2176]{1,0:T(8,128)(2,1)S(1)}, bf16[32,2176]{1,0:T(8,128)(2,1)S(1)}, u32[]{:S(2)}, u32[]{:S(2)}) collective-permute-start(bf16[32,2176]{1,0:T(8,128)(2,1)S(1)} %get-tuple-element.28), channel_id=1, source_target_pairs={{0,12},{4,8},{8,4},{12,0},{16,28},{20,24},{24,20},{28,16},{1,13},{... | collective-permute-start | bytes 417800 | tf_op jit(solution)/shard_map/ppermute | solution.py:326
  30.0 8.5 %collective-permute-start.17 = (bf16[32,2176]{1,0:T(8,128)(2,1)S(1)}, bf16[32,2176]{1,0:T(8,128)(2,1)S(1)}, u32[]{:S(2)}, u32[]{:S(2)}) collective-permute-start(bf16[32,2176]{1,0:T(8,128)(2,1)S(1)} %shard_map.75.near), channel_id=1, source_target_pairs={{0,24},{4,28},{8,16},{12,20},{16,8},{20,12},{24,0},{28,4},{1,25},{... | collective-permute-start | bytes 417800 | tf_op jit(solution)/shard_map/ppermute | solution.py:326
  36.3 6.9 %collective-permute-start.13 = (bf16[32,2176]{1,0:T(8,128)(2,1)S(1)}, bf16[32,2176]{1,0:T(8,128)(2,1)S(1)}, u32[]{:S(2)}, u32[]{:S(2)}) collective-permute-start(bf16[32,2176]{1,0:T(8,128)(2,1)S(1)} %shard_map.77.near), channel_id=1, source_target_pairs={{0,24},{4,28},{8,16},{12,20},{16,8},{20,12},{24,0},{28,4},{1,25},{... | collective-permute-start | bytes 417800 | tf_op jit(solution)/shard_map/ppermute | solution.py:326
  38.8 7.7 %collective-permute-start.18 = (bf16[32,2048]{1,0:T(8,128)(2,1)S(1)}, bf16[32,2048]{1,0:T(8,128)(2,1)S(1)}, u32[]{:S(2)}, u32[]{:S(2)}) collective-permute-start(bf16[32,2048]{1,0:T(8,128)(2,1)S(1)} %shard_map.79.refs_4_), channel_id=1, source_target_pairs={{0,4},{4,0},{8,12},{12,8},{16,20},{20,16},{24,28},{28,24},{1,5},{5... | collective-permute-start | bytes 393224 | tf_op jit(solution)/shard_map/ppermute | solution.py:326
  41.2 6.3 %collective-permute-start.19 = (bf16[32,2048]{1,0:T(8,128)(2,1)S(1)}, bf16[32,2048]{1,0:T(8,128)(2,1)S(1)}, u32[]{:S(2)}, u32[]{:S(2)}) collective-permute-start(bf16[32,2048]{1,0:T(8,128)(2,1)S(1)} %shard_map.79.refs_4_), channel_id=1, source_target_pairs={{0,8},{4,12},{8,0},{12,4},{16,24},{20,28},{24,16},{28,20},{1,9},{5... | collective-permute-start | bytes 393224 | tf_op jit(solution)/shard_map/ppermute | solution.py:326
  42.6 6.9 %collective-permute-start.20 = (bf16[32,2048]{1,0:T(8,128)(2,1)S(1)}, bf16[32,2048]{1,0:T(8,128)(2,1)S(1)}, u32[]{:S(2)}, u32[]{:S(2)}) collective-permute-start(bf16[32,2048]{1,0:T(8,128)(2,1)S(1)} %shard_map.79.refs_4_), channel_id=1, source_target_pairs={{0,12},{4,8},{8,4},{12,0},{16,28},{20,24},{24,20},{28,16},{1,13},{... | collective-permute-start | bytes 393224 | tf_op jit(solution)/shard_map/ppermute | solution.py:326
  43.5 7.3 %collective-permute-start.14 = (bf16[32,2048]{1,0:T(8,128)(2,1)S(1)}, bf16[32,2048]{1,0:T(8,128)(2,1)S(1)}, u32[]{:S(2)}, u32[]{:S(2)}) collective-permute-start(bf16[32,2048]{1,0:T(8,128)(2,1)S(1)} %shard_map.78.refs_0_), channel_id=1, source_target_pairs={{0,4},{4,0},{8,12},{12,8},{16,20},{20,16},{24,28},{28,24},{1,5},{5... | collective-permute-start | bytes 393224 | tf_op jit(solution)/shard_map/ppermute | solution.py:326
  45.1 5.7 %collective-permute-start.15 = (bf16[32,2048]{1,0:T(8,128)(2,1)S(1)}, bf16[32,2048]{1,0:T(8,128)(2,1)S(1)}, u32[]{:S(2)}, u32[]{:S(2)}) collective-permute-start(bf16[32,2048]{1,0:T(8,128)(2,1)S(1)} %shard_map.78.refs_0_), channel_id=1, source_target_pairs={{0,8},{4,12},{8,0},{12,4},{16,24},{20,28},{24,16},{28,20},{1,9},{5... | collective-permute-start | bytes 393224 | tf_op jit(solution)/shard_map/ppermute | solution.py:326
  46.5 5.9 %collective-permute-start.16 = (bf16[32,2048]{1,0:T(8,128)(2,1)S(1)}, bf16[32,2048]{1,0:T(8,128)(2,1)S(1)}, u32[]{:S(2)}, u32[]{:S(2)}) collective-permute-start(bf16[32,2048]{1,0:T(8,128)(2,1)S(1)} %shard_map.78.refs_0_), channel_id=1, source_target_pairs={{0,12},{4,8},{8,4},{12,0},{16,28},{20,24},{24,20},{28,16},{1,13},{... | collective-permute-start | bytes 393224 | tf_op jit(solution)/shard_map/ppermute | solution.py:326
  53.7 1.6 %collective-permute-start.21 = (bf16[128,1024]{1,0:T(8,128)(2,1)S(1)}, bf16[128,1024]{1,0:T(8,128)(2,1)S(1)}, u32[]{:S(2)}, u32[]{:S(2)}) collective-permute-start(bf16[128,1024]{1,0:T(8,128)(2,1)S(1)} %get-tuple-element.30), channel_id=1, source_target_pairs={{0,1},{1,0},{2,3},{3,2},{4,5},{5,4},{6,7},{7,6},{8,9},{9,8},{10,11... | collective-permute-start | bytes 786440 | tf_op jit(solution)/shard_map/ppermute | solution.py:326
  55.4 5.6 %collective-permute-start.22 = (bf16[64,1024]{1,0:T(8,128)(2,1)S(1)}, bf16[64,1024]{1,0:T(8,128)(2,1)S(1)}, u32[]{:S(2)}, u32[]{:S(2)}) collective-permute-start(bf16[64,1024]{1,0:T(8,128)(2,1)S(1)} %slice.15), channel_id=1, source_target_pairs={{0,2},{1,3},{2,0},{3,1},{4,6},{5,7},{6,4},{7,5},{8,10},{9,11},{10,... | collective-permute-start | bytes 393224 | tf_op jit(solution)/shard_map/ppermute | solution.py:326

commit v3 on v2

--- a/solution.py
+++ b/solution.py
@@ -50,7 +50,9 @@
         return ((row // self.rows) ^ mine) * self.rows + row % self.rows
 
 
-def fetch_kernel(plan, pages_dev, select_hbm, table_hbm, stands_hbm, keys, values, k_out, v_out, info, select, table, stands, rows, k_buf, v_buf, sems, int_sems):
+def fetch_kernel(plan, pages_dev, *refs):
+    select_hbm, table_hbm, stands_hbm, queries, keys, values, k_out, v_out, info, q_out = refs[:10]
+    select, table, stands, rows, k_buf, v_buf, sems, int_sems = refs[10:]
     me = lax.axis_index("pages")
     blocks, picked = k_buf.shape[:2]
     span = k_buf.shape[2]
@@ -59,14 +61,14 @@
     low = me * pages_dev
     loads = [
         pltpu.make_async_copy(a, b, int_sems.at[i])
-        for i, (a, b) in enumerate(((select_hbm, select), (table_hbm, table), (stands_hbm, stands)))
+        for i, (a, b) in enumerate(((select_hbm, select), (table_hbm, table), (stands_hbm, stands), (queries, q_out)))
     ]
     for load in loads:
         load.start()
     row = lax.broadcasted_iota(jnp.int32, (span, span), 0)
     column = lax.broadcasted_iota(jnp.int32, (span, span), 1)
     apart = (column == (row % page) * heads + row // page).astype(F32).astype(BF16)
-    for load in loads:
+    for load in loads[:3]:
         load.wait()
     for lb in range(blocks):
         block = plan.block(me, lb)
@@ -113,21 +115,25 @@
                     here = slice(slot * page, (slot + 1) * page)
                     k_out[lb, g, here, :] = split[g * page : (g + 1) * page, :LANES]
                     v_out[lb, g, here, :LANES] = split[g * page : (g + 1) * page, LANES:]
-
-
-def fetch(plan, select, table, stands, keys, values):
+    loads[3].wait()
+
+
+def fetch(plan, select, table, stands, queries, keys, values):
     pages_dev, page, heads, size = keys.shape
     blocks, picked = select.shape[0], PICKED_PAGES
     span = page * heads
+    flat = (pages_dev, span, size)
+    operands = (select, table, stands, queries, keys.reshape(flat), values.reshape(flat))
     return pl.pallas_call(
         functools.partial(fetch_kernel, plan, pages_dev),
         out_shape=(
             jax.ShapeDtypeStruct((blocks, heads, picked * page, size), BF16),
             jax.ShapeDtypeStruct((blocks, heads, picked * page, size + LANES), BF16),
             jax.ShapeDtypeStruct((blocks, 3), jnp.int32),
+            jax.ShapeDtypeStruct(queries.shape, queries.dtype),
         ),
-        in_specs=[pl.BlockSpec(memory_space=pltpu.HBM)] * 5,
-        out_specs=(in_vmem(), in_vmem(), in_smem()),
+        in_specs=[pl.BlockSpec(memory_space=pltpu.HBM)] * len(operands),
+        out_specs=(in_vmem(), in_vmem(), in_smem(), in_vmem()),
         scratch_shapes=[
             SMEM(select.shape, jnp.int32),
             SMEM(table.shape, jnp.int32),
@@ -136,11 +142,11 @@
             VMEM((blocks, picked, span, size), BF16),
             VMEM((blocks, picked, span, size), BF16),
             pltpu.SemaphoreType.DMA((blocks, picked, 2)),
-            pltpu.SemaphoreType.DMA((3,)),
+            pltpu.SemaphoreType.DMA((4,)),
         ],
         compiler_params=params(16),
         cost_estimate=pl.CostEstimate(flops=2 * 10**9, bytes_accessed=8 * 2**20, transcendentals=0),
-    )(*(pltpu.with_memory_space_constraint(x, pltpu.HBM) for x in (select, table, stands, keys.reshape(pages_dev, span, size), values.reshape(pages_dev, span, size))))
+    )(*(pltpu.with_memory_space_constraint(x, pltpu.HBM) for x in operands))
 
 
 def pack_stats(lse, heads):
@@ -179,27 +185,29 @@
         query_pos = info[lb, 2] * page + plan.offsets(me, lb, shape)
         allowed = key_pos <= query_pos
         stats = jnp.zeros((page, LANES), F32)
-        for g in range(kv_heads):
-            for t in range(0, repeat, tile):
-                first = g * repeat + t
-                q = jnp.concatenate(
-                    [m[:, h * size : (h + 1) * size] for h in range(first, first + tile) for m in queries], axis=0
-                )
-                scores = scale * lax.dot_general(
-                    q, k_ref[lb, g], (((1,), (1,)), ((), ())), preferred_element_type=F32
-                )
-                scores = jnp.concatenate([jnp.where(allowed, scores[:, :page], FLOOR), scores[:, page:]], axis=1)
-                peak = jnp.max(scores, axis=1, keepdims=True)
-                weights = jnp.exp2(scores - peak).astype(BF16)
-                both = jnp.dot(weights, v_ref[lb, g], preferred_element_type=F32)
-                total = both[:, size:]
-                out = (both[:, :size] / total).astype(BF16)
-                lse = peak + jnp.log2(total)
-                for i in range(tile):
-                    h = first + i
-                    stats = jnp.where(lane == h, lse[i * page : (i + 1) * page], stats)
-                    for c in range(chunks):
-                        outs[c][:, h * size : (h + 1) * size] = out[i * page + c * part : i * page + (c + 1) * part]
+        def product(first):
+            q = jnp.concatenate(
+                [m[:, h * size : (h + 1) * size] for h in range(first, first + tile) for m in queries], axis=0
+            )
+            return lax.dot_general(q, k_ref[lb, first // repeat], (((1,), (1,)), ((), ())), preferred_element_type=F32)
+
+        ahead = product(0)
+        for first in range(0, heads, tile):
+            scores = scale * ahead
+            if first + tile < heads:
+                ahead = product(first + tile)
+            scores = jnp.concatenate([jnp.where(allowed, scores[:, :page], FLOOR), scores[:, page:]], axis=1)
+            peak = jnp.max(scores, axis=1, keepdims=True)
+            weights = jnp.exp2(scores - peak).astype(BF16)
+            both = jnp.dot(weights, v_ref[lb, first // repeat], preferred_element_type=F32)
+            total = both[:, size:]
+            out = (both[:, :size] / total).astype(BF16)
+            lse = peak + jnp.log2(total)
+            for i in range(tile):
+                h = first + i
+                stats = jnp.where(lane == h, lse[i * page : (i + 1) * page], stats)
+                for c in range(chunks):
+                    outs[c][:, h * size : (h + 1) * size] = out[i * page + c * part : i * page + (c + 1) * part]
         packed = pack_stats(stats, heads)
         for c in range(chunks):
             outs[c][:, width:] = packed[c * part : (c + 1) * part]
@@ -212,7 +220,7 @@
 
 
 def attend(plan, heads, lb, pages, queries):
-    keys, values, info = pages
+    keys, values, info, _ = pages
     part = plan.page // plan.chunks
     shape = jax.ShapeDtypeStruct((part, queries[0].shape[1] + LANES), BF16)
     return pl.pallas_call(
@@ -225,7 +233,7 @@
     )(info, *queries, keys, values)
 
 
-def merged(parts, stats, heads, size):
+def merged(parts, stats):
     top = functools.reduce(jnp.maximum, stats)
     shares = [jnp.exp2(s - top) for s in stats]
     total = functools.reduce(jnp.add, shares)
@@ -243,12 +251,7 @@
     sources, out = refs[:-1], refs[-1]
     width = out.shape[1] - LANES
     size = width // heads
-    head, lse = merged(
-        [lambda h, r=r: r[:, h * size : (h + 1) * size] for r in sources],
-        [unpack_stats(r[:, width:], heads) for r in sources],
-        heads,
-        size,
-    )
+    head, lse = merged([heads_of(r, size) for r in sources], [unpack_stats(r[:, width:], heads) for r in sources])
     for h in range(heads):
         out[:, h * size : (h + 1) * size] = head(h).astype(BF16)
     out[:, width:] = pack_stats(lse, heads)
@@ -264,15 +267,14 @@
     )(*sources)
 
 
+def heads_of(ref, size):
+    return lambda h: ref[:, h * size : (h + 1) * size]
+
+
 def finish_kernel(heads, near, far, out):
     width = out.shape[1]
     size = width // heads
-    head, _ = merged(
-        [lambda h, r=r: r[:, h * size : (h + 1) * size] for r in (near, far)],
-        [unpack_stats(r[:, width:], heads) for r in (near, far)],
-        heads,
-        size,
-    )
+    head, _ = merged([heads_of(r, size) for r in (near, far)], [unpack_stats(r[:, width:], heads) for r in (near, far)])
     for h in range(heads):
         out[:, h * size : (h + 1) * size] = head(h).astype(BF16)
 
@@ -287,38 +289,48 @@
     )(near, far)
 
 
-def project_kernel(plan, ways, *refs):
-    sources, weight, outs, rows_ref = refs[: plan.n], refs[plan.n], refs[plan.n + 1 : -1], refs[-1]
+def merge_finish_kernel(heads, *refs):
+    merge_kernel(heads, *refs[:-3], refs[-2])
+    finish_kernel(heads, refs[-2], refs[-3], refs[-1])
+
+
+def merge_finish(heads, far, *sources):
+    rows, wide = far.shape
+    return pl.pallas_call(
+        functools.partial(merge_finish_kernel, heads),
+        out_shape=(jax.ShapeDtypeStruct((rows, wide), BF16), jax.ShapeDtypeStruct((rows, wide - LANES), BF16)),
+        in_specs=[in_vmem()] * (len(sources) + 1),
+        out_specs=(in_vmem(),) * 2,
+        compiler_params=params(8),
+    )(*sources, far)
+
+
+def project_kernel(plan, lb, *refs):
+    sources, weight, (keep, send, rows_ref) = refs[: plan.group], refs[plan.group], refs[plan.group + 1 :]
     me, column = lax.axis_index("pages"), lax.axis_index("mp")
     rows = plan.rows
-    holders = plan.n // ways
-    for k in range(plan.group):
-        for half in range(2):
-            device = me ^ k ^ (half * plan.cross)
-            place = ((device // holders) ^ column) * holders + device % holders
-            rows_ref[pl.ds(pl.multiple_of(place * rows, rows), rows), :] = sources[half * plan.group + k][...]
+    holders = plan.group // 2
+    for i, k in enumerate((*others(plan), 0)):
+        device = me ^ k ^ (lb * plan.cross)
+        place = ((device // holders % 2) ^ (column % 2)) * holders + device % holders
+        rows_ref[pl.ds(pl.multiple_of(place * rows, rows), rows), :] = sources[i][...]
+    product = jnp.dot(rows_ref[...], weight[...], preferred_element_type=F32)
     part = holders * rows
-    product = jnp.dot(rows_ref[...], weight[...], preferred_element_type=F32)
-    keep, send = outs
-    for i, w in enumerate(range(0, ways, 2)):
-        keep[i * part : (i + 1) * part, :] = product[w * part : (w + 1) * part]
-        send[i * part : (i + 1) * part, :] = product[(w + 1) * part : (w + 2) * part].astype(BF16)
-
-
-def project(plan, ways, sources, weight):
-    total = plan.n * plan.rows
+    keep[...] = product[:part]
+    send[...] = product[part:].astype(BF16)
+
+
+def project(plan, lb, sources, weight):
     columns = weight.shape[1]
-    return pl.pallas_call(
-        functools.partial(project_kernel, plan, ways),
-        out_shape=(
-            jax.ShapeDtypeStruct((total // 2, columns), F32),
-            jax.ShapeDtypeStruct((total // 2, columns), BF16),
-        ),
-        in_specs=[in_vmem()] * (plan.n + 1),
+    part = plan.page // 2
+    return pl.pallas_call(
+        functools.partial(project_kernel, plan, lb),
+        out_shape=(jax.ShapeDtypeStruct((part, columns), F32), jax.ShapeDtypeStruct((part, columns), BF16)),
+        in_specs=[in_vmem()] * (plan.group + 1),
         out_specs=(in_vmem(), in_vmem()),
-        scratch_shapes=[VMEM((total, weight.shape[0]), BF16)],
+        scratch_shapes=[VMEM((plan.page, weight.shape[0]), BF16)],
         compiler_params=params(24),
-    )(*sources, weight)
+    )(*(sources[k] for k in (*others(plan), 0)), weight)
 
 
 def swap(x, axis, distance):
@@ -326,24 +338,33 @@
     return lax.ppermute(x, axis, [(i, i ^ distance) for i in range(n)])
 
 
+def others(plan):
+    return range(plan.group - 1, 0, -1)
+
+
 def spread(x, plan):
-    return [x] + [swap(x, "pages", k) for k in range(1, plan.group)]
+    return {0: x} | {k: swap(x, "pages", k) for k in others(plan)}
 
 
 def by_halves(plan, heads, queries, weight, pages):
     far = swap(queries, "pages", plan.cross)
-    chunks = [spread(queries, plan), spread(far, plan)]
-    near = []
-    for lb in range(plan.blocks):
-        outs = attend(plan, heads, lb, pages, chunks[lb])
-        near.append(merge(heads, outs[0], *(swap(outs[k], "pages", k) for k in range(1, plan.group))))
-    across = [swap(x, "pages", plan.cross) for x in near]
-    others = spread(finish(heads, near[1], across[0]), plan)
-    mine = spread(finish(heads, near[0], across[1]), plan)
-    keep, send = project(plan, lax.axis_size("mp"), mine + others, weight)
-    total = keep + swap(send, "mp", 1).astype(F32)
-    part = total.shape[0] // 2
-    return (total[:part] + swap(total[part:].astype(BF16), "mp", 2).astype(F32)).astype(BF16)
+    received = []
+    for lb, rows in enumerate((pages[3], far)):
+        chunks = spread(rows, plan)
+        outs = attend(plan, heads, lb, pages, [chunks[k] for k in range(plan.group)])
+        received.append([swap(outs[k], "pages", k) for k in others(plan)] + [outs[0]])
+    near = merge(heads, *received[0])
+    near_far, far_rows = merge_finish(heads, swap(near, "pages", plan.cross), *received[1])
+    across = swap(near_far, "pages", plan.cross)
+    sums = [None, None]
+    for lb in (1, 0):
+        rows = far_rows if lb else finish(heads, near, across)
+        keep, send = project(plan, lb, spread(rows, plan), weight)
+        sums[lb] = keep + swap(send, "mp", 1).astype(F32)
+    stays = plan.block(lax.axis_index("pages"), 0) == lax.axis_index("mp") // 2
+    mine = jnp.where(stays, sums[0], sums[1])
+    away = jnp.where(stays, sums[1], sums[0]).astype(BF16)
+    return (mine + swap(away, "mp", 2).astype(F32)).astype(BF16)
 
 
 def by_gathers(plan, heads, queries, weight, pages):
@@ -372,7 +393,7 @@
     n, ways = lax.axis_size("pages"), lax.axis_size("mp")
     plan = Plan(n, ways, queries.shape[0], select.shape[0], cached_keys.shape[1])
     heads = queries.shape[1] // cached_keys.shape[3]
-    pages = fetch(plan, select, page_table, block_page, cached_keys, cached_values)
+    pages = fetch(plan, select, page_table, block_page, queries, cached_keys, cached_values)
     way = by_halves if plan.halves else by_gathers
     return way(plan, heads, queries, out_weight, pages)
 

time: 61.9 us -> 66 us (1.066); the launches traced: 61.7 us -> 67.3 us
  waiting for transfers between devices: 16.3 us -> 27.4 us
  starting transfers between devices: 31.6 us -> 26.1 us
    ppermute x23 -> x24, waiting for transfers between devices: 16.3 us -> 27.4 us  [swap(): return lax.ppermute(x, axis, [(i, i ^ distance) for i in range(n)])]
    ppermute x23 -> x24, starting transfers between devices: 31.6 us -> 26.1 us  [swap(): return lax.ppermute(x, axis, [(i, i ^ distance) for i in range(n)])]
    pallas_call x1 -> x3, Pallas kernels: 1.33 us -> 2.47 us  [the longest x2 1.57 us: project(): pl.pallas_call(functools.partial(project_kernel, plan, lb), out_shape=(ja...]
  transfers between devices with their start and end apart: 23 -> 24, of which waited for: 10 -> 12; matrix products, arithmetic and copies ran while one was open for 0% -> 0% of each run, Pallas kernels for 19% -> 18%
where the time goes in v3:
time: 66 us; the launch traced here: 67.3 us
  waiting for transfers between devices  27.4 us (42%)
  starting transfers between devices  26.1 us (40%)
  Pallas kernels  12.8 us (19%)
  other arithmetic  0.78 us (1%)
    ppermute x24, waiting for transfers between devices, swap(): return lax.ppermute(x, axis, [(i, i ^ distance) for i in range(n)])  27.4 us
    ppermute x24, starting transfers between devices, swap(): return lax.ppermute(x, axis, [(i, i ^ distance) for i in range(n)])  26.1 us
    pallas_call x2, Pallas kernels, attend(): pl.pallas_call(functools.partial(attend_kernel, plan, heads, lb), out_sha...  5.86 us
    pallas_call x1, Pallas kernels, fetch(): pl.pallas_call(functools.partial(fetch_kernel, plan, pages_dev), out_shap...  3.69 us
    pallas_call x2, Pallas kernels, project(): pl.pallas_call(functools.partial(project_kernel, plan, lb), out_shape=(ja...  1.57 us
  transfers between devices with their start and end apart: 24, of which 12 were waited for; matrix products, arithmetic and copies ran while one was open for 0% of the time, Pallas kernels for 18%

profile of v3, /device:TPU:0, one launch (start us, length us, event | category | flops | bytes accessed | tf_op | source)
XLA Modules:
  0.0 67.3 jit_solution(14425632833420659129)
XLA Ops:
  0.0 5.0 %collective-permute-start.6 = (bf16[32,2048]{1,0:T(8,128)(2,1)}, bf16[32,2048]{1,0:T(8,128)(2,1)S(1)}, u32[]{:S(2)}, u32[]{:S(2)}) collective-permute-start(bf16[32,2048]{1,0:T(8,128)(2,1)} %refs_3_.1), channel_id=1, source_target_pairs={{0,24},{4,28},{8,16},{12,20},{16,8},{20,12},{24,0},{28,4},{1,25},{... | collective-permute-start | bytes 393224 | tf_op jit(solution)/shard_map/ppermute | solution.py:338
  5.0 3.7 %shard_map.73 = (bf16[2,2,768,128]{3,2,1,0:T(8,128)(2,1)S(1)}, bf16[2,2,768,256]{3,2,1,0:T(8,128)(2,1)S(1)}, s32[2,3]{1,0:T(2,128)S(1)}, bf16[32,2048]{1,0:T(8,128)(2,1)S(1)}) custom-call(s32[2,24]{1,0:T(2,128)} %refs_0_.1, s32[128]{0:T(128)} %refs_1_.1, s32[2]{0:T(128)} %refs_2_.1, bf16[32,2048]{1,0:T(8,128)(2,1)} %refs_3_.1, ...), custom_call_target="tpu_custom_call" | custom-call | flops 2000000000 | bytes 8388608 | tf_op jit(solution)/shard_map/pallas_call | solution.py:127
  8.8 0.1 collective-permute-start
  8.8 0.1 collective-permute-start.1
  8.9 3.4 %collective-permute-start.2 = (bf16[32,2048]{1,0:T(8,128)(2,1)S(1)}, bf16[32,2048]{1,0:T(8,128)(2,1)S(1)}, u32[]{:S(2)}, u32[]{:S(2)}) collective-permute-start(bf16[32,2048]{1,0:T(8,128)(2,1)S(1)} %get-tuple-element.24.refs_0_), channel_id=1, source_target_pairs={{0,12},{4,8},{8,4},{12,0},{16,28},{20,24},{24,20},{28,16},{1,13},{... | collective-permute-start | bytes 393224 | tf_op jit(solution)/shard_map/ppermute | solution.py:338
  12.3 0.1 collective-permute-start.7
  12.4 0.5 collective-permute-start.8
  12.9 1.8 %collective-permute-done.refs_1_ = bf16[32,2048]{1,0:T(8,128)(2,1)S(1)} collective-permute-done((bf16[32,2048]{1,0:T(8,128)(2,1)S(1)}, bf16[32,2048]{1,0:T(8,128)(2,1)S(1)}, u32[]{:S(2)}, u32[]{:S(2)}) %collective-permute-start) | collective-permute-done | bytes 131104 | tf_op jit(solution)/shard_map/ppermute | solution.py:338
  14.7 1.1 %collective-permute-start.9 = (bf16[32,2048]{1,0:T(8,128)(2,1)S(1)}, bf16[32,2048]{1,0:T(8,128)(2,1)S(1)}, u32[]{:S(2)}, u32[]{:S(2)}) collective-permute-start(bf16[32,2048]{1,0:T(8,128)(2,1)S(1)} %collective-permute-done.6.refs_0_), channel_id=1, source_target_pairs={{0,12},{4,8},{8,4},{12,0},{16,28},{20,24},{24,20},{28,16},{1,13},{... | collective-permute-start | bytes 393224 | tf_op jit(solution)/shard_map/ppermute | solution.py:338
  15.8 3.8 %collective-permute-done.2.refs_3_ = bf16[32,2048]{1,0:T(8,128)(2,1)S(1)} collective-permute-done((bf16[32,2048]{1,0:T(8,128)(2,1)S(1)}, bf16[32,2048]{1,0:T(8,128)(2,1)S(1)}, u32[]{:S(2)}, u32[]{:S(2)}) %collective-permute-start.2) | collective-permute-done | bytes 131104 | tf_op jit(solution)/shard_map/ppermute | solution.py:338
  19.6 2.9 %shard_map.74 = (bf16[32,2176]{1,0:T(8,128)(2,1)S(1)}, bf16[32,2176]{1,0:T(8,128)(2,1)S(1)}, bf16[32,2176]{1,0:T(8,128)(2,1)S(1)}, bf16[32,2176]{1,0:T(8,128)(2,1)S(1)}) custom-call(s32[2,3]{1,0:T(2,128)S(1)} %get-tuple-element.23.info, bf16[32,2048]{1,0:T(8,128)(2,1)S(1)} %get-tuple-element.24.refs_0_, bf16[32,2048]{1,0:T(8,128)(2,1)S(1)} %collective-permute-done.refs_1_, ...), custom_call_target="tpu_custom_call" | custom-call | flops 2000000000 | bytes 4194304 | tf_op jit(solution)/shard_map/pallas_call | solution.py:226
  22.6 0.1 collective-permute-start.3
  22.6 0.1 collective-permute-start.4
  22.7 0.0 copy-start
  22.7 3.4 %collective-permute-start.5 = (bf16[32,2176]{1,0:T(8,128)(2,1)S(1)}, bf16[32,2176]{1,0:T(8,128)(2,1)S(1)}, u32[]{:S(2)}, u32[]{:S(2)}) collective-permute-start(bf16[32,2176]{1,0:T(8,128)(2,1)S(1)} %get-tuple-element.29), channel_id=1, source_target_pairs={{0,4},{4,0},{8,12},{12,8},{16,20},{20,16},{24,28},{28,24},{1,5},{5... | collective-permute-start | bytes 417800 | tf_op jit(solution)/shard_map/ppermute | solution.py:338
  26.1 0.0 collective-permute-done.9.refs_3_
  26.1 2.9 %shard_map.76 = (bf16[32,2176]{1,0:T(8,128)(2,1)S(1)}, bf16[32,2176]{1,0:T(8,128)(2,1)S(1)}, bf16[32,2176]{1,0:T(8,128)(2,1)S(1)}, bf16[32,2176]{1,0:T(8,128)(2,1)S(1)}) custom-call(s32[2,3]{1,0:T(2,128)S(1)} %get-tuple-element.23.info, bf16[32,2048]{1,0:T(8,128)(2,1)S(1)} %collective-permute-done.6.refs_0_, ...), custom_call_target="tpu_custom_call" | custom-call | flops 2000000000 | bytes 4194304 | tf_op jit(solution)/shard_map/pallas_call | solution.py:226
  29.1 0.1 collective-permute-start.10
  29.2 0.1 collective-permute-start.11
  29.3 0.0 collective-permute-done.3.refs_0_
  29.3 3.3 %collective-permute-start.12 = (bf16[32,2176]{1,0:T(8,128)(2,1)S(1)}, bf16[32,2176]{1,0:T(8,128)(2,1)S(1)}, u32[]{:S(2)}, u32[]{:S(2)}) collective-permute-start(bf16[32,2176]{1,0:T(8,128)(2,1)S(1)} %get-tuple-element.33), channel_id=1, source_target_pairs={{0,4},{4,0},{8,12},{12,8},{16,20},{20,16},{24,28},{28,24},{1,5},{5... | collective-permute-start | bytes 417800 | tf_op jit(solution)/shard_map/ppermute | solution.py:338
  32.6 0.4 collective-permute-done.5.refs_2_
  33.0 0.5 shard_map.75.near
  33.5 0.1 collective-permute-start.13
  33.6 2.6 %collective-permute-done.10.refs_0_ = bf16[32,2176]{1,0:T(8,128)(2,1)S(1)} collective-permute-done((bf16[32,2176]{1,0:T(8,128)(2,1)S(1)}, bf16[32,2176]{1,0:T(8,128)(2,1)S(1)}, u32[]{:S(2)}, u32[]{:S(2)}) %collective-permute-start.10) | collective-permute-done | bytes 139296 | tf_op jit(solution)/shard_map/ppermute | solution.py:338
  36.2 0.0 collective-permute-done.11.refs_1_
  36.2 0.9 %collective-permute-done.12.refs_2_ = bf16[32,2176]{1,0:T(8,128)(2,1)S(1)} collective-permute-done((bf16[32,2176]{1,0:T(8,128)(2,1)S(1)}, bf16[32,2176]{1,0:T(8,128)(2,1)S(1)}, u32[]{:S(2)}, u32[]{:S(2)}) %collective-permute-start.12) | collective-permute-done | bytes 139296 | tf_op jit(solution)/shard_map/ppermute | solution.py:338
  37.0 3.4 %collective-permute-done.13.refs_4_ = bf16[32,2176]{1,0:T(8,128)(2,1)S(1)} collective-permute-done((bf16[32,2176]{1,0:T(8,128)(2,1)S(1)}, bf16[32,2176]{1,0:T(8,128)(2,1)S(1)}, u32[]{:S(2)}, u32[]{:S(2)}) %collective-permute-start.13) | collective-permute-done | bytes 139296 | tf_op jit(solution)/shard_map/ppermute | solution.py:338
  40.4 0.9 %shard_map.77 = (bf16[32,2176]{1,0:T(8,128)(2,1)S(1)}, bf16[32,2048]{1,0:T(8,128)(2,1)S(1)}) custom-call(bf16[32,2176]{1,0:T(8,128)(2,1)S(1)} %collective-permute-done.10.refs_0_, bf16[32,2176]{1,0:T(8,128)(2,1)S(1)} %collective-permute-done.11.refs_1_, bf16[32,2176]{1,0:T(8,128)(2,1)S(1)} %collective-permute-done.12.refs_2_, ...), custom_call_target="tpu_custom_call" | custom-call | tf_op jit(solution)/shard_map/pallas_call | solution.py:299
  41.4 0.2 collective-permute-start.14
  41.6 3.7 %collective-permute-start.20 = (bf16[32,2048]{1,0:T(8,128)(2,1)S(1)}, bf16[32,2048]{1,0:T(8,128)(2,1)S(1)}, u32[]{:S(2)}, u32[]{:S(2)}) collective-permute-start(bf16[32,2048]{1,0:T(8,128)(2,1)S(1)} %get-tuple-element.38.refs_3_), channel_id=1, source_target_pairs={{0,8},{4,12},{8,0},{12,4},{16,24},{20,28},{24,16},{28,20},{1,9},{5... | collective-permute-start | bytes 393224 | tf_op jit(solution)/shard_map/ppermute | solution.py:338
  45.2 4.5 %collective-permute-done.14.far = bf16[32,2176]{1,0:T(8,128)(2,1)S(1)} collective-permute-done((bf16[32,2176]{1,0:T(8,128)(2,1)S(1)}, bf16[32,2176]{1,0:T(8,128)(2,1)S(1)}, u32[]{:S(2)}, u32[]{:S(2)}) %collective-permute-start.14) | collective-permute-done | bytes 139296 | tf_op jit(solution)/shard_map/ppermute | solution.py:338
  49.7 0.3 shard_map.78.refs_3_
  50.1 0.1 collective-permute-start.15
  50.1 3.5 %collective-permute-start.16 = (bf16[32,2048]{1,0:T(8,128)(2,1)S(1)}, bf16[32,2048]{1,0:T(8,128)(2,1)S(1)}, u32[]{:S(2)}, u32[]{:S(2)}) collective-permute-start(bf16[32,2048]{1,0:T(8,128)(2,1)S(1)} %shard_map.78.refs_3_), channel_id=1, source_target_pairs={{0,8},{4,12},{8,0},{12,4},{16,24},{20,28},{24,16},{28,20},{1,9},{5... | collective-permute-start | bytes 393224 | tf_op jit(solution)/shard_map/ppermute | solution.py:338
  53.7 0.0 collective-permute-done.20.refs_1_
  53.7 0.8 %shard_map.80 = (f32[64,1024]{1,0:T(8,128)S(1)}, bf16[64,1024]{1,0:T(8,128)(2,1)S(1)}) custom-call(bf16[32,2048]{1,0:T(8,128)(2,1)S(1)} %collective-permute-done.19.refs_0_, bf16[32,2048]{1,0:T(8,128)(2,1)S(1)} %collective-permute-done.20.refs_1_, bf16[32,2048]{1,0:T(8,128)(2,1)S(1)} %collective-permute-done.21.refs_2_, ...), custom_call_target="tpu_custom_call" | custom-call | tf_op jit(solution)/shard_map/pallas_call | solution.py:326
  54.5 0.1 collective-permute-start.22
  54.6 1.4 %collective-permute-done.15.refs_0_ = bf16[32,2048]{1,0:T(8,128)(2,1)S(1)} collective-permute-done((bf16[32,2048]{1,0:T(8,128)(2,1)S(1)}, bf16[32,2048]{1,0:T(8,128)(2,1)S(1)}, u32[]{:S(2)}, u32[]{:S(2)}) %collective-permute-start.15) | collective-permute-done | bytes 131104 | tf_op jit(solution)/shard_map/ppermute | solution.py:338
  56.0 2.0 %collective-permute-done.16.refs_1_ = bf16[32,2048]{1,0:T(8,128)(2,1)S(1)} collective-permute-done((bf16[32,2048]{1,0:T(8,128)(2,1)S(1)}, bf16[32,2048]{1,0:T(8,128)(2,1)S(1)}, u32[]{:S(2)}, u32[]{:S(2)}) %collective-permute-start.16) | collective-permute-done | bytes 131104 | tf_op jit(solution)/shard_map/ppermute | solution.py:338
  58.0 0.6 collective-permute-done.17.refs_2_
  58.7 0.8 %shard_map.79 = (f32[64,1024]{1,0:T(8,128)S(1)}, bf16[64,1024]{1,0:T(8,128)(2,1)S(1)}) custom-call(bf16[32,2048]{1,0:T(8,128)(2,1)S(1)} %collective-permute-done.15.refs_0_, bf16[32,2048]{1,0:T(8,128)(2,1)S(1)} %collective-permute-done.16.refs_1_, bf16[32,2048]{1,0:T(8,128)(2,1)S(1)} %collective-permute-done.17.refs_2_, ...), custom_call_target="tpu_custom_call" | custom-call | tf_op jit(solution)/shard_map/pallas_call | solution.py:326
  59.5 0.1 collective-permute-start.18
  59.6 1.3 %collective-permute-done.18 = bf16[64,1024]{1,0:T(8,128)(2,1)S(1)} collective-permute-done((bf16[64,1024]{1,0:T(8,128)(2,1)S(1)}, bf16[64,1024]{1,0:T(8,128)(2,1)S(1)}, u32[]{:S(2)}, u32[]{:S(2)}) %collective-permute-start.18) | collective-permute-done | bytes 131104 | tf_op jit(solution)/shard_map/ppermute | solution.py:338
  60.9 0.1 select_convert_fusion
  60.9 1.0 %collective-permute-start.23 = (bf16[64,1024]{1,0:T(8,128)(2,1)S(1)}, bf16[64,1024]{1,0:T(8,128)(2,1)S(1)}, u32[]{:S(2)}, u32[]{:S(2)}) collective-permute-start(bf16[64,1024]{1,0:T(8,128)(2,1)S(1)} %select_convert_fusion), channel_id=1, source_target_pairs={{0,2},{1,3},{2,0},{3,1},{4,6},{5,7},{6,4},{7,5},{8,10},{9,11},{10,... | collective-permute-start | bytes 393224 | tf_op jit(solution)/shard_map/ppermute | solution.py:338
  61.9 4.6 %collective-permute-done.23 = bf16[64,1024]{1,0:T(8,128)(2,1)S(1)} collective-permute-done((bf16[64,1024]{1,0:T(8,128)(2,1)S(1)}, bf16[64,1024]{1,0:T(8,128)(2,1)S(1)}, u32[]{:S(2)}, u32[]{:S(2)}) %collective-permute-start.23) | collective-permute-done | bytes 131104 | tf_op jit(solution)/shard_map/ppermute | solution.py:338
  66.5 0.7 %add_convert_fusion = bf16[64,1024]{1,0:T(8,128)(2,1)} fusion(bf16[64,1024]{1,0:T(8,128)(2,1)S(1)} %collective-permute-done.23, f32[64,1024]{1,0:T(8,128)S(1)} %get-tuple-element.36, bf16[64,1024]{1,0:T(8,128)(2,1)S(1)} %collective-permute-done.18, f32[64,1024]{1,0:T(8,128)S(1)} %get-tuple-element.39, bf16[64,1024]{1,0:T(8,128)(2,1)S(1)} %collective-permute-done.22, ...), kind=kLoop, calls=%fused_computation | loop fusion | flops 524288 | bytes 1048577 | tf_op jit(solution)/shard_map/convert_element_type | solution.py:367
  (12 shorter events, 0.0 us)
Async XLA Ops:
  0.0 12.3 %collective-permute-start.6 = (bf16[32,2048]{1,0:T(8,128)(2,1)}, bf16[32,2048]{1,0:T(8,128)(2,1)S(1)}, u32[]{:S(2)}, u32[]{:S(2)}) collective-permute-start(bf16[32,2048]{1,0:T(8,128)(2,1)} %refs_3_.1), channel_id=1, source_target_pairs={{0,24},{4,28},{8,16},{12,20},{16,8},{20,12},{24,0},{28,4},{1,25},{... | collective-permute-start | bytes 393224 | tf_op jit(solution)/shard_map/ppermute | solution.py:338
  8.8 5.9 %collective-permute-start = (bf16[32,2048]{1,0:T(8,128)(2,1)S(1)}, bf16[32,2048]{1,0:T(8,128)(2,1)S(1)}, u32[]{:S(2)}, u32[]{:S(2)}) collective-permute-start(bf16[32,2048]{1,0:T(8,128)(2,1)S(1)} %get-tuple-element.24.refs_0_), channel_id=1, source_target_pairs={{0,4},{4,0},{8,12},{12,8},{16,20},{20,16},{24,28},{28,24},{1,5},{5... | collective-permute-start | bytes 393224 | tf_op jit(solution)/shard_map/ppermute | solution.py:338
  8.8 7.0 %collective-permute-start.1 = (bf16[32,2048]{1,0:T(8,128)(2,1)S(1)}, bf16[32,2048]{1,0:T(8,128)(2,1)S(1)}, u32[]{:S(2)}, u32[]{:S(2)}) collective-permute-start(bf16[32,2048]{1,0:T(8,128)(2,1)S(1)} %get-tuple-element.24.refs_0_), channel_id=1, source_target_pairs={{0,8},{4,12},{8,0},{12,4},{16,24},{20,28},{24,16},{28,20},{1,9},{5... | collective-permute-start | bytes 393224 | tf_op jit(solution)/shard_map/ppermute | solution.py:338
  8.9 10.7 %collective-permute-start.2 = (bf16[32,2048]{1,0:T(8,128)(2,1)S(1)}, bf16[32,2048]{1,0:T(8,128)(2,1)S(1)}, u32[]{:S(2)}, u32[]{:S(2)}) collective-permute-start(bf16[32,2048]{1,0:T(8,128)(2,1)S(1)} %get-tuple-element.24.refs_0_), channel_id=1, source_target_pairs={{0,12},{4,8},{8,4},{12,0},{16,28},{20,24},{24,20},{28,16},{1,13},{... | collective-permute-start | bytes 393224 | tf_op jit(solution)/shard_map/ppermute | solution.py:338
  12.3 10.4 %collective-permute-start.7 = (bf16[32,2048]{1,0:T(8,128)(2,1)S(1)}, bf16[32,2048]{1,0:T(8,128)(2,1)S(1)}, u32[]{:S(2)}, u32[]{:S(2)}) collective-permute-start(bf16[32,2048]{1,0:T(8,128)(2,1)S(1)} %collective-permute-done.6.refs_0_), channel_id=1, source_target_pairs={{0,4},{4,0},{8,12},{12,8},{16,20},{20,16},{24,28},{28,24},{1,5},{5... | collective-permute-start | bytes 393224 | tf_op jit(solution)/shard_map/ppermute | solution.py:338
  12.4 13.7 %collective-permute-start.8 = (bf16[32,2048]{1,0:T(8,128)(2,1)S(1)}, bf16[32,2048]{1,0:T(8,128)(2,1)S(1)}, u32[]{:S(2)}, u32[]{:S(2)}) collective-permute-start(bf16[32,2048]{1,0:T(8,128)(2,1)S(1)} %collective-permute-done.6.refs_0_), channel_id=1, source_target_pairs={{0,8},{4,12},{8,0},{12,4},{16,24},{20,28},{24,16},{28,20},{1,9},{5... | collective-permute-start | bytes 393224 | tf_op jit(solution)/shard_map/ppermute | solution.py:338
  14.7 11.5 %collective-permute-start.9 = (bf16[32,2048]{1,0:T(8,128)(2,1)S(1)}, bf16[32,2048]{1,0:T(8,128)(2,1)S(1)}, u32[]{:S(2)}, u32[]{:S(2)}) collective-permute-start(bf16[32,2048]{1,0:T(8,128)(2,1)S(1)} %collective-permute-done.6.refs_0_), channel_id=1, source_target_pairs={{0,12},{4,8},{8,4},{12,0},{16,28},{20,24},{24,20},{28,16},{1,13},{... | collective-permute-start | bytes 393224 | tf_op jit(solution)/shard_map/ppermute | solution.py:338
  22.6 6.7 %collective-permute-start.3 = (bf16[32,2176]{1,0:T(8,128)(2,1)S(1)}, bf16[32,2176]{1,0:T(8,128)(2,1)S(1)}, u32[]{:S(2)}, u32[]{:S(2)}) collective-permute-start(bf16[32,2176]{1,0:T(8,128)(2,1)S(1)} %get-tuple-element.27), channel_id=1, source_target_pairs={{0,12},{4,8},{8,4},{12,0},{16,28},{20,24},{24,20},{28,16},{1,13},{... | collective-permute-start | bytes 417800 | tf_op jit(solution)/shard_map/ppermute | solution.py:338
  22.6 10.0 %collective-permute-start.4 = (bf16[32,2176]{1,0:T(8,128)(2,1)S(1)}, bf16[32,2176]{1,0:T(8,128)(2,1)S(1)}, u32[]{:S(2)}, u32[]{:S(2)}) collective-permute-start(bf16[32,2176]{1,0:T(8,128)(2,1)S(1)} %get-tuple-element.28), channel_id=1, source_target_pairs={{0,8},{4,12},{8,0},{12,4},{16,24},{20,28},{24,16},{28,20},{1,9},{5... | collective-permute-start | bytes 417800 | tf_op jit(solution)/shard_map/ppermute | solution.py:338
  22.7 31.0 %copy-start = (bf16[2048,1024]{1,0:T(8,128)(2,1)S(1)}, bf16[2048,1024]{1,0:T(8,128)(2,1)}, u32[]{:S(2)}) copy-start(bf16[2048,1024]{1,0:T(8,128)(2,1)} %refs_4_.3) | copy-start | bytes 12582916
  22.7 10.3 %collective-permute-start.5 = (bf16[32,2176]{1,0:T(8,128)(2,1)S(1)}, bf16[32,2176]{1,0:T(8,128)(2,1)S(1)}, u32[]{:S(2)}, u32[]{:S(2)}) collective-permute-start(bf16[32,2176]{1,0:T(8,128)(2,1)S(1)} %get-tuple-element.29), channel_id=1, source_target_pairs={{0,4},{4,0},{8,12},{12,8},{16,20},{20,16},{24,28},{28,24},{1,5},{5... | collective-permute-start | bytes 417800 | tf_op jit(solution)/shard_map/ppermute | solution.py:338
  29.1 7.1 %collective-permute-start.10 = (bf16[32,2176]{1,0:T(8,128)(2,1)S(1)}, bf16[32,2176]{1,0:T(8,128)(2,1)S(1)}, u32[]{:S(2)}, u32[]{:S(2)}) collective-permute-start(bf16[32,2176]{1,0:T(8,128)(2,1)S(1)} %get-tuple-element.31), channel_id=1, source_target_pairs={{0,12},{4,8},{8,4},{12,0},{16,28},{20,24},{24,20},{28,16},{1,13},{... | collective-permute-start | bytes 417800 | tf_op jit(solution)/shard_map/ppermute | solution.py:338
  29.2 7.0 %collective-permute-start.11 = (bf16[32,2176]{1,0:T(8,128)(2,1)S(1)}, bf16[32,2176]{1,0:T(8,128)(2,1)S(1)}, u32[]{:S(2)}, u32[]{:S(2)}) collective-permute-start(bf16[32,2176]{1,0:T(8,128)(2,1)S(1)} %get-tuple-element.32), channel_id=1, source_target_pairs={{0,8},{4,12},{8,0},{12,4},{16,24},{20,28},{24,16},{28,20},{1,9},{5... | collective-permute-start | bytes 417800 | tf_op jit(solution)/shard_map/ppermute | solution.py:338
  29.3 7.7 %collective-permute-start.12 = (bf16[32,2176]{1,0:T(8,128)(2,1)S(1)}, bf16[32,2176]{1,0:T(8,128)(2,1)S(1)}, u32[]{:S(2)}, u32[]{:S(2)}) collective-permute-start(bf16[32,2176]{1,0:T(8,128)(2,1)S(1)} %get-tuple-element.33), channel_id=1, source_target_pairs={{0,4},{4,0},{8,12},{12,8},{16,20},{20,16},{24,28},{28,24},{1,5},{5... | collective-permute-start | bytes 417800 | tf_op jit(solution)/shard_map/ppermute | solution.py:338
  33.5 7.0 %collective-permute-start.13 = (bf16[32,2176]{1,0:T(8,128)(2,1)S(1)}, bf16[32,2176]{1,0:T(8,128)(2,1)S(1)}, u32[]{:S(2)}, u32[]{:S(2)}) collective-permute-start(bf16[32,2176]{1,0:T(8,128)(2,1)S(1)} %shard_map.75.near), channel_id=1, source_target_pairs={{0,24},{4,28},{8,16},{12,20},{16,8},{20,12},{24,0},{28,4},{1,25},{... | collective-permute-start | bytes 417800 | tf_op jit(solution)/shard_map/ppermute | solution.py:338
  41.4 8.4 %collective-permute-start.14 = (bf16[32,2176]{1,0:T(8,128)(2,1)S(1)}, bf16[32,2176]{1,0:T(8,128)(2,1)S(1)}, u32[]{:S(2)}, u32[]{:S(2)}) collective-permute-start(bf16[32,2176]{1,0:T(8,128)(2,1)S(1)} %get-tuple-element.35), channel_id=1, source_target_pairs={{0,24},{4,28},{8,16},{12,20},{16,8},{20,12},{24,0},{28,4},{1,25},{... | collective-permute-start | bytes 417800 | tf_op jit(solution)/shard_map/ppermute | solution.py:338
  41.5 12.1 %collective-permute-start.19 = (bf16[32,2048]{1,0:T(8,128)(2,1)S(1)}, bf16[32,2048]{1,0:T(8,128)(2,1)S(1)}, u32[]{:S(2)}, u32[]{:S(2)}) collective-permute-start(bf16[32,2048]{1,0:T(8,128)(2,1)S(1)} %get-tuple-element.38.refs_3_), channel_id=1, source_target_pairs={{0,12},{4,8},{8,4},{12,0},{16,28},{20,24},{24,20},{28,16},{1,13},{... | collective-permute-start | bytes 393224 | tf_op jit(solution)/shard_map/ppermute | solution.py:338
  41.6 12.2 %collective-permute-start.20 = (bf16[32,2048]{1,0:T(8,128)(2,1)S(1)}, bf16[32,2048]{1,0:T(8,128)(2,1)S(1)}, u32[]{:S(2)}, u32[]{:S(2)}) collective-permute-start(bf16[32,2048]{1,0:T(8,128)(2,1)S(1)} %get-tuple-element.38.refs_3_), channel_id=1, source_target_pairs={{0,8},{4,12},{8,0},{12,4},{16,24},{20,28},{24,16},{28,20},{1,9},{5... | collective-permute-start | bytes 393224 | tf_op jit(solution)/shard_map/ppermute | solution.py:338
  45.2 8.5 %collective-permute-start.21 = (bf16[32,2048]{1,0:T(8,128)(2,1)S(1)}, bf16[32,2048]{1,0:T(8,128)(2,1)S(1)}, u32[]{:S(2)}, u32[]{:S(2)}) collective-permute-start(bf16[32,2048]{1,0:T(8,128)(2,1)S(1)} %get-tuple-element.38.refs_3_), channel_id=1, source_target_pairs={{0,4},{4,0},{8,12},{12,8},{16,20},{20,16},{24,28},{28,24},{1,5},{5... | collective-permute-start | bytes 393224 | tf_op jit(solution)/shard_map/ppermute | solution.py:338
  50.1 5.9 %collective-permute-start.15 = (bf16[32,2048]{1,0:T(8,128)(2,1)S(1)}, bf16[32,2048]{1,0:T(8,128)(2,1)S(1)}, u32[]{:S(2)}, u32[]{:S(2)}) collective-permute-start(bf16[32,2048]{1,0:T(8,128)(2,1)S(1)} %shard_map.78.refs_3_), channel_id=1, source_target_pairs={{0,12},{4,8},{8,4},{12,0},{16,28},{20,24},{24,20},{28,16},{1,13},{... | collective-permute-start | bytes 393224 | tf_op jit(solution)/shard_map/ppermute | solution.py:338
  50.1 7.9 %collective-permute-start.16 = (bf16[32,2048]{1,0:T(8,128)(2,1)S(1)}, bf16[32,2048]{1,0:T(8,128)(2,1)S(1)}, u32[]{:S(2)}, u32[]{:S(2)}) collective-permute-start(bf16[32,2048]{1,0:T(8,128)(2,1)S(1)} %shard_map.78.refs_3_), channel_id=1, source_target_pairs={{0,8},{4,12},{8,0},{12,4},{16,24},{20,28},{24,16},{28,20},{1,9},{5... | collective-permute-start | bytes 393224 | tf_op jit(solution)/shard_map/ppermute | solution.py:338
  53.7 5.0 %collective-permute-start.17 = (bf16[32,2048]{1,0:T(8,128)(2,1)S(1)}, bf16[32,2048]{1,0:T(8,128)(2,1)S(1)}, u32[]{:S(2)}, u32[]{:S(2)}) collective-permute-start(bf16[32,2048]{1,0:T(8,128)(2,1)S(1)} %shard_map.78.refs_3_), channel_id=1, source_target_pairs={{0,4},{4,0},{8,12},{12,8},{16,20},{20,16},{24,28},{28,24},{1,5},{5... | collective-permute-start | bytes 393224 | tf_op jit(solution)/shard_map/ppermute | solution.py:338
  54.5 5.0 %collective-permute-start.22 = (bf16[64,1024]{1,0:T(8,128)(2,1)S(1)}, bf16[64,1024]{1,0:T(8,128)(2,1)S(1)}, u32[]{:S(2)}, u32[]{:S(2)}) collective-permute-start(bf16[64,1024]{1,0:T(8,128)(2,1)S(1)} %get-tuple-element.40), channel_id=1, source_target_pairs={{0,1},{1,0},{2,3},{3,2},{4,5},{5,4},{6,7},{7,6},{8,9},{9,8},{10,11... | collective-permute-start | bytes 393224 | tf_op jit(solution)/shard_map/ppermute | solution.py:338
  59.5 1.4 %collective-permute-start.18 = (bf16[64,1024]{1,0:T(8,128)(2,1)S(1)}, bf16[64,1024]{1,0:T(8,128)(2,1)S(1)}, u32[]{:S(2)}, u32[]{:S(2)}) collective-permute-start(bf16[64,1024]{1,0:T(8,128)(2,1)S(1)} %get-tuple-element.37), channel_id=1, source_target_pairs={{0,1},{1,0},{2,3},{3,2},{4,5},{5,4},{6,7},{7,6},{8,9},{9,8},{10,11... | collective-permute-start | bytes 393224 | tf_op jit(solution)/shard_map/ppermute | solution.py:338
  60.9 5.6 %collective-permute-start.23 = (bf16[64,1024]{1,0:T(8,128)(2,1)S(1)}, bf16[64,1024]{1,0:T(8,128)(2,1)S(1)}, u32[]{:S(2)}, u32[]{:S(2)}) collective-permute-start(bf16[64,1024]{1,0:T(8,128)(2,1)S(1)} %select_convert_fusion), channel_id=1, source_target_pairs={{0,2},{1,3},{2,0},{3,1},{4,6},{5,7},{6,4},{7,5},{8,10},{9,11},{10,... | collective-permute-start | bytes 393224 | tf_op jit(solution)/shard_map/ppermute | solution.py:338

commit v4 on v3

--- a/solution.py
+++ b/solution.py
@@ -50,9 +50,7 @@
         return ((row // self.rows) ^ mine) * self.rows + row % self.rows
 
 
-def fetch_kernel(plan, pages_dev, *refs):
-    select_hbm, table_hbm, stands_hbm, queries, keys, values, k_out, v_out, info, q_out = refs[:10]
-    select, table, stands, rows, k_buf, v_buf, sems, int_sems = refs[10:]
+def fetch_kernel(plan, pages_dev, select_hbm, table_hbm, stands_hbm, keys, values, k_out, v_out, info, select, table, stands, rows, k_buf, v_buf, sems, int_sems):
     me = lax.axis_index("pages")
     blocks, picked = k_buf.shape[:2]
     span = k_buf.shape[2]
@@ -61,14 +59,14 @@
     low = me * pages_dev
     loads = [
         pltpu.make_async_copy(a, b, int_sems.at[i])
-        for i, (a, b) in enumerate(((select_hbm, select), (table_hbm, table), (stands_hbm, stands), (queries, q_out)))
+        for i, (a, b) in enumerate(((select_hbm, select), (table_hbm, table), (stands_hbm, stands)))
     ]
     for load in loads:
         load.start()
     row = lax.broadcasted_iota(jnp.int32, (span, span), 0)
     column = lax.broadcasted_iota(jnp.int32, (span, span), 1)
     apart = (column == (row % page) * heads + row // page).astype(F32).astype(BF16)
-    for load in loads[:3]:
+    for load in loads:
         load.wait()
     for lb in range(blocks):
         block = plan.block(me, lb)
@@ -115,25 +113,21 @@
                     here = slice(slot * page, (slot + 1) * page)
                     k_out[lb, g, here, :] = split[g * page : (g + 1) * page, :LANES]
                     v_out[lb, g, here, :LANES] = split[g * page : (g + 1) * page, LANES:]
-    loads[3].wait()
-
-
-def fetch(plan, select, table, stands, queries, keys, values):
+
+
+def fetch(plan, select, table, stands, keys, values):
     pages_dev, page, heads, size = keys.shape
     blocks, picked = select.shape[0], PICKED_PAGES
     span = page * heads
-    flat = (pages_dev, span, size)
-    operands = (select, table, stands, queries, keys.reshape(flat), values.reshape(flat))
     return pl.pallas_call(
         functools.partial(fetch_kernel, plan, pages_dev),
         out_shape=(
             jax.ShapeDtypeStruct((blocks, heads, picked * page, size), BF16),
             jax.ShapeDtypeStruct((blocks, heads, picked * page, size + LANES), BF16),
             jax.ShapeDtypeStruct((blocks, 3), jnp.int32),
-            jax.ShapeDtypeStruct(queries.shape, queries.dtype),
         ),
-        in_specs=[pl.BlockSpec(memory_space=pltpu.HBM)] * len(operands),
-        out_specs=(in_vmem(), in_vmem(), in_smem(), in_vmem()),
+        in_specs=[pl.BlockSpec(memory_space=pltpu.HBM)] * 5,
+        out_specs=(in_vmem(), in_vmem(), in_smem()),
         scratch_shapes=[
             SMEM(select.shape, jnp.int32),
             SMEM(table.shape, jnp.int32),
@@ -142,11 +136,11 @@
             VMEM((blocks, picked, span, size), BF16),
             VMEM((blocks, picked, span, size), BF16),
             pltpu.SemaphoreType.DMA((blocks, picked, 2)),
-            pltpu.SemaphoreType.DMA((4,)),
+            pltpu.SemaphoreType.DMA((3,)),
         ],
         compiler_params=params(16),
         cost_estimate=pl.CostEstimate(flops=2 * 10**9, bytes_accessed=8 * 2**20, transcendentals=0),
-    )(*(pltpu.with_memory_space_constraint(x, pltpu.HBM) for x in operands))
+    )(*(pltpu.with_memory_space_constraint(x, pltpu.HBM) for x in (select, table, stands, keys.reshape(pages_dev, span, size), values.reshape(pages_dev, span, size))))
 
 
 def pack_stats(lse, heads):
@@ -220,7 +214,7 @@
 
 
 def attend(plan, heads, lb, pages, queries):
-    keys, values, info, _ = pages
+    keys, values, info = pages
     part = plan.page // plan.chunks
     shape = jax.ShapeDtypeStruct((part, queries[0].shape[1] + LANES), BF16)
     return pl.pallas_call(
@@ -289,31 +283,15 @@
     )(near, far)
 
 
-def merge_finish_kernel(heads, *refs):
-    merge_kernel(heads, *refs[:-3], refs[-2])
-    finish_kernel(heads, refs[-2], refs[-3], refs[-1])
-
-
-def merge_finish(heads, far, *sources):
-    rows, wide = far.shape
-    return pl.pallas_call(
-        functools.partial(merge_finish_kernel, heads),
-        out_shape=(jax.ShapeDtypeStruct((rows, wide), BF16), jax.ShapeDtypeStruct((rows, wide - LANES), BF16)),
-        in_specs=[in_vmem()] * (len(sources) + 1),
-        out_specs=(in_vmem(),) * 2,
-        compiler_params=params(8),
-    )(*sources, far)
-
-
 def project_kernel(plan, lb, *refs):
     sources, weight, (keep, send, rows_ref) = refs[: plan.group], refs[plan.group], refs[plan.group + 1 :]
     me, column = lax.axis_index("pages"), lax.axis_index("mp")
     rows = plan.rows
     holders = plan.group // 2
-    for i, k in enumerate((*others(plan), 0)):
+    for k in range(plan.group):
         device = me ^ k ^ (lb * plan.cross)
         place = ((device // holders % 2) ^ (column % 2)) * holders + device % holders
-        rows_ref[pl.ds(pl.multiple_of(place * rows, rows), rows), :] = sources[i][...]
+        rows_ref[pl.ds(pl.multiple_of(place * rows, rows), rows), :] = sources[k][...]
     product = jnp.dot(rows_ref[...], weight[...], preferred_element_type=F32)
     part = holders * rows
     keep[...] = product[:part]
@@ -330,7 +308,7 @@
         out_specs=(in_vmem(), in_vmem()),
         scratch_shapes=[VMEM((plan.page, weight.shape[0]), BF16)],
         compiler_params=params(24),
-    )(*(sources[k] for k in (*others(plan), 0)), weight)
+    )(*(sources[k] for k in range(plan.group)), weight)
 
 
 def swap(x, axis, distance):
@@ -339,7 +317,7 @@
 
 
 def others(plan):
-    return range(plan.group - 1, 0, -1)
+    return range(1, plan.group)
 
 
 def spread(x, plan):
@@ -348,17 +326,15 @@
 
 def by_halves(plan, heads, queries, weight, pages):
     far = swap(queries, "pages", plan.cross)
-    received = []
-    for lb, rows in enumerate((pages[3], far)):
+    near = []
+    for lb, rows in enumerate((queries, far)):
         chunks = spread(rows, plan)
         outs = attend(plan, heads, lb, pages, [chunks[k] for k in range(plan.group)])
-        received.append([swap(outs[k], "pages", k) for k in others(plan)] + [outs[0]])
-    near = merge(heads, *received[0])
-    near_far, far_rows = merge_finish(heads, swap(near, "pages", plan.cross), *received[1])
-    across = swap(near_far, "pages", plan.cross)
+        near.append(merge(heads, outs[0], *(swap(outs[k], "pages", k) for k in others(plan))))
+    across = [swap(x, "pages", plan.cross) for x in near]
     sums = [None, None]
     for lb in (1, 0):
-        rows = far_rows if lb else finish(heads, near, across)
+        rows = finish(heads, near[lb], across[1 - lb])
         keep, send = project(plan, lb, spread(rows, plan), weight)
         sums[lb] = keep + swap(send, "mp", 1).astype(F32)
     stays = plan.block(lax.axis_index("pages"), 0) == lax.axis_index("mp") // 2
@@ -393,7 +369,7 @@
     n, ways = lax.axis_size("pages"), lax.axis_size("mp")
     plan = Plan(n, ways, queries.shape[0], select.shape[0], cached_keys.shape[1])
     heads = queries.shape[1] // cached_keys.shape[3]
-    pages = fetch(plan, select, page_table, block_page, queries, cached_keys, cached_values)
+    pages = fetch(plan, select, page_table, block_page, cached_keys, cached_values)
     way = by_halves if plan.halves else by_gathers
     return way(plan, heads, queries, out_weight, pages)
 

time: 66 us -> 61.3 us (0.929); the launches traced: 67.3 us -> 60.9 us
  starting transfers between devices: 26.1 us -> 37.4 us
  waiting for transfers between devices: 27.4 us -> 16.1 us
  Pallas kernels: 12.8 us -> 6.43 us
    ppermute x24, starting transfers between devices: 26.1 us -> 37.4 us  [swap(): return lax.ppermute(x, axis, [(i, i ^ distance) for i in range(n)])]
    ppermute x24, waiting for transfers between devices: 27.4 us -> 16.1 us  [swap(): return lax.ppermute(x, axis, [(i, i ^ distance) for i in range(n)])]
    pallas_call x2, Pallas kernels: 5.86 us -> 1.29 us  [attend(): pl.pallas_call(functools.partial(attend_kernel, plan, heads, lb), out_sha...]
    pallas_call x1, Pallas kernels: 3.69 us -> 1.97 us  [fetch(): pl.pallas_call(functools.partial(fetch_kernel, plan, pages_dev), out_shap...]
    pallas_call x1 -> x0, Pallas kernels: 0.9 us -> none  [merge_finish(): pl.pallas_call(functools.partial(merge_finish_kernel, heads), out_shape=(...]
  transfers between devices with their start and end apart: 24 -> 24, of which waited for: 12 -> 12; matrix products, arithmetic and copies ran while one was open for 0% -> 0% of each run, Pallas kernels for 18% -> 11%
where the time goes in v4:
time: 61.3 us; the launch traced here: 60.9 us
  starting transfers between devices  37.4 us (61%)
  waiting for transfers between devices  16.1 us (26%)
  Pallas kernels  6.43 us (10%)
  other arithmetic  0.78 us (1%)
    ppermute x24, starting transfers between devices, swap(): return lax.ppermute(x, axis, [(i, i ^ distance) for i in range(n)])  37.4 us
    ppermute x24, waiting for transfers between devices, swap(): return lax.ppermute(x, axis, [(i, i ^ distance) for i in range(n)])  16.1 us
    pallas_call x1, Pallas kernels, fetch(): pl.pallas_call(functools.partial(fetch_kernel, plan, pages_dev), out_shap...  1.97 us
    pallas_call x2, Pallas kernels, project(): pl.pallas_call(functools.partial(project_kernel, plan, lb), out_shape=(ja...  1.57 us
    pallas_call x2, Pallas kernels, attend(): pl.pallas_call(functools.partial(attend_kernel, plan, heads, lb), out_sha...  1.29 us
  transfers between devices with their start and end apart: 24, of which 12 were waited for; matrix products, arithmetic and copies ran while one was open for 0% of the time, Pallas kernels for 11%

profile of v4, /device:TPU:0, one launch (start us, length us, event | category | flops | bytes accessed | tf_op | source)
XLA Modules:
  0.0 60.9 jit_solution(6445077153537801494)
XLA Ops:
  0.0 5.0 %collective-permute-start.6 = (bf16[32,2048]{1,0:T(8,128)(2,1)}, bf16[32,2048]{1,0:T(8,128)(2,1)S(1)}, u32[]{:S(2)}, u32[]{:S(2)}) collective-permute-start(bf16[32,2048]{1,0:T(8,128)(2,1)} %refs_0_.1), channel_id=1, source_target_pairs={{0,24},{4,28},{8,16},{12,20},{16,8},{20,12},{24,0},{28,4},{1,25},{... | collective-permute-start | bytes 393224 | tf_op jit(solution)/shard_map/ppermute | solution.py:316
  5.1 1.5 %collective-permute-start = (bf16[32,2048]{1,0:T(8,128)(2,1)}, bf16[32,2048]{1,0:T(8,128)(2,1)S(1)}, u32[]{:S(2)}, u32[]{:S(2)}) collective-permute-start(bf16[32,2048]{1,0:T(8,128)(2,1)} %refs_0_.1), channel_id=1, source_target_pairs={{0,4},{4,0},{8,12},{12,8},{16,20},{20,16},{24,28},{28,24},{1,5},{5... | collective-permute-start | bytes 393224 | tf_op jit(solution)/shard_map/ppermute | solution.py:316
  6.5 2.0 %collective-permute-start.2 = (bf16[32,2048]{1,0:T(8,128)(2,1)}, bf16[32,2048]{1,0:T(8,128)(2,1)S(1)}, u32[]{:S(2)}, u32[]{:S(2)}) collective-permute-start(bf16[32,2048]{1,0:T(8,128)(2,1)} %refs_0_.1), channel_id=1, source_target_pairs={{0,12},{4,8},{8,4},{12,0},{16,28},{20,24},{24,20},{28,16},{1,13},{... | collective-permute-start | bytes 393224 | tf_op jit(solution)/shard_map/ppermute | solution.py:316
  8.5 2.0 %shard_map.73 = (bf16[2,2,768,128]{3,2,1,0:T(8,128)(2,1)S(1)}, bf16[2,2,768,256]{3,2,1,0:T(8,128)(2,1)S(1)}, s32[2,3]{1,0:T(2,128)S(1)}) custom-call(s32[2,24]{1,0:T(2,128)} %select_hbm.1, s32[128]{0:T(128)} %table_hbm.1, s32[2]{0:T(128)} %stands_hbm.1, bf16[16,256,128]{2,1,0:T(8,128)(2,1)} %bitcast.2, bf16[16,256,128]{2,1,0:T(8,128)(2,1)} %bitcast.3), custom_call_target="tpu_custom_call" | custom-call | flops 2000000000 | bytes 8388608 | tf_op jit(solution)/shard_map/pallas_call | solution.py:122
  10.5 0.0 collective-permute-done.6.refs_0_
  10.5 3.3 %collective-permute-start.7 = (bf16[32,2048]{1,0:T(8,128)(2,1)S(1)}, bf16[32,2048]{1,0:T(8,128)(2,1)S(1)}, u32[]{:S(2)}, u32[]{:S(2)}) collective-permute-start(bf16[32,2048]{1,0:T(8,128)(2,1)S(1)} %collective-permute-done.6.refs_0_), channel_id=1, source_target_pairs={{0,4},{4,0},{8,12},{12,8},{16,20},{20,16},{24,28},{28,24},{1,5},{5... | collective-permute-start | bytes 393224 | tf_op jit(solution)/shard_map/ppermute | solution.py:316
  13.8 0.0 collective-permute-start.8
  13.8 0.0 collective-permute-done.refs_1_
  13.8 1.5 %collective-permute-start.9 = (bf16[32,2048]{1,0:T(8,128)(2,1)S(1)}, bf16[32,2048]{1,0:T(8,128)(2,1)S(1)}, u32[]{:S(2)}, u32[]{:S(2)}) collective-permute-start(bf16[32,2048]{1,0:T(8,128)(2,1)S(1)} %collective-permute-done.6.refs_0_), channel_id=1, source_target_pairs={{0,12},{4,8},{8,4},{12,0},{16,28},{20,24},{24,20},{28,16},{1,13},{... | collective-permute-start | bytes 393224 | tf_op jit(solution)/shard_map/ppermute | solution.py:316
  15.4 0.0 collective-permute-done.1.refs_2_
  15.4 0.9 %collective-permute-done.2.refs_3_ = bf16[32,2048]{1,0:T(8,128)(2,1)S(1)} collective-permute-done((bf16[32,2048]{1,0:T(8,128)(2,1)}, bf16[32,2048]{1,0:T(8,128)(2,1)S(1)}, u32[]{:S(2)}, u32[]{:S(2)}) %collective-permute-start.2) | collective-permute-done | bytes 131104 | tf_op jit(solution)/shard_map/ppermute | solution.py:316
  16.3 0.6 %shard_map.74 = (bf16[32,2176]{1,0:T(8,128)(2,1)S(1)}, bf16[32,2176]{1,0:T(8,128)(2,1)S(1)}, bf16[32,2176]{1,0:T(8,128)(2,1)S(1)}, bf16[32,2176]{1,0:T(8,128)(2,1)S(1)}) custom-call(s32[2,3]{1,0:T(2,128)S(1)} %get-tuple-element.20.info, bf16[32,2048]{1,0:T(8,128)(2,1)S(1)} %copy-done.1, bf16[32,2048]{1,0:T(8,128)(2,1)S(1)} %collective-permute-done.refs_1_, ...), custom_call_target="tpu_custom_call" | custom-call | flops 2000000000 | bytes 4194304 | tf_op jit(solution)/shard_map/pallas_call | solution.py:220
  16.9 3.4 %collective-permute-start.3 = (bf16[32,2176]{1,0:T(8,128)(2,1)S(1)}, bf16[32,2176]{1,0:T(8,128)(2,1)S(1)}, u32[]{:S(2)}, u32[]{:S(2)}) collective-permute-start(bf16[32,2176]{1,0:T(8,128)(2,1)S(1)} %get-tuple-element.24), channel_id=1, source_target_pairs={{0,4},{4,0},{8,12},{12,8},{16,20},{20,16},{24,28},{28,24},{1,5},{5... | collective-permute-start | bytes 417800 | tf_op jit(solution)/shard_map/ppermute | solution.py:316
  20.3 1.3 %collective-permute-start.4 = (bf16[32,2176]{1,0:T(8,128)(2,1)S(1)}, bf16[32,2176]{1,0:T(8,128)(2,1)S(1)}, u32[]{:S(2)}, u32[]{:S(2)}) collective-permute-start(bf16[32,2176]{1,0:T(8,128)(2,1)S(1)} %get-tuple-element.25), channel_id=1, source_target_pairs={{0,8},{4,12},{8,0},{12,4},{16,24},{20,28},{24,16},{28,20},{1,9},{5... | collective-permute-start | bytes 417800 | tf_op jit(solution)/shard_map/ppermute | solution.py:316
  21.6 0.3 collective-permute-start.5
  21.9 0.6 %shard_map.76 = (bf16[32,2176]{1,0:T(8,128)(2,1)S(1)}, bf16[32,2176]{1,0:T(8,128)(2,1)S(1)}, bf16[32,2176]{1,0:T(8,128)(2,1)S(1)}, bf16[32,2176]{1,0:T(8,128)(2,1)S(1)}) custom-call(s32[2,3]{1,0:T(2,128)S(1)} %get-tuple-element.20.info, bf16[32,2048]{1,0:T(8,128)(2,1)S(1)} %collective-permute-done.6.refs_0_, ...), custom_call_target="tpu_custom_call" | custom-call | flops 2000000000 | bytes 4194304 | tf_op jit(solution)/shard_map/pallas_call | solution.py:220
  22.5 4.3 %collective-permute-start.10 = (bf16[32,2176]{1,0:T(8,128)(2,1)S(1)}, bf16[32,2176]{1,0:T(8,128)(2,1)S(1)}, u32[]{:S(2)}, u32[]{:S(2)}) collective-permute-start(bf16[32,2176]{1,0:T(8,128)(2,1)S(1)} %get-tuple-element.28), channel_id=1, source_target_pairs={{0,4},{4,0},{8,12},{12,8},{16,20},{20,16},{24,28},{28,24},{1,5},{5... | collective-permute-start | bytes 417800 | tf_op jit(solution)/shard_map/ppermute | solution.py:316
  26.8 1.3 %collective-permute-start.11 = (bf16[32,2176]{1,0:T(8,128)(2,1)S(1)}, bf16[32,2176]{1,0:T(8,128)(2,1)S(1)}, u32[]{:S(2)}, u32[]{:S(2)}) collective-permute-start(bf16[32,2176]{1,0:T(8,128)(2,1)S(1)} %get-tuple-element.29), channel_id=1, source_target_pairs={{0,8},{4,12},{8,0},{12,4},{16,24},{20,28},{24,16},{28,20},{1,9},{5... | collective-permute-start | bytes 417800 | tf_op jit(solution)/shard_map/ppermute | solution.py:316
  28.1 0.3 collective-permute-start.12
  28.4 0.8 %collective-permute-done.5.refs_3_ = bf16[32,2176]{1,0:T(8,128)(2,1)S(1)} collective-permute-done((bf16[32,2176]{1,0:T(8,128)(2,1)S(1)}, bf16[32,2176]{1,0:T(8,128)(2,1)S(1)}, u32[]{:S(2)}, u32[]{:S(2)}) %collective-permute-start.5) | collective-permute-done | bytes 139296 | tf_op jit(solution)/shard_map/ppermute | solution.py:316
  29.2 0.5 shard_map.75.near
  29.6 1.6 %collective-permute-start.18 = (bf16[32,2176]{1,0:T(8,128)(2,1)S(1)}, bf16[32,2176]{1,0:T(8,128)(2,1)S(1)}, u32[]{:S(2)}, u32[]{:S(2)}) collective-permute-start(bf16[32,2176]{1,0:T(8,128)(2,1)S(1)} %shard_map.75.near), channel_id=1, source_target_pairs={{0,24},{4,28},{8,16},{12,20},{16,8},{20,12},{24,0},{28,4},{1,25},{... | collective-permute-start | bytes 417800 | tf_op jit(solution)/shard_map/ppermute | solution.py:316
  31.3 0.5 collective-permute-done.10.refs_1_
  31.7 1.3 %collective-permute-done.11.refs_2_ = bf16[32,2176]{1,0:T(8,128)(2,1)S(1)} collective-permute-done((bf16[32,2176]{1,0:T(8,128)(2,1)S(1)}, bf16[32,2176]{1,0:T(8,128)(2,1)S(1)}, u32[]{:S(2)}, u32[]{:S(2)}) %collective-permute-start.11) | collective-permute-done | bytes 139296 | tf_op jit(solution)/shard_map/ppermute | solution.py:316
  33.0 2.6 %collective-permute-done.12.refs_3_ = bf16[32,2176]{1,0:T(8,128)(2,1)S(1)} collective-permute-done((bf16[32,2176]{1,0:T(8,128)(2,1)S(1)}, bf16[32,2176]{1,0:T(8,128)(2,1)S(1)}, u32[]{:S(2)}, u32[]{:S(2)}) %collective-permute-start.12) | collective-permute-done | bytes 139296 | tf_op jit(solution)/shard_map/ppermute | solution.py:316
  35.6 0.5 shard_map.77.near
  36.0 1.4 %collective-permute-start.13 = (bf16[32,2176]{1,0:T(8,128)(2,1)S(1)}, bf16[32,2176]{1,0:T(8,128)(2,1)S(1)}, u32[]{:S(2)}, u32[]{:S(2)}) collective-permute-start(bf16[32,2176]{1,0:T(8,128)(2,1)S(1)} %shard_map.77.near), channel_id=1, source_target_pairs={{0,24},{4,28},{8,16},{12,20},{16,8},{20,12},{24,0},{28,4},{1,25},{... | collective-permute-start | bytes 417800 | tf_op jit(solution)/shard_map/ppermute | solution.py:316
  37.4 0.4 collective-permute-done.18.far
  37.8 0.3 shard_map.80.refs_0_
  38.1 2.3 %collective-permute-start.19 = (bf16[32,2048]{1,0:T(8,128)(2,1)S(1)}, bf16[32,2048]{1,0:T(8,128)(2,1)S(1)}, u32[]{:S(2)}, u32[]{:S(2)}) collective-permute-start(bf16[32,2048]{1,0:T(8,128)(2,1)S(1)} %shard_map.80.refs_0_), channel_id=1, source_target_pairs={{0,4},{4,0},{8,12},{12,8},{16,20},{20,16},{24,28},{28,24},{1,5},{5... | collective-permute-start | bytes 393224 | tf_op jit(solution)/shard_map/ppermute | solution.py:316
  40.4 2.1 %collective-permute-start.20 = (bf16[32,2048]{1,0:T(8,128)(2,1)S(1)}, bf16[32,2048]{1,0:T(8,128)(2,1)S(1)}, u32[]{:S(2)}, u32[]{:S(2)}) collective-permute-start(bf16[32,2048]{1,0:T(8,128)(2,1)S(1)} %shard_map.80.refs_0_), channel_id=1, source_target_pairs={{0,8},{4,12},{8,0},{12,4},{16,24},{20,28},{24,16},{28,20},{1,9},{5... | collective-permute-start | bytes 393224 | tf_op jit(solution)/shard_map/ppermute | solution.py:316
  42.5 0.5 collective-permute-done.13.far
  43.0 0.3 shard_map.78.refs_0_
  43.3 1.4 %collective-permute-start.14 = (bf16[32,2048]{1,0:T(8,128)(2,1)S(1)}, bf16[32,2048]{1,0:T(8,128)(2,1)S(1)}, u32[]{:S(2)}, u32[]{:S(2)}) collective-permute-start(bf16[32,2048]{1,0:T(8,128)(2,1)S(1)} %shard_map.78.refs_0_), channel_id=1, source_target_pairs={{0,4},{4,0},{8,12},{12,8},{16,20},{20,16},{24,28},{28,24},{1,5},{5... | collective-permute-start | bytes 393224 | tf_op jit(solution)/shard_map/ppermute | solution.py:316
  44.7 1.7 %collective-permute-start.15 = (bf16[32,2048]{1,0:T(8,128)(2,1)S(1)}, bf16[32,2048]{1,0:T(8,128)(2,1)S(1)}, u32[]{:S(2)}, u32[]{:S(2)}) collective-permute-start(bf16[32,2048]{1,0:T(8,128)(2,1)S(1)} %shard_map.78.refs_0_), channel_id=1, source_target_pairs={{0,8},{4,12},{8,0},{12,4},{16,24},{20,28},{24,16},{28,20},{1,9},{5... | collective-permute-start | bytes 393224 | tf_op jit(solution)/shard_map/ppermute | solution.py:316
  46.4 1.1 %collective-permute-start.16 = (bf16[32,2048]{1,0:T(8,128)(2,1)S(1)}, bf16[32,2048]{1,0:T(8,128)(2,1)S(1)}, u32[]{:S(2)}, u32[]{:S(2)}) collective-permute-start(bf16[32,2048]{1,0:T(8,128)(2,1)S(1)} %shard_map.78.refs_0_), channel_id=1, source_target_pairs={{0,12},{4,8},{8,4},{12,0},{16,28},{20,24},{24,20},{28,16},{1,13},{... | collective-permute-start | bytes 393224 | tf_op jit(solution)/shard_map/ppermute | solution.py:316
  47.5 1.9 %collective-permute-done.21.refs_3_ = bf16[32,2048]{1,0:T(8,128)(2,1)S(1)} collective-permute-done((bf16[32,2048]{1,0:T(8,128)(2,1)S(1)}, bf16[32,2048]{1,0:T(8,128)(2,1)S(1)}, u32[]{:S(2)}, u32[]{:S(2)}) %collective-permute-start.21) | collective-permute-done | bytes 131104 | tf_op jit(solution)/shard_map/ppermute | solution.py:316
  49.4 0.8 %shard_map.81 = (f32[64,1024]{1,0:T(8,128)S(1)}, bf16[64,1024]{1,0:T(8,128)(2,1)S(1)}) custom-call(bf16[32,2048]{1,0:T(8,128)(2,1)S(1)} %shard_map.80.refs_0_, bf16[32,2048]{1,0:T(8,128)(2,1)S(1)} %collective-permute-done.19.refs_1_, bf16[32,2048]{1,0:T(8,128)(2,1)S(1)} %collective-permute-done.20.refs_2_, ...), custom_call_target="tpu_custom_call" | custom-call | tf_op jit(solution)/shard_map/pallas_call | solution.py:304
  50.2 0.1 collective-permute-start.22
  50.3 0.4 collective-permute-done.14.refs_1_
  50.7 1.6 %collective-permute-done.16.refs_3_ = bf16[32,2048]{1,0:T(8,128)(2,1)S(1)} collective-permute-done((bf16[32,2048]{1,0:T(8,128)(2,1)S(1)}, bf16[32,2048]{1,0:T(8,128)(2,1)S(1)}, u32[]{:S(2)}, u32[]{:S(2)}) %collective-permute-start.16) | collective-permute-done | bytes 131104 | tf_op jit(solution)/shard_map/ppermute | solution.py:316
  52.3 0.8 %shard_map.79 = (f32[64,1024]{1,0:T(8,128)S(1)}, bf16[64,1024]{1,0:T(8,128)(2,1)S(1)}) custom-call(bf16[32,2048]{1,0:T(8,128)(2,1)S(1)} %shard_map.78.refs_0_, bf16[32,2048]{1,0:T(8,128)(2,1)S(1)} %collective-permute-done.14.refs_1_, bf16[32,2048]{1,0:T(8,128)(2,1)S(1)} %collective-permute-done.15.refs_2_, ...), custom_call_target="tpu_custom_call" | custom-call | tf_op jit(solution)/shard_map/pallas_call | solution.py:304
  53.1 0.1 collective-permute-start.17
  53.2 1.3 %collective-permute-done.17 = bf16[64,1024]{1,0:T(8,128)(2,1)S(1)} collective-permute-done((bf16[64,1024]{1,0:T(8,128)(2,1)S(1)}, bf16[64,1024]{1,0:T(8,128)(2,1)S(1)}, u32[]{:S(2)}, u32[]{:S(2)}) %collective-permute-start.17) | collective-permute-done | bytes 131104 | tf_op jit(solution)/shard_map/ppermute | solution.py:316
  54.5 0.1 select_convert_fusion
  54.5 1.6 %collective-permute-start.23 = (bf16[64,1024]{1,0:T(8,128)(2,1)S(1)}, bf16[64,1024]{1,0:T(8,128)(2,1)S(1)}, u32[]{:S(2)}, u32[]{:S(2)}) collective-permute-start(bf16[64,1024]{1,0:T(8,128)(2,1)S(1)} %select_convert_fusion), channel_id=1, source_target_pairs={{0,2},{1,3},{2,0},{3,1},{4,6},{5,7},{6,4},{7,5},{8,10},{9,11},{10,... | collective-permute-start | bytes 393224 | tf_op jit(solution)/shard_map/ppermute | solution.py:316
  56.1 4.0 %collective-permute-done.23 = bf16[64,1024]{1,0:T(8,128)(2,1)S(1)} collective-permute-done((bf16[64,1024]{1,0:T(8,128)(2,1)S(1)}, bf16[64,1024]{1,0:T(8,128)(2,1)S(1)}, u32[]{:S(2)}, u32[]{:S(2)}) %collective-permute-start.23) | collective-permute-done | bytes 131104 | tf_op jit(solution)/shard_map/ppermute | solution.py:316
  60.1 0.7 %add_convert_fusion = bf16[64,1024]{1,0:T(8,128)(2,1)} fusion(bf16[64,1024]{1,0:T(8,128)(2,1)S(1)} %collective-permute-done.23, f32[64,1024]{1,0:T(8,128)S(1)} %get-tuple-element.31, bf16[64,1024]{1,0:T(8,128)(2,1)S(1)} %collective-permute-done.17, f32[64,1024]{1,0:T(8,128)S(1)} %get-tuple-element.33, bf16[64,1024]{1,0:T(8,128)(2,1)S(1)} %collective-permute-done.22, ...), kind=kLoop, calls=%fused_computation | loop fusion | flops 524288 | bytes 1048577 | tf_op jit(solution)/shard_map/convert_element_type | solution.py:343
  (15 shorter events, 0.0 us)
Async XLA Ops:
  0.0 16.3 %copy-start.1 = (bf16[32,2048]{1,0:T(8,128)(2,1)S(1)}, bf16[32,2048]{1,0:T(8,128)(2,1)}, u32[]{:S(2)}) copy-start(bf16[32,2048]{1,0:T(8,128)(2,1)} %refs_0_.1) | copy-start | bytes 393220
  0.0 10.5 %collective-permute-start.6 = (bf16[32,2048]{1,0:T(8,128)(2,1)}, bf16[32,2048]{1,0:T(8,128)(2,1)S(1)}, u32[]{:S(2)}, u32[]{:S(2)}) collective-permute-start(bf16[32,2048]{1,0:T(8,128)(2,1)} %refs_0_.1), channel_id=1, source_target_pairs={{0,24},{4,28},{8,16},{12,20},{16,8},{20,12},{24,0},{28,4},{1,25},{... | collective-permute-start | bytes 393224 | tf_op jit(solution)/shard_map/ppermute | solution.py:316
  5.1 8.8 %collective-permute-start = (bf16[32,2048]{1,0:T(8,128)(2,1)}, bf16[32,2048]{1,0:T(8,128)(2,1)S(1)}, u32[]{:S(2)}, u32[]{:S(2)}) collective-permute-start(bf16[32,2048]{1,0:T(8,128)(2,1)} %refs_0_.1), channel_id=1, source_target_pairs={{0,4},{4,0},{8,12},{12,8},{16,20},{20,16},{24,28},{28,24},{1,5},{5... | collective-permute-start | bytes 393224 | tf_op jit(solution)/shard_map/ppermute | solution.py:316
  6.5 8.8 %collective-permute-start.1 = (bf16[32,2048]{1,0:T(8,128)(2,1)}, bf16[32,2048]{1,0:T(8,128)(2,1)S(1)}, u32[]{:S(2)}, u32[]{:S(2)}) collective-permute-start(bf16[32,2048]{1,0:T(8,128)(2,1)} %refs_0_.1), channel_id=1, source_target_pairs={{0,8},{4,12},{8,0},{12,4},{16,24},{20,28},{24,16},{28,20},{1,9},{5... | collective-permute-start | bytes 393224 | tf_op jit(solution)/shard_map/ppermute | solution.py:316
  6.5 9.7 %collective-permute-start.2 = (bf16[32,2048]{1,0:T(8,128)(2,1)}, bf16[32,2048]{1,0:T(8,128)(2,1)S(1)}, u32[]{:S(2)}, u32[]{:S(2)}) collective-permute-start(bf16[32,2048]{1,0:T(8,128)(2,1)} %refs_0_.1), channel_id=1, source_target_pairs={{0,12},{4,8},{8,4},{12,0},{16,28},{20,24},{24,20},{28,16},{1,13},{... | collective-permute-start | bytes 393224 | tf_op jit(solution)/shard_map/ppermute | solution.py:316
  10.5 11.1 %collective-permute-start.7 = (bf16[32,2048]{1,0:T(8,128)(2,1)S(1)}, bf16[32,2048]{1,0:T(8,128)(2,1)S(1)}, u32[]{:S(2)}, u32[]{:S(2)}) collective-permute-start(bf16[32,2048]{1,0:T(8,128)(2,1)S(1)} %collective-permute-done.6.refs_0_), channel_id=1, source_target_pairs={{0,4},{4,0},{8,12},{12,8},{16,20},{20,16},{24,28},{28,24},{1,5},{5... | collective-permute-start | bytes 393224 | tf_op jit(solution)/shard_map/ppermute | solution.py:316
  13.8 8.1 %collective-permute-start.8 = (bf16[32,2048]{1,0:T(8,128)(2,1)S(1)}, bf16[32,2048]{1,0:T(8,128)(2,1)S(1)}, u32[]{:S(2)}, u32[]{:S(2)}) collective-permute-start(bf16[32,2048]{1,0:T(8,128)(2,1)S(1)} %collective-permute-done.6.refs_0_), channel_id=1, source_target_pairs={{0,8},{4,12},{8,0},{12,4},{16,24},{20,28},{24,16},{28,20},{1,9},{5... | collective-permute-start | bytes 393224 | tf_op jit(solution)/shard_map/ppermute | solution.py:316
  13.8 8.1 %collective-permute-start.9 = (bf16[32,2048]{1,0:T(8,128)(2,1)S(1)}, bf16[32,2048]{1,0:T(8,128)(2,1)S(1)}, u32[]{:S(2)}, u32[]{:S(2)}) collective-permute-start(bf16[32,2048]{1,0:T(8,128)(2,1)S(1)} %collective-permute-done.6.refs_0_), channel_id=1, source_target_pairs={{0,12},{4,8},{8,4},{12,0},{16,28},{20,24},{24,20},{28,16},{1,13},{... | collective-permute-start | bytes 393224 | tf_op jit(solution)/shard_map/ppermute | solution.py:316
  16.9 11.2 %collective-permute-start.3 = (bf16[32,2176]{1,0:T(8,128)(2,1)S(1)}, bf16[32,2176]{1,0:T(8,128)(2,1)S(1)}, u32[]{:S(2)}, u32[]{:S(2)}) collective-permute-start(bf16[32,2176]{1,0:T(8,128)(2,1)S(1)} %get-tuple-element.24), channel_id=1, source_target_pairs={{0,4},{4,0},{8,12},{12,8},{16,20},{20,16},{24,28},{28,24},{1,5},{5... | collective-permute-start | bytes 417800 | tf_op jit(solution)/shard_map/ppermute | solution.py:316
  20.3 8.1 %collective-permute-start.4 = (bf16[32,2176]{1,0:T(8,128)(2,1)S(1)}, bf16[32,2176]{1,0:T(8,128)(2,1)S(1)}, u32[]{:S(2)}, u32[]{:S(2)}) collective-permute-start(bf16[32,2176]{1,0:T(8,128)(2,1)S(1)} %get-tuple-element.25), channel_id=1, source_target_pairs={{0,8},{4,12},{8,0},{12,4},{16,24},{20,28},{24,16},{28,20},{1,9},{5... | collective-permute-start | bytes 417800 | tf_op jit(solution)/shard_map/ppermute | solution.py:316
  21.6 27.8 %copy-start = (bf16[2048,1024]{1,0:T(8,128)(2,1)S(1)}, bf16[2048,1024]{1,0:T(8,128)(2,1)}, u32[]{:S(2)}) copy-start(bf16[2048,1024]{1,0:T(8,128)(2,1)} %refs_4_.3) | copy-start | bytes 12582916
  21.6 7.5 %collective-permute-start.5 = (bf16[32,2176]{1,0:T(8,128)(2,1)S(1)}, bf16[32,2176]{1,0:T(8,128)(2,1)S(1)}, u32[]{:S(2)}, u32[]{:S(2)}) collective-permute-start(bf16[32,2176]{1,0:T(8,128)(2,1)S(1)} %get-tuple-element.26), channel_id=1, source_target_pairs={{0,12},{4,8},{8,4},{12,0},{16,28},{20,24},{24,20},{28,16},{1,13},{... | collective-permute-start | bytes 417800 | tf_op jit(solution)/shard_map/ppermute | solution.py:316
  22.5 9.2 %collective-permute-start.10 = (bf16[32,2176]{1,0:T(8,128)(2,1)S(1)}, bf16[32,2176]{1,0:T(8,128)(2,1)S(1)}, u32[]{:S(2)}, u32[]{:S(2)}) collective-permute-start(bf16[32,2176]{1,0:T(8,128)(2,1)S(1)} %get-tuple-element.28), channel_id=1, source_target_pairs={{0,4},{4,0},{8,12},{12,8},{16,20},{20,16},{24,28},{28,24},{1,5},{5... | collective-permute-start | bytes 417800 | tf_op jit(solution)/shard_map/ppermute | solution.py:316
  26.8 6.2 %collective-permute-start.11 = (bf16[32,2176]{1,0:T(8,128)(2,1)S(1)}, bf16[32,2176]{1,0:T(8,128)(2,1)S(1)}, u32[]{:S(2)}, u32[]{:S(2)}) collective-permute-start(bf16[32,2176]{1,0:T(8,128)(2,1)S(1)} %get-tuple-element.29), channel_id=1, source_target_pairs={{0,8},{4,12},{8,0},{12,4},{16,24},{20,28},{24,16},{28,20},{1,9},{5... | collective-permute-start | bytes 417800 | tf_op jit(solution)/shard_map/ppermute | solution.py:316
  28.1 7.4 %collective-permute-start.12 = (bf16[32,2176]{1,0:T(8,128)(2,1)S(1)}, bf16[32,2176]{1,0:T(8,128)(2,1)S(1)}, u32[]{:S(2)}, u32[]{:S(2)}) collective-permute-start(bf16[32,2176]{1,0:T(8,128)(2,1)S(1)} %get-tuple-element.30), channel_id=1, source_target_pairs={{0,12},{4,8},{8,4},{12,0},{16,28},{20,24},{24,20},{28,16},{1,13},{... | collective-permute-start | bytes 417800 | tf_op jit(solution)/shard_map/ppermute | solution.py:316
  29.6 8.2 %collective-permute-start.18 = (bf16[32,2176]{1,0:T(8,128)(2,1)S(1)}, bf16[32,2176]{1,0:T(8,128)(2,1)S(1)}, u32[]{:S(2)}, u32[]{:S(2)}) collective-permute-start(bf16[32,2176]{1,0:T(8,128)(2,1)S(1)} %shard_map.75.near), channel_id=1, source_target_pairs={{0,24},{4,28},{8,16},{12,20},{16,8},{20,12},{24,0},{28,4},{1,25},{... | collective-permute-start | bytes 417800 | tf_op jit(solution)/shard_map/ppermute | solution.py:316
  36.0 6.9 %collective-permute-start.13 = (bf16[32,2176]{1,0:T(8,128)(2,1)S(1)}, bf16[32,2176]{1,0:T(8,128)(2,1)S(1)}, u32[]{:S(2)}, u32[]{:S(2)}) collective-permute-start(bf16[32,2176]{1,0:T(8,128)(2,1)S(1)} %shard_map.77.near), channel_id=1, source_target_pairs={{0,24},{4,28},{8,16},{12,20},{16,8},{20,12},{24,0},{28,4},{1,25},{... | collective-permute-start | bytes 417800 | tf_op jit(solution)/shard_map/ppermute | solution.py:316
  38.1 8.3 %collective-permute-start.19 = (bf16[32,2048]{1,0:T(8,128)(2,1)S(1)}, bf16[32,2048]{1,0:T(8,128)(2,1)S(1)}, u32[]{:S(2)}, u32[]{:S(2)}) collective-permute-start(bf16[32,2048]{1,0:T(8,128)(2,1)S(1)} %shard_map.80.refs_0_), channel_id=1, source_target_pairs={{0,4},{4,0},{8,12},{12,8},{16,20},{20,16},{24,28},{28,24},{1,5},{5... | collective-permute-start | bytes 393224 | tf_op jit(solution)/shard_map/ppermute | solution.py:316
  40.4 7.0 %collective-permute-start.20 = (bf16[32,2048]{1,0:T(8,128)(2,1)S(1)}, bf16[32,2048]{1,0:T(8,128)(2,1)S(1)}, u32[]{:S(2)}, u32[]{:S(2)}) collective-permute-start(bf16[32,2048]{1,0:T(8,128)(2,1)S(1)} %shard_map.80.refs_0_), channel_id=1, source_target_pairs={{0,8},{4,12},{8,0},{12,4},{16,24},{20,28},{24,16},{28,20},{1,9},{5... | collective-permute-start | bytes 393224 | tf_op jit(solution)/shard_map/ppermute | solution.py:316
  42.5 6.9 %collective-permute-start.21 = (bf16[32,2048]{1,0:T(8,128)(2,1)S(1)}, bf16[32,2048]{1,0:T(8,128)(2,1)S(1)}, u32[]{:S(2)}, u32[]{:S(2)}) collective-permute-start(bf16[32,2048]{1,0:T(8,128)(2,1)S(1)} %shard_map.80.refs_0_), channel_id=1, source_target_pairs={{0,12},{4,8},{8,4},{12,0},{16,28},{20,24},{24,20},{28,16},{1,13},{... | collective-permute-start | bytes 393224 | tf_op jit(solution)/shard_map/ppermute | solution.py:316
  43.3 7.4 %collective-permute-start.14 = (bf16[32,2048]{1,0:T(8,128)(2,1)S(1)}, bf16[32,2048]{1,0:T(8,128)(2,1)S(1)}, u32[]{:S(2)}, u32[]{:S(2)}) collective-permute-start(bf16[32,2048]{1,0:T(8,128)(2,1)S(1)} %shard_map.78.refs_0_), channel_id=1, source_target_pairs={{0,4},{4,0},{8,12},{12,8},{16,20},{20,16},{24,28},{28,24},{1,5},{5... | collective-permute-start | bytes 393224 | tf_op jit(solution)/shard_map/ppermute | solution.py:316
  44.7 6.0 %collective-permute-start.15 = (bf16[32,2048]{1,0:T(8,128)(2,1)S(1)}, bf16[32,2048]{1,0:T(8,128)(2,1)S(1)}, u32[]{:S(2)}, u32[]{:S(2)}) collective-permute-start(bf16[32,2048]{1,0:T(8,128)(2,1)S(1)} %shard_map.78.refs_0_), channel_id=1, source_target_pairs={{0,8},{4,12},{8,0},{12,4},{16,24},{20,28},{24,16},{28,20},{1,9},{5... | collective-permute-start | bytes 393224 | tf_op jit(solution)/shard_map/ppermute | solution.py:316
  46.4 5.9 %collective-permute-start.16 = (bf16[32,2048]{1,0:T(8,128)(2,1)S(1)}, bf16[32,2048]{1,0:T(8,128)(2,1)S(1)}, u32[]{:S(2)}, u32[]{:S(2)}) collective-permute-start(bf16[32,2048]{1,0:T(8,128)(2,1)S(1)} %shard_map.78.refs_0_), channel_id=1, source_target_pairs={{0,12},{4,8},{8,4},{12,0},{16,28},{20,24},{24,20},{28,16},{1,13},{... | collective-permute-start | bytes 393224 | tf_op jit(solution)/shard_map/ppermute | solution.py:316
  50.2 3.0 %collective-permute-start.22 = (bf16[64,1024]{1,0:T(8,128)(2,1)S(1)}, bf16[64,1024]{1,0:T(8,128)(2,1)S(1)}, u32[]{:S(2)}, u32[]{:S(2)}) collective-permute-start(bf16[64,1024]{1,0:T(8,128)(2,1)S(1)} %get-tuple-element.34), channel_id=1, source_target_pairs={{0,1},{1,0},{2,3},{3,2},{4,5},{5,4},{6,7},{7,6},{8,9},{9,8},{10,11... | collective-permute-start | bytes 393224 | tf_op jit(solution)/shard_map/ppermute | solution.py:316
  53.1 1.4 %collective-permute-start.17 = (bf16[64,1024]{1,0:T(8,128)(2,1)S(1)}, bf16[64,1024]{1,0:T(8,128)(2,1)S(1)}, u32[]{:S(2)}, u32[]{:S(2)}) collective-permute-start(bf16[64,1024]{1,0:T(8,128)(2,1)S(1)} %get-tuple-element.32), channel_id=1, source_target_pairs={{0,1},{1,0},{2,3},{3,2},{4,5},{5,4},{6,7},{7,6},{8,9},{9,8},{10,11... | collective-permute-start | bytes 393224 | tf_op jit(solution)/shard_map/ppermute | solution.py:316
  54.5 5.6 %collective-permute-start.23 = (bf16[64,1024]{1,0:T(8,128)(2,1)S(1)}, bf16[64,1024]{1,0:T(8,128)(2,1)S(1)}, u32[]{:S(2)}, u32[]{:S(2)}) collective-permute-start(bf16[64,1024]{1,0:T(8,128)(2,1)S(1)} %select_convert_fusion), channel_id=1, source_target_pairs={{0,2},{1,3},{2,0},{3,1},{4,6},{5,7},{6,4},{7,5},{8,10},{9,11},{10,... | collective-permute-start | bytes 393224 | tf_op jit(solution)/shard_map/ppermute | solution.py:316

commit v5 on v3

--- a/solution.py
+++ b/solution.py
@@ -33,37 +33,51 @@
 
 class Plan:
     def __init__(self, n, ways, rows, blocks, page):
-        self.n, self.rows, self.blocks, self.page = n, rows, blocks, page
+        self.n, self.ways, self.rows, self.blocks, self.page = n, ways, rows, blocks, page
         self.group = n // blocks
         self.halves = blocks == 2 and n == 8 and ways == 4 and rows * self.group == page
         self.cross = n * 3 // 4
-        self.chunks = self.group if self.halves else 1
 
     def block(self, me, lb):
         return (me // self.group) ^ lb if self.halves else lb
+
+    def holder(self, me, column, lb, chunk):
+        turned = chunk // 2 + chunk % 2 * 2
+        return me ^ (lb * self.cross) ^ jnp.where(column % 2 == 0, turned, chunk)
 
     def offsets(self, me, lb, shape):
         row = lax.broadcasted_iota(jnp.int32, shape, 0) % self.page
         if not self.halves:
             return row
-        mine = (me ^ (lb * self.cross)) % self.group
-        return ((row // self.rows) ^ mine) * self.rows + row % self.rows
+        holder = self.holder(me, lax.axis_index("mp"), lb, row // self.rows)
+        return holder % self.group * self.rows + row % self.rows
+
+    def swap(self, x, turn):
+        pairs = [
+            (p * self.ways + m, (p ^ (1 + (m + turn) % 2)) * self.ways + m)
+            for p in range(self.n)
+            for m in range(self.ways)
+        ]
+        return lax.ppermute(x, ("pages", "mp"), pairs)
 
 
 def fetch_kernel(plan, pages_dev, *refs):
     select_hbm, table_hbm, stands_hbm, queries, keys, values, k_out, v_out, info, q_out = refs[:10]
     select, table, stands, rows, k_buf, v_buf, sems, int_sems = refs[10:]
     me = lax.axis_index("pages")
-    blocks, picked = k_buf.shape[:2]
-    span = k_buf.shape[2]
-    heads = k_out.shape[1]
+    blocks, heads = k_out.shape[:2]
+    span = k_buf.shape[1]
     page = span // heads
+    picked = k_out.shape[2] // page
     low = me * pages_dev
     loads = [
         pltpu.make_async_copy(a, b, int_sems.at[i])
-        for i, (a, b) in enumerate(((select_hbm, select), (table_hbm, table), (stands_hbm, stands), (queries, q_out)))
+        for i, (a, b) in enumerate(((select_hbm, select), (table_hbm, table), (stands_hbm, stands), (queries, q_out.at[: queries.shape[0]])))
     ]
-    for load in loads:
+    whole = [
+        pltpu.make_async_copy(a, b, sems.at[i]) for i, (a, b) in enumerate(((keys, k_buf), (values, v_buf)))
+    ]
+    for load in loads + whole:
         load.start()
     row = lax.broadcasted_iota(jnp.int32, (span, span), 0)
     column = lax.broadcasted_iota(jnp.int32, (span, span), 1)
@@ -92,13 +106,8 @@
         info[lb, 0] = count
         info[lb, 1] = rows[blocks + lb, 0]
 
-        @pl.when(count > 0)
-        def _(lb=lb):
-            for slot in range(picked):
-                local = jnp.clip(rows[lb, slot], 0, pages_dev - 1)
-                pltpu.make_async_copy(keys.at[local], k_buf.at[lb, slot], sems.at[lb, slot, 0]).start()
-                pltpu.make_async_copy(values.at[local], v_buf.at[lb, slot], sems.at[lb, slot, 1]).start()
-
+    for load in whole:
+        load.wait()
     for lb in range(blocks):
 
         @pl.when(info[lb, 0] > 0)
@@ -106,10 +115,8 @@
             for g in range(heads):
                 v_out[lb, g, :, LANES:] = jnp.ones((picked * page, LANES), BF16)
             for slot in range(picked):
-                pltpu.make_async_copy(keys.at[0], k_buf.at[lb, slot], sems.at[lb, slot, 0]).wait()
-                pltpu.make_async_copy(values.at[0], v_buf.at[lb, slot], sems.at[lb, slot, 1]).wait()
-            for slot in range(picked):
-                both = jnp.concatenate([k_buf[lb, slot], v_buf[lb, slot]], axis=1)
+                local = jnp.clip(rows[lb, slot], 0, pages_dev - 1)
+                both = jnp.concatenate([k_buf[local], v_buf[local]], axis=1)
                 split = jnp.dot(apart, both, preferred_element_type=F32).astype(BF16)
                 for g in range(heads):
                     here = slice(slot * page, (slot + 1) * page)
@@ -130,7 +137,7 @@
             jax.ShapeDtypeStruct((blocks, heads, picked * page, size), BF16),
             jax.ShapeDtypeStruct((blocks, heads, picked * page, size + LANES), BF16),
             jax.ShapeDtypeStruct((blocks, 3), jnp.int32),
-            jax.ShapeDtypeStruct(queries.shape, queries.dtype),
+            jax.ShapeDtypeStruct((2 * queries.shape[0], queries.shape[1]), queries.dtype),
         ),
         in_specs=[pl.BlockSpec(memory_space=pltpu.HBM)] * len(operands),
         out_specs=(in_vmem(), in_vmem(), in_smem(), in_vmem()),
@@ -139,9 +146,9 @@
             SMEM(table.shape, jnp.int32),
             SMEM(stands.shape, jnp.int32),
             SMEM((2 * blocks, picked + 1), jnp.int32),
-            VMEM((blocks, picked, span, size), BF16),
-            VMEM((blocks, picked, span, size), BF16),
-            pltpu.SemaphoreType.DMA((blocks, picked, 2)),
+            VMEM((pages_dev, span, size), BF16),
+            VMEM((pages_dev, span, size), BF16),
+            pltpu.SemaphoreType.DMA((2,)),
             pltpu.SemaphoreType.DMA((4,)),
         ],
         compiler_params=params(16),
@@ -168,7 +175,7 @@
 
 def attend_kernel(plan, heads, lb, info, *refs):
     me = lax.axis_index("pages")
-    chunks, page = plan.chunks, plan.page
+    chunks, page = len(refs) // 2 - 1, plan.page
     queries, (k_ref, v_ref), outs = refs[:chunks], refs[chunks : chunks + 2], refs[chunks + 2 :]
     kv_heads, size = k_ref.shape[1], k_ref.shape[3]
     repeat = heads // kv_heads
@@ -221,13 +228,13 @@
 
 def attend(plan, heads, lb, pages, queries):
     keys, values, info, _ = pages
-    part = plan.page // plan.chunks
+    part = plan.page // len(queries)
     shape = jax.ShapeDtypeStruct((part, queries[0].shape[1] + LANES), BF16)
     return pl.pallas_call(
         functools.partial(attend_kernel, plan, heads, lb),
-        out_shape=(shape,) * plan.chunks,
+        out_shape=(shape,) * len(queries),
         in_specs=[in_smem()] + [in_vmem()] * (len(queries) + 2),
-        out_specs=(in_vmem(),) * plan.chunks,
+        out_specs=(in_vmem(),) * len(queries),
         compiler_params=params(32),
         cost_estimate=pl.CostEstimate(flops=2 * 10**9, bytes_accessed=4 * 2**20, transcendentals=10**6),
     )(info, *queries, keys, values)
@@ -247,28 +254,34 @@
     return head, top + jnp.log2(total)
 
 
-def merge_kernel(heads, *refs):
-    sources, out = refs[:-1], refs[-1]
-    width = out.shape[1] - LANES
+def heads_of(ref, size):
+    return lambda h: ref[:, h * size : (h + 1) * size]
+
+
+def merge_kernel(heads, first, second, *outs):
+    width = first.shape[1] - LANES
     size = width // heads
+    part = outs[0].shape[0]
+    sources = (first, second)
     head, lse = merged([heads_of(r, size) for r in sources], [unpack_stats(r[:, width:], heads) for r in sources])
     for h in range(heads):
-        out[:, h * size : (h + 1) * size] = head(h).astype(BF16)
-    out[:, width:] = pack_stats(lse, heads)
-
-
-def merge(heads, *sources):
+        block = head(h).astype(BF16)
+        for i, out in enumerate(outs):
+            out[:, h * size : (h + 1) * size] = block[i * part : (i + 1) * part]
+    packed = pack_stats(lse, heads)
+    for i, out in enumerate(outs):
+        out[:, width:] = packed[i * part : (i + 1) * part]
+
+
+def merge(heads, first, second, parts):
+    rows, wide = first.shape
     return pl.pallas_call(
         functools.partial(merge_kernel, heads),
-        out_shape=jax.ShapeDtypeStruct(sources[0].shape, BF16),
-        in_specs=[in_vmem()] * len(sources),
-        out_specs=in_vmem(),
+        out_shape=(jax.ShapeDtypeStruct((rows // parts, wide), BF16),) * parts,
+        in_specs=[in_vmem()] * 2,
+        out_specs=(in_vmem(),) * parts,
         compiler_params=params(8),
-    )(*sources)
-
-
-def heads_of(ref, size):
-    return lambda h: ref[:, h * size : (h + 1) * size]
+    )(first, second)
 
 
 def finish_kernel(heads, near, far, out):
@@ -289,31 +302,16 @@
     )(near, far)
 
 
-def merge_finish_kernel(heads, *refs):
-    merge_kernel(heads, *refs[:-3], refs[-2])
-    finish_kernel(heads, refs[-2], refs[-3], refs[-1])
-
-
-def merge_finish(heads, far, *sources):
-    rows, wide = far.shape
-    return pl.pallas_call(
-        functools.partial(merge_finish_kernel, heads),
-        out_shape=(jax.ShapeDtypeStruct((rows, wide), BF16), jax.ShapeDtypeStruct((rows, wide - LANES), BF16)),
-        in_specs=[in_vmem()] * (len(sources) + 1),
-        out_specs=(in_vmem(),) * 2,
-        compiler_params=params(8),
-    )(*sources, far)
-
-
 def project_kernel(plan, lb, *refs):
-    sources, weight, (keep, send, rows_ref) = refs[: plan.group], refs[plan.group], refs[plan.group + 1 :]
+    sources, (weight, keep, send, rows_ref) = refs[:-4], refs[-4:]
     me, column = lax.axis_index("pages"), lax.axis_index("mp")
     rows = plan.rows
     holders = plan.group // 2
-    for i, k in enumerate((*others(plan), 0)):
-        device = me ^ k ^ (lb * plan.cross)
+    for chunk in range(plan.group):
+        device = plan.holder(me, column, lb, chunk)
         place = ((device // holders % 2) ^ (column % 2)) * holders + device % holders
-        rows_ref[pl.ds(pl.multiple_of(place * rows, rows), rows), :] = sources[i][...]
+        here = slice(chunk % 2 * rows, (chunk % 2 + 1) * rows)
+        rows_ref[pl.ds(pl.multiple_of(place * rows, rows), rows), :] = sources[chunk // 2][here, :]
     product = jnp.dot(rows_ref[...], weight[...], preferred_element_type=F32)
     part = holders * rows
     keep[...] = product[:part]
@@ -326,11 +324,11 @@
     return pl.pallas_call(
         functools.partial(project_kernel, plan, lb),
         out_shape=(jax.ShapeDtypeStruct((part, columns), F32), jax.ShapeDtypeStruct((part, columns), BF16)),
-        in_specs=[in_vmem()] * (plan.group + 1),
+        in_specs=[in_vmem()] * (len(sources) + 1),
         out_specs=(in_vmem(), in_vmem()),
         scratch_shapes=[VMEM((plan.page, weight.shape[0]), BF16)],
         compiler_params=params(24),
-    )(*(sources[k] for k in (*others(plan), 0)), weight)
+    )(*sources, weight)
 
 
 def swap(x, axis, distance):
@@ -338,27 +336,31 @@
     return lax.ppermute(x, axis, [(i, i ^ distance) for i in range(n)])
 
 
-def others(plan):
-    return range(plan.group - 1, 0, -1)
-
-
-def spread(x, plan):
-    return {0: x} | {k: swap(x, "pages", k) for k in others(plan)}
+def spread(x, plan, pair=None):
+    arrived = plan.swap(x, 1)
+    if pair is None:
+        pair = jnp.concatenate([x, arrived], axis=0)
+    else:
+        pair = lax.dynamic_update_slice(pair, arrived, (x.shape[0], 0))
+    return [pair, plan.swap(pair, 0)]
+
+
+def gathered(plan, heads, outs):
+    keep, send = outs
+    stay, go = merge(heads, keep, plan.swap(send, 0), 2)
+    return merge(heads, stay, plan.swap(go, 1), 1)[0]
 
 
 def by_halves(plan, heads, queries, weight, pages):
     far = swap(queries, "pages", plan.cross)
-    received = []
-    for lb, rows in enumerate((pages[3], far)):
-        chunks = spread(rows, plan)
-        outs = attend(plan, heads, lb, pages, [chunks[k] for k in range(plan.group)])
-        received.append([swap(outs[k], "pages", k) for k in others(plan)] + [outs[0]])
-    near = merge(heads, *received[0])
-    near_far, far_rows = merge_finish(heads, swap(near, "pages", plan.cross), *received[1])
-    across = swap(near_far, "pages", plan.cross)
+    near = [
+        gathered(plan, heads, attend(plan, heads, lb, pages, spread(x, plan, pair)))
+        for lb, (x, pair) in enumerate(((queries, pages[3]), (far, None)))
+    ]
+    across = [swap(x, "pages", plan.cross) for x in near]
     sums = [None, None]
     for lb in (1, 0):
-        rows = far_rows if lb else finish(heads, near, across)
+        rows = finish(heads, near[lb], across[1 - lb])
         keep, send = project(plan, lb, spread(rows, plan), weight)
         sums[lb] = keep + swap(send, "mp", 1).astype(F32)
     stays = plan.block(lax.axis_index("pages"), 0) == lax.axis_index("mp") // 2
@@ -370,18 +372,18 @@
 def by_gathers(plan, heads, queries, weight, pages):
     width = queries.shape[1]
     size = width // heads
-    gathered = lax.all_gather(queries, "pages", axis=0, tiled=True)
-    rows = gathered.shape[0]
+    every = lax.all_gather(queries, "pages", axis=0, tiled=True)
+    rows = every.shape[0]
     outs = [
-        attend(plan, heads, lb, pages, [gathered[lb * plan.page : (lb + 1) * plan.page]])[0]
+        attend(plan, heads, lb, pages, [every[lb * plan.page : (lb + 1) * plan.page]])[0]
         for lb in range(plan.blocks)
     ]
     out = jnp.concatenate(outs, axis=0)
     packed = out[:, width : width + 3 * heads].astype(F32)
     lse = packed[:, :heads] + packed[:, heads : 2 * heads] + packed[:, 2 * heads :]
-    every = lax.all_gather(lse, "pages")
-    top = jnp.max(every, axis=0)
-    share = jnp.exp2(lse - top) / jnp.sum(jnp.exp2(every - top), axis=0)
+    stats = lax.all_gather(lse, "pages")
+    top = jnp.max(stats, axis=0)
+    share = jnp.exp2(lse - top) / jnp.sum(jnp.exp2(stats - top), axis=0)
     part = (out[:, :width].reshape(rows, heads, size).astype(F32) * share[..., None]).reshape(1, rows, width)
     received = lax.all_to_all(part.astype(BF16), "pages", split_axis=1, concat_axis=0, tiled=True)
     mixed = jnp.sum(received, axis=0, dtype=F32).astype(BF16)

time: 66 us -> 69.1 us (1.047)
  waiting for transfers between devices: 27.4 us -> 38.4 us
  starting transfers between devices: 26.1 us -> 17.5 us
    ppermute x0 -> x12, waiting for transfers between devices: none -> 27.1 us  [swap(): return lax.ppermute(x, ('pages', 'mp'), pairs)]
    ppermute x24 -> x6, starting transfers between devices: 26.1 us -> 8.9 us  [swap(): return lax.ppermute(x, axis, [(i, i ^ distance) for i in range(n)])]
    ppermute x24 -> x6, waiting for transfers between devices: 27.4 us -> 11.3 us  [swap(): return lax.ppermute(x, axis, [(i, i ^ distance) for i in range(n)])]
    ppermute x0 -> x12, starting transfers between devices: none -> 8.6 us  [swap(): return lax.ppermute(x, ('pages', 'mp'), pairs)]
    pallas_call x2 -> x4, Pallas kernels: 1.37 us -> 1.61 us  [merge(): pl.pallas_call(functools.partial(merge_kernel, heads), out_shape=(jax.Sha...]
  transfers between devices with their start and end apart: 24 -> 18, of which waited for: 12 -> 14; matrix products, arithmetic and copies ran while one was open for 0% -> 0% of each run, Pallas kernels for 18% -> 18%
where the time goes in v5:
time: 69.1 us; the launch traced here: 69.8 us
  waiting for transfers between devices  38.4 us (56%)
  starting transfers between devices  17.5 us (25%)
  Pallas kernels  12.9 us (19%)
  other arithmetic  0.82 us (1%)
    ppermute x12, waiting for transfers between devices, swap(): return lax.ppermute(x, ('pages', 'mp'), pairs)  27.1 us
    ppermute x6, waiting for transfers between devices, swap(): return lax.ppermute(x, axis, [(i, i ^ distance) for i in range(n)])  11.3 us
    ppermute x6, starting transfers between devices, swap(): return lax.ppermute(x, axis, [(i, i ^ distance) for i in range(n)])  8.9 us
    ppermute x12, starting transfers between devices, swap(): return lax.ppermute(x, ('pages', 'mp'), pairs)  8.6 us
    pallas_call x2, Pallas kernels, attend(): pl.pallas_call(functools.partial(attend_kernel, plan, heads, lb), out_sha...  5.98 us
    pallas_call x1, Pallas kernels, fetch(): pl.pallas_call(functools.partial(fetch_kernel, plan, pages_dev), out_shap...  3.06 us
    pallas_call x4, Pallas kernels, merge(): pl.pallas_call(functools.partial(merge_kernel, heads), out_shape=(jax.Sha...  1.61 us
    pallas_call x2, Pallas kernels, project(): pl.pallas_call(functools.partial(project_kernel, plan, lb), out_shape=(ja...  1.57 us
  transfers between devices with their start and end apart: 18, of which 14 were waited for; matrix products, arithmetic and copies ran while one was open for 0% of the time, Pallas kernels for 18%

profile of v5, /device:TPU:0, one launch (start us, length us, event | category | flops | bytes accessed | tf_op | source)
XLA Modules:
  0.0 69.8 jit_solution(461166691858949185)
XLA Ops:
  0.0 3.0 %collective-permute-start = (bf16[32,2048]{1,0:T(8,128)(2,1)}, bf16[32,2048]{1,0:T(8,128)(2,1)S(1)}, u32[]{:S(2)}, u32[]{:S(2)}) collective-permute-start(bf16[32,2048]{1,0:T(8,128)(2,1)} %refs_3_.1), channel_id=1, source_target_pairs={{0,8},{1,5},{2,10},{3,7},{4,12},{5,1},{6,14},{7,3},{8,0},{9,13},{1... | collective-permute-start | bytes 393224 | tf_op jit(solution)/shard_map/ppermute | solution.py:61
  3.0 2.5 %collective-permute-start.4 = (bf16[32,2048]{1,0:T(8,128)(2,1)}, bf16[32,2048]{1,0:T(8,128)(2,1)S(1)}, u32[]{:S(2)}, u32[]{:S(2)}) collective-permute-start(bf16[32,2048]{1,0:T(8,128)(2,1)} %refs_3_.1), channel_id=1, source_target_pairs={{0,24},{4,28},{8,16},{12,20},{16,8},{20,12},{24,0},{28,4},{1,25},{... | collective-permute-start | bytes 393224 | tf_op jit(solution)/shard_map/ppermute | solution.py:336
  5.5 3.1 %shard_map.73 = (bf16[2,2,768,128]{3,2,1,0:T(8,128)(2,1)S(1)}, bf16[2,2,768,256]{3,2,1,0:T(8,128)(2,1)S(1)}, s32[2,3]{1,0:T(2,128)S(1)}, bf16[64,2048]{1,0:T(8,128)(2,1)S(1)}) custom-call(s32[2,24]{1,0:T(2,128)} %refs_0_.1, s32[128]{0:T(128)} %refs_1_.1, s32[2]{0:T(128)} %refs_2_.3, bf16[32,2048]{1,0:T(8,128)(2,1)} %refs_3_.1, ...), custom_call_target="tpu_custom_call" | custom-call | flops 2000000000 | bytes 8388608 | tf_op jit(solution)/shard_map/pallas_call | solution.py:134
  8.6 0.0 collective-permute-done
  8.6 1.6 %collective-permute-start.1 = (bf16[64,2048]{1,0:T(8,128)(2,1)S(1)}, bf16[64,2048]{1,0:T(8,128)(2,1)S(1)}, u32[]{:S(2)}, u32[]{:S(2)}) collective-permute-start(bf16[64,2048]{1,0:T(8,128)(2,1)S(1)} %constant_dynamic-update-slice_fusion.2.refs_0_), channel_id=1, source_target_pairs={{0,4},{1,9},{2,6},{3,11},{4,0},{5,13},{6,2},{7,15},{8,12},{9,1},{1... | collective-permute-start | bytes 786440 | tf_op jit(solution)/shard_map/ppermute | solution.py:61
  10.1 2.1 %collective-permute-done.4 = bf16[32,2048]{1,0:T(8,128)(2,1)S(1)} collective-permute-done((bf16[32,2048]{1,0:T(8,128)(2,1)}, bf16[32,2048]{1,0:T(8,128)(2,1)S(1)}, u32[]{:S(2)}, u32[]{:S(2)}) %collective-permute-start.4) | collective-permute-done | bytes 131104 | tf_op jit(solution)/shard_map/ppermute | solution.py:336
  12.3 0.0 collective-permute-start.5
  12.3 5.0 %collective-permute-done.5 = bf16[32,2048]{1,0:T(8,128)(2,1)S(1)} collective-permute-done((bf16[32,2048]{1,0:T(8,128)(2,1)S(1)}, bf16[32,2048]{1,0:T(8,128)(2,1)S(1)}, u32[]{:S(2)}, u32[]{:S(2)}) %collective-permute-start.5) | collective-permute-done | bytes 131104 | tf_op jit(solution)/shard_map/ppermute | solution.py:61
  17.3 0.1 collective-permute-start.6
  17.4 3.0 %shard_map.74 = (bf16[64,2176]{1,0:T(8,128)(2,1)S(1)}, bf16[64,2176]{1,0:T(8,128)(2,1)S(1)}) custom-call(s32[2,3]{1,0:T(2,128)S(1)} %get-tuple-element.21.info, bf16[64,2048]{1,0:T(8,128)(2,1)S(1)} %constant_dynamic-update-slice_fusion.2.refs_0_, bf16[64,2048]{1,0:T(8,128)(2,1)S(1)} %collective-permute-done.1.refs_1_, ...), custom_call_target="tpu_custom_call" | custom-call | flops 2000000000 | bytes 4194304 | tf_op jit(solution)/shard_map/pallas_call | solution.py:233
  20.4 0.0 copy-start
  20.4 2.1 %collective-permute-start.2 = (bf16[64,2176]{1,0:T(8,128)(2,1)S(1)}, bf16[64,2176]{1,0:T(8,128)(2,1)S(1)}, u32[]{:S(2)}, u32[]{:S(2)}) collective-permute-start(bf16[64,2176]{1,0:T(8,128)(2,1)S(1)} %get-tuple-element.26), channel_id=1, source_target_pairs={{0,4},{1,9},{2,6},{3,11},{4,0},{5,13},{6,2},{7,15},{8,12},{9,1},{1... | collective-permute-start | bytes 835592 | tf_op jit(solution)/shard_map/ppermute | solution.py:61
  22.4 1.3 %collective-permute-done.6.refs_1_ = bf16[64,2048]{1,0:T(8,128)(2,1)S(1)} collective-permute-done((bf16[64,2048]{1,0:T(8,128)(2,1)S(1)}, bf16[64,2048]{1,0:T(8,128)(2,1)S(1)}, u32[]{:S(2)}, u32[]{:S(2)}) %collective-permute-start.6) | collective-permute-done | bytes 262176 | tf_op jit(solution)/shard_map/ppermute | solution.py:61
  23.7 3.0 %shard_map.77 = (bf16[64,2176]{1,0:T(8,128)(2,1)S(1)}, bf16[64,2176]{1,0:T(8,128)(2,1)S(1)}) custom-call(s32[2,3]{1,0:T(2,128)S(1)} %get-tuple-element.21.info, bf16[64,2048]{1,0:T(8,128)(2,1)S(1)} %constant_dynamic-update-slice_fusion.refs_0_, bf16[64,2048]{1,0:T(8,128)(2,1)S(1)} %collective-permute-done.6.refs_1_, ...), custom_call_target="tpu_custom_call" | custom-call | flops 2000000000 | bytes 4194304 | tf_op jit(solution)/shard_map/pallas_call | solution.py:233
  26.7 0.1 collective-permute-start.7
  26.8 0.4 collective-permute-done.2.second
  27.2 0.5 shard_map.75
  27.6 0.1 collective-permute-start.3
  27.7 6.7 %collective-permute-done.7.second = bf16[64,2176]{1,0:T(8,128)(2,1)S(1)} collective-permute-done((bf16[64,2176]{1,0:T(8,128)(2,1)S(1)}, bf16[64,2176]{1,0:T(8,128)(2,1)S(1)}, u32[]{:S(2)}, u32[]{:S(2)}) %collective-permute-start.7) | collective-permute-done | bytes 278560 | tf_op jit(solution)/shard_map/ppermute | solution.py:61
  34.4 0.5 shard_map.78
  34.9 0.1 collective-permute-start.8
  35.0 0.0 collective-permute-done.3.second
  35.0 0.3 shard_map.76.near
  35.3 2.9 %collective-permute-start.13 = (bf16[32,2176]{1,0:T(8,128)(2,1)S(1)}, bf16[32,2176]{1,0:T(8,128)(2,1)S(1)}, u32[]{:S(2)}, u32[]{:S(2)}) collective-permute-start(bf16[32,2176]{1,0:T(8,128)(2,1)S(1)} %shard_map.76.near), channel_id=1, source_target_pairs={{0,24},{4,28},{8,16},{12,20},{16,8},{20,12},{24,0},{28,4},{1,25},{... | collective-permute-start | bytes 417800 | tf_op jit(solution)/shard_map/ppermute | solution.py:336
  38.2 2.3 %collective-permute-done.8.second = bf16[32,2176]{1,0:T(8,128)(2,1)S(1)} collective-permute-done((bf16[32,2176]{1,0:T(8,128)(2,1)S(1)}, bf16[32,2176]{1,0:T(8,128)(2,1)S(1)}, u32[]{:S(2)}, u32[]{:S(2)}) %collective-permute-start.8) | collective-permute-done | bytes 139296 | tf_op jit(solution)/shard_map/ppermute | solution.py:61
  40.6 0.3 shard_map.79.near
  40.9 1.8 %collective-permute-start.9 = (bf16[32,2176]{1,0:T(8,128)(2,1)S(1)}, bf16[32,2176]{1,0:T(8,128)(2,1)S(1)}, u32[]{:S(2)}, u32[]{:S(2)}) collective-permute-start(bf16[32,2176]{1,0:T(8,128)(2,1)S(1)} %shard_map.79.near), channel_id=1, source_target_pairs={{0,24},{4,28},{8,16},{12,20},{16,8},{20,12},{24,0},{28,4},{1,25},{... | collective-permute-start | bytes 417800 | tf_op jit(solution)/shard_map/ppermute | solution.py:336
  42.7 1.2 %collective-permute-done.13.far = bf16[32,2176]{1,0:T(8,128)(2,1)S(1)} collective-permute-done((bf16[32,2176]{1,0:T(8,128)(2,1)S(1)}, bf16[32,2176]{1,0:T(8,128)(2,1)S(1)}, u32[]{:S(2)}, u32[]{:S(2)}) %collective-permute-start.13) | collective-permute-done | bytes 139296 | tf_op jit(solution)/shard_map/ppermute | solution.py:336
  43.9 0.3 shard_map.82
  44.3 1.1 %collective-permute-start.14 = (bf16[32,2048]{1,0:T(8,128)(2,1)S(1)}, bf16[32,2048]{1,0:T(8,128)(2,1)S(1)}, u32[]{:S(2)}, u32[]{:S(2)}) collective-permute-start(bf16[32,2048]{1,0:T(8,128)(2,1)S(1)} %shard_map.82), channel_id=1, source_target_pairs={{0,8},{1,5},{2,10},{3,7},{4,12},{5,1},{6,14},{7,3},{8,0},{9,13},{1... | collective-permute-start | bytes 393224 | tf_op jit(solution)/shard_map/ppermute | solution.py:61
  45.3 2.6 %collective-permute-done.9.far = bf16[32,2176]{1,0:T(8,128)(2,1)S(1)} collective-permute-done((bf16[32,2176]{1,0:T(8,128)(2,1)S(1)}, bf16[32,2176]{1,0:T(8,128)(2,1)S(1)}, u32[]{:S(2)}, u32[]{:S(2)}) %collective-permute-start.9) | collective-permute-done | bytes 139296 | tf_op jit(solution)/shard_map/ppermute | solution.py:336
  47.9 0.3 shard_map.80
  48.3 0.1 collective-permute-start.10
  48.3 2.5 %collective-permute-done.14 = bf16[32,2048]{1,0:T(8,128)(2,1)S(1)} collective-permute-done((bf16[32,2048]{1,0:T(8,128)(2,1)S(1)}, bf16[32,2048]{1,0:T(8,128)(2,1)S(1)}, u32[]{:S(2)}, u32[]{:S(2)}) %collective-permute-start.14) | collective-permute-done | bytes 131104 | tf_op jit(solution)/shard_map/ppermute | solution.py:61
  50.8 0.5 collective-permute-start.15
  51.3 3.5 %collective-permute-done.10 = bf16[32,2048]{1,0:T(8,128)(2,1)S(1)} collective-permute-done((bf16[32,2048]{1,0:T(8,128)(2,1)S(1)}, bf16[32,2048]{1,0:T(8,128)(2,1)S(1)}, u32[]{:S(2)}, u32[]{:S(2)}) %collective-permute-start.10) | collective-permute-done | bytes 131104 | tf_op jit(solution)/shard_map/ppermute | solution.py:61
  54.8 0.1 collective-permute-start.11
  54.9 2.4 %collective-permute-done.15.refs_1_ = bf16[64,2048]{1,0:T(8,128)(2,1)S(1)} collective-permute-done((bf16[64,2048]{1,0:T(8,128)(2,1)S(1)}, bf16[64,2048]{1,0:T(8,128)(2,1)S(1)}, u32[]{:S(2)}, u32[]{:S(2)}) %collective-permute-start.15) | collective-permute-done | bytes 262176 | tf_op jit(solution)/shard_map/ppermute | solution.py:61
  57.3 0.8 %shard_map.83 = (f32[64,1024]{1,0:T(8,128)S(1)}, bf16[64,1024]{1,0:T(8,128)(2,1)S(1)}) custom-call(bf16[64,2048]{1,0:T(8,128)(2,1)S(1)} %pad_maximum_fusion.1.refs_0_, bf16[64,2048]{1,0:T(8,128)(2,1)S(1)} %collective-permute-done.15.refs_1_, bf16[2048,1024]{1,0:T(8,128)(2,1)S(1)} %copy-done), custom_call_target="tpu_custom_call" | custom-call | tf_op jit(solution)/shard_map/pallas_call | solution.py:324
  58.1 0.1 collective-permute-start.16
  58.1 3.1 %collective-permute-done.11.refs_1_ = bf16[64,2048]{1,0:T(8,128)(2,1)S(1)} collective-permute-done((bf16[64,2048]{1,0:T(8,128)(2,1)S(1)}, bf16[64,2048]{1,0:T(8,128)(2,1)S(1)}, u32[]{:S(2)}, u32[]{:S(2)}) %collective-permute-start.11) | collective-permute-done | bytes 262176 | tf_op jit(solution)/shard_map/ppermute | solution.py:61
  61.2 0.8 %shard_map.81 = (f32[64,1024]{1,0:T(8,128)S(1)}, bf16[64,1024]{1,0:T(8,128)(2,1)S(1)}) custom-call(bf16[64,2048]{1,0:T(8,128)(2,1)S(1)} %pad_maximum_fusion.refs_0_, bf16[64,2048]{1,0:T(8,128)(2,1)S(1)} %collective-permute-done.11.refs_1_, bf16[2048,1024]{1,0:T(8,128)(2,1)S(1)} %copy-done), custom_call_target="tpu_custom_call" | custom-call | tf_op jit(solution)/shard_map/pallas_call | solution.py:324
  62.0 0.1 collective-permute-start.12
  62.1 1.3 %collective-permute-done.12 = bf16[64,1024]{1,0:T(8,128)(2,1)S(1)} collective-permute-done((bf16[64,1024]{1,0:T(8,128)(2,1)S(1)}, bf16[64,1024]{1,0:T(8,128)(2,1)S(1)}, u32[]{:S(2)}, u32[]{:S(2)}) %collective-permute-start.12) | collective-permute-done | bytes 131104 | tf_op jit(solution)/shard_map/ppermute | solution.py:336
  63.4 0.1 select_convert_fusion
  63.5 1.6 %collective-permute-start.17 = (bf16[64,1024]{1,0:T(8,128)(2,1)S(1)}, bf16[64,1024]{1,0:T(8,128)(2,1)S(1)}, u32[]{:S(2)}, u32[]{:S(2)}) collective-permute-start(bf16[64,1024]{1,0:T(8,128)(2,1)S(1)} %select_convert_fusion), channel_id=1, source_target_pairs={{0,2},{1,3},{2,0},{3,1},{4,6},{5,7},{6,4},{7,5},{8,10},{9,11},{10,... | collective-permute-start | bytes 393224 | tf_op jit(solution)/shard_map/ppermute | solution.py:336
  65.1 4.0 %collective-permute-done.17 = bf16[64,1024]{1,0:T(8,128)(2,1)S(1)} collective-permute-done((bf16[64,1024]{1,0:T(8,128)(2,1)S(1)}, bf16[64,1024]{1,0:T(8,128)(2,1)S(1)}, u32[]{:S(2)}, u32[]{:S(2)}) %collective-permute-start.17) | collective-permute-done | bytes 131104 | tf_op jit(solution)/shard_map/ppermute | solution.py:336
  69.1 0.7 %add_convert_fusion = bf16[64,1024]{1,0:T(8,128)(2,1)} fusion(bf16[64,1024]{1,0:T(8,128)(2,1)S(1)} %collective-permute-done.17, f32[64,1024]{1,0:T(8,128)S(1)} %get-tuple-element.33, bf16[64,1024]{1,0:T(8,128)(2,1)S(1)} %collective-permute-done.12, f32[64,1024]{1,0:T(8,128)S(1)} %get-tuple-element.35, bf16[64,1024]{1,0:T(8,128)(2,1)S(1)} %collective-permute-done.16, ...), kind=kLoop, calls=%fused_computation.2 | loop fusion | flops 524288 | bytes 1048577 | tf_op jit(solution)/shard_map/convert_element_type | solution.py:369
  (8 shorter events, 0.1 us)
Async XLA Ops:
  0.0 8.6 %collective-permute-start = (bf16[32,2048]{1,0:T(8,128)(2,1)}, bf16[32,2048]{1,0:T(8,128)(2,1)S(1)}, u32[]{:S(2)}, u32[]{:S(2)}) collective-permute-start(bf16[32,2048]{1,0:T(8,128)(2,1)} %refs_3_.1), channel_id=1, source_target_pairs={{0,8},{1,5},{2,10},{3,7},{4,12},{5,1},{6,14},{7,3},{8,0},{9,13},{1... | collective-permute-start | bytes 393224 | tf_op jit(solution)/shard_map/ppermute | solution.py:61
  3.0 9.3 %collective-permute-start.4 = (bf16[32,2048]{1,0:T(8,128)(2,1)}, bf16[32,2048]{1,0:T(8,128)(2,1)S(1)}, u32[]{:S(2)}, u32[]{:S(2)}) collective-permute-start(bf16[32,2048]{1,0:T(8,128)(2,1)} %refs_3_.1), channel_id=1, source_target_pairs={{0,24},{4,28},{8,16},{12,20},{16,8},{20,12},{24,0},{28,4},{1,25},{... | collective-permute-start | bytes 393224 | tf_op jit(solution)/shard_map/ppermute | solution.py:336
  8.6 8.8 %collective-permute-start.1 = (bf16[64,2048]{1,0:T(8,128)(2,1)S(1)}, bf16[64,2048]{1,0:T(8,128)(2,1)S(1)}, u32[]{:S(2)}, u32[]{:S(2)}) collective-permute-start(bf16[64,2048]{1,0:T(8,128)(2,1)S(1)} %constant_dynamic-update-slice_fusion.2.refs_0_), channel_id=1, source_target_pairs={{0,4},{1,9},{2,6},{3,11},{4,0},{5,13},{6,2},{7,15},{8,12},{9,1},{1... | collective-permute-start | bytes 786440 | tf_op jit(solution)/shard_map/ppermute | solution.py:61
  12.3 5.0 %collective-permute-start.5 = (bf16[32,2048]{1,0:T(8,128)(2,1)S(1)}, bf16[32,2048]{1,0:T(8,128)(2,1)S(1)}, u32[]{:S(2)}, u32[]{:S(2)}) collective-permute-start(bf16[32,2048]{1,0:T(8,128)(2,1)S(1)} %collective-permute-done.4), channel_id=1, source_target_pairs={{0,8},{1,5},{2,10},{3,7},{4,12},{5,1},{6,14},{7,3},{8,0},{9,13},{1... | collective-permute-start | bytes 393224 | tf_op jit(solution)/shard_map/ppermute | solution.py:61
  17.3 6.4 %collective-permute-start.6 = (bf16[64,2048]{1,0:T(8,128)(2,1)S(1)}, bf16[64,2048]{1,0:T(8,128)(2,1)S(1)}, u32[]{:S(2)}, u32[]{:S(2)}) collective-permute-start(bf16[64,2048]{1,0:T(8,128)(2,1)S(1)} %constant_dynamic-update-slice_fusion.refs_0_), channel_id=1, source_target_pairs={{0,4},{1,9},{2,6},{3,11},{4,0},{5,13},{6,2},{7,15},{8,12},{9,1},{1... | collective-permute-start | bytes 786440 | tf_op jit(solution)/shard_map/ppermute | solution.py:61
  20.4 36.9 %copy-start = (bf16[2048,1024]{1,0:T(8,128)(2,1)S(1)}, bf16[2048,1024]{1,0:T(8,128)(2,1)}, u32[]{:S(2)}) copy-start(bf16[2048,1024]{1,0:T(8,128)(2,1)} %refs_2_.5) | copy-start | bytes 12582916
  20.4 6.8 %collective-permute-start.2 = (bf16[64,2176]{1,0:T(8,128)(2,1)S(1)}, bf16[64,2176]{1,0:T(8,128)(2,1)S(1)}, u32[]{:S(2)}, u32[]{:S(2)}) collective-permute-start(bf16[64,2176]{1,0:T(8,128)(2,1)S(1)} %get-tuple-element.26), channel_id=1, source_target_pairs={{0,4},{1,9},{2,6},{3,11},{4,0},{5,13},{6,2},{7,15},{8,12},{9,1},{1... | collective-permute-start | bytes 835592 | tf_op jit(solution)/shard_map/ppermute | solution.py:61
  26.7 7.7 %collective-permute-start.7 = (bf16[64,2176]{1,0:T(8,128)(2,1)S(1)}, bf16[64,2176]{1,0:T(8,128)(2,1)S(1)}, u32[]{:S(2)}, u32[]{:S(2)}) collective-permute-start(bf16[64,2176]{1,0:T(8,128)(2,1)S(1)} %get-tuple-element.30), channel_id=1, source_target_pairs={{0,4},{1,9},{2,6},{3,11},{4,0},{5,13},{6,2},{7,15},{8,12},{9,1},{1... | collective-permute-start | bytes 835592 | tf_op jit(solution)/shard_map/ppermute | solution.py:61
  27.6 7.3 %collective-permute-start.3 = (bf16[32,2176]{1,0:T(8,128)(2,1)S(1)}, bf16[32,2176]{1,0:T(8,128)(2,1)S(1)}, u32[]{:S(2)}, u32[]{:S(2)}) collective-permute-start(bf16[32,2176]{1,0:T(8,128)(2,1)S(1)} %get-tuple-element.28), channel_id=1, source_target_pairs={{0,8},{1,5},{2,10},{3,7},{4,12},{5,1},{6,14},{7,3},{8,0},{9,13},{1... | collective-permute-start | bytes 417800 | tf_op jit(solution)/shard_map/ppermute | solution.py:61
  34.9 5.7 %collective-permute-start.8 = (bf16[32,2176]{1,0:T(8,128)(2,1)S(1)}, bf16[32,2176]{1,0:T(8,128)(2,1)S(1)}, u32[]{:S(2)}, u32[]{:S(2)}) collective-permute-start(bf16[32,2176]{1,0:T(8,128)(2,1)S(1)} %get-tuple-element.32), channel_id=1, source_target_pairs={{0,8},{1,5},{2,10},{3,7},{4,12},{5,1},{6,14},{7,3},{8,0},{9,13},{1... | collective-permute-start | bytes 417800 | tf_op jit(solution)/shard_map/ppermute | solution.py:61
  35.3 8.6 %collective-permute-start.13 = (bf16[32,2176]{1,0:T(8,128)(2,1)S(1)}, bf16[32,2176]{1,0:T(8,128)(2,1)S(1)}, u32[]{:S(2)}, u32[]{:S(2)}) collective-permute-start(bf16[32,2176]{1,0:T(8,128)(2,1)S(1)} %shard_map.76.near), channel_id=1, source_target_pairs={{0,24},{4,28},{8,16},{12,20},{16,8},{20,12},{24,0},{28,4},{1,25},{... | collective-permute-start | bytes 417800 | tf_op jit(solution)/shard_map/ppermute | solution.py:336
  40.9 7.0 %collective-permute-start.9 = (bf16[32,2176]{1,0:T(8,128)(2,1)S(1)}, bf16[32,2176]{1,0:T(8,128)(2,1)S(1)}, u32[]{:S(2)}, u32[]{:S(2)}) collective-permute-start(bf16[32,2176]{1,0:T(8,128)(2,1)S(1)} %shard_map.79.near), channel_id=1, source_target_pairs={{0,24},{4,28},{8,16},{12,20},{16,8},{20,12},{24,0},{28,4},{1,25},{... | collective-permute-start | bytes 417800 | tf_op jit(solution)/shard_map/ppermute | solution.py:336
  44.3 6.5 %collective-permute-start.14 = (bf16[32,2048]{1,0:T(8,128)(2,1)S(1)}, bf16[32,2048]{1,0:T(8,128)(2,1)S(1)}, u32[]{:S(2)}, u32[]{:S(2)}) collective-permute-start(bf16[32,2048]{1,0:T(8,128)(2,1)S(1)} %shard_map.82), channel_id=1, source_target_pairs={{0,8},{1,5},{2,10},{3,7},{4,12},{5,1},{6,14},{7,3},{8,0},{9,13},{1... | collective-permute-start | bytes 393224 | tf_op jit(solution)/shard_map/ppermute | solution.py:61
  48.3 6.5 %collective-permute-start.10 = (bf16[32,2048]{1,0:T(8,128)(2,1)S(1)}, bf16[32,2048]{1,0:T(8,128)(2,1)S(1)}, u32[]{:S(2)}, u32[]{:S(2)}) collective-permute-start(bf16[32,2048]{1,0:T(8,128)(2,1)S(1)} %shard_map.80), channel_id=1, source_target_pairs={{0,8},{1,5},{2,10},{3,7},{4,12},{5,1},{6,14},{7,3},{8,0},{9,13},{1... | collective-permute-start | bytes 393224 | tf_op jit(solution)/shard_map/ppermute | solution.py:61
  50.8 6.4 %collective-permute-start.15 = (bf16[64,2048]{1,0:T(8,128)(2,1)S(1)}, bf16[64,2048]{1,0:T(8,128)(2,1)S(1)}, u32[]{:S(2)}, u32[]{:S(2)}) collective-permute-start(bf16[64,2048]{1,0:T(8,128)(2,1)S(1)} %pad_maximum_fusion.1.refs_0_), channel_id=1, source_target_pairs={{0,4},{1,9},{2,6},{3,11},{4,0},{5,13},{6,2},{7,15},{8,12},{9,1},{1... | collective-permute-start | bytes 786440 | tf_op jit(solution)/shard_map/ppermute | solution.py:61
  54.8 6.4 %collective-permute-start.11 = (bf16[64,2048]{1,0:T(8,128)(2,1)S(1)}, bf16[64,2048]{1,0:T(8,128)(2,1)S(1)}, u32[]{:S(2)}, u32[]{:S(2)}) collective-permute-start(bf16[64,2048]{1,0:T(8,128)(2,1)S(1)} %pad_maximum_fusion.refs_0_), channel_id=1, source_target_pairs={{0,4},{1,9},{2,6},{3,11},{4,0},{5,13},{6,2},{7,15},{8,12},{9,1},{1... | collective-permute-start | bytes 786440 | tf_op jit(solution)/shard_map/ppermute | solution.py:61
  58.1 4.1 %collective-permute-start.16 = (bf16[64,1024]{1,0:T(8,128)(2,1)S(1)}, bf16[64,1024]{1,0:T(8,128)(2,1)S(1)}, u32[]{:S(2)}, u32[]{:S(2)}) collective-permute-start(bf16[64,1024]{1,0:T(8,128)(2,1)S(1)} %get-tuple-element.36), channel_id=1, source_target_pairs={{0,1},{1,0},{2,3},{3,2},{4,5},{5,4},{6,7},{7,6},{8,9},{9,8},{10,11... | collective-permute-start | bytes 393224 | tf_op jit(solution)/shard_map/ppermute | solution.py:336
  62.0 1.4 %collective-permute-start.12 = (bf16[64,1024]{1,0:T(8,128)(2,1)S(1)}, bf16[64,1024]{1,0:T(8,128)(2,1)S(1)}, u32[]{:S(2)}, u32[]{:S(2)}) collective-permute-start(bf16[64,1024]{1,0:T(8,128)(2,1)S(1)} %get-tuple-element.34), channel_id=1, source_target_pairs={{0,1},{1,0},{2,3},{3,2},{4,5},{5,4},{6,7},{7,6},{8,9},{9,8},{10,11... | collective-permute-start | bytes 393224 | tf_op jit(solution)/shard_map/ppermute | solution.py:336
  63.5 5.6 %collective-permute-start.17 = (bf16[64,1024]{1,0:T(8,128)(2,1)S(1)}, bf16[64,1024]{1,0:T(8,128)(2,1)S(1)}, u32[]{:S(2)}, u32[]{:S(2)}) collective-permute-start(bf16[64,1024]{1,0:T(8,128)(2,1)S(1)} %select_convert_fusion), channel_id=1, source_target_pairs={{0,2},{1,3},{2,0},{3,1},{4,6},{5,7},{6,4},{7,5},{8,10},{9,11},{10,... | collective-permute-start | bytes 393224 | tf_op jit(solution)/shard_map/ppermute | solution.py:336

commit v6 on v4

--- a/solution.py
+++ b/solution.py
@@ -33,7 +33,7 @@
 
 class Plan:
     def __init__(self, n, ways, rows, blocks, page):
-        self.n, self.rows, self.blocks, self.page = n, rows, blocks, page
+        self.n, self.ways, self.rows, self.blocks, self.page = n, ways, rows, blocks, page
         self.group = n // blocks
         self.halves = blocks == 2 and n == 8 and ways == 4 and rows * self.group == page
         self.cross = n * 3 // 4
@@ -42,26 +42,41 @@
     def block(self, me, lb):
         return (me // self.group) ^ lb if self.halves else lb
 
+    def holder(self, me, column, lb, chunk):
+        turned = chunk // 2 + chunk % 2 * 2
+        return me ^ (lb * self.cross) ^ jnp.where(column % 2 == 0, chunk, turned)
+
     def offsets(self, me, lb, shape):
         row = lax.broadcasted_iota(jnp.int32, shape, 0) % self.page
         if not self.halves:
             return row
-        mine = (me ^ (lb * self.cross)) % self.group
-        return ((row // self.rows) ^ mine) * self.rows + row % self.rows
+        holder = self.holder(me, lax.axis_index("mp"), lb, row // self.rows)
+        return holder % self.group * self.rows + row % self.rows
+
+    def swap(self, x, chunk):
+        pairs = []
+        for p in range(self.n):
+            for m in range(self.ways):
+                turned = chunk // 2 + chunk % 2 * 2
+                pairs.append((p * self.ways + m, (p ^ (turned if m % 2 else chunk)) * self.ways + m))
+        return lax.ppermute(x, ("pages", "mp"), pairs)
 
 
 def fetch_kernel(plan, pages_dev, select_hbm, table_hbm, stands_hbm, keys, values, k_out, v_out, info, select, table, stands, rows, k_buf, v_buf, sems, int_sems):
     me = lax.axis_index("pages")
-    blocks, picked = k_buf.shape[:2]
-    span = k_buf.shape[2]
-    heads = k_out.shape[1]
+    blocks, heads = k_out.shape[:2]
+    span = k_buf.shape[1]
     page = span // heads
+    picked = k_out.shape[2] // page
     low = me * pages_dev
     loads = [
         pltpu.make_async_copy(a, b, int_sems.at[i])
         for i, (a, b) in enumerate(((select_hbm, select), (table_hbm, table), (stands_hbm, stands)))
     ]
-    for load in loads:
+    whole = [
+        pltpu.make_async_copy(a, b, sems.at[i]) for i, (a, b) in enumerate(((keys, k_buf), (values, v_buf)))
+    ]
+    for load in loads + whole:
         load.start()
     row = lax.broadcasted_iota(jnp.int32, (span, span), 0)
     column = lax.broadcasted_iota(jnp.int32, (span, span), 1)
@@ -90,13 +105,8 @@
         info[lb, 0] = count
         info[lb, 1] = rows[blocks + lb, 0]
 
-        @pl.when(count > 0)
-        def _(lb=lb):
-            for slot in range(picked):
-                local = jnp.clip(rows[lb, slot], 0, pages_dev - 1)
-                pltpu.make_async_copy(keys.at[local], k_buf.at[lb, slot], sems.at[lb, slot, 0]).start()
-                pltpu.make_async_copy(values.at[local], v_buf.at[lb, slot], sems.at[lb, slot, 1]).start()
-
+    for load in whole:
+        load.wait()
     for lb in range(blocks):
 
         @pl.when(info[lb, 0] > 0)
@@ -104,10 +114,8 @@
             for g in range(heads):
                 v_out[lb, g, :, LANES:] = jnp.ones((picked * page, LANES), BF16)
             for slot in range(picked):
-                pltpu.make_async_copy(keys.at[0], k_buf.at[lb, slot], sems.at[lb, slot, 0]).wait()
-                pltpu.make_async_copy(values.at[0], v_buf.at[lb, slot], sems.at[lb, slot, 1]).wait()
-            for slot in range(picked):
-                both = jnp.concatenate([k_buf[lb, slot], v_buf[lb, slot]], axis=1)
+                local = jnp.clip(rows[lb, slot], 0, pages_dev - 1)
+                both = jnp.concatenate([k_buf[local], v_buf[local]], axis=1)
                 split = jnp.dot(apart, both, preferred_element_type=F32).astype(BF16)
                 for g in range(heads):
                     here = slice(slot * page, (slot + 1) * page)
@@ -133,9 +141,9 @@
             SMEM(table.shape, jnp.int32),
             SMEM(stands.shape, jnp.int32),
             SMEM((2 * blocks, picked + 1), jnp.int32),
-            VMEM((blocks, picked, span, size), BF16),
-            VMEM((blocks, picked, span, size), BF16),
-            pltpu.SemaphoreType.DMA((blocks, picked, 2)),
+            VMEM((pages_dev, span, size), BF16),
+            VMEM((pages_dev, span, size), BF16),
+            pltpu.SemaphoreType.DMA((2,)),
             pltpu.SemaphoreType.DMA((3,)),
         ],
         compiler_params=params(16),
@@ -289,7 +297,7 @@
     rows = plan.rows
     holders = plan.group // 2
     for k in range(plan.group):
-        device = me ^ k ^ (lb * plan.cross)
+        device = plan.holder(me, column, lb, k)
         place = ((device // holders % 2) ^ (column % 2)) * holders + device % holders
         rows_ref[pl.ds(pl.multiple_of(place * rows, rows), rows), :] = sources[k][...]
     product = jnp.dot(rows_ref[...], weight[...], preferred_element_type=F32)
@@ -321,7 +329,7 @@
 
 
 def spread(x, plan):
-    return {0: x} | {k: swap(x, "pages", k) for k in others(plan)}
+    return {0: x} | {k: plan.swap(x, k) for k in others(plan)}
 
 
 def by_halves(plan, heads, queries, weight, pages):
@@ -330,7 +338,7 @@
     for lb, rows in enumerate((queries, far)):
         chunks = spread(rows, plan)
         outs = attend(plan, heads, lb, pages, [chunks[k] for k in range(plan.group)])
-        near.append(merge(heads, outs[0], *(swap(outs[k], "pages", k) for k in others(plan))))
+        near.append(merge(heads, outs[0], *(plan.swap(outs[k], k) for k in others(plan))))
     across = [swap(x, "pages", plan.cross) for x in near]
     sums = [None, None]
     for lb in (1, 0):

time: 61.3 us -> 60.7 us (level)
  Pallas kernels: 6.43 us -> 12.1 us
  starting transfers between devices: 37.4 us -> 33.8 us
  waiting for transfers between devices: 16.1 us -> 13.7 us
    ppermute x24 -> x6, starting transfers between devices: 37.4 us -> 10.1 us  [swap(): return lax.ppermute(x, axis, [(i, i ^ distance) for i in range(n)])]
    ppermute x0 -> x18, starting transfers between devices: none -> 23.7 us  [swap(): return lax.ppermute(x, ('pages', 'mp'), pairs)]
    ppermute x24 -> x6, waiting for transfers between devices: 16.1 us -> 6.27 us  [swap(): return lax.ppermute(x, axis, [(i, i ^ distance) for i in range(n)])]
    ppermute x0 -> x18, waiting for transfers between devices: none -> 7.38 us  [swap(): return lax.ppermute(x, ('pages', 'mp'), pairs)]
    pallas_call x2, Pallas kernels: 1.29 us -> 5.96 us  [attend(): pl.pallas_call(functools.partial(attend_kernel, plan, heads, lb), out_sha...]
    pallas_call x1, Pallas kernels: 1.97 us -> 3.01 us  [fetch(): pl.pallas_call(functools.partial(fetch_kernel, plan, pages_dev), out_shap...]
  transfers between devices with their start and end apart: 24 -> 24, of which waited for: 12 -> 10; matrix products, arithmetic and copies ran while one was open for 0% -> 0% of each run, Pallas kernels for 11% -> 20%
where the time goes in v6:
time: 60.7 us; the launch traced here: 60.6 us
  starting transfers between devices  33.8 us (56%)
  waiting for transfers between devices  13.7 us (23%)
  Pallas kernels  12.1 us (20%)
  other arithmetic  0.78 us (1%)
    ppermute x18, starting transfers between devices, swap(): return lax.ppermute(x, ('pages', 'mp'), pairs)  23.7 us
    ppermute x6, starting transfers between devices, swap(): return lax.ppermute(x, axis, [(i, i ^ distance) for i in range(n)])  10.1 us
    ppermute x18, waiting for transfers between devices, swap(): return lax.ppermute(x, ('pages', 'mp'), pairs)  7.38 us
    ppermute x6, waiting for transfers between devices, swap(): return lax.ppermute(x, axis, [(i, i ^ distance) for i in range(n)])  6.27 us
    pallas_call x2, Pallas kernels, attend(): pl.pallas_call(functools.partial(attend_kernel, plan, heads, lb), out_sha...  5.96 us
    pallas_call x1, Pallas kernels, fetch(): pl.pallas_call(functools.partial(fetch_kernel, plan, pages_dev), out_shap...  3.01 us
    pallas_call x2, Pallas kernels, project(): pl.pallas_call(functools.partial(project_kernel, plan, lb), out_shape=(ja...  1.57 us
  transfers between devices with their start and end apart: 24, of which 10 were waited for; matrix products, arithmetic and copies ran while one was open for 0% of the time, Pallas kernels for 20%

profile of v6, /device:TPU:0, one launch (start us, length us, event | category | flops | bytes accessed | tf_op | source)
XLA Modules:
  0.0 60.6 jit_solution(14700497226916791766)
XLA Ops:
  0.0 5.0 %collective-permute-start.6 = (bf16[32,2048]{1,0:T(8,128)(2,1)}, bf16[32,2048]{1,0:T(8,128)(2,1)S(1)}, u32[]{:S(2)}, u32[]{:S(2)}) collective-permute-start(bf16[32,2048]{1,0:T(8,128)(2,1)} %refs_0_.1), channel_id=1, source_target_pairs={{0,24},{4,28},{8,16},{12,20},{16,8},{20,12},{24,0},{28,4},{1,25},{... | collective-permute-start | bytes 393224 | tf_op jit(solution)/shard_map/ppermute | solution.py:324
  5.1 1.5 %collective-permute-start = (bf16[32,2048]{1,0:T(8,128)(2,1)}, bf16[32,2048]{1,0:T(8,128)(2,1)S(1)}, u32[]{:S(2)}, u32[]{:S(2)}) collective-permute-start(bf16[32,2048]{1,0:T(8,128)(2,1)} %refs_0_.1), channel_id=1, source_target_pairs={{0,4},{1,9},{2,6},{3,11},{4,0},{5,13},{6,2},{7,15},{8,12},{9,1},{1... | collective-permute-start | bytes 393224 | tf_op jit(solution)/shard_map/ppermute | solution.py:62
  6.5 0.0 collective-permute-start.1
  6.5 2.0 %collective-permute-start.2 = (bf16[32,2048]{1,0:T(8,128)(2,1)}, bf16[32,2048]{1,0:T(8,128)(2,1)S(1)}, u32[]{:S(2)}, u32[]{:S(2)}) collective-permute-start(bf16[32,2048]{1,0:T(8,128)(2,1)} %refs_0_.1), channel_id=1, source_target_pairs={{0,12},{1,13},{2,14},{3,15},{4,8},{5,9},{6,10},{7,11},{8,4},{9,5},... | collective-permute-start | bytes 393224 | tf_op jit(solution)/shard_map/ppermute | solution.py:62
  8.5 3.0 %shard_map.73 = (bf16[2,2,768,128]{3,2,1,0:T(8,128)(2,1)S(1)}, bf16[2,2,768,256]{3,2,1,0:T(8,128)(2,1)S(1)}, s32[2,3]{1,0:T(2,128)S(1)}) custom-call(s32[2,24]{1,0:T(2,128)} %select_hbm.1, s32[128]{0:T(128)} %table_hbm.1, s32[2]{0:T(128)} %stands_hbm.1, bf16[16,256,128]{2,1,0:T(8,128)(2,1)} %bitcast.2, bf16[16,256,128]{2,1,0:T(8,128)(2,1)} %bitcast.3), custom_call_target="tpu_custom_call" | custom-call | flops 2000000000 | bytes 8388608 | tf_op jit(solution)/shard_map/pallas_call | solution.py:130
  11.6 0.0 collective-permute-done.6.refs_0_
  11.6 0.7 %collective-permute-start.7 = (bf16[32,2048]{1,0:T(8,128)(2,1)S(1)}, bf16[32,2048]{1,0:T(8,128)(2,1)S(1)}, u32[]{:S(2)}, u32[]{:S(2)}) collective-permute-start(bf16[32,2048]{1,0:T(8,128)(2,1)S(1)} %collective-permute-done.6.refs_0_), channel_id=1, source_target_pairs={{0,4},{1,9},{2,6},{3,11},{4,0},{5,13},{6,2},{7,15},{8,12},{9,1},{1... | collective-permute-start | bytes 393224 | tf_op jit(solution)/shard_map/ppermute | solution.py:62
  12.3 0.8 %collective-permute-start.8 = (bf16[32,2048]{1,0:T(8,128)(2,1)S(1)}, bf16[32,2048]{1,0:T(8,128)(2,1)S(1)}, u32[]{:S(2)}, u32[]{:S(2)}) collective-permute-start(bf16[32,2048]{1,0:T(8,128)(2,1)S(1)} %collective-permute-done.6.refs_0_), channel_id=1, source_target_pairs={{0,8},{1,5},{2,10},{3,7},{4,12},{5,1},{6,14},{7,3},{8,0},{9,13},{1... | collective-permute-start | bytes 393224 | tf_op jit(solution)/shard_map/ppermute | solution.py:62
  13.1 2.0 %collective-permute-start.9 = (bf16[32,2048]{1,0:T(8,128)(2,1)S(1)}, bf16[32,2048]{1,0:T(8,128)(2,1)S(1)}, u32[]{:S(2)}, u32[]{:S(2)}) collective-permute-start(bf16[32,2048]{1,0:T(8,128)(2,1)S(1)} %collective-permute-done.6.refs_0_), channel_id=1, source_target_pairs={{0,12},{1,13},{2,14},{3,15},{4,8},{5,9},{6,10},{7,11},{8,4},{9,5},... | collective-permute-start | bytes 393224 | tf_op jit(solution)/shard_map/ppermute | solution.py:62
  15.1 0.0 collective-permute-done.1.refs_2_
  15.1 1.1 %collective-permute-done.2.refs_3_ = bf16[32,2048]{1,0:T(8,128)(2,1)S(1)} collective-permute-done((bf16[32,2048]{1,0:T(8,128)(2,1)}, bf16[32,2048]{1,0:T(8,128)(2,1)S(1)}, u32[]{:S(2)}, u32[]{:S(2)}) %collective-permute-start.2) | collective-permute-done | bytes 131104 | tf_op jit(solution)/shard_map/ppermute | solution.py:62
  16.3 3.0 %shard_map.74 = (bf16[32,2176]{1,0:T(8,128)(2,1)S(1)}, bf16[32,2176]{1,0:T(8,128)(2,1)S(1)}, bf16[32,2176]{1,0:T(8,128)(2,1)S(1)}, bf16[32,2176]{1,0:T(8,128)(2,1)S(1)}) custom-call(s32[2,3]{1,0:T(2,128)S(1)} %get-tuple-element.20.info, bf16[32,2048]{1,0:T(8,128)(2,1)S(1)} %copy-done.1, bf16[32,2048]{1,0:T(8,128)(2,1)S(1)} %collective-permute-done.refs_1_, ...), custom_call_target="tpu_custom_call" | custom-call | flops 2000000000 | bytes 4194304 | tf_op jit(solution)/shard_map/pallas_call | solution.py:228
  19.2 0.1 collective-permute-start.3
  19.3 2.5 %collective-permute-start.4 = (bf16[32,2176]{1,0:T(8,128)(2,1)S(1)}, bf16[32,2176]{1,0:T(8,128)(2,1)S(1)}, u32[]{:S(2)}, u32[]{:S(2)}) collective-permute-start(bf16[32,2176]{1,0:T(8,128)(2,1)S(1)} %get-tuple-element.25), channel_id=1, source_target_pairs={{0,8},{1,5},{2,10},{3,7},{4,12},{5,1},{6,14},{7,3},{8,0},{9,13},{1... | collective-permute-start | bytes 417800 | tf_op jit(solution)/shard_map/ppermute | solution.py:62
  21.8 0.0 collective-permute-done.7.refs_1_
  21.8 1.0 %collective-permute-start.5 = (bf16[32,2176]{1,0:T(8,128)(2,1)S(1)}, bf16[32,2176]{1,0:T(8,128)(2,1)S(1)}, u32[]{:S(2)}, u32[]{:S(2)}) collective-permute-start(bf16[32,2176]{1,0:T(8,128)(2,1)S(1)} %get-tuple-element.26), channel_id=1, source_target_pairs={{0,12},{1,13},{2,14},{3,15},{4,8},{5,9},{6,10},{7,11},{8,4},{9,5},... | collective-permute-start | bytes 417800 | tf_op jit(solution)/shard_map/ppermute | solution.py:62
  22.8 0.0 collective-permute-done.8.refs_2_
  22.8 3.0 %shard_map.76 = (bf16[32,2176]{1,0:T(8,128)(2,1)S(1)}, bf16[32,2176]{1,0:T(8,128)(2,1)S(1)}, bf16[32,2176]{1,0:T(8,128)(2,1)S(1)}, bf16[32,2176]{1,0:T(8,128)(2,1)S(1)}) custom-call(s32[2,3]{1,0:T(2,128)S(1)} %get-tuple-element.20.info, bf16[32,2048]{1,0:T(8,128)(2,1)S(1)} %collective-permute-done.6.refs_0_, ...), custom_call_target="tpu_custom_call" | custom-call | flops 2000000000 | bytes 4194304 | tf_op jit(solution)/shard_map/pallas_call | solution.py:228
  25.8 0.1 collective-permute-start.10
  25.9 2.5 %collective-permute-start.11 = (bf16[32,2176]{1,0:T(8,128)(2,1)S(1)}, bf16[32,2176]{1,0:T(8,128)(2,1)S(1)}, u32[]{:S(2)}, u32[]{:S(2)}) collective-permute-start(bf16[32,2176]{1,0:T(8,128)(2,1)S(1)} %get-tuple-element.29), channel_id=1, source_target_pairs={{0,8},{1,5},{2,10},{3,7},{4,12},{5,1},{6,14},{7,3},{8,0},{9,13},{1... | collective-permute-start | bytes 417800 | tf_op jit(solution)/shard_map/ppermute | solution.py:62
  28.4 1.0 %collective-permute-start.12 = (bf16[32,2176]{1,0:T(8,128)(2,1)S(1)}, bf16[32,2176]{1,0:T(8,128)(2,1)S(1)}, u32[]{:S(2)}, u32[]{:S(2)}) collective-permute-start(bf16[32,2176]{1,0:T(8,128)(2,1)S(1)} %get-tuple-element.30), channel_id=1, source_target_pairs={{0,12},{1,13},{2,14},{3,15},{4,8},{5,9},{6,10},{7,11},{8,4},{9,5},... | collective-permute-start | bytes 417800 | tf_op jit(solution)/shard_map/ppermute | solution.py:62
  29.4 0.5 shard_map.75.near
  29.8 1.8 %collective-permute-start.18 = (bf16[32,2176]{1,0:T(8,128)(2,1)S(1)}, bf16[32,2176]{1,0:T(8,128)(2,1)S(1)}, u32[]{:S(2)}, u32[]{:S(2)}) collective-permute-start(bf16[32,2176]{1,0:T(8,128)(2,1)S(1)} %shard_map.75.near), channel_id=1, source_target_pairs={{0,24},{4,28},{8,16},{12,20},{16,8},{20,12},{24,0},{28,4},{1,25},{... | collective-permute-start | bytes 417800 | tf_op jit(solution)/shard_map/ppermute | solution.py:324
  31.7 0.5 collective-permute-done.10.refs_1_
  32.2 3.1 %collective-permute-done.12.refs_3_ = bf16[32,2176]{1,0:T(8,128)(2,1)S(1)} collective-permute-done((bf16[32,2176]{1,0:T(8,128)(2,1)S(1)}, bf16[32,2176]{1,0:T(8,128)(2,1)S(1)}, u32[]{:S(2)}, u32[]{:S(2)}) %collective-permute-start.12) | collective-permute-done | bytes 139296 | tf_op jit(solution)/shard_map/ppermute | solution.py:62
  35.4 0.5 shard_map.77.near
  35.8 1.5 %collective-permute-start.13 = (bf16[32,2176]{1,0:T(8,128)(2,1)S(1)}, bf16[32,2176]{1,0:T(8,128)(2,1)S(1)}, u32[]{:S(2)}, u32[]{:S(2)}) collective-permute-start(bf16[32,2176]{1,0:T(8,128)(2,1)S(1)} %shard_map.77.near), channel_id=1, source_target_pairs={{0,24},{4,28},{8,16},{12,20},{16,8},{20,12},{24,0},{28,4},{1,25},{... | collective-permute-start | bytes 417800 | tf_op jit(solution)/shard_map/ppermute | solution.py:324
  37.3 0.3 collective-permute-done.18.far
  37.6 0.3 shard_map.80.refs_0_
  38.0 1.7 %collective-permute-start.19 = (bf16[32,2048]{1,0:T(8,128)(2,1)S(1)}, bf16[32,2048]{1,0:T(8,128)(2,1)S(1)}, u32[]{:S(2)}, u32[]{:S(2)}) collective-permute-start(bf16[32,2048]{1,0:T(8,128)(2,1)S(1)} %shard_map.80.refs_0_), channel_id=1, source_target_pairs={{0,4},{1,9},{2,6},{3,11},{4,0},{5,13},{6,2},{7,15},{8,12},{9,1},{1... | collective-permute-start | bytes 393224 | tf_op jit(solution)/shard_map/ppermute | solution.py:62
  39.7 2.5 %collective-permute-start.20 = (bf16[32,2048]{1,0:T(8,128)(2,1)S(1)}, bf16[32,2048]{1,0:T(8,128)(2,1)S(1)}, u32[]{:S(2)}, u32[]{:S(2)}) collective-permute-start(bf16[32,2048]{1,0:T(8,128)(2,1)S(1)} %shard_map.80.refs_0_), channel_id=1, source_target_pairs={{0,8},{1,5},{2,10},{3,7},{4,12},{5,1},{6,14},{7,3},{8,0},{9,13},{1... | collective-permute-start | bytes 393224 | tf_op jit(solution)/shard_map/ppermute | solution.py:62
  42.2 0.7 %collective-permute-done.13.far = bf16[32,2176]{1,0:T(8,128)(2,1)S(1)} collective-permute-done((bf16[32,2176]{1,0:T(8,128)(2,1)S(1)}, bf16[32,2176]{1,0:T(8,128)(2,1)S(1)}, u32[]{:S(2)}, u32[]{:S(2)}) %collective-permute-start.13) | collective-permute-done | bytes 139296 | tf_op jit(solution)/shard_map/ppermute | solution.py:324
  42.9 0.3 shard_map.78.refs_0_
  43.2 1.1 %collective-permute-start.14 = (bf16[32,2048]{1,0:T(8,128)(2,1)S(1)}, bf16[32,2048]{1,0:T(8,128)(2,1)S(1)}, u32[]{:S(2)}, u32[]{:S(2)}) collective-permute-start(bf16[32,2048]{1,0:T(8,128)(2,1)S(1)} %shard_map.78.refs_0_), channel_id=1, source_target_pairs={{0,4},{1,9},{2,6},{3,11},{4,0},{5,13},{6,2},{7,15},{8,12},{9,1},{1... | collective-permute-start | bytes 393224 | tf_op jit(solution)/shard_map/ppermute | solution.py:62
  44.3 1.8 %collective-permute-start.15 = (bf16[32,2048]{1,0:T(8,128)(2,1)S(1)}, bf16[32,2048]{1,0:T(8,128)(2,1)S(1)}, u32[]{:S(2)}, u32[]{:S(2)}) collective-permute-start(bf16[32,2048]{1,0:T(8,128)(2,1)S(1)} %shard_map.78.refs_0_), channel_id=1, source_target_pairs={{0,8},{1,5},{2,10},{3,7},{4,12},{5,1},{6,14},{7,3},{8,0},{9,13},{1... | collective-permute-start | bytes 393224 | tf_op jit(solution)/shard_map/ppermute | solution.py:62
  46.1 2.4 %collective-permute-start.16 = (bf16[32,2048]{1,0:T(8,128)(2,1)S(1)}, bf16[32,2048]{1,0:T(8,128)(2,1)S(1)}, u32[]{:S(2)}, u32[]{:S(2)}) collective-permute-start(bf16[32,2048]{1,0:T(8,128)(2,1)S(1)} %shard_map.78.refs_0_), channel_id=1, source_target_pairs={{0,12},{1,13},{2,14},{3,15},{4,8},{5,9},{6,10},{7,11},{8,4},{9,5},... | collective-permute-start | bytes 393224 | tf_op jit(solution)/shard_map/ppermute | solution.py:62
  48.5 0.4 collective-permute-done.21.refs_3_
  49.0 0.8 %shard_map.81 = (f32[64,1024]{1,0:T(8,128)S(1)}, bf16[64,1024]{1,0:T(8,128)(2,1)S(1)}) custom-call(bf16[32,2048]{1,0:T(8,128)(2,1)S(1)} %shard_map.80.refs_0_, bf16[32,2048]{1,0:T(8,128)(2,1)S(1)} %collective-permute-done.19.refs_1_, bf16[32,2048]{1,0:T(8,128)(2,1)S(1)} %collective-permute-done.20.refs_2_, ...), custom_call_target="tpu_custom_call" | custom-call | tf_op jit(solution)/shard_map/pallas_call | solution.py:312
  49.8 0.1 collective-permute-start.22
  49.8 0.4 collective-permute-done.14.refs_1_
  50.3 1.7 %collective-permute-done.16.refs_3_ = bf16[32,2048]{1,0:T(8,128)(2,1)S(1)} collective-permute-done((bf16[32,2048]{1,0:T(8,128)(2,1)S(1)}, bf16[32,2048]{1,0:T(8,128)(2,1)S(1)}, u32[]{:S(2)}, u32[]{:S(2)}) %collective-permute-start.16) | collective-permute-done | bytes 131104 | tf_op jit(solution)/shard_map/ppermute | solution.py:62
  52.0 0.8 %shard_map.79 = (f32[64,1024]{1,0:T(8,128)S(1)}, bf16[64,1024]{1,0:T(8,128)(2,1)S(1)}) custom-call(bf16[32,2048]{1,0:T(8,128)(2,1)S(1)} %shard_map.78.refs_0_, bf16[32,2048]{1,0:T(8,128)(2,1)S(1)} %collective-permute-done.14.refs_1_, bf16[32,2048]{1,0:T(8,128)(2,1)S(1)} %collective-permute-done.15.refs_2_, ...), custom_call_target="tpu_custom_call" | custom-call | tf_op jit(solution)/shard_map/pallas_call | solution.py:312
  52.8 0.1 collective-permute-start.17
  52.9 1.3 %collective-permute-done.17 = bf16[64,1024]{1,0:T(8,128)(2,1)S(1)} collective-permute-done((bf16[64,1024]{1,0:T(8,128)(2,1)S(1)}, bf16[64,1024]{1,0:T(8,128)(2,1)S(1)}, u32[]{:S(2)}, u32[]{:S(2)}) %collective-permute-start.17) | collective-permute-done | bytes 131104 | tf_op jit(solution)/shard_map/ppermute | solution.py:324
  54.2 0.1 select_convert_fusion
  54.2 1.6 %collective-permute-start.23 = (bf16[64,1024]{1,0:T(8,128)(2,1)S(1)}, bf16[64,1024]{1,0:T(8,128)(2,1)S(1)}, u32[]{:S(2)}, u32[]{:S(2)}) collective-permute-start(bf16[64,1024]{1,0:T(8,128)(2,1)S(1)} %select_convert_fusion), channel_id=1, source_target_pairs={{0,2},{1,3},{2,0},{3,1},{4,6},{5,7},{6,4},{7,5},{8,10},{9,11},{10,... | collective-permute-start | bytes 393224 | tf_op jit(solution)/shard_map/ppermute | solution.py:324
  55.8 4.0 %collective-permute-done.23 = bf16[64,1024]{1,0:T(8,128)(2,1)S(1)} collective-permute-done((bf16[64,1024]{1,0:T(8,128)(2,1)S(1)}, bf16[64,1024]{1,0:T(8,128)(2,1)S(1)}, u32[]{:S(2)}, u32[]{:S(2)}) %collective-permute-start.23) | collective-permute-done | bytes 131104 | tf_op jit(solution)/shard_map/ppermute | solution.py:324
  59.8 0.7 %add_convert_fusion = bf16[64,1024]{1,0:T(8,128)(2,1)} fusion(bf16[64,1024]{1,0:T(8,128)(2,1)S(1)} %collective-permute-done.23, f32[64,1024]{1,0:T(8,128)S(1)} %get-tuple-element.31, bf16[64,1024]{1,0:T(8,128)(2,1)S(1)} %collective-permute-done.17, f32[64,1024]{1,0:T(8,128)S(1)} %get-tuple-element.33, bf16[64,1024]{1,0:T(8,128)(2,1)S(1)} %collective-permute-done.22, ...), kind=kLoop, calls=%fused_computation | loop fusion | flops 524288 | bytes 1048577 | tf_op jit(solution)/shard_map/convert_element_type | solution.py:351
  (15 shorter events, 0.0 us)
Async XLA Ops:
  0.0 16.3 %copy-start.1 = (bf16[32,2048]{1,0:T(8,128)(2,1)S(1)}, bf16[32,2048]{1,0:T(8,128)(2,1)}, u32[]{:S(2)}) copy-start(bf16[32,2048]{1,0:T(8,128)(2,1)} %refs_0_.1) | copy-start | bytes 393220
  0.0 11.6 %collective-permute-start.6 = (bf16[32,2048]{1,0:T(8,128)(2,1)}, bf16[32,2048]{1,0:T(8,128)(2,1)S(1)}, u32[]{:S(2)}, u32[]{:S(2)}) collective-permute-start(bf16[32,2048]{1,0:T(8,128)(2,1)} %refs_0_.1), channel_id=1, source_target_pairs={{0,24},{4,28},{8,16},{12,20},{16,8},{20,12},{24,0},{28,4},{1,25},{... | collective-permute-start | bytes 393224 | tf_op jit(solution)/shard_map/ppermute | solution.py:324
  5.1 8.1 %collective-permute-start = (bf16[32,2048]{1,0:T(8,128)(2,1)}, bf16[32,2048]{1,0:T(8,128)(2,1)S(1)}, u32[]{:S(2)}, u32[]{:S(2)}) collective-permute-start(bf16[32,2048]{1,0:T(8,128)(2,1)} %refs_0_.1), channel_id=1, source_target_pairs={{0,4},{1,9},{2,6},{3,11},{4,0},{5,13},{6,2},{7,15},{8,12},{9,1},{1... | collective-permute-start | bytes 393224 | tf_op jit(solution)/shard_map/ppermute | solution.py:62
  6.5 8.6 %collective-permute-start.1 = (bf16[32,2048]{1,0:T(8,128)(2,1)}, bf16[32,2048]{1,0:T(8,128)(2,1)S(1)}, u32[]{:S(2)}, u32[]{:S(2)}) collective-permute-start(bf16[32,2048]{1,0:T(8,128)(2,1)} %refs_0_.1), channel_id=1, source_target_pairs={{0,8},{1,5},{2,10},{3,7},{4,12},{5,1},{6,14},{7,3},{8,0},{9,13},{1... | collective-permute-start | bytes 393224 | tf_op jit(solution)/shard_map/ppermute | solution.py:62
  6.5 9.7 %collective-permute-start.2 = (bf16[32,2048]{1,0:T(8,128)(2,1)}, bf16[32,2048]{1,0:T(8,128)(2,1)S(1)}, u32[]{:S(2)}, u32[]{:S(2)}) collective-permute-start(bf16[32,2048]{1,0:T(8,128)(2,1)} %refs_0_.1), channel_id=1, source_target_pairs={{0,12},{1,13},{2,14},{3,15},{4,8},{5,9},{6,10},{7,11},{8,4},{9,5},... | collective-permute-start | bytes 393224 | tf_op jit(solution)/shard_map/ppermute | solution.py:62
  11.6 10.2 %collective-permute-start.7 = (bf16[32,2048]{1,0:T(8,128)(2,1)S(1)}, bf16[32,2048]{1,0:T(8,128)(2,1)S(1)}, u32[]{:S(2)}, u32[]{:S(2)}) collective-permute-start(bf16[32,2048]{1,0:T(8,128)(2,1)S(1)} %collective-permute-done.6.refs_0_), channel_id=1, source_target_pairs={{0,4},{1,9},{2,6},{3,11},{4,0},{5,13},{6,2},{7,15},{8,12},{9,1},{1... | collective-permute-start | bytes 393224 | tf_op jit(solution)/shard_map/ppermute | solution.py:62
  12.3 10.5 %collective-permute-start.8 = (bf16[32,2048]{1,0:T(8,128)(2,1)S(1)}, bf16[32,2048]{1,0:T(8,128)(2,1)S(1)}, u32[]{:S(2)}, u32[]{:S(2)}) collective-permute-start(bf16[32,2048]{1,0:T(8,128)(2,1)S(1)} %collective-permute-done.6.refs_0_), channel_id=1, source_target_pairs={{0,8},{1,5},{2,10},{3,7},{4,12},{5,1},{6,14},{7,3},{8,0},{9,13},{1... | collective-permute-start | bytes 393224 | tf_op jit(solution)/shard_map/ppermute | solution.py:62
  13.1 9.7 %collective-permute-start.9 = (bf16[32,2048]{1,0:T(8,128)(2,1)S(1)}, bf16[32,2048]{1,0:T(8,128)(2,1)S(1)}, u32[]{:S(2)}, u32[]{:S(2)}) collective-permute-start(bf16[32,2048]{1,0:T(8,128)(2,1)S(1)} %collective-permute-done.6.refs_0_), channel_id=1, source_target_pairs={{0,12},{1,13},{2,14},{3,15},{4,8},{5,9},{6,10},{7,11},{8,4},{9,5},... | collective-permute-start | bytes 393224 | tf_op jit(solution)/shard_map/ppermute | solution.py:62
  19.2 9.1 %collective-permute-start.3 = (bf16[32,2176]{1,0:T(8,128)(2,1)S(1)}, bf16[32,2176]{1,0:T(8,128)(2,1)S(1)}, u32[]{:S(2)}, u32[]{:S(2)}) collective-permute-start(bf16[32,2176]{1,0:T(8,128)(2,1)S(1)} %get-tuple-element.24), channel_id=1, source_target_pairs={{0,4},{1,9},{2,6},{3,11},{4,0},{5,13},{6,2},{7,15},{8,12},{9,1},{1... | collective-permute-start | bytes 417800 | tf_op jit(solution)/shard_map/ppermute | solution.py:62
  19.3 10.0 %collective-permute-start.4 = (bf16[32,2176]{1,0:T(8,128)(2,1)S(1)}, bf16[32,2176]{1,0:T(8,128)(2,1)S(1)}, u32[]{:S(2)}, u32[]{:S(2)}) collective-permute-start(bf16[32,2176]{1,0:T(8,128)(2,1)S(1)} %get-tuple-element.25), channel_id=1, source_target_pairs={{0,8},{1,5},{2,10},{3,7},{4,12},{5,1},{6,14},{7,3},{8,0},{9,13},{1... | collective-permute-start | bytes 417800 | tf_op jit(solution)/shard_map/ppermute | solution.py:62
  21.8 27.2 %copy-start = (bf16[2048,1024]{1,0:T(8,128)(2,1)S(1)}, bf16[2048,1024]{1,0:T(8,128)(2,1)}, u32[]{:S(2)}) copy-start(bf16[2048,1024]{1,0:T(8,128)(2,1)} %refs_4_.3) | copy-start | bytes 12582916
  21.8 7.6 %collective-permute-start.5 = (bf16[32,2176]{1,0:T(8,128)(2,1)S(1)}, bf16[32,2176]{1,0:T(8,128)(2,1)S(1)}, u32[]{:S(2)}, u32[]{:S(2)}) collective-permute-start(bf16[32,2176]{1,0:T(8,128)(2,1)S(1)} %get-tuple-element.26), channel_id=1, source_target_pairs={{0,12},{1,13},{2,14},{3,15},{4,8},{5,9},{6,10},{7,11},{8,4},{9,5},... | collective-permute-start | bytes 417800 | tf_op jit(solution)/shard_map/ppermute | solution.py:62
  25.8 6.4 %collective-permute-start.10 = (bf16[32,2176]{1,0:T(8,128)(2,1)S(1)}, bf16[32,2176]{1,0:T(8,128)(2,1)S(1)}, u32[]{:S(2)}, u32[]{:S(2)}) collective-permute-start(bf16[32,2176]{1,0:T(8,128)(2,1)S(1)} %get-tuple-element.28), channel_id=1, source_target_pairs={{0,4},{1,9},{2,6},{3,11},{4,0},{5,13},{6,2},{7,15},{8,12},{9,1},{1... | collective-permute-start | bytes 417800 | tf_op jit(solution)/shard_map/ppermute | solution.py:62
  25.9 6.4 %collective-permute-start.11 = (bf16[32,2176]{1,0:T(8,128)(2,1)S(1)}, bf16[32,2176]{1,0:T(8,128)(2,1)S(1)}, u32[]{:S(2)}, u32[]{:S(2)}) collective-permute-start(bf16[32,2176]{1,0:T(8,128)(2,1)S(1)} %get-tuple-element.29), channel_id=1, source_target_pairs={{0,8},{1,5},{2,10},{3,7},{4,12},{5,1},{6,14},{7,3},{8,0},{9,13},{1... | collective-permute-start | bytes 417800 | tf_op jit(solution)/shard_map/ppermute | solution.py:62
  28.4 7.0 %collective-permute-start.12 = (bf16[32,2176]{1,0:T(8,128)(2,1)S(1)}, bf16[32,2176]{1,0:T(8,128)(2,1)S(1)}, u32[]{:S(2)}, u32[]{:S(2)}) collective-permute-start(bf16[32,2176]{1,0:T(8,128)(2,1)S(1)} %get-tuple-element.30), channel_id=1, source_target_pairs={{0,12},{1,13},{2,14},{3,15},{4,8},{5,9},{6,10},{7,11},{8,4},{9,5},... | collective-permute-start | bytes 417800 | tf_op jit(solution)/shard_map/ppermute | solution.py:62
  29.8 7.8 %collective-permute-start.18 = (bf16[32,2176]{1,0:T(8,128)(2,1)S(1)}, bf16[32,2176]{1,0:T(8,128)(2,1)S(1)}, u32[]{:S(2)}, u32[]{:S(2)}) collective-permute-start(bf16[32,2176]{1,0:T(8,128)(2,1)S(1)} %shard_map.75.near), channel_id=1, source_target_pairs={{0,24},{4,28},{8,16},{12,20},{16,8},{20,12},{24,0},{28,4},{1,25},{... | collective-permute-start | bytes 417800 | tf_op jit(solution)/shard_map/ppermute | solution.py:324
  35.8 7.0 %collective-permute-start.13 = (bf16[32,2176]{1,0:T(8,128)(2,1)S(1)}, bf16[32,2176]{1,0:T(8,128)(2,1)S(1)}, u32[]{:S(2)}, u32[]{:S(2)}) collective-permute-start(bf16[32,2176]{1,0:T(8,128)(2,1)S(1)} %shard_map.77.near), channel_id=1, source_target_pairs={{0,24},{4,28},{8,16},{12,20},{16,8},{20,12},{24,0},{28,4},{1,25},{... | collective-permute-start | bytes 417800 | tf_op jit(solution)/shard_map/ppermute | solution.py:324
  38.0 8.1 %collective-permute-start.19 = (bf16[32,2048]{1,0:T(8,128)(2,1)S(1)}, bf16[32,2048]{1,0:T(8,128)(2,1)S(1)}, u32[]{:S(2)}, u32[]{:S(2)}) collective-permute-start(bf16[32,2048]{1,0:T(8,128)(2,1)S(1)} %shard_map.80.refs_0_), channel_id=1, source_target_pairs={{0,4},{1,9},{2,6},{3,11},{4,0},{5,13},{6,2},{7,15},{8,12},{9,1},{1... | collective-permute-start | bytes 393224 | tf_op jit(solution)/shard_map/ppermute | solution.py:62
  39.7 8.8 %collective-permute-start.20 = (bf16[32,2048]{1,0:T(8,128)(2,1)S(1)}, bf16[32,2048]{1,0:T(8,128)(2,1)S(1)}, u32[]{:S(2)}, u32[]{:S(2)}) collective-permute-start(bf16[32,2048]{1,0:T(8,128)(2,1)S(1)} %shard_map.80.refs_0_), channel_id=1, source_target_pairs={{0,8},{1,5},{2,10},{3,7},{4,12},{5,1},{6,14},{7,3},{8,0},{9,13},{1... | collective-permute-start | bytes 393224 | tf_op jit(solution)/shard_map/ppermute | solution.py:62
  42.2 6.8 %collective-permute-start.21 = (bf16[32,2048]{1,0:T(8,128)(2,1)S(1)}, bf16[32,2048]{1,0:T(8,128)(2,1)S(1)}, u32[]{:S(2)}, u32[]{:S(2)}) collective-permute-start(bf16[32,2048]{1,0:T(8,128)(2,1)S(1)} %shard_map.80.refs_0_), channel_id=1, source_target_pairs={{0,12},{1,13},{2,14},{3,15},{4,8},{5,9},{6,10},{7,11},{8,4},{9,5},... | collective-permute-start | bytes 393224 | tf_op jit(solution)/shard_map/ppermute | solution.py:62
  43.2 7.1 %collective-permute-start.14 = (bf16[32,2048]{1,0:T(8,128)(2,1)S(1)}, bf16[32,2048]{1,0:T(8,128)(2,1)S(1)}, u32[]{:S(2)}, u32[]{:S(2)}) collective-permute-start(bf16[32,2048]{1,0:T(8,128)(2,1)S(1)} %shard_map.78.refs_0_), channel_id=1, source_target_pairs={{0,4},{1,9},{2,6},{3,11},{4,0},{5,13},{6,2},{7,15},{8,12},{9,1},{1... | collective-permute-start | bytes 393224 | tf_op jit(solution)/shard_map/ppermute | solution.py:62
  44.3 6.0 %collective-permute-start.15 = (bf16[32,2048]{1,0:T(8,128)(2,1)S(1)}, bf16[32,2048]{1,0:T(8,128)(2,1)S(1)}, u32[]{:S(2)}, u32[]{:S(2)}) collective-permute-start(bf16[32,2048]{1,0:T(8,128)(2,1)S(1)} %shard_map.78.refs_0_), channel_id=1, source_target_pairs={{0,8},{1,5},{2,10},{3,7},{4,12},{5,1},{6,14},{7,3},{8,0},{9,13},{1... | collective-permute-start | bytes 393224 | tf_op jit(solution)/shard_map/ppermute | solution.py:62
  46.1 5.9 %collective-permute-start.16 = (bf16[32,2048]{1,0:T(8,128)(2,1)S(1)}, bf16[32,2048]{1,0:T(8,128)(2,1)S(1)}, u32[]{:S(2)}, u32[]{:S(2)}) collective-permute-start(bf16[32,2048]{1,0:T(8,128)(2,1)S(1)} %shard_map.78.refs_0_), channel_id=1, source_target_pairs={{0,12},{1,13},{2,14},{3,15},{4,8},{5,9},{6,10},{7,11},{8,4},{9,5},... | collective-permute-start | bytes 393224 | tf_op jit(solution)/shard_map/ppermute | solution.py:62
  49.8 3.1 %collective-permute-start.22 = (bf16[64,1024]{1,0:T(8,128)(2,1)S(1)}, bf16[64,1024]{1,0:T(8,128)(2,1)S(1)}, u32[]{:S(2)}, u32[]{:S(2)}) collective-permute-start(bf16[64,1024]{1,0:T(8,128)(2,1)S(1)} %get-tuple-element.34), channel_id=1, source_target_pairs={{0,1},{1,0},{2,3},{3,2},{4,5},{5,4},{6,7},{7,6},{8,9},{9,8},{10,11... | collective-permute-start | bytes 393224 | tf_op jit(solution)/shard_map/ppermute | solution.py:324
  52.8 1.4 %collective-permute-start.17 = (bf16[64,1024]{1,0:T(8,128)(2,1)S(1)}, bf16[64,1024]{1,0:T(8,128)(2,1)S(1)}, u32[]{:S(2)}, u32[]{:S(2)}) collective-permute-start(bf16[64,1024]{1,0:T(8,128)(2,1)S(1)} %get-tuple-element.32), channel_id=1, source_target_pairs={{0,1},{1,0},{2,3},{3,2},{4,5},{5,4},{6,7},{7,6},{8,9},{9,8},{10,11... | collective-permute-start | bytes 393224 | tf_op jit(solution)/shard_map/ppermute | solution.py:324
  54.2 5.6 %collective-permute-start.23 = (bf16[64,1024]{1,0:T(8,128)(2,1)S(1)}, bf16[64,1024]{1,0:T(8,128)(2,1)S(1)}, u32[]{:S(2)}, u32[]{:S(2)}) collective-permute-start(bf16[64,1024]{1,0:T(8,128)(2,1)S(1)} %select_convert_fusion), channel_id=1, source_target_pairs={{0,2},{1,3},{2,0},{3,1},{4,6},{5,7},{6,4},{7,5},{8,10},{9,11},{10,... | collective-permute-start | bytes 393224 | tf_op jit(solution)/shard_map/ppermute | solution.py:324

commit v7 on v6

--- a/solution.py
+++ b/solution.py
@@ -33,7 +33,7 @@
 
 class Plan:
     def __init__(self, n, ways, rows, blocks, page):
-        self.n, self.ways, self.rows, self.blocks, self.page = n, ways, rows, blocks, page
+        self.n, self.rows, self.blocks, self.page = n, rows, blocks, page
         self.group = n // blocks
         self.halves = blocks == 2 and n == 8 and ways == 4 and rows * self.group == page
         self.cross = n * 3 // 4
@@ -42,24 +42,12 @@
     def block(self, me, lb):
         return (me // self.group) ^ lb if self.halves else lb
 
-    def holder(self, me, column, lb, chunk):
-        turned = chunk // 2 + chunk % 2 * 2
-        return me ^ (lb * self.cross) ^ jnp.where(column % 2 == 0, chunk, turned)
-
     def offsets(self, me, lb, shape):
         row = lax.broadcasted_iota(jnp.int32, shape, 0) % self.page
         if not self.halves:
             return row
-        holder = self.holder(me, lax.axis_index("mp"), lb, row // self.rows)
-        return holder % self.group * self.rows + row % self.rows
-
-    def swap(self, x, chunk):
-        pairs = []
-        for p in range(self.n):
-            for m in range(self.ways):
-                turned = chunk // 2 + chunk % 2 * 2
-                pairs.append((p * self.ways + m, (p ^ (turned if m % 2 else chunk)) * self.ways + m))
-        return lax.ppermute(x, ("pages", "mp"), pairs)
+        mine = (me ^ (lb * self.cross)) % self.group
+        return ((row // self.rows) ^ mine) * self.rows + row % self.rows
 
 
 def fetch_kernel(plan, pages_dev, select_hbm, table_hbm, stands_hbm, keys, values, k_out, v_out, info, select, table, stands, rows, k_buf, v_buf, sems, int_sems):
@@ -291,15 +279,19 @@
     )(near, far)
 
 
+def sources_of(plan, lb):
+    return range(plan.group) if lb else reversed(range(plan.group))
+
+
 def project_kernel(plan, lb, *refs):
     sources, weight, (keep, send, rows_ref) = refs[: plan.group], refs[plan.group], refs[plan.group + 1 :]
     me, column = lax.axis_index("pages"), lax.axis_index("mp")
     rows = plan.rows
     holders = plan.group // 2
-    for k in range(plan.group):
-        device = plan.holder(me, column, lb, k)
+    for i, k in enumerate(sources_of(plan, lb)):
+        device = me ^ k ^ (lb * plan.cross)
         place = ((device // holders % 2) ^ (column % 2)) * holders + device % holders
-        rows_ref[pl.ds(pl.multiple_of(place * rows, rows), rows), :] = sources[k][...]
+        rows_ref[pl.ds(pl.multiple_of(place * rows, rows), rows), :] = sources[i][...]
     product = jnp.dot(rows_ref[...], weight[...], preferred_element_type=F32)
     part = holders * rows
     keep[...] = product[:part]
@@ -316,7 +308,7 @@
         out_specs=(in_vmem(), in_vmem()),
         scratch_shapes=[VMEM((plan.page, weight.shape[0]), BF16)],
         compiler_params=params(24),
-    )(*(sources[k] for k in range(plan.group)), weight)
+    )(*(sources[k] for k in sources_of(plan, lb)), weight)
 
 
 def swap(x, axis, distance):
@@ -329,7 +321,7 @@
 
 
 def spread(x, plan):
-    return {0: x} | {k: plan.swap(x, k) for k in others(plan)}
+    return {0: x} | {k: swap(x, "pages", k) for k in others(plan)}
 
 
 def by_halves(plan, heads, queries, weight, pages):
@@ -338,7 +330,7 @@
     for lb, rows in enumerate((queries, far)):
         chunks = spread(rows, plan)
         outs = attend(plan, heads, lb, pages, [chunks[k] for k in range(plan.group)])
-        near.append(merge(heads, outs[0], *(plan.swap(outs[k], k) for k in others(plan))))
+        near.append(merge(heads, *(swap(outs[k], "pages", k) for k in reversed(others(plan))), outs[0]))
     across = [swap(x, "pages", plan.cross) for x in near]
     sums = [None, None]
     for lb in (1, 0):

time: 60.7 us -> 62.1 us (1.023)
  starting transfers between devices: 33.8 us -> 41 us
  Pallas kernels: 12.1 us -> 6.65 us
    ppermute x6 -> x24, starting transfers between devices: 10.1 us -> 41 us  [swap(): return lax.ppermute(x, axis, [(i, i ^ distance) for i in range(n)])]
    ppermute x18 -> x0, starting transfers between devices: 23.7 us -> none  [swap(): return lax.ppermute(x, ('pages', 'mp'), pairs)]
    ppermute x18 -> x0, waiting for transfers between devices: 7.38 us -> none  [swap(): return lax.ppermute(x, ('pages', 'mp'), pairs)]
    ppermute x6 -> x24, waiting for transfers between devices: 6.27 us -> 13.4 us  [swap(): return lax.ppermute(x, axis, [(i, i ^ distance) for i in range(n)])]
    pallas_call x2, Pallas kernels: 5.96 us -> 1.29 us  [attend(): pl.pallas_call(functools.partial(attend_kernel, plan, heads, lb), out_sha...]
    pallas_call x1, Pallas kernels: 3.01 us -> 2.19 us  [fetch(): pl.pallas_call(functools.partial(fetch_kernel, plan, pages_dev), out_shap...]
  transfers between devices with their start and end apart: 24 -> 24, of which waited for: 10 -> 10; matrix products, arithmetic and copies ran while one was open for 0% -> 0% of each run, Pallas kernels for 20% -> 11%
where the time goes in v7:
time: 62.1 us; the launch traced here: 61.9 us
  starting transfers between devices  41 us (66%)
  waiting for transfers between devices  13.4 us (22%)
  Pallas kernels  6.65 us (11%)
  other arithmetic  0.78 us (1%)
    ppermute x24, starting transfers between devices, swap(): return lax.ppermute(x, axis, [(i, i ^ distance) for i in range(n)])  41 us
    ppermute x24, waiting for transfers between devices, swap(): return lax.ppermute(x, axis, [(i, i ^ distance) for i in range(n)])  13.4 us
    pallas_call x1, Pallas kernels, fetch(): pl.pallas_call(functools.partial(fetch_kernel, plan, pages_dev), out_shap...  2.19 us
    pallas_call x2, Pallas kernels, project(): pl.pallas_call(functools.partial(project_kernel, plan, lb), out_shape=(ja...  1.57 us
    pallas_call x2, Pallas kernels, attend(): pl.pallas_call(functools.partial(attend_kernel, plan, heads, lb), out_sha...  1.29 us
  transfers between devices with their start and end apart: 24, of which 10 were waited for; matrix products, arithmetic and copies ran while one was open for 0% of the time, Pallas kernels for 11%

profile of v7, /device:TPU:0, one launch (start us, length us, event | category | flops | bytes accessed | tf_op | source)
XLA Modules:
  0.0 61.9 jit_solution(16751258706916228845)
XLA Ops:
  0.0 5.0 %collective-permute-start.6 = (bf16[32,2048]{1,0:T(8,128)(2,1)}, bf16[32,2048]{1,0:T(8,128)(2,1)S(1)}, u32[]{:S(2)}, u32[]{:S(2)}) collective-permute-start(bf16[32,2048]{1,0:T(8,128)(2,1)} %refs_0_.1), channel_id=1, source_target_pairs={{0,24},{4,28},{8,16},{12,20},{16,8},{20,12},{24,0},{28,4},{1,25},{... | collective-permute-start | bytes 393224 | tf_op jit(solution)/shard_map/ppermute | solution.py:316
  5.1 1.5 %collective-permute-start = (bf16[32,2048]{1,0:T(8,128)(2,1)}, bf16[32,2048]{1,0:T(8,128)(2,1)S(1)}, u32[]{:S(2)}, u32[]{:S(2)}) collective-permute-start(bf16[32,2048]{1,0:T(8,128)(2,1)} %refs_0_.1), channel_id=1, source_target_pairs={{0,4},{4,0},{8,12},{12,8},{16,20},{20,16},{24,28},{28,24},{1,5},{5... | collective-permute-start | bytes 393224 | tf_op jit(solution)/shard_map/ppermute | solution.py:316
  6.5 0.0 collective-permute-start.1
  6.5 2.0 %collective-permute-start.2 = (bf16[32,2048]{1,0:T(8,128)(2,1)}, bf16[32,2048]{1,0:T(8,128)(2,1)S(1)}, u32[]{:S(2)}, u32[]{:S(2)}) collective-permute-start(bf16[32,2048]{1,0:T(8,128)(2,1)} %refs_0_.1), channel_id=1, source_target_pairs={{0,12},{4,8},{8,4},{12,0},{16,28},{20,24},{24,20},{28,16},{1,13},{... | collective-permute-start | bytes 393224 | tf_op jit(solution)/shard_map/ppermute | solution.py:316
  8.5 2.2 %shard_map.73 = (bf16[2,2,768,128]{3,2,1,0:T(8,128)(2,1)S(1)}, bf16[2,2,768,256]{3,2,1,0:T(8,128)(2,1)S(1)}, s32[2,3]{1,0:T(2,128)S(1)}) custom-call(s32[2,24]{1,0:T(2,128)} %select_hbm.1, s32[128]{0:T(128)} %table_hbm.1, s32[2]{0:T(128)} %stands_hbm.1, bf16[16,256,128]{2,1,0:T(8,128)(2,1)} %bitcast.2, bf16[16,256,128]{2,1,0:T(8,128)(2,1)} %bitcast.3), custom_call_target="tpu_custom_call" | custom-call | flops 2000000000 | bytes 8388608 | tf_op jit(solution)/shard_map/pallas_call | solution.py:118
  10.7 0.0 collective-permute-done.6.refs_0_
  10.8 2.4 %collective-permute-start.7 = (bf16[32,2048]{1,0:T(8,128)(2,1)S(1)}, bf16[32,2048]{1,0:T(8,128)(2,1)S(1)}, u32[]{:S(2)}, u32[]{:S(2)}) collective-permute-start(bf16[32,2048]{1,0:T(8,128)(2,1)S(1)} %collective-permute-done.6.refs_0_), channel_id=1, source_target_pairs={{0,4},{4,0},{8,12},{12,8},{16,20},{20,16},{24,28},{28,24},{1,5},{5... | collective-permute-start | bytes 393224 | tf_op jit(solution)/shard_map/ppermute | solution.py:316
  13.1 0.0 collective-permute-done.refs_1_
  13.1 1.5 %collective-permute-start.9 = (bf16[32,2048]{1,0:T(8,128)(2,1)S(1)}, bf16[32,2048]{1,0:T(8,128)(2,1)S(1)}, u32[]{:S(2)}, u32[]{:S(2)}) collective-permute-start(bf16[32,2048]{1,0:T(8,128)(2,1)S(1)} %collective-permute-done.6.refs_0_), channel_id=1, source_target_pairs={{0,12},{4,8},{8,4},{12,0},{16,28},{20,24},{24,20},{28,16},{1,13},{... | collective-permute-start | bytes 393224 | tf_op jit(solution)/shard_map/ppermute | solution.py:316
  14.7 1.6 %collective-permute-done.2.refs_3_ = bf16[32,2048]{1,0:T(8,128)(2,1)S(1)} collective-permute-done((bf16[32,2048]{1,0:T(8,128)(2,1)}, bf16[32,2048]{1,0:T(8,128)(2,1)S(1)}, u32[]{:S(2)}, u32[]{:S(2)}) %collective-permute-start.2) | collective-permute-done | bytes 131104 | tf_op jit(solution)/shard_map/ppermute | solution.py:316
  16.3 0.6 %shard_map.74 = (bf16[32,2176]{1,0:T(8,128)(2,1)S(1)}, bf16[32,2176]{1,0:T(8,128)(2,1)S(1)}, bf16[32,2176]{1,0:T(8,128)(2,1)S(1)}, bf16[32,2176]{1,0:T(8,128)(2,1)S(1)}) custom-call(s32[2,3]{1,0:T(2,128)S(1)} %get-tuple-element.20.info, bf16[32,2048]{1,0:T(8,128)(2,1)S(1)} %copy-done.1, bf16[32,2048]{1,0:T(8,128)(2,1)S(1)} %collective-permute-done.refs_1_, ...), custom_call_target="tpu_custom_call" | custom-call | flops 2000000000 | bytes 4194304 | tf_op jit(solution)/shard_map/pallas_call | solution.py:216
  16.9 2.0 %collective-permute-start.3 = (bf16[32,2176]{1,0:T(8,128)(2,1)S(1)}, bf16[32,2176]{1,0:T(8,128)(2,1)S(1)}, u32[]{:S(2)}, u32[]{:S(2)}) collective-permute-start(bf16[32,2176]{1,0:T(8,128)(2,1)S(1)} %get-tuple-element.23), channel_id=1, source_target_pairs={{0,12},{4,8},{8,4},{12,0},{16,28},{20,24},{24,20},{28,16},{1,13},{... | collective-permute-start | bytes 417800 | tf_op jit(solution)/shard_map/ppermute | solution.py:316
  18.9 2.5 %collective-permute-start.4 = (bf16[32,2176]{1,0:T(8,128)(2,1)S(1)}, bf16[32,2176]{1,0:T(8,128)(2,1)S(1)}, u32[]{:S(2)}, u32[]{:S(2)}) collective-permute-start(bf16[32,2176]{1,0:T(8,128)(2,1)S(1)} %get-tuple-element.24), channel_id=1, source_target_pairs={{0,8},{4,12},{8,0},{12,4},{16,24},{20,28},{24,16},{28,20},{1,9},{5... | collective-permute-start | bytes 417800 | tf_op jit(solution)/shard_map/ppermute | solution.py:316
  21.3 1.4 %collective-permute-start.5 = (bf16[32,2176]{1,0:T(8,128)(2,1)S(1)}, bf16[32,2176]{1,0:T(8,128)(2,1)S(1)}, u32[]{:S(2)}, u32[]{:S(2)}) collective-permute-start(bf16[32,2176]{1,0:T(8,128)(2,1)S(1)} %get-tuple-element.25), channel_id=1, source_target_pairs={{0,4},{4,0},{8,12},{12,8},{16,20},{20,16},{24,28},{28,24},{1,5},{5... | collective-permute-start | bytes 417800 | tf_op jit(solution)/shard_map/ppermute | solution.py:316
  22.8 0.0 collective-permute-done.8.refs_2_
  22.8 0.0 collective-permute-done.9.refs_3_
  22.8 0.6 %shard_map.76 = (bf16[32,2176]{1,0:T(8,128)(2,1)S(1)}, bf16[32,2176]{1,0:T(8,128)(2,1)S(1)}, bf16[32,2176]{1,0:T(8,128)(2,1)S(1)}, bf16[32,2176]{1,0:T(8,128)(2,1)S(1)}) custom-call(s32[2,3]{1,0:T(2,128)S(1)} %get-tuple-element.20.info, bf16[32,2048]{1,0:T(8,128)(2,1)S(1)} %collective-permute-done.6.refs_0_, ...), custom_call_target="tpu_custom_call" | custom-call | flops 2000000000 | bytes 4194304 | tf_op jit(solution)/shard_map/pallas_call | solution.py:216
  23.4 1.5 %collective-permute-start.10 = (bf16[32,2176]{1,0:T(8,128)(2,1)S(1)}, bf16[32,2176]{1,0:T(8,128)(2,1)S(1)}, u32[]{:S(2)}, u32[]{:S(2)}) collective-permute-start(bf16[32,2176]{1,0:T(8,128)(2,1)S(1)} %get-tuple-element.27), channel_id=1, source_target_pairs={{0,12},{4,8},{8,4},{12,0},{16,28},{20,24},{24,20},{28,16},{1,13},{... | collective-permute-start | bytes 417800 | tf_op jit(solution)/shard_map/ppermute | solution.py:316
  24.9 3.0 %collective-permute-start.11 = (bf16[32,2176]{1,0:T(8,128)(2,1)S(1)}, bf16[32,2176]{1,0:T(8,128)(2,1)S(1)}, u32[]{:S(2)}, u32[]{:S(2)}) collective-permute-start(bf16[32,2176]{1,0:T(8,128)(2,1)S(1)} %get-tuple-element.28), channel_id=1, source_target_pairs={{0,8},{4,12},{8,0},{12,4},{16,24},{20,28},{24,16},{28,20},{1,9},{5... | collective-permute-start | bytes 417800 | tf_op jit(solution)/shard_map/ppermute | solution.py:316
  27.8 0.0 collective-permute-done.3.refs_0_
  27.8 1.3 %collective-permute-start.12 = (bf16[32,2176]{1,0:T(8,128)(2,1)S(1)}, bf16[32,2176]{1,0:T(8,128)(2,1)S(1)}, u32[]{:S(2)}, u32[]{:S(2)}) collective-permute-start(bf16[32,2176]{1,0:T(8,128)(2,1)S(1)} %get-tuple-element.29), channel_id=1, source_target_pairs={{0,4},{4,0},{8,12},{12,8},{16,20},{20,16},{24,28},{28,24},{1,5},{5... | collective-permute-start | bytes 417800 | tf_op jit(solution)/shard_map/ppermute | solution.py:316
  29.2 0.0 collective-permute-done.4.refs_1_
  29.2 0.5 collective-permute-done.5.refs_2_
  29.7 0.5 shard_map.75.near
  30.2 2.6 %collective-permute-start.18 = (bf16[32,2176]{1,0:T(8,128)(2,1)S(1)}, bf16[32,2176]{1,0:T(8,128)(2,1)S(1)}, u32[]{:S(2)}, u32[]{:S(2)}) collective-permute-start(bf16[32,2176]{1,0:T(8,128)(2,1)S(1)} %shard_map.75.near), channel_id=1, source_target_pairs={{0,24},{4,28},{8,16},{12,20},{16,8},{20,12},{24,0},{28,4},{1,25},{... | collective-permute-start | bytes 417800 | tf_op jit(solution)/shard_map/ppermute | solution.py:316
  32.8 0.4 collective-permute-done.10.refs_0_
  33.2 0.5 shard_map.77.near
  33.7 2.8 %collective-permute-start.13 = (bf16[32,2176]{1,0:T(8,128)(2,1)S(1)}, bf16[32,2176]{1,0:T(8,128)(2,1)S(1)}, u32[]{:S(2)}, u32[]{:S(2)}) collective-permute-start(bf16[32,2176]{1,0:T(8,128)(2,1)S(1)} %shard_map.77.near), channel_id=1, source_target_pairs={{0,24},{4,28},{8,16},{12,20},{16,8},{20,12},{24,0},{28,4},{1,25},{... | collective-permute-start | bytes 417800 | tf_op jit(solution)/shard_map/ppermute | solution.py:316
  36.5 1.5 %collective-permute-done.18.far = bf16[32,2176]{1,0:T(8,128)(2,1)S(1)} collective-permute-done((bf16[32,2176]{1,0:T(8,128)(2,1)S(1)}, bf16[32,2176]{1,0:T(8,128)(2,1)S(1)}, u32[]{:S(2)}, u32[]{:S(2)}) %collective-permute-start.18) | collective-permute-done | bytes 139296 | tf_op jit(solution)/shard_map/ppermute | solution.py:316
  38.0 0.3 shard_map.80.refs_0_
  38.3 0.7 %collective-permute-start.19 = (bf16[32,2048]{1,0:T(8,128)(2,1)S(1)}, bf16[32,2048]{1,0:T(8,128)(2,1)S(1)}, u32[]{:S(2)}, u32[]{:S(2)}) collective-permute-start(bf16[32,2048]{1,0:T(8,128)(2,1)S(1)} %shard_map.80.refs_0_), channel_id=1, source_target_pairs={{0,4},{4,0},{8,12},{12,8},{16,20},{20,16},{24,28},{28,24},{1,5},{5... | collective-permute-start | bytes 393224 | tf_op jit(solution)/shard_map/ppermute | solution.py:316
  39.1 4.9 %collective-permute-start.20 = (bf16[32,2048]{1,0:T(8,128)(2,1)S(1)}, bf16[32,2048]{1,0:T(8,128)(2,1)S(1)}, u32[]{:S(2)}, u32[]{:S(2)}) collective-permute-start(bf16[32,2048]{1,0:T(8,128)(2,1)S(1)} %shard_map.80.refs_0_), channel_id=1, source_target_pairs={{0,8},{4,12},{8,0},{12,4},{16,24},{20,28},{24,16},{28,20},{1,9},{5... | collective-permute-start | bytes 393224 | tf_op jit(solution)/shard_map/ppermute | solution.py:316
  44.0 0.3 shard_map.78.refs_3_
  44.3 3.0 %collective-permute-start.14 = (bf16[32,2048]{1,0:T(8,128)(2,1)S(1)}, bf16[32,2048]{1,0:T(8,128)(2,1)S(1)}, u32[]{:S(2)}, u32[]{:S(2)}) collective-permute-start(bf16[32,2048]{1,0:T(8,128)(2,1)S(1)} %shard_map.78.refs_3_), channel_id=1, source_target_pairs={{0,12},{4,8},{8,4},{12,0},{16,28},{20,24},{24,20},{28,16},{1,13},{... | collective-permute-start | bytes 393224 | tf_op jit(solution)/shard_map/ppermute | solution.py:316
  47.3 0.6 %collective-permute-start.16 = (bf16[32,2048]{1,0:T(8,128)(2,1)S(1)}, bf16[32,2048]{1,0:T(8,128)(2,1)S(1)}, u32[]{:S(2)}, u32[]{:S(2)}) collective-permute-start(bf16[32,2048]{1,0:T(8,128)(2,1)S(1)} %shard_map.78.refs_3_), channel_id=1, source_target_pairs={{0,4},{4,0},{8,12},{12,8},{16,20},{20,16},{24,28},{28,24},{1,5},{5... | collective-permute-start | bytes 393224 | tf_op jit(solution)/shard_map/ppermute | solution.py:316
  48.0 0.4 collective-permute-done.20.refs_2_
  48.3 1.7 %collective-permute-done.21.refs_3_ = bf16[32,2048]{1,0:T(8,128)(2,1)S(1)} collective-permute-done((bf16[32,2048]{1,0:T(8,128)(2,1)S(1)}, bf16[32,2048]{1,0:T(8,128)(2,1)S(1)}, u32[]{:S(2)}, u32[]{:S(2)}) %collective-permute-start.21) | collective-permute-done | bytes 131104 | tf_op jit(solution)/shard_map/ppermute | solution.py:316
  50.1 0.8 %shard_map.81 = (f32[64,1024]{1,0:T(8,128)S(1)}, bf16[64,1024]{1,0:T(8,128)(2,1)S(1)}) custom-call(bf16[32,2048]{1,0:T(8,128)(2,1)S(1)} %shard_map.80.refs_0_, bf16[32,2048]{1,0:T(8,128)(2,1)S(1)} %collective-permute-done.19.refs_1_, bf16[32,2048]{1,0:T(8,128)(2,1)S(1)} %collective-permute-done.20.refs_2_, ...), custom_call_target="tpu_custom_call" | custom-call | tf_op jit(solution)/shard_map/pallas_call | solution.py:304
  50.9 0.1 collective-permute-start.22
  50.9 0.6 collective-permute-done.14.refs_0_
  51.5 1.5 %collective-permute-done.15.refs_1_ = bf16[32,2048]{1,0:T(8,128)(2,1)S(1)} collective-permute-done((bf16[32,2048]{1,0:T(8,128)(2,1)S(1)}, bf16[32,2048]{1,0:T(8,128)(2,1)S(1)}, u32[]{:S(2)}, u32[]{:S(2)}) %collective-permute-start.15) | collective-permute-done | bytes 131104 | tf_op jit(solution)/shard_map/ppermute | solution.py:316
  53.1 0.8 %shard_map.79 = (f32[64,1024]{1,0:T(8,128)S(1)}, bf16[64,1024]{1,0:T(8,128)(2,1)S(1)}) custom-call(bf16[32,2048]{1,0:T(8,128)(2,1)S(1)} %collective-permute-done.14.refs_0_, bf16[32,2048]{1,0:T(8,128)(2,1)S(1)} %collective-permute-done.15.refs_1_, bf16[32,2048]{1,0:T(8,128)(2,1)S(1)} %collective-permute-done.16.refs_2_, ...), custom_call_target="tpu_custom_call" | custom-call | tf_op jit(solution)/shard_map/pallas_call | solution.py:304
  53.9 0.1 collective-permute-start.17
  54.0 1.3 %collective-permute-done.17 = bf16[64,1024]{1,0:T(8,128)(2,1)S(1)} collective-permute-done((bf16[64,1024]{1,0:T(8,128)(2,1)S(1)}, bf16[64,1024]{1,0:T(8,128)(2,1)S(1)}, u32[]{:S(2)}, u32[]{:S(2)}) %collective-permute-start.17) | collective-permute-done | bytes 131104 | tf_op jit(solution)/shard_map/ppermute | solution.py:316
  55.3 0.1 select_convert_fusion
  55.3 2.1 %collective-permute-start.23 = (bf16[64,1024]{1,0:T(8,128)(2,1)S(1)}, bf16[64,1024]{1,0:T(8,128)(2,1)S(1)}, u32[]{:S(2)}, u32[]{:S(2)}) collective-permute-start(bf16[64,1024]{1,0:T(8,128)(2,1)S(1)} %select_convert_fusion), channel_id=1, source_target_pairs={{0,2},{1,3},{2,0},{3,1},{4,6},{5,7},{6,4},{7,5},{8,10},{9,11},{10,... | collective-permute-start | bytes 393224 | tf_op jit(solution)/shard_map/ppermute | solution.py:316
  57.4 3.8 %collective-permute-done.23 = bf16[64,1024]{1,0:T(8,128)(2,1)S(1)} collective-permute-done((bf16[64,1024]{1,0:T(8,128)(2,1)S(1)}, bf16[64,1024]{1,0:T(8,128)(2,1)S(1)}, u32[]{:S(2)}, u32[]{:S(2)}) %collective-permute-start.23) | collective-permute-done | bytes 131104 | tf_op jit(solution)/shard_map/ppermute | solution.py:316
  61.2 0.7 %add_convert_fusion = bf16[64,1024]{1,0:T(8,128)(2,1)} fusion(bf16[64,1024]{1,0:T(8,128)(2,1)S(1)} %collective-permute-done.23, f32[64,1024]{1,0:T(8,128)S(1)} %get-tuple-element.31, bf16[64,1024]{1,0:T(8,128)(2,1)S(1)} %collective-permute-done.17, f32[64,1024]{1,0:T(8,128)S(1)} %get-tuple-element.33, bf16[64,1024]{1,0:T(8,128)(2,1)S(1)} %collective-permute-done.22, ...), kind=kLoop, calls=%fused_computation | loop fusion | flops 524288 | bytes 1048577 | tf_op jit(solution)/shard_map/convert_element_type | solution.py:343
  (15 shorter events, 0.0 us)
Async XLA Ops:
  0.0 16.3 %copy-start.1 = (bf16[32,2048]{1,0:T(8,128)(2,1)S(1)}, bf16[32,2048]{1,0:T(8,128)(2,1)}, u32[]{:S(2)}) copy-start(bf16[32,2048]{1,0:T(8,128)(2,1)} %refs_0_.1) | copy-start | bytes 393220
  0.0 10.7 %collective-permute-start.6 = (bf16[32,2048]{1,0:T(8,128)(2,1)}, bf16[32,2048]{1,0:T(8,128)(2,1)S(1)}, u32[]{:S(2)}, u32[]{:S(2)}) collective-permute-start(bf16[32,2048]{1,0:T(8,128)(2,1)} %refs_0_.1), channel_id=1, source_target_pairs={{0,24},{4,28},{8,16},{12,20},{16,8},{20,12},{24,0},{28,4},{1,25},{... | collective-permute-start | bytes 393224 | tf_op jit(solution)/shard_map/ppermute | solution.py:316
  5.1 8.1 %collective-permute-start = (bf16[32,2048]{1,0:T(8,128)(2,1)}, bf16[32,2048]{1,0:T(8,128)(2,1)S(1)}, u32[]{:S(2)}, u32[]{:S(2)}) collective-permute-start(bf16[32,2048]{1,0:T(8,128)(2,1)} %refs_0_.1), channel_id=1, source_target_pairs={{0,4},{4,0},{8,12},{12,8},{16,20},{20,16},{24,28},{28,24},{1,5},{5... | collective-permute-start | bytes 393224 | tf_op jit(solution)/shard_map/ppermute | solution.py:316
  6.5 8.1 %collective-permute-start.1 = (bf16[32,2048]{1,0:T(8,128)(2,1)}, bf16[32,2048]{1,0:T(8,128)(2,1)S(1)}, u32[]{:S(2)}, u32[]{:S(2)}) collective-permute-start(bf16[32,2048]{1,0:T(8,128)(2,1)} %refs_0_.1), channel_id=1, source_target_pairs={{0,8},{4,12},{8,0},{12,4},{16,24},{20,28},{24,16},{28,20},{1,9},{5... | collective-permute-start | bytes 393224 | tf_op jit(solution)/shard_map/ppermute | solution.py:316
  6.5 9.7 %collective-permute-start.2 = (bf16[32,2048]{1,0:T(8,128)(2,1)}, bf16[32,2048]{1,0:T(8,128)(2,1)S(1)}, u32[]{:S(2)}, u32[]{:S(2)}) collective-permute-start(bf16[32,2048]{1,0:T(8,128)(2,1)} %refs_0_.1), channel_id=1, source_target_pairs={{0,12},{4,8},{8,4},{12,0},{16,28},{20,24},{24,20},{28,16},{1,13},{... | collective-permute-start | bytes 393224 | tf_op jit(solution)/shard_map/ppermute | solution.py:316
  10.8 10.6 %collective-permute-start.7 = (bf16[32,2048]{1,0:T(8,128)(2,1)S(1)}, bf16[32,2048]{1,0:T(8,128)(2,1)S(1)}, u32[]{:S(2)}, u32[]{:S(2)}) collective-permute-start(bf16[32,2048]{1,0:T(8,128)(2,1)S(1)} %collective-permute-done.6.refs_0_), channel_id=1, source_target_pairs={{0,4},{4,0},{8,12},{12,8},{16,20},{20,16},{24,28},{28,24},{1,5},{5... | collective-permute-start | bytes 393224 | tf_op jit(solution)/shard_map/ppermute | solution.py:316
  13.1 9.6 %collective-permute-start.8 = (bf16[32,2048]{1,0:T(8,128)(2,1)S(1)}, bf16[32,2048]{1,0:T(8,128)(2,1)S(1)}, u32[]{:S(2)}, u32[]{:S(2)}) collective-permute-start(bf16[32,2048]{1,0:T(8,128)(2,1)S(1)} %collective-permute-done.6.refs_0_), channel_id=1, source_target_pairs={{0,8},{4,12},{8,0},{12,4},{16,24},{20,28},{24,16},{28,20},{1,9},{5... | collective-permute-start | bytes 393224 | tf_op jit(solution)/shard_map/ppermute | solution.py:316
  13.1 9.6 %collective-permute-start.9 = (bf16[32,2048]{1,0:T(8,128)(2,1)S(1)}, bf16[32,2048]{1,0:T(8,128)(2,1)S(1)}, u32[]{:S(2)}, u32[]{:S(2)}) collective-permute-start(bf16[32,2048]{1,0:T(8,128)(2,1)S(1)} %collective-permute-done.6.refs_0_), channel_id=1, source_target_pairs={{0,12},{4,8},{8,4},{12,0},{16,28},{20,24},{24,20},{28,16},{1,13},{... | collective-permute-start | bytes 393224 | tf_op jit(solution)/shard_map/ppermute | solution.py:316
  16.9 10.9 %collective-permute-start.3 = (bf16[32,2176]{1,0:T(8,128)(2,1)S(1)}, bf16[32,2176]{1,0:T(8,128)(2,1)S(1)}, u32[]{:S(2)}, u32[]{:S(2)}) collective-permute-start(bf16[32,2176]{1,0:T(8,128)(2,1)S(1)} %get-tuple-element.23), channel_id=1, source_target_pairs={{0,12},{4,8},{8,4},{12,0},{16,28},{20,24},{24,20},{28,16},{1,13},{... | collective-permute-start | bytes 417800 | tf_op jit(solution)/shard_map/ppermute | solution.py:316
  18.9 10.3 %collective-permute-start.4 = (bf16[32,2176]{1,0:T(8,128)(2,1)S(1)}, bf16[32,2176]{1,0:T(8,128)(2,1)S(1)}, u32[]{:S(2)}, u32[]{:S(2)}) collective-permute-start(bf16[32,2176]{1,0:T(8,128)(2,1)S(1)} %get-tuple-element.24), channel_id=1, source_target_pairs={{0,8},{4,12},{8,0},{12,4},{16,24},{20,28},{24,16},{28,20},{1,9},{5... | collective-permute-start | bytes 417800 | tf_op jit(solution)/shard_map/ppermute | solution.py:316
  21.3 28.7 %copy-start = (bf16[2048,1024]{1,0:T(8,128)(2,1)S(1)}, bf16[2048,1024]{1,0:T(8,128)(2,1)}, u32[]{:S(2)}) copy-start(bf16[2048,1024]{1,0:T(8,128)(2,1)} %refs_4_.3) | copy-start | bytes 12582916
  21.3 8.4 %collective-permute-start.5 = (bf16[32,2176]{1,0:T(8,128)(2,1)S(1)}, bf16[32,2176]{1,0:T(8,128)(2,1)S(1)}, u32[]{:S(2)}, u32[]{:S(2)}) collective-permute-start(bf16[32,2176]{1,0:T(8,128)(2,1)S(1)} %get-tuple-element.25), channel_id=1, source_target_pairs={{0,4},{4,0},{8,12},{12,8},{16,20},{20,16},{24,28},{28,24},{1,5},{5... | collective-permute-start | bytes 417800 | tf_op jit(solution)/shard_map/ppermute | solution.py:316
  23.4 9.8 %collective-permute-start.10 = (bf16[32,2176]{1,0:T(8,128)(2,1)S(1)}, bf16[32,2176]{1,0:T(8,128)(2,1)S(1)}, u32[]{:S(2)}, u32[]{:S(2)}) collective-permute-start(bf16[32,2176]{1,0:T(8,128)(2,1)S(1)} %get-tuple-element.27), channel_id=1, source_target_pairs={{0,12},{4,8},{8,4},{12,0},{16,28},{20,24},{24,20},{28,16},{1,13},{... | collective-permute-start | bytes 417800 | tf_op jit(solution)/shard_map/ppermute | solution.py:316
  24.9 8.3 %collective-permute-start.11 = (bf16[32,2176]{1,0:T(8,128)(2,1)S(1)}, bf16[32,2176]{1,0:T(8,128)(2,1)S(1)}, u32[]{:S(2)}, u32[]{:S(2)}) collective-permute-start(bf16[32,2176]{1,0:T(8,128)(2,1)S(1)} %get-tuple-element.28), channel_id=1, source_target_pairs={{0,8},{4,12},{8,0},{12,4},{16,24},{20,28},{24,16},{28,20},{1,9},{5... | collective-permute-start | bytes 417800 | tf_op jit(solution)/shard_map/ppermute | solution.py:316
  27.8 5.3 %collective-permute-start.12 = (bf16[32,2176]{1,0:T(8,128)(2,1)S(1)}, bf16[32,2176]{1,0:T(8,128)(2,1)S(1)}, u32[]{:S(2)}, u32[]{:S(2)}) collective-permute-start(bf16[32,2176]{1,0:T(8,128)(2,1)S(1)} %get-tuple-element.29), channel_id=1, source_target_pairs={{0,4},{4,0},{8,12},{12,8},{16,20},{20,16},{24,28},{28,24},{1,5},{5... | collective-permute-start | bytes 417800 | tf_op jit(solution)/shard_map/ppermute | solution.py:316
  30.2 7.8 %collective-permute-start.18 = (bf16[32,2176]{1,0:T(8,128)(2,1)S(1)}, bf16[32,2176]{1,0:T(8,128)(2,1)S(1)}, u32[]{:S(2)}, u32[]{:S(2)}) collective-permute-start(bf16[32,2176]{1,0:T(8,128)(2,1)S(1)} %shard_map.75.near), channel_id=1, source_target_pairs={{0,24},{4,28},{8,16},{12,20},{16,8},{20,12},{24,0},{28,4},{1,25},{... | collective-permute-start | bytes 417800 | tf_op jit(solution)/shard_map/ppermute | solution.py:316
  33.7 10.3 %collective-permute-start.13 = (bf16[32,2176]{1,0:T(8,128)(2,1)S(1)}, bf16[32,2176]{1,0:T(8,128)(2,1)S(1)}, u32[]{:S(2)}, u32[]{:S(2)}) collective-permute-start(bf16[32,2176]{1,0:T(8,128)(2,1)S(1)} %shard_map.77.near), channel_id=1, source_target_pairs={{0,24},{4,28},{8,16},{12,20},{16,8},{20,12},{24,0},{28,4},{1,25},{... | collective-permute-start | bytes 417800 | tf_op jit(solution)/shard_map/ppermute | solution.py:316
  38.3 9.0 %collective-permute-start.19 = (bf16[32,2048]{1,0:T(8,128)(2,1)S(1)}, bf16[32,2048]{1,0:T(8,128)(2,1)S(1)}, u32[]{:S(2)}, u32[]{:S(2)}) collective-permute-start(bf16[32,2048]{1,0:T(8,128)(2,1)S(1)} %shard_map.80.refs_0_), channel_id=1, source_target_pairs={{0,4},{4,0},{8,12},{12,8},{16,20},{20,16},{24,28},{28,24},{1,5},{5... | collective-permute-start | bytes 393224 | tf_op jit(solution)/shard_map/ppermute | solution.py:316
  39.1 9.3 %collective-permute-start.20 = (bf16[32,2048]{1,0:T(8,128)(2,1)S(1)}, bf16[32,2048]{1,0:T(8,128)(2,1)S(1)}, u32[]{:S(2)}, u32[]{:S(2)}) collective-permute-start(bf16[32,2048]{1,0:T(8,128)(2,1)S(1)} %shard_map.80.refs_0_), channel_id=1, source_target_pairs={{0,8},{4,12},{8,0},{12,4},{16,24},{20,28},{24,16},{28,20},{1,9},{5... | collective-permute-start | bytes 393224 | tf_op jit(solution)/shard_map/ppermute | solution.py:316
  44.0 6.1 %collective-permute-start.21 = (bf16[32,2048]{1,0:T(8,128)(2,1)S(1)}, bf16[32,2048]{1,0:T(8,128)(2,1)S(1)}, u32[]{:S(2)}, u32[]{:S(2)}) collective-permute-start(bf16[32,2048]{1,0:T(8,128)(2,1)S(1)} %shard_map.80.refs_0_), channel_id=1, source_target_pairs={{0,12},{4,8},{8,4},{12,0},{16,28},{20,24},{24,20},{28,16},{1,13},{... | collective-permute-start | bytes 393224 | tf_op jit(solution)/shard_map/ppermute | solution.py:316
  44.3 7.2 %collective-permute-start.14 = (bf16[32,2048]{1,0:T(8,128)(2,1)S(1)}, bf16[32,2048]{1,0:T(8,128)(2,1)S(1)}, u32[]{:S(2)}, u32[]{:S(2)}) collective-permute-start(bf16[32,2048]{1,0:T(8,128)(2,1)S(1)} %shard_map.78.refs_3_), channel_id=1, source_target_pairs={{0,12},{4,8},{8,4},{12,0},{16,28},{20,24},{24,20},{28,16},{1,13},{... | collective-permute-start | bytes 393224 | tf_op jit(solution)/shard_map/ppermute | solution.py:316
  47.3 5.8 %collective-permute-start.15 = (bf16[32,2048]{1,0:T(8,128)(2,1)S(1)}, bf16[32,2048]{1,0:T(8,128)(2,1)S(1)}, u32[]{:S(2)}, u32[]{:S(2)}) collective-permute-start(bf16[32,2048]{1,0:T(8,128)(2,1)S(1)} %shard_map.78.refs_3_), channel_id=1, source_target_pairs={{0,8},{4,12},{8,0},{12,4},{16,24},{20,28},{24,16},{28,20},{1,9},{5... | collective-permute-start | bytes 393224 | tf_op jit(solution)/shard_map/ppermute | solution.py:316
  47.3 5.7 %collective-permute-start.16 = (bf16[32,2048]{1,0:T(8,128)(2,1)S(1)}, bf16[32,2048]{1,0:T(8,128)(2,1)S(1)}, u32[]{:S(2)}, u32[]{:S(2)}) collective-permute-start(bf16[32,2048]{1,0:T(8,128)(2,1)S(1)} %shard_map.78.refs_3_), channel_id=1, source_target_pairs={{0,4},{4,0},{8,12},{12,8},{16,20},{20,16},{24,28},{28,24},{1,5},{5... | collective-permute-start | bytes 393224 | tf_op jit(solution)/shard_map/ppermute | solution.py:316
  50.9 3.1 %collective-permute-start.22 = (bf16[64,1024]{1,0:T(8,128)(2,1)S(1)}, bf16[64,1024]{1,0:T(8,128)(2,1)S(1)}, u32[]{:S(2)}, u32[]{:S(2)}) collective-permute-start(bf16[64,1024]{1,0:T(8,128)(2,1)S(1)} %get-tuple-element.34), channel_id=1, source_target_pairs={{0,1},{1,0},{2,3},{3,2},{4,5},{5,4},{6,7},{7,6},{8,9},{9,8},{10,11... | collective-permute-start | bytes 393224 | tf_op jit(solution)/shard_map/ppermute | solution.py:316
  53.9 1.4 %collective-permute-start.17 = (bf16[64,1024]{1,0:T(8,128)(2,1)S(1)}, bf16[64,1024]{1,0:T(8,128)(2,1)S(1)}, u32[]{:S(2)}, u32[]{:S(2)}) collective-permute-start(bf16[64,1024]{1,0:T(8,128)(2,1)S(1)} %get-tuple-element.32), channel_id=1, source_target_pairs={{0,1},{1,0},{2,3},{3,2},{4,5},{5,4},{6,7},{7,6},{8,9},{9,8},{10,11... | collective-permute-start | bytes 393224 | tf_op jit(solution)/shard_map/ppermute | solution.py:316
  55.3 5.9 %collective-permute-start.23 = (bf16[64,1024]{1,0:T(8,128)(2,1)S(1)}, bf16[64,1024]{1,0:T(8,128)(2,1)S(1)}, u32[]{:S(2)}, u32[]{:S(2)}) collective-permute-start(bf16[64,1024]{1,0:T(8,128)(2,1)S(1)} %select_convert_fusion), channel_id=1, source_target_pairs={{0,2},{1,3},{2,0},{3,1},{4,6},{5,7},{6,4},{7,5},{8,10},{9,11},{10,... | collective-permute-start | bytes 393224 | tf_op jit(solution)/shard_map/ppermute | solution.py:316

commit v8 on v4

--- a/solution.py
+++ b/solution.py
@@ -33,7 +33,7 @@
 
 class Plan:
     def __init__(self, n, ways, rows, blocks, page):
-        self.n, self.rows, self.blocks, self.page = n, rows, blocks, page
+        self.n, self.ways, self.rows, self.blocks, self.page = n, ways, rows, blocks, page
         self.group = n // blocks
         self.halves = blocks == 2 and n == 8 and ways == 4 and rows * self.group == page
         self.cross = n * 3 // 4
@@ -284,31 +284,42 @@
 
 
 def project_kernel(plan, lb, *refs):
-    sources, weight, (keep, send, rows_ref) = refs[: plan.group], refs[plan.group], refs[plan.group + 1 :]
+    sources, (weight, keep, send, rows_ref) = refs[:-4], refs[-4:]
     me, column = lax.axis_index("pages"), lax.axis_index("mp")
     rows = plan.rows
     holders = plan.group // 2
-    for k in range(plan.group):
+    for k, source in enumerate(sources):
         device = me ^ k ^ (lb * plan.cross)
         place = ((device // holders % 2) ^ (column % 2)) * holders + device % holders
-        rows_ref[pl.ds(pl.multiple_of(place * rows, rows), rows), :] = sources[k][...]
+        rows_ref[pl.ds(pl.multiple_of(place * rows, rows), rows), :] = source[...]
     product = jnp.dot(rows_ref[...], weight[...], preferred_element_type=F32)
     part = holders * rows
     keep[...] = product[:part]
     send[...] = product[part:].astype(BF16)
 
 
-def project(plan, lb, sources, weight):
+def project_pair_kernel(plan, *refs):
+    sources, (weight, keep, send, rows_ref) = refs[:-4], refs[-4:]
+    me = lax.axis_index("pages")
+    rows = plan.rows
+    for k, source in enumerate(sources):
+        rows_ref[pl.ds(pl.multiple_of((me ^ k) % 2 * rows, rows), rows), :] = source[...]
+    product = jnp.dot(rows_ref[...], weight[...], preferred_element_type=F32)
+    keep[...] = product
+    send[...] = product.astype(BF16)
+
+
+def project(plan, kernel, sources, weight):
     columns = weight.shape[1]
     part = plan.page // 2
     return pl.pallas_call(
-        functools.partial(project_kernel, plan, lb),
+        kernel,
         out_shape=(jax.ShapeDtypeStruct((part, columns), F32), jax.ShapeDtypeStruct((part, columns), BF16)),
-        in_specs=[in_vmem()] * (plan.group + 1),
+        in_specs=[in_vmem()] * (len(sources) + 1),
         out_specs=(in_vmem(), in_vmem()),
-        scratch_shapes=[VMEM((plan.page, weight.shape[0]), BF16)],
+        scratch_shapes=[VMEM((len(sources) * plan.rows, weight.shape[0]), BF16)],
         compiler_params=params(24),
-    )(*(sources[k] for k in range(plan.group)), weight)
+    )(*sources, weight)
 
 
 def swap(x, axis, distance):
@@ -318,6 +329,16 @@
 
 def others(plan):
     return range(1, plan.group)
+
+
+def swap_y(plan, x, late):
+    pairs = [
+        (p * plan.ways + m, p * plan.ways + (m ^ 2))
+        for p in range(plan.n)
+        for m in range(plan.ways)
+        if (p // 2 + m) % 2 == late
+    ]
+    return lax.ppermute(x, ("pages", "mp"), pairs)
 
 
 def spread(x, plan):
@@ -332,15 +353,25 @@
         outs = attend(plan, heads, lb, pages, [chunks[k] for k in range(plan.group)])
         near.append(merge(heads, outs[0], *(swap(outs[k], "pages", k) for k in others(plan))))
     across = [swap(x, "pages", plan.cross) for x in near]
-    sums = [None, None]
-    for lb in (1, 0):
-        rows = finish(heads, near[lb], across[1 - lb])
-        keep, send = project(plan, lb, spread(rows, plan), weight)
-        sums[lb] = keep + swap(send, "mp", 1).astype(F32)
-    stays = plan.block(lax.axis_index("pages"), 0) == lax.axis_index("mp") // 2
-    mine = jnp.where(stays, sums[0], sums[1])
-    away = jnp.where(stays, sums[1], sums[0]).astype(BF16)
-    return (mine + swap(away, "mp", 2).astype(F32)).astype(BF16)
+    far_rows = spread(finish(heads, near[1], across[0]), plan)
+    rows = spread(finish(heads, near[0], across[1]), plan)
+    keep, send = project(plan, functools.partial(project_kernel, plan, 1), [far_rows[k] for k in range(plan.group)], weight)
+    far_sum = keep + swap(send, "mp", 1).astype(F32)
+    me, column = lax.axis_index("pages"), lax.axis_index("mp")
+    stays = plan.block(me, 0) == column // 2
+    halves, arrived, aways = [], [], []
+    for late in range(2):
+        pair = [rows[2 * late], rows[2 * late + 1]]
+        keep, send = project(plan, functools.partial(project_pair_kernel, plan), pair, weight)
+        if late:
+            send, aways[0] = lax.optimization_barrier((send, aways[0]))
+        halves.append(keep + swap(send, "mp", 1).astype(F32))
+        away = jnp.where(stays, far_sum, halves[late]).astype(BF16)
+        aways.append(away)
+    arrived = [swap_y(plan, away, late) for late, away in enumerate(aways)]
+    here = (me // 2 + column) % 2 == 0
+    mine = jnp.where(stays, jnp.where(here, halves[0], halves[1]), far_sum)
+    return (mine + arrived[0].astype(F32) + arrived[1].astype(F32)).astype(BF16)
 
 
 def by_gathers(plan, heads, queries, weight, pages):

time: 61.3 us -> 64.4 us (1.051)
  Pallas kernels: 6.43 us -> 13.7 us
  starting transfers between devices: 37.4 us -> 32.8 us
  local copies, waits for them, and re-layouts: 0.01 us -> 2.2 us
  waiting for transfers between devices: 16.1 us -> 14 us
    ppermute x24, starting transfers between devices: 37.4 us -> 28.7 us  [swap(): return lax.ppermute(x, axis, [(i, i ^ distance) for i in range(n)])]
    ppermute x24, waiting for transfers between devices: 16.1 us -> 10.5 us  [swap(): return lax.ppermute(x, axis, [(i, i ^ distance) for i in range(n)])]
    pallas_call x2, Pallas kernels: 1.29 us -> 5.88 us  [attend(): pl.pallas_call(functools.partial(attend_kernel, plan, heads, lb), out_sha...]
    ppermute x0 -> x2, starting transfers between devices: none -> 4.09 us  [swap_y(): return lax.ppermute(x, ('pages', 'mp'), pairs)]
    ppermute x0 -> x2, waiting for transfers between devices: none -> 3.54 us  [swap_y(): return lax.ppermute(x, ('pages', 'mp'), pairs)]
    unnamed x4 -> x6, local copies, waits for them, and re-layouts: 0.01 us -> 2.2 us
    pallas_call x1, Pallas kernels: 1.97 us -> 3.7 us  [fetch(): pl.pallas_call(functools.partial(fetch_kernel, plan, pages_dev), out_shap...]
    pallas_call x2 -> x3, Pallas kernels: 1.57 us -> 2.48 us  [project(): pl.pallas_call(kernel, out_shape=(jax.ShapeDtypeStruct((part, columns), F...]
  transfers between devices with their start and end apart: 24 -> 26, of which waited for: 12 -> 10; matrix products, arithmetic and copies ran while one was open for 0% -> 0% of each run, Pallas kernels for 11% -> 21%
where the time goes in v8:
time: 64.4 us; the launch traced here: 63.8 us
  starting transfers between devices  32.8 us (51%)
  waiting for transfers between devices  14 us (22%)
  Pallas kernels  13.7 us (21%)
  local copies, waits for them, and re-layouts  2.2 us (3%)
  other arithmetic  0.91 us (1%)
    ppermute x24, starting transfers between devices, swap(): return lax.ppermute(x, axis, [(i, i ^ distance) for i in range(n)])  28.7 us
    ppermute x24, waiting for transfers between devices, swap(): return lax.ppermute(x, axis, [(i, i ^ distance) for i in range(n)])  10.5 us
    pallas_call x2, Pallas kernels, attend(): pl.pallas_call(functools.partial(attend_kernel, plan, heads, lb), out_sha...  5.88 us
    ppermute x2, starting transfers between devices, swap_y(): return lax.ppermute(x, ('pages', 'mp'), pairs)  4.09 us
    pallas_call x1, Pallas kernels, fetch(): pl.pallas_call(functools.partial(fetch_kernel, plan, pages_dev), out_shap...  3.7 us
    ppermute x2, waiting for transfers between devices, swap_y(): return lax.ppermute(x, ('pages', 'mp'), pairs)  3.54 us
    pallas_call x3, Pallas kernels, project(): pl.pallas_call(kernel, out_shape=(jax.ShapeDtypeStruct((part, columns), F...  2.48 us
    unnamed x6, local copies, waits for them, and re-layouts  2.2 us
  transfers between devices with their start and end apart: 26, of which 10 were waited for; matrix products, arithmetic and copies ran while one was open for 0% of the time, Pallas kernels for 21%

profile of v8, /device:TPU:0, one launch (start us, length us, event | category | flops | bytes accessed | tf_op | source)
XLA Modules:
  0.0 63.8 jit_solution(1532373546990378689)
XLA Ops:
  0.0 5.0 %collective-permute-start.6 = (bf16[32,2048]{1,0:T(8,128)(2,1)}, bf16[32,2048]{1,0:T(8,128)(2,1)S(1)}, u32[]{:S(2)}, u32[]{:S(2)}) collective-permute-start(bf16[32,2048]{1,0:T(8,128)(2,1)} %refs_0_.1), channel_id=1, source_target_pairs={{0,24},{4,28},{8,16},{12,20},{16,8},{20,12},{24,0},{28,4},{1,25},{... | collective-permute-start | bytes 393224 | tf_op jit(solution)/shard_map/ppermute | solution.py:327
  5.1 1.5 %collective-permute-start = (bf16[32,2048]{1,0:T(8,128)(2,1)}, bf16[32,2048]{1,0:T(8,128)(2,1)S(1)}, u32[]{:S(2)}, u32[]{:S(2)}) collective-permute-start(bf16[32,2048]{1,0:T(8,128)(2,1)} %refs_0_.1), channel_id=1, source_target_pairs={{0,4},{4,0},{8,12},{12,8},{16,20},{20,16},{24,28},{28,24},{1,5},{5... | collective-permute-start | bytes 393224 | tf_op jit(solution)/shard_map/ppermute | solution.py:327
  6.5 2.0 %collective-permute-start.2 = (bf16[32,2048]{1,0:T(8,128)(2,1)}, bf16[32,2048]{1,0:T(8,128)(2,1)S(1)}, u32[]{:S(2)}, u32[]{:S(2)}) collective-permute-start(bf16[32,2048]{1,0:T(8,128)(2,1)} %refs_0_.1), channel_id=1, source_target_pairs={{0,12},{4,8},{8,4},{12,0},{16,28},{20,24},{24,20},{28,16},{1,13},{... | collective-permute-start | bytes 393224 | tf_op jit(solution)/shard_map/ppermute | solution.py:327
  8.5 3.7 %shard_map.73 = (bf16[2,2,768,128]{3,2,1,0:T(8,128)(2,1)S(1)}, bf16[2,2,768,256]{3,2,1,0:T(8,128)(2,1)S(1)}, s32[2,3]{1,0:T(2,128)S(1)}) custom-call(s32[2,24]{1,0:T(2,128)} %select_hbm.1, s32[128]{0:T(128)} %table_hbm.1, s32[2]{0:T(128)} %stands_hbm.1, bf16[16,256,128]{2,1,0:T(8,128)(2,1)} %bitcast.2, bf16[16,256,128]{2,1,0:T(8,128)(2,1)} %bitcast.3), custom_call_target="tpu_custom_call" | custom-call | flops 2000000000 | bytes 8388608 | tf_op jit(solution)/shard_map/pallas_call | solution.py:122
  12.3 0.0 collective-permute-done.6.refs_0_
  12.3 1.6 %collective-permute-start.7 = (bf16[32,2048]{1,0:T(8,128)(2,1)S(1)}, bf16[32,2048]{1,0:T(8,128)(2,1)S(1)}, u32[]{:S(2)}, u32[]{:S(2)}) collective-permute-start(bf16[32,2048]{1,0:T(8,128)(2,1)S(1)} %collective-permute-done.6.refs_0_), channel_id=1, source_target_pairs={{0,4},{4,0},{8,12},{12,8},{16,20},{20,16},{24,28},{28,24},{1,5},{5... | collective-permute-start | bytes 393224 | tf_op jit(solution)/shard_map/ppermute | solution.py:327
  13.8 2.0 %collective-permute-start.9 = (bf16[32,2048]{1,0:T(8,128)(2,1)S(1)}, bf16[32,2048]{1,0:T(8,128)(2,1)S(1)}, u32[]{:S(2)}, u32[]{:S(2)}) collective-permute-start(bf16[32,2048]{1,0:T(8,128)(2,1)S(1)} %collective-permute-done.6.refs_0_), channel_id=1, source_target_pairs={{0,12},{4,8},{8,4},{12,0},{16,28},{20,24},{24,20},{28,16},{1,13},{... | collective-permute-start | bytes 393224 | tf_op jit(solution)/shard_map/ppermute | solution.py:327
  15.8 0.0 collective-permute-done.1.refs_2_
  15.8 0.2 collective-permute-done.2.refs_3_
  16.1 2.9 %shard_map.74 = (bf16[32,2176]{1,0:T(8,128)(2,1)S(1)}, bf16[32,2176]{1,0:T(8,128)(2,1)S(1)}, bf16[32,2176]{1,0:T(8,128)(2,1)S(1)}, bf16[32,2176]{1,0:T(8,128)(2,1)S(1)}) custom-call(s32[2,3]{1,0:T(2,128)S(1)} %get-tuple-element.24.info, bf16[32,2048]{1,0:T(8,128)(2,1)S(1)} %copy-done.2, bf16[32,2048]{1,0:T(8,128)(2,1)S(1)} %collective-permute-done.refs_1_, ...), custom_call_target="tpu_custom_call" | custom-call | flops 2000000000 | bytes 4194304 | tf_op jit(solution)/shard_map/pallas_call | solution.py:220
  19.0 1.3 %collective-permute-start.3 = (bf16[32,2176]{1,0:T(8,128)(2,1)S(1)}, bf16[32,2176]{1,0:T(8,128)(2,1)S(1)}, u32[]{:S(2)}, u32[]{:S(2)}) collective-permute-start(bf16[32,2176]{1,0:T(8,128)(2,1)S(1)} %get-tuple-element.28), channel_id=1, source_target_pairs={{0,4},{4,0},{8,12},{12,8},{16,20},{20,16},{24,28},{28,24},{1,5},{5... | collective-permute-start | bytes 417800 | tf_op jit(solution)/shard_map/ppermute | solution.py:327
  20.4 2.2 %collective-permute-start.5 = (bf16[32,2176]{1,0:T(8,128)(2,1)S(1)}, bf16[32,2176]{1,0:T(8,128)(2,1)S(1)}, u32[]{:S(2)}, u32[]{:S(2)}) collective-permute-start(bf16[32,2176]{1,0:T(8,128)(2,1)S(1)} %get-tuple-element.30), channel_id=1, source_target_pairs={{0,12},{4,8},{8,4},{12,0},{16,28},{20,24},{24,20},{28,16},{1,13},{... | collective-permute-start | bytes 417800 | tf_op jit(solution)/shard_map/ppermute | solution.py:327
  22.6 0.0 collective-permute-done.9.refs_3_
  22.6 2.9 %shard_map.76 = (bf16[32,2176]{1,0:T(8,128)(2,1)S(1)}, bf16[32,2176]{1,0:T(8,128)(2,1)S(1)}, bf16[32,2176]{1,0:T(8,128)(2,1)S(1)}, bf16[32,2176]{1,0:T(8,128)(2,1)S(1)}) custom-call(s32[2,3]{1,0:T(2,128)S(1)} %get-tuple-element.24.info, bf16[32,2048]{1,0:T(8,128)(2,1)S(1)} %collective-permute-done.6.refs_0_, ...), custom_call_target="tpu_custom_call" | custom-call | flops 2000000000 | bytes 4194304 | tf_op jit(solution)/shard_map/pallas_call | solution.py:220
  25.5 1.3 %collective-permute-start.10 = (bf16[32,2176]{1,0:T(8,128)(2,1)S(1)}, bf16[32,2176]{1,0:T(8,128)(2,1)S(1)}, u32[]{:S(2)}, u32[]{:S(2)}) collective-permute-start(bf16[32,2176]{1,0:T(8,128)(2,1)S(1)} %get-tuple-element.32), channel_id=1, source_target_pairs={{0,4},{4,0},{8,12},{12,8},{16,20},{20,16},{24,28},{28,24},{1,5},{5... | collective-permute-start | bytes 417800 | tf_op jit(solution)/shard_map/ppermute | solution.py:327
  26.9 2.2 %collective-permute-start.12 = (bf16[32,2176]{1,0:T(8,128)(2,1)S(1)}, bf16[32,2176]{1,0:T(8,128)(2,1)S(1)}, u32[]{:S(2)}, u32[]{:S(2)}) collective-permute-start(bf16[32,2176]{1,0:T(8,128)(2,1)S(1)} %get-tuple-element.34), channel_id=1, source_target_pairs={{0,12},{4,8},{8,4},{12,0},{16,28},{20,24},{24,20},{28,16},{1,13},{... | collective-permute-start | bytes 417800 | tf_op jit(solution)/shard_map/ppermute | solution.py:327
  29.1 0.5 shard_map.75.near
  29.6 1.5 %collective-permute-start.18 = (bf16[32,2176]{1,0:T(8,128)(2,1)S(1)}, bf16[32,2176]{1,0:T(8,128)(2,1)S(1)}, u32[]{:S(2)}, u32[]{:S(2)}) collective-permute-start(bf16[32,2176]{1,0:T(8,128)(2,1)S(1)} %shard_map.75.near), channel_id=1, source_target_pairs={{0,24},{4,28},{8,16},{12,20},{16,8},{20,12},{24,0},{28,4},{1,25},{... | collective-permute-start | bytes 417800 | tf_op jit(solution)/shard_map/ppermute | solution.py:327
  31.1 1.1 %collective-permute-done.10.refs_1_ = bf16[32,2176]{1,0:T(8,128)(2,1)S(1)} collective-permute-done((bf16[32,2176]{1,0:T(8,128)(2,1)S(1)}, bf16[32,2176]{1,0:T(8,128)(2,1)S(1)}, u32[]{:S(2)}, u32[]{:S(2)}) %collective-permute-start.10) | collective-permute-done | bytes 139296 | tf_op jit(solution)/shard_map/ppermute | solution.py:327
  32.1 0.5 collective-permute-done.11.refs_2_
  32.7 2.5 %collective-permute-done.12.refs_3_ = bf16[32,2176]{1,0:T(8,128)(2,1)S(1)} collective-permute-done((bf16[32,2176]{1,0:T(8,128)(2,1)S(1)}, bf16[32,2176]{1,0:T(8,128)(2,1)S(1)}, u32[]{:S(2)}, u32[]{:S(2)}) %collective-permute-start.12) | collective-permute-done | bytes 139296 | tf_op jit(solution)/shard_map/ppermute | solution.py:327
  35.2 0.5 shard_map.77.near
  35.7 0.2 collective-permute-start.13
  35.9 1.7 %collective-permute-done.18.far = bf16[32,2176]{1,0:T(8,128)(2,1)S(1)} collective-permute-done((bf16[32,2176]{1,0:T(8,128)(2,1)S(1)}, bf16[32,2176]{1,0:T(8,128)(2,1)S(1)}, u32[]{:S(2)}, u32[]{:S(2)}) %collective-permute-start.18) | collective-permute-done | bytes 139296 | tf_op jit(solution)/shard_map/ppermute | solution.py:327
  37.6 0.3 shard_map.81.refs_0_
  37.9 1.0 %collective-permute-start.19 = (bf16[32,2048]{1,0:T(8,128)(2,1)S(1)}, bf16[32,2048]{1,0:T(8,128)(2,1)S(1)}, u32[]{:S(2)}, u32[]{:S(2)}) collective-permute-start(bf16[32,2048]{1,0:T(8,128)(2,1)S(1)} %shard_map.81.refs_0_), channel_id=1, source_target_pairs={{0,4},{4,0},{8,12},{12,8},{16,20},{20,16},{24,28},{28,24},{1,5},{5... | collective-permute-start | bytes 393224 | tf_op jit(solution)/shard_map/ppermute | solution.py:327
  38.9 1.6 %collective-permute-start.20 = (bf16[32,2048]{1,0:T(8,128)(2,1)S(1)}, bf16[32,2048]{1,0:T(8,128)(2,1)S(1)}, u32[]{:S(2)}, u32[]{:S(2)}) collective-permute-start(bf16[32,2048]{1,0:T(8,128)(2,1)S(1)} %shard_map.81.refs_0_), channel_id=1, source_target_pairs={{0,8},{4,12},{8,0},{12,4},{16,24},{20,28},{24,16},{28,20},{1,9},{5... | collective-permute-start | bytes 393224 | tf_op jit(solution)/shard_map/ppermute | solution.py:327
  40.5 1.0 %collective-permute-start.21 = (bf16[32,2048]{1,0:T(8,128)(2,1)S(1)}, bf16[32,2048]{1,0:T(8,128)(2,1)S(1)}, u32[]{:S(2)}, u32[]{:S(2)}) collective-permute-start(bf16[32,2048]{1,0:T(8,128)(2,1)S(1)} %shard_map.81.refs_0_), channel_id=1, source_target_pairs={{0,12},{4,8},{8,4},{12,0},{16,28},{20,24},{24,20},{28,16},{1,13},{... | collective-permute-start | bytes 393224 | tf_op jit(solution)/shard_map/ppermute | solution.py:327
  41.5 1.8 %collective-permute-done.13.far = bf16[32,2176]{1,0:T(8,128)(2,1)S(1)} collective-permute-done((bf16[32,2176]{1,0:T(8,128)(2,1)S(1)}, bf16[32,2176]{1,0:T(8,128)(2,1)S(1)}, u32[]{:S(2)}, u32[]{:S(2)}) %collective-permute-start.13) | collective-permute-done | bytes 139296 | tf_op jit(solution)/shard_map/ppermute | solution.py:327
  43.3 0.3 shard_map.78.refs_0_
  43.6 1.5 %collective-permute-start.14 = (bf16[32,2048]{1,0:T(8,128)(2,1)S(1)}, bf16[32,2048]{1,0:T(8,128)(2,1)S(1)}, u32[]{:S(2)}, u32[]{:S(2)}) collective-permute-start(bf16[32,2048]{1,0:T(8,128)(2,1)S(1)} %shard_map.78.refs_0_), channel_id=1, source_target_pairs={{0,4},{4,0},{8,12},{12,8},{16,20},{20,16},{24,28},{28,24},{1,5},{5... | collective-permute-start | bytes 393224 | tf_op jit(solution)/shard_map/ppermute | solution.py:327
  45.1 2.4 %collective-permute-start.17 = (bf16[32,2048]{1,0:T(8,128)(2,1)S(1)}, bf16[32,2048]{1,0:T(8,128)(2,1)S(1)}, u32[]{:S(2)}, u32[]{:S(2)}) collective-permute-start(bf16[32,2048]{1,0:T(8,128)(2,1)S(1)} %shard_map.78.refs_0_), channel_id=1, source_target_pairs={{0,12},{4,8},{8,4},{12,0},{16,28},{20,24},{24,20},{28,16},{1,13},{... | collective-permute-start | bytes 393224 | tf_op jit(solution)/shard_map/ppermute | solution.py:327
  47.6 1.7 %collective-permute-done.21.refs_3_ = bf16[32,2048]{1,0:T(8,128)(2,1)S(1)} collective-permute-done((bf16[32,2048]{1,0:T(8,128)(2,1)S(1)}, bf16[32,2048]{1,0:T(8,128)(2,1)S(1)}, u32[]{:S(2)}, u32[]{:S(2)}) %collective-permute-start.21) | collective-permute-done | bytes 131104 | tf_op jit(solution)/shard_map/ppermute | solution.py:327
  49.3 0.8 %shard_map.82 = (f32[64,1024]{1,0:T(8,128)S(1)}, bf16[64,1024]{1,0:T(8,128)(2,1)S(1)}) custom-call(bf16[32,2048]{1,0:T(8,128)(2,1)S(1)} %shard_map.81.refs_0_, bf16[32,2048]{1,0:T(8,128)(2,1)S(1)} %collective-permute-done.19.refs_1_, bf16[32,2048]{1,0:T(8,128)(2,1)S(1)} %collective-permute-done.20.refs_2_, ...), custom_call_target="tpu_custom_call" | custom-call | tf_op jit(solution)/shard_map/pallas_call | solution.py:315
  50.1 0.1 collective-permute-start.22
  50.2 0.4 collective-permute-done.14.refs_1_
  50.6 0.9 %shard_map.79 = (f32[64,1024]{1,0:T(8,128)S(1)}, bf16[64,1024]{1,0:T(8,128)(2,1)S(1)}) custom-call(bf16[32,2048]{1,0:T(8,128)(2,1)S(1)} %shard_map.78.refs_0_, bf16[32,2048]{1,0:T(8,128)(2,1)S(1)} %collective-permute-done.14.refs_1_, bf16[2048,1024]{1,0:T(8,128)(2,1)S(1)} %copy-done), custom_call_target="tpu_custom_call" | custom-call | tf_op jit(solution)/shard_map/pallas_call | solution.py:315
  51.4 0.1 collective-permute-start.15
  51.6 0.4 collective-permute-done.17.refs_1_
  52.0 2.2 %copy-done.1 = bf16[2048,1024]{1,0:T(8,128)(2,1)S(1)} copy-done((bf16[2048,1024]{1,0:T(8,128)(2,1)S(1)}, bf16[2048,1024]{1,0:T(8,128)(2,1)}, u32[]{:S(2)}) %copy-start.1) | copy-done | bytes 4194328
  54.2 0.8 %shard_map.80 = (f32[64,1024]{1,0:T(8,128)S(1)}, bf16[64,1024]{1,0:T(8,128)(2,1)S(1)}) custom-call(bf16[32,2048]{1,0:T(8,128)(2,1)S(1)} %collective-permute-done.16.refs_0_, bf16[32,2048]{1,0:T(8,128)(2,1)S(1)} %collective-permute-done.17.refs_1_, bf16[2048,1024]{1,0:T(8,128)(2,1)S(1)} %copy-done.1), custom_call_target="tpu_custom_call" | custom-call | tf_op jit(solution)/shard_map/pallas_call | solution.py:315
  55.1 0.1 select_convert_fusion.1
  55.1 0.1 collective-permute-start.23
  55.2 3.4 %collective-permute-start.24 = (bf16[64,1024]{1,0:T(8,128)(2,1)S(1)}, bf16[64,1024]{1,0:T(8,128)(2,1)S(1)}, u32[]{:S(2)}, u32[]{:S(2)}) collective-permute-start(bf16[64,1024]{1,0:T(8,128)(2,1)S(1)} %select_convert_fusion.1), channel_id=1, source_target_pairs={{0,2},{2,0},{4,6},{6,4},{9,11},{11,9},{13,15},{15,13},{16,18},{18,... | collective-permute-start | bytes 393224 | tf_op jit(solution)/shard_map/ppermute | solution.py:341
  58.7 0.1 select_convert_fusion
  58.7 0.7 %collective-permute-start.25 = (bf16[64,1024]{1,0:T(8,128)(2,1)S(1)}, bf16[64,1024]{1,0:T(8,128)(2,1)S(1)}, u32[]{:S(2)}, u32[]{:S(2)}) collective-permute-start(bf16[64,1024]{1,0:T(8,128)(2,1)S(1)} %select_convert_fusion), channel_id=1, source_target_pairs={{1,3},{3,1},{5,7},{7,5},{8,10},{10,8},{12,14},{14,12},{17,19},{19,... | collective-permute-start | bytes 393224 | tf_op jit(solution)/shard_map/ppermute | solution.py:341
  59.4 3.5 %collective-permute-done.24 = bf16[64,1024]{1,0:T(8,128)(2,1)S(1)} collective-permute-done((bf16[64,1024]{1,0:T(8,128)(2,1)S(1)}, bf16[64,1024]{1,0:T(8,128)(2,1)S(1)}, u32[]{:S(2)}, u32[]{:S(2)}) %collective-permute-start.24) | collective-permute-done | bytes 131104 | tf_op jit(solution)/shard_map/ppermute | solution.py:341
  63.0 0.8 %add_convert_fusion = bf16[64,1024]{1,0:T(8,128)(2,1)} fusion(bf16[64,1024]{1,0:T(8,128)(2,1)S(1)} %collective-permute-done.25, bf16[64,1024]{1,0:T(8,128)(2,1)S(1)} %collective-permute-done.24, f32[64,1024]{1,0:T(8,128)S(1)} %get-tuple-element.35, bf16[64,1024]{1,0:T(8,128)(2,1)S(1)} %collective-permute-done.15, f32[64,1024]{1,0:T(8,128)S(1)} %get-tuple-element.37, ...), kind=kLoop, calls=%fused_computation | loop fusion | flops 851968 | bytes 1572866 | tf_op jit(solution)/shard_map/convert_element_type | solution.py:374
  (23 shorter events, 0.1 us)
Async XLA Ops:
  0.0 16.1 %copy-start.2 = (bf16[32,2048]{1,0:T(8,128)(2,1)S(1)}, bf16[32,2048]{1,0:T(8,128)(2,1)}, u32[]{:S(2)}) copy-start(bf16[32,2048]{1,0:T(8,128)(2,1)} %refs_0_.1) | copy-start | bytes 393220
  0.0 12.3 %collective-permute-start.6 = (bf16[32,2048]{1,0:T(8,128)(2,1)}, bf16[32,2048]{1,0:T(8,128)(2,1)S(1)}, u32[]{:S(2)}, u32[]{:S(2)}) collective-permute-start(bf16[32,2048]{1,0:T(8,128)(2,1)} %refs_0_.1), channel_id=1, source_target_pairs={{0,24},{4,28},{8,16},{12,20},{16,8},{20,12},{24,0},{28,4},{1,25},{... | collective-permute-start | bytes 393224 | tf_op jit(solution)/shard_map/ppermute | solution.py:327
  5.1 8.8 %collective-permute-start = (bf16[32,2048]{1,0:T(8,128)(2,1)}, bf16[32,2048]{1,0:T(8,128)(2,1)S(1)}, u32[]{:S(2)}, u32[]{:S(2)}) collective-permute-start(bf16[32,2048]{1,0:T(8,128)(2,1)} %refs_0_.1), channel_id=1, source_target_pairs={{0,4},{4,0},{8,12},{12,8},{16,20},{20,16},{24,28},{28,24},{1,5},{5... | collective-permute-start | bytes 393224 | tf_op jit(solution)/shard_map/ppermute | solution.py:327
  6.5 9.3 %collective-permute-start.1 = (bf16[32,2048]{1,0:T(8,128)(2,1)}, bf16[32,2048]{1,0:T(8,128)(2,1)S(1)}, u32[]{:S(2)}, u32[]{:S(2)}) collective-permute-start(bf16[32,2048]{1,0:T(8,128)(2,1)} %refs_0_.1), channel_id=1, source_target_pairs={{0,8},{4,12},{8,0},{12,4},{16,24},{20,28},{24,16},{28,20},{1,9},{5... | collective-permute-start | bytes 393224 | tf_op jit(solution)/shard_map/ppermute | solution.py:327
  6.5 9.5 %collective-permute-start.2 = (bf16[32,2048]{1,0:T(8,128)(2,1)}, bf16[32,2048]{1,0:T(8,128)(2,1)S(1)}, u32[]{:S(2)}, u32[]{:S(2)}) collective-permute-start(bf16[32,2048]{1,0:T(8,128)(2,1)} %refs_0_.1), channel_id=1, source_target_pairs={{0,12},{4,8},{8,4},{12,0},{16,28},{20,24},{24,20},{28,16},{1,13},{... | collective-permute-start | bytes 393224 | tf_op jit(solution)/shard_map/ppermute | solution.py:327
  12.3 8.1 %collective-permute-start.7 = (bf16[32,2048]{1,0:T(8,128)(2,1)S(1)}, bf16[32,2048]{1,0:T(8,128)(2,1)S(1)}, u32[]{:S(2)}, u32[]{:S(2)}) collective-permute-start(bf16[32,2048]{1,0:T(8,128)(2,1)S(1)} %collective-permute-done.6.refs_0_), channel_id=1, source_target_pairs={{0,4},{4,0},{8,12},{12,8},{16,20},{20,16},{24,28},{28,24},{1,5},{5... | collective-permute-start | bytes 393224 | tf_op jit(solution)/shard_map/ppermute | solution.py:327
  13.8 8.8 %collective-permute-start.8 = (bf16[32,2048]{1,0:T(8,128)(2,1)S(1)}, bf16[32,2048]{1,0:T(8,128)(2,1)S(1)}, u32[]{:S(2)}, u32[]{:S(2)}) collective-permute-start(bf16[32,2048]{1,0:T(8,128)(2,1)S(1)} %collective-permute-done.6.refs_0_), channel_id=1, source_target_pairs={{0,8},{4,12},{8,0},{12,4},{16,24},{20,28},{24,16},{28,20},{1,9},{5... | collective-permute-start | bytes 393224 | tf_op jit(solution)/shard_map/ppermute | solution.py:327
  13.8 8.8 %collective-permute-start.9 = (bf16[32,2048]{1,0:T(8,128)(2,1)S(1)}, bf16[32,2048]{1,0:T(8,128)(2,1)S(1)}, u32[]{:S(2)}, u32[]{:S(2)}) collective-permute-start(bf16[32,2048]{1,0:T(8,128)(2,1)S(1)} %collective-permute-done.6.refs_0_), channel_id=1, source_target_pairs={{0,12},{4,8},{8,4},{12,0},{16,28},{20,24},{24,20},{28,16},{1,13},{... | collective-permute-start | bytes 393224 | tf_op jit(solution)/shard_map/ppermute | solution.py:327
  19.0 7.8 %collective-permute-start.3 = (bf16[32,2176]{1,0:T(8,128)(2,1)S(1)}, bf16[32,2176]{1,0:T(8,128)(2,1)S(1)}, u32[]{:S(2)}, u32[]{:S(2)}) collective-permute-start(bf16[32,2176]{1,0:T(8,128)(2,1)S(1)} %get-tuple-element.28), channel_id=1, source_target_pairs={{0,4},{4,0},{8,12},{12,8},{16,20},{20,16},{24,28},{28,24},{1,5},{5... | collective-permute-start | bytes 417800 | tf_op jit(solution)/shard_map/ppermute | solution.py:327
  20.3 8.8 %collective-permute-start.4 = (bf16[32,2176]{1,0:T(8,128)(2,1)S(1)}, bf16[32,2176]{1,0:T(8,128)(2,1)S(1)}, u32[]{:S(2)}, u32[]{:S(2)}) collective-permute-start(bf16[32,2176]{1,0:T(8,128)(2,1)S(1)} %get-tuple-element.29), channel_id=1, source_target_pairs={{0,8},{4,12},{8,0},{12,4},{16,24},{20,28},{24,16},{28,20},{1,9},{5... | collective-permute-start | bytes 417800 | tf_op jit(solution)/shard_map/ppermute | solution.py:327
  20.3 28.9 %copy-start = (bf16[2048,1024]{1,0:T(8,128)(2,1)S(1)}, bf16[2048,1024]{1,0:T(8,128)(2,1)}, u32[]{:S(2)}) copy-start(bf16[2048,1024]{1,0:T(8,128)(2,1)} %refs_4_.1) | copy-start | bytes 12582916
  20.4 8.7 %collective-permute-start.5 = (bf16[32,2176]{1,0:T(8,128)(2,1)S(1)}, bf16[32,2176]{1,0:T(8,128)(2,1)S(1)}, u32[]{:S(2)}, u32[]{:S(2)}) collective-permute-start(bf16[32,2176]{1,0:T(8,128)(2,1)S(1)} %get-tuple-element.30), channel_id=1, source_target_pairs={{0,12},{4,8},{8,4},{12,0},{16,28},{20,24},{24,20},{28,16},{1,13},{... | collective-permute-start | bytes 417800 | tf_op jit(solution)/shard_map/ppermute | solution.py:327
  25.5 6.6 %collective-permute-start.10 = (bf16[32,2176]{1,0:T(8,128)(2,1)S(1)}, bf16[32,2176]{1,0:T(8,128)(2,1)S(1)}, u32[]{:S(2)}, u32[]{:S(2)}) collective-permute-start(bf16[32,2176]{1,0:T(8,128)(2,1)S(1)} %get-tuple-element.32), channel_id=1, source_target_pairs={{0,4},{4,0},{8,12},{12,8},{16,20},{20,16},{24,28},{28,24},{1,5},{5... | collective-permute-start | bytes 417800 | tf_op jit(solution)/shard_map/ppermute | solution.py:327
  26.8 5.8 %collective-permute-start.11 = (bf16[32,2176]{1,0:T(8,128)(2,1)S(1)}, bf16[32,2176]{1,0:T(8,128)(2,1)S(1)}, u32[]{:S(2)}, u32[]{:S(2)}) collective-permute-start(bf16[32,2176]{1,0:T(8,128)(2,1)S(1)} %get-tuple-element.33), channel_id=1, source_target_pairs={{0,8},{4,12},{8,0},{12,4},{16,24},{20,28},{24,16},{28,20},{1,9},{5... | collective-permute-start | bytes 417800 | tf_op jit(solution)/shard_map/ppermute | solution.py:327
  26.9 8.4 %collective-permute-start.12 = (bf16[32,2176]{1,0:T(8,128)(2,1)S(1)}, bf16[32,2176]{1,0:T(8,128)(2,1)S(1)}, u32[]{:S(2)}, u32[]{:S(2)}) collective-permute-start(bf16[32,2176]{1,0:T(8,128)(2,1)S(1)} %get-tuple-element.34), channel_id=1, source_target_pairs={{0,12},{4,8},{8,4},{12,0},{16,28},{20,24},{24,20},{28,16},{1,13},{... | collective-permute-start | bytes 417800 | tf_op jit(solution)/shard_map/ppermute | solution.py:327
  29.6 8.0 %collective-permute-start.18 = (bf16[32,2176]{1,0:T(8,128)(2,1)S(1)}, bf16[32,2176]{1,0:T(8,128)(2,1)S(1)}, u32[]{:S(2)}, u32[]{:S(2)}) collective-permute-start(bf16[32,2176]{1,0:T(8,128)(2,1)S(1)} %shard_map.75.near), channel_id=1, source_target_pairs={{0,24},{4,28},{8,16},{12,20},{16,8},{20,12},{24,0},{28,4},{1,25},{... | collective-permute-start | bytes 417800 | tf_op jit(solution)/shard_map/ppermute | solution.py:327
  35.7 7.6 %collective-permute-start.13 = (bf16[32,2176]{1,0:T(8,128)(2,1)S(1)}, bf16[32,2176]{1,0:T(8,128)(2,1)S(1)}, u32[]{:S(2)}, u32[]{:S(2)}) collective-permute-start(bf16[32,2176]{1,0:T(8,128)(2,1)S(1)} %shard_map.77.near), channel_id=1, source_target_pairs={{0,24},{4,28},{8,16},{12,20},{16,8},{20,12},{24,0},{28,4},{1,25},{... | collective-permute-start | bytes 417800 | tf_op jit(solution)/shard_map/ppermute | solution.py:327
  37.9 7.2 %collective-permute-start.19 = (bf16[32,2048]{1,0:T(8,128)(2,1)S(1)}, bf16[32,2048]{1,0:T(8,128)(2,1)S(1)}, u32[]{:S(2)}, u32[]{:S(2)}) collective-permute-start(bf16[32,2048]{1,0:T(8,128)(2,1)S(1)} %shard_map.81.refs_0_), channel_id=1, source_target_pairs={{0,4},{4,0},{8,12},{12,8},{16,20},{20,16},{24,28},{28,24},{1,5},{5... | collective-permute-start | bytes 393224 | tf_op jit(solution)/shard_map/ppermute | solution.py:327
  38.9 8.7 %collective-permute-start.20 = (bf16[32,2048]{1,0:T(8,128)(2,1)S(1)}, bf16[32,2048]{1,0:T(8,128)(2,1)S(1)}, u32[]{:S(2)}, u32[]{:S(2)}) collective-permute-start(bf16[32,2048]{1,0:T(8,128)(2,1)S(1)} %shard_map.81.refs_0_), channel_id=1, source_target_pairs={{0,8},{4,12},{8,0},{12,4},{16,24},{20,28},{24,16},{28,20},{1,9},{5... | collective-permute-start | bytes 393224 | tf_op jit(solution)/shard_map/ppermute | solution.py:327
  40.5 8.8 %collective-permute-start.21 = (bf16[32,2048]{1,0:T(8,128)(2,1)S(1)}, bf16[32,2048]{1,0:T(8,128)(2,1)S(1)}, u32[]{:S(2)}, u32[]{:S(2)}) collective-permute-start(bf16[32,2048]{1,0:T(8,128)(2,1)S(1)} %shard_map.81.refs_0_), channel_id=1, source_target_pairs={{0,12},{4,8},{8,4},{12,0},{16,28},{20,24},{24,20},{28,16},{1,13},{... | collective-permute-start | bytes 393224 | tf_op jit(solution)/shard_map/ppermute | solution.py:327
  43.6 7.0 %collective-permute-start.14 = (bf16[32,2048]{1,0:T(8,128)(2,1)S(1)}, bf16[32,2048]{1,0:T(8,128)(2,1)S(1)}, u32[]{:S(2)}, u32[]{:S(2)}) collective-permute-start(bf16[32,2048]{1,0:T(8,128)(2,1)S(1)} %shard_map.78.refs_0_), channel_id=1, source_target_pairs={{0,4},{4,0},{8,12},{12,8},{16,20},{20,16},{24,28},{28,24},{1,5},{5... | collective-permute-start | bytes 393224 | tf_op jit(solution)/shard_map/ppermute | solution.py:327
  45.1 6.5 %collective-permute-start.16 = (bf16[32,2048]{1,0:T(8,128)(2,1)S(1)}, bf16[32,2048]{1,0:T(8,128)(2,1)S(1)}, u32[]{:S(2)}, u32[]{:S(2)}) collective-permute-start(bf16[32,2048]{1,0:T(8,128)(2,1)S(1)} %shard_map.78.refs_0_), channel_id=1, source_target_pairs={{0,8},{4,12},{8,0},{12,4},{16,24},{20,28},{24,16},{28,20},{1,9},{5... | collective-permute-start | bytes 393224 | tf_op jit(solution)/shard_map/ppermute | solution.py:327
  45.1 6.9 %collective-permute-start.17 = (bf16[32,2048]{1,0:T(8,128)(2,1)S(1)}, bf16[32,2048]{1,0:T(8,128)(2,1)S(1)}, u32[]{:S(2)}, u32[]{:S(2)}) collective-permute-start(bf16[32,2048]{1,0:T(8,128)(2,1)S(1)} %shard_map.78.refs_0_), channel_id=1, source_target_pairs={{0,12},{4,8},{8,4},{12,0},{16,28},{20,24},{24,20},{28,16},{1,13},{... | collective-permute-start | bytes 393224 | tf_op jit(solution)/shard_map/ppermute | solution.py:327
  50.1 5.0 %collective-permute-start.22 = (bf16[64,1024]{1,0:T(8,128)(2,1)S(1)}, bf16[64,1024]{1,0:T(8,128)(2,1)S(1)}, u32[]{:S(2)}, u32[]{:S(2)}) collective-permute-start(bf16[64,1024]{1,0:T(8,128)(2,1)S(1)} %get-tuple-element.40), channel_id=1, source_target_pairs={{0,1},{1,0},{2,3},{3,2},{4,5},{5,4},{6,7},{7,6},{8,9},{9,8},{10,11... | collective-permute-start | bytes 393224 | tf_op jit(solution)/shard_map/ppermute | solution.py:327
  51.4 3.6 %collective-permute-start.15 = (bf16[64,1024]{1,0:T(8,128)(2,1)S(1)}, bf16[64,1024]{1,0:T(8,128)(2,1)S(1)}, u32[]{:S(2)}, u32[]{:S(2)}) collective-permute-start(bf16[64,1024]{1,0:T(8,128)(2,1)S(1)} %get-tuple-element.36), channel_id=1, source_target_pairs={{0,1},{1,0},{2,3},{3,2},{4,5},{5,4},{6,7},{7,6},{8,9},{9,8},{10,11... | collective-permute-start | bytes 393224 | tf_op jit(solution)/shard_map/ppermute | solution.py:327
  52.0 2.2 %copy-start.1 = (bf16[2048,1024]{1,0:T(8,128)(2,1)S(1)}, bf16[2048,1024]{1,0:T(8,128)(2,1)}, u32[]{:S(2)}) copy-start(bf16[2048,1024]{1,0:T(8,128)(2,1)} %refs_4_.1) | copy-start | bytes 12582916
  55.1 3.5 %collective-permute-start.23 = (bf16[64,1024]{1,0:T(8,128)(2,1)S(1)}, bf16[64,1024]{1,0:T(8,128)(2,1)S(1)}, u32[]{:S(2)}, u32[]{:S(2)}) collective-permute-start(bf16[64,1024]{1,0:T(8,128)(2,1)S(1)} %get-tuple-element.41), channel_id=1, source_target_pairs={{0,1},{1,0},{2,3},{3,2},{4,5},{5,4},{6,7},{7,6},{8,9},{9,8},{10,11... | collective-permute-start | bytes 393224 | tf_op jit(solution)/shard_map/ppermute | solution.py:327
  55.2 7.8 %collective-permute-start.24 = (bf16[64,1024]{1,0:T(8,128)(2,1)S(1)}, bf16[64,1024]{1,0:T(8,128)(2,1)S(1)}, u32[]{:S(2)}, u32[]{:S(2)}) collective-permute-start(bf16[64,1024]{1,0:T(8,128)(2,1)S(1)} %select_convert_fusion.1), channel_id=1, source_target_pairs={{0,2},{2,0},{4,6},{6,4},{9,11},{11,9},{13,15},{15,13},{16,18},{18,... | collective-permute-start | bytes 393224 | tf_op jit(solution)/shard_map/ppermute | solution.py:341
  58.7 4.2 %collective-permute-start.25 = (bf16[64,1024]{1,0:T(8,128)(2,1)S(1)}, bf16[64,1024]{1,0:T(8,128)(2,1)S(1)}, u32[]{:S(2)}, u32[]{:S(2)}) collective-permute-start(bf16[64,1024]{1,0:T(8,128)(2,1)S(1)} %select_convert_fusion), channel_id=1, source_target_pairs={{1,3},{3,1},{5,7},{7,5},{8,10},{10,8},{12,14},{14,12},{17,19},{19,... | collective-permute-start | bytes 393224 | tf_op jit(solution)/shard_map/ppermute | solution.py:341

commit v9 on v7

--- a/solution.py
+++ b/solution.py
@@ -36,7 +36,7 @@
         self.n, self.rows, self.blocks, self.page = n, rows, blocks, page
         self.group = n // blocks
         self.halves = blocks == 2 and n == 8 and ways == 4 and rows * self.group == page
-        self.cross = n * 3 // 4
+        self.cross = n // 2
         self.chunks = self.group if self.halves else 1
 
     def block(self, me, lb):
@@ -279,19 +279,15 @@
     )(near, far)
 
 
-def sources_of(plan, lb):
-    return range(plan.group) if lb else reversed(range(plan.group))
-
-
 def project_kernel(plan, lb, *refs):
     sources, weight, (keep, send, rows_ref) = refs[: plan.group], refs[plan.group], refs[plan.group + 1 :]
     me, column = lax.axis_index("pages"), lax.axis_index("mp")
     rows = plan.rows
     holders = plan.group // 2
-    for i, k in enumerate(sources_of(plan, lb)):
+    for k in range(plan.group):
         device = me ^ k ^ (lb * plan.cross)
         place = ((device // holders % 2) ^ (column % 2)) * holders + device % holders
-        rows_ref[pl.ds(pl.multiple_of(place * rows, rows), rows), :] = sources[i][...]
+        rows_ref[pl.ds(pl.multiple_of(place * rows, rows), rows), :] = sources[k][...]
     product = jnp.dot(rows_ref[...], weight[...], preferred_element_type=F32)
     part = holders * rows
     keep[...] = product[:part]
@@ -308,7 +304,7 @@
         out_specs=(in_vmem(), in_vmem()),
         scratch_shapes=[VMEM((plan.page, weight.shape[0]), BF16)],
         compiler_params=params(24),
-    )(*(sources[k] for k in sources_of(plan, lb)), weight)
+    )(*(sources[k] for k in range(plan.group)), weight)
 
 
 def swap(x, axis, distance):
@@ -330,7 +326,7 @@
     for lb, rows in enumerate((queries, far)):
         chunks = spread(rows, plan)
         outs = attend(plan, heads, lb, pages, [chunks[k] for k in range(plan.group)])
-        near.append(merge(heads, *(swap(outs[k], "pages", k) for k in reversed(others(plan))), outs[0]))
+        near.append(merge(heads, outs[0], *(swap(outs[k], "pages", k) for k in others(plan))))
     across = [swap(x, "pages", plan.cross) for x in near]
     sums = [None, None]
     for lb in (1, 0):

time: 62.1 us -> 62.3 us (level)
  waiting for transfers between devices: 13.4 us -> 22 us
  starting transfers between devices: 41 us -> 32.8 us
    ppermute x24, waiting for transfers between devices: 13.4 us -> 22 us  [swap(): return lax.ppermute(x, axis, [(i, i ^ distance) for i in range(n)])]
    ppermute x24, starting transfers between devices: 41 us -> 32.8 us  [swap(): return lax.ppermute(x, axis, [(i, i ^ distance) for i in range(n)])]
  transfers between devices with their start and end apart: 24 -> 24, of which waited for: 10 -> 12; matrix products, arithmetic and copies ran while one was open for 0% -> 0% of each run, Pallas kernels for 11% -> 11%
where the time goes in v9:
time: 62.3 us; the launch traced here: 62.4 us
  starting transfers between devices  32.8 us (53%)
  waiting for transfers between devices  22 us (35%)
  Pallas kernels  6.65 us (11%)
  other arithmetic  0.78 us (1%)
    ppermute x24, starting transfers between devices, swap(): return lax.ppermute(x, axis, [(i, i ^ distance) for i in range(n)])  32.8 us
    ppermute x24, waiting for transfers between devices, swap(): return lax.ppermute(x, axis, [(i, i ^ distance) for i in range(n)])  22 us
    pallas_call x1, Pallas kernels, fetch(): pl.pallas_call(functools.partial(fetch_kernel, plan, pages_dev), out_shap...  2.19 us
    pallas_call x2, Pallas kernels, project(): pl.pallas_call(functools.partial(project_kernel, plan, lb), out_shape=(ja...  1.57 us
    pallas_call x2, Pallas kernels, attend(): pl.pallas_call(functools.partial(attend_kernel, plan, heads, lb), out_sha...  1.29 us
  transfers between devices with their start and end apart: 24, of which 12 were waited for; matrix products, arithmetic and copies ran while one was open for 0% of the time, Pallas kernels for 11%

profile of v9, /device:TPU:0, one launch (start us, length us, event | category | flops | bytes accessed | tf_op | source)
XLA Modules:
  0.0 62.4 jit_solution(7596281563727045908)
XLA Ops:
  0.0 4.0 %collective-permute-start.6 = (bf16[32,2048]{1,0:T(8,128)(2,1)}, bf16[32,2048]{1,0:T(8,128)(2,1)S(1)}, u32[]{:S(2)}, u32[]{:S(2)}) collective-permute-start(bf16[32,2048]{1,0:T(8,128)(2,1)} %refs_0_.1), channel_id=1, source_target_pairs={{0,16},{4,20},{8,24},{12,28},{16,0},{20,4},{24,8},{28,12},{1,17},{... | collective-permute-start | bytes 393224 | tf_op jit(solution)/shard_map/ppermute | solution.py:312
  4.0 1.5 %collective-permute-start = (bf16[32,2048]{1,0:T(8,128)(2,1)}, bf16[32,2048]{1,0:T(8,128)(2,1)S(1)}, u32[]{:S(2)}, u32[]{:S(2)}) collective-permute-start(bf16[32,2048]{1,0:T(8,128)(2,1)} %refs_0_.1), channel_id=1, source_target_pairs={{0,4},{4,0},{8,12},{12,8},{16,20},{20,16},{24,28},{28,24},{1,5},{5... | collective-permute-start | bytes 393224 | tf_op jit(solution)/shard_map/ppermute | solution.py:312
  5.5 1.6 %collective-permute-start.1 = (bf16[32,2048]{1,0:T(8,128)(2,1)}, bf16[32,2048]{1,0:T(8,128)(2,1)S(1)}, u32[]{:S(2)}, u32[]{:S(2)}) collective-permute-start(bf16[32,2048]{1,0:T(8,128)(2,1)} %refs_0_.1), channel_id=1, source_target_pairs={{0,8},{4,12},{8,0},{12,4},{16,24},{20,28},{24,16},{28,20},{1,9},{5... | collective-permute-start | bytes 393224 | tf_op jit(solution)/shard_map/ppermute | solution.py:312
  7.1 0.4 collective-permute-start.2
  7.5 2.2 %shard_map.73 = (bf16[2,2,768,128]{3,2,1,0:T(8,128)(2,1)S(1)}, bf16[2,2,768,256]{3,2,1,0:T(8,128)(2,1)S(1)}, s32[2,3]{1,0:T(2,128)S(1)}) custom-call(s32[2,24]{1,0:T(2,128)} %select_hbm.1, s32[128]{0:T(128)} %table_hbm.1, s32[2]{0:T(128)} %stands_hbm.1, bf16[16,256,128]{2,1,0:T(8,128)(2,1)} %bitcast.2, bf16[16,256,128]{2,1,0:T(8,128)(2,1)} %bitcast.3), custom_call_target="tpu_custom_call" | custom-call | flops 2000000000 | bytes 8388608 | tf_op jit(solution)/shard_map/pallas_call | solution.py:118
  9.7 1.0 %collective-permute-done.6.refs_0_ = bf16[32,2048]{1,0:T(8,128)(2,1)S(1)} collective-permute-done((bf16[32,2048]{1,0:T(8,128)(2,1)}, bf16[32,2048]{1,0:T(8,128)(2,1)S(1)}, u32[]{:S(2)}, u32[]{:S(2)}) %collective-permute-start.6) | collective-permute-done | bytes 131104 | tf_op jit(solution)/shard_map/ppermute | solution.py:312
  10.7 1.5 %collective-permute-start.7 = (bf16[32,2048]{1,0:T(8,128)(2,1)S(1)}, bf16[32,2048]{1,0:T(8,128)(2,1)S(1)}, u32[]{:S(2)}, u32[]{:S(2)}) collective-permute-start(bf16[32,2048]{1,0:T(8,128)(2,1)S(1)} %collective-permute-done.6.refs_0_), channel_id=1, source_target_pairs={{0,4},{4,0},{8,12},{12,8},{16,20},{20,16},{24,28},{28,24},{1,5},{5... | collective-permute-start | bytes 393224 | tf_op jit(solution)/shard_map/ppermute | solution.py:312
  12.2 1.5 %collective-permute-start.8 = (bf16[32,2048]{1,0:T(8,128)(2,1)S(1)}, bf16[32,2048]{1,0:T(8,128)(2,1)S(1)}, u32[]{:S(2)}, u32[]{:S(2)}) collective-permute-start(bf16[32,2048]{1,0:T(8,128)(2,1)S(1)} %collective-permute-done.6.refs_0_), channel_id=1, source_target_pairs={{0,8},{4,12},{8,0},{12,4},{16,24},{20,28},{24,16},{28,20},{1,9},{5... | collective-permute-start | bytes 393224 | tf_op jit(solution)/shard_map/ppermute | solution.py:312
  13.7 0.0 collective-permute-done.refs_1_
  13.7 0.5 collective-permute-start.9
  14.2 0.0 collective-permute-done.1.refs_2_
  14.2 1.9 %collective-permute-done.2.refs_3_ = bf16[32,2048]{1,0:T(8,128)(2,1)S(1)} collective-permute-done((bf16[32,2048]{1,0:T(8,128)(2,1)}, bf16[32,2048]{1,0:T(8,128)(2,1)S(1)}, u32[]{:S(2)}, u32[]{:S(2)}) %collective-permute-start.2) | collective-permute-done | bytes 131104 | tf_op jit(solution)/shard_map/ppermute | solution.py:312
  16.1 0.6 %shard_map.74 = (bf16[32,2176]{1,0:T(8,128)(2,1)S(1)}, bf16[32,2176]{1,0:T(8,128)(2,1)S(1)}, bf16[32,2176]{1,0:T(8,128)(2,1)S(1)}, bf16[32,2176]{1,0:T(8,128)(2,1)S(1)}) custom-call(s32[2,3]{1,0:T(2,128)S(1)} %get-tuple-element.20.info, bf16[32,2048]{1,0:T(8,128)(2,1)S(1)} %copy-done.1, bf16[32,2048]{1,0:T(8,128)(2,1)S(1)} %collective-permute-done.refs_1_, ...), custom_call_target="tpu_custom_call" | custom-call | flops 2000000000 | bytes 4194304 | tf_op jit(solution)/shard_map/pallas_call | solution.py:216
  16.8 3.7 %collective-permute-start.3 = (bf16[32,2176]{1,0:T(8,128)(2,1)S(1)}, bf16[32,2176]{1,0:T(8,128)(2,1)S(1)}, u32[]{:S(2)}, u32[]{:S(2)}) collective-permute-start(bf16[32,2176]{1,0:T(8,128)(2,1)S(1)} %get-tuple-element.24), channel_id=1, source_target_pairs={{0,4},{4,0},{8,12},{12,8},{16,20},{20,16},{24,28},{28,24},{1,5},{5... | collective-permute-start | bytes 417800 | tf_op jit(solution)/shard_map/ppermute | solution.py:312
  20.5 0.0 collective-permute-start.4
  20.5 1.5 %collective-permute-start.5 = (bf16[32,2176]{1,0:T(8,128)(2,1)S(1)}, bf16[32,2176]{1,0:T(8,128)(2,1)S(1)}, u32[]{:S(2)}, u32[]{:S(2)}) collective-permute-start(bf16[32,2176]{1,0:T(8,128)(2,1)S(1)} %get-tuple-element.26), channel_id=1, source_target_pairs={{0,12},{4,8},{8,4},{12,0},{16,28},{20,24},{24,20},{28,16},{1,13},{... | collective-permute-start | bytes 417800 | tf_op jit(solution)/shard_map/ppermute | solution.py:312
  22.0 0.6 %shard_map.76 = (bf16[32,2176]{1,0:T(8,128)(2,1)S(1)}, bf16[32,2176]{1,0:T(8,128)(2,1)S(1)}, bf16[32,2176]{1,0:T(8,128)(2,1)S(1)}, bf16[32,2176]{1,0:T(8,128)(2,1)S(1)}) custom-call(s32[2,3]{1,0:T(2,128)S(1)} %get-tuple-element.20.info, bf16[32,2048]{1,0:T(8,128)(2,1)S(1)} %collective-permute-done.6.refs_0_, ...), custom_call_target="tpu_custom_call" | custom-call | flops 2000000000 | bytes 4194304 | tf_op jit(solution)/shard_map/pallas_call | solution.py:216
  22.7 4.3 %collective-permute-start.10 = (bf16[32,2176]{1,0:T(8,128)(2,1)S(1)}, bf16[32,2176]{1,0:T(8,128)(2,1)S(1)}, u32[]{:S(2)}, u32[]{:S(2)}) collective-permute-start(bf16[32,2176]{1,0:T(8,128)(2,1)S(1)} %get-tuple-element.28), channel_id=1, source_target_pairs={{0,4},{4,0},{8,12},{12,8},{16,20},{20,16},{24,28},{28,24},{1,5},{5... | collective-permute-start | bytes 417800 | tf_op jit(solution)/shard_map/ppermute | solution.py:312
  27.0 0.1 collective-permute-start.11
  27.0 1.5 %collective-permute-start.12 = (bf16[32,2176]{1,0:T(8,128)(2,1)S(1)}, bf16[32,2176]{1,0:T(8,128)(2,1)S(1)}, u32[]{:S(2)}, u32[]{:S(2)}) collective-permute-start(bf16[32,2176]{1,0:T(8,128)(2,1)S(1)} %get-tuple-element.30), channel_id=1, source_target_pairs={{0,12},{4,8},{8,4},{12,0},{16,28},{20,24},{24,20},{28,16},{1,13},{... | collective-permute-start | bytes 417800 | tf_op jit(solution)/shard_map/ppermute | solution.py:312
  28.5 0.5 shard_map.75.near
  29.0 1.1 %collective-permute-start.18 = (bf16[32,2176]{1,0:T(8,128)(2,1)S(1)}, bf16[32,2176]{1,0:T(8,128)(2,1)S(1)}, u32[]{:S(2)}, u32[]{:S(2)}) collective-permute-start(bf16[32,2176]{1,0:T(8,128)(2,1)S(1)} %shard_map.75.near), channel_id=1, source_target_pairs={{0,16},{4,20},{8,24},{12,28},{16,0},{20,4},{24,8},{28,12},{1,17},{... | collective-permute-start | bytes 417800 | tf_op jit(solution)/shard_map/ppermute | solution.py:312
  30.1 1.0 %collective-permute-done.10.refs_1_ = bf16[32,2176]{1,0:T(8,128)(2,1)S(1)} collective-permute-done((bf16[32,2176]{1,0:T(8,128)(2,1)S(1)}, bf16[32,2176]{1,0:T(8,128)(2,1)S(1)}, u32[]{:S(2)}, u32[]{:S(2)}) %collective-permute-start.10) | collective-permute-done | bytes 139296 | tf_op jit(solution)/shard_map/ppermute | solution.py:312
  31.1 2.0 %collective-permute-done.11.refs_2_ = bf16[32,2176]{1,0:T(8,128)(2,1)S(1)} collective-permute-done((bf16[32,2176]{1,0:T(8,128)(2,1)S(1)}, bf16[32,2176]{1,0:T(8,128)(2,1)S(1)}, u32[]{:S(2)}, u32[]{:S(2)}) %collective-permute-start.11) | collective-permute-done | bytes 139296 | tf_op jit(solution)/shard_map/ppermute | solution.py:312
  33.0 1.5 %collective-permute-done.12.refs_3_ = bf16[32,2176]{1,0:T(8,128)(2,1)S(1)} collective-permute-done((bf16[32,2176]{1,0:T(8,128)(2,1)S(1)}, bf16[32,2176]{1,0:T(8,128)(2,1)S(1)}, u32[]{:S(2)}, u32[]{:S(2)}) %collective-permute-start.12) | collective-permute-done | bytes 139296 | tf_op jit(solution)/shard_map/ppermute | solution.py:312
  34.5 0.5 shard_map.77.near
  35.0 1.9 %collective-permute-start.13 = (bf16[32,2176]{1,0:T(8,128)(2,1)S(1)}, bf16[32,2176]{1,0:T(8,128)(2,1)S(1)}, u32[]{:S(2)}, u32[]{:S(2)}) collective-permute-start(bf16[32,2176]{1,0:T(8,128)(2,1)S(1)} %shard_map.77.near), channel_id=1, source_target_pairs={{0,16},{4,20},{8,24},{12,28},{16,0},{20,4},{24,8},{28,12},{1,17},{... | collective-permute-start | bytes 417800 | tf_op jit(solution)/shard_map/ppermute | solution.py:312
  36.9 2.5 %collective-permute-done.18.far = bf16[32,2176]{1,0:T(8,128)(2,1)S(1)} collective-permute-done((bf16[32,2176]{1,0:T(8,128)(2,1)S(1)}, bf16[32,2176]{1,0:T(8,128)(2,1)S(1)}, u32[]{:S(2)}, u32[]{:S(2)}) %collective-permute-start.18) | collective-permute-done | bytes 139296 | tf_op jit(solution)/shard_map/ppermute | solution.py:312
  39.4 0.3 shard_map.80.refs_0_
  39.7 1.7 %collective-permute-start.19 = (bf16[32,2048]{1,0:T(8,128)(2,1)S(1)}, bf16[32,2048]{1,0:T(8,128)(2,1)S(1)}, u32[]{:S(2)}, u32[]{:S(2)}) collective-permute-start(bf16[32,2048]{1,0:T(8,128)(2,1)S(1)} %shard_map.80.refs_0_), channel_id=1, source_target_pairs={{0,4},{4,0},{8,12},{12,8},{16,20},{20,16},{24,28},{28,24},{1,5},{5... | collective-permute-start | bytes 393224 | tf_op jit(solution)/shard_map/ppermute | solution.py:312
  41.4 1.9 %collective-permute-start.21 = (bf16[32,2048]{1,0:T(8,128)(2,1)S(1)}, bf16[32,2048]{1,0:T(8,128)(2,1)S(1)}, u32[]{:S(2)}, u32[]{:S(2)}) collective-permute-start(bf16[32,2048]{1,0:T(8,128)(2,1)S(1)} %shard_map.80.refs_0_), channel_id=1, source_target_pairs={{0,12},{4,8},{8,4},{12,0},{16,28},{20,24},{24,20},{28,16},{1,13},{... | collective-permute-start | bytes 393224 | tf_op jit(solution)/shard_map/ppermute | solution.py:312
  43.3 0.3 shard_map.78.refs_0_
  43.6 2.1 %collective-permute-start.14 = (bf16[32,2048]{1,0:T(8,128)(2,1)S(1)}, bf16[32,2048]{1,0:T(8,128)(2,1)S(1)}, u32[]{:S(2)}, u32[]{:S(2)}) collective-permute-start(bf16[32,2048]{1,0:T(8,128)(2,1)S(1)} %shard_map.78.refs_0_), channel_id=1, source_target_pairs={{0,4},{4,0},{8,12},{12,8},{16,20},{20,16},{24,28},{28,24},{1,5},{5... | collective-permute-start | bytes 393224 | tf_op jit(solution)/shard_map/ppermute | solution.py:312
  45.7 1.2 %collective-permute-done.19.refs_1_ = bf16[32,2048]{1,0:T(8,128)(2,1)S(1)} collective-permute-done((bf16[32,2048]{1,0:T(8,128)(2,1)S(1)}, bf16[32,2048]{1,0:T(8,128)(2,1)S(1)}, u32[]{:S(2)}, u32[]{:S(2)}) %collective-permute-start.19) | collective-permute-done | bytes 131104 | tf_op jit(solution)/shard_map/ppermute | solution.py:312
  46.9 0.3 collective-permute-start.16
  47.3 0.4 collective-permute-done.20.refs_2_
  47.7 2.9 %collective-permute-done.21.refs_3_ = bf16[32,2048]{1,0:T(8,128)(2,1)S(1)} collective-permute-done((bf16[32,2048]{1,0:T(8,128)(2,1)S(1)}, bf16[32,2048]{1,0:T(8,128)(2,1)S(1)}, u32[]{:S(2)}, u32[]{:S(2)}) %collective-permute-start.21) | collective-permute-done | bytes 131104 | tf_op jit(solution)/shard_map/ppermute | solution.py:312
  50.6 0.8 %shard_map.81 = (f32[64,1024]{1,0:T(8,128)S(1)}, bf16[64,1024]{1,0:T(8,128)(2,1)S(1)}) custom-call(bf16[32,2048]{1,0:T(8,128)(2,1)S(1)} %shard_map.80.refs_0_, bf16[32,2048]{1,0:T(8,128)(2,1)S(1)} %collective-permute-done.19.refs_1_, bf16[32,2048]{1,0:T(8,128)(2,1)S(1)} %collective-permute-done.20.refs_2_, ...), custom_call_target="tpu_custom_call" | custom-call | tf_op jit(solution)/shard_map/pallas_call | solution.py:300
  51.4 0.1 collective-permute-start.22
  51.5 0.0 collective-permute-done.14.refs_1_
  51.5 2.3 %collective-permute-done.16.refs_3_ = bf16[32,2048]{1,0:T(8,128)(2,1)S(1)} collective-permute-done((bf16[32,2048]{1,0:T(8,128)(2,1)S(1)}, bf16[32,2048]{1,0:T(8,128)(2,1)S(1)}, u32[]{:S(2)}, u32[]{:S(2)}) %collective-permute-start.16) | collective-permute-done | bytes 131104 | tf_op jit(solution)/shard_map/ppermute | solution.py:312
  53.7 0.8 %shard_map.79 = (f32[64,1024]{1,0:T(8,128)S(1)}, bf16[64,1024]{1,0:T(8,128)(2,1)S(1)}) custom-call(bf16[32,2048]{1,0:T(8,128)(2,1)S(1)} %shard_map.78.refs_0_, bf16[32,2048]{1,0:T(8,128)(2,1)S(1)} %collective-permute-done.14.refs_1_, bf16[32,2048]{1,0:T(8,128)(2,1)S(1)} %collective-permute-done.15.refs_2_, ...), custom_call_target="tpu_custom_call" | custom-call | tf_op jit(solution)/shard_map/pallas_call | solution.py:300
  54.5 0.1 collective-permute-start.17
  54.6 1.3 %collective-permute-done.17 = bf16[64,1024]{1,0:T(8,128)(2,1)S(1)} collective-permute-done((bf16[64,1024]{1,0:T(8,128)(2,1)S(1)}, bf16[64,1024]{1,0:T(8,128)(2,1)S(1)}, u32[]{:S(2)}, u32[]{:S(2)}) %collective-permute-start.17) | collective-permute-done | bytes 131104 | tf_op jit(solution)/shard_map/ppermute | solution.py:312
  55.9 0.1 select_convert_fusion
  56.0 1.6 %collective-permute-start.23 = (bf16[64,1024]{1,0:T(8,128)(2,1)S(1)}, bf16[64,1024]{1,0:T(8,128)(2,1)S(1)}, u32[]{:S(2)}, u32[]{:S(2)}) collective-permute-start(bf16[64,1024]{1,0:T(8,128)(2,1)S(1)} %select_convert_fusion), channel_id=1, source_target_pairs={{0,2},{1,3},{2,0},{3,1},{4,6},{5,7},{6,4},{7,5},{8,10},{9,11},{10,... | collective-permute-start | bytes 393224 | tf_op jit(solution)/shard_map/ppermute | solution.py:312
  57.6 4.0 %collective-permute-done.23 = bf16[64,1024]{1,0:T(8,128)(2,1)S(1)} collective-permute-done((bf16[64,1024]{1,0:T(8,128)(2,1)S(1)}, bf16[64,1024]{1,0:T(8,128)(2,1)S(1)}, u32[]{:S(2)}, u32[]{:S(2)}) %collective-permute-start.23) | collective-permute-done | bytes 131104 | tf_op jit(solution)/shard_map/ppermute | solution.py:312
  61.6 0.7 %add_convert_fusion = bf16[64,1024]{1,0:T(8,128)(2,1)} fusion(bf16[64,1024]{1,0:T(8,128)(2,1)S(1)} %collective-permute-done.23, f32[64,1024]{1,0:T(8,128)S(1)} %get-tuple-element.31, bf16[64,1024]{1,0:T(8,128)(2,1)S(1)} %collective-permute-done.17, f32[64,1024]{1,0:T(8,128)S(1)} %get-tuple-element.33, bf16[64,1024]{1,0:T(8,128)(2,1)S(1)} %collective-permute-done.22, ...), kind=kLoop, calls=%fused_computation | loop fusion | flops 524288 | bytes 1048577 | tf_op jit(solution)/shard_map/convert_element_type | solution.py:339
  (15 shorter events, 0.0 us)
Async XLA Ops:
  0.0 16.1 %copy-start.1 = (bf16[32,2048]{1,0:T(8,128)(2,1)S(1)}, bf16[32,2048]{1,0:T(8,128)(2,1)}, u32[]{:S(2)}) copy-start(bf16[32,2048]{1,0:T(8,128)(2,1)} %refs_0_.1) | copy-start | bytes 393220
  0.0 10.7 %collective-permute-start.6 = (bf16[32,2048]{1,0:T(8,128)(2,1)}, bf16[32,2048]{1,0:T(8,128)(2,1)S(1)}, u32[]{:S(2)}, u32[]{:S(2)}) collective-permute-start(bf16[32,2048]{1,0:T(8,128)(2,1)} %refs_0_.1), channel_id=1, source_target_pairs={{0,16},{4,20},{8,24},{12,28},{16,0},{20,4},{24,8},{28,12},{1,17},{... | collective-permute-start | bytes 393224 | tf_op jit(solution)/shard_map/ppermute | solution.py:312
  4.0 9.7 %collective-permute-start = (bf16[32,2048]{1,0:T(8,128)(2,1)}, bf16[32,2048]{1,0:T(8,128)(2,1)S(1)}, u32[]{:S(2)}, u32[]{:S(2)}) collective-permute-start(bf16[32,2048]{1,0:T(8,128)(2,1)} %refs_0_.1), channel_id=1, source_target_pairs={{0,4},{4,0},{8,12},{12,8},{16,20},{20,16},{24,28},{28,24},{1,5},{5... | collective-permute-start | bytes 393224 | tf_op jit(solution)/shard_map/ppermute | solution.py:312
  5.5 8.7 %collective-permute-start.1 = (bf16[32,2048]{1,0:T(8,128)(2,1)}, bf16[32,2048]{1,0:T(8,128)(2,1)S(1)}, u32[]{:S(2)}, u32[]{:S(2)}) collective-permute-start(bf16[32,2048]{1,0:T(8,128)(2,1)} %refs_0_.1), channel_id=1, source_target_pairs={{0,8},{4,12},{8,0},{12,4},{16,24},{20,28},{24,16},{28,20},{1,9},{5... | collective-permute-start | bytes 393224 | tf_op jit(solution)/shard_map/ppermute | solution.py:312
  7.1 9.0 %collective-permute-start.2 = (bf16[32,2048]{1,0:T(8,128)(2,1)}, bf16[32,2048]{1,0:T(8,128)(2,1)S(1)}, u32[]{:S(2)}, u32[]{:S(2)}) collective-permute-start(bf16[32,2048]{1,0:T(8,128)(2,1)} %refs_0_.1), channel_id=1, source_target_pairs={{0,12},{4,8},{8,4},{12,0},{16,28},{20,24},{24,20},{28,16},{1,13},{... | collective-permute-start | bytes 393224 | tf_op jit(solution)/shard_map/ppermute | solution.py:312
  10.7 9.7 %collective-permute-start.7 = (bf16[32,2048]{1,0:T(8,128)(2,1)S(1)}, bf16[32,2048]{1,0:T(8,128)(2,1)S(1)}, u32[]{:S(2)}, u32[]{:S(2)}) collective-permute-start(bf16[32,2048]{1,0:T(8,128)(2,1)S(1)} %collective-permute-done.6.refs_0_), channel_id=1, source_target_pairs={{0,4},{4,0},{8,12},{12,8},{16,20},{20,16},{24,28},{28,24},{1,5},{5... | collective-permute-start | bytes 393224 | tf_op jit(solution)/shard_map/ppermute | solution.py:312
  12.2 9.8 %collective-permute-start.8 = (bf16[32,2048]{1,0:T(8,128)(2,1)S(1)}, bf16[32,2048]{1,0:T(8,128)(2,1)S(1)}, u32[]{:S(2)}, u32[]{:S(2)}) collective-permute-start(bf16[32,2048]{1,0:T(8,128)(2,1)S(1)} %collective-permute-done.6.refs_0_), channel_id=1, source_target_pairs={{0,8},{4,12},{8,0},{12,4},{16,24},{20,28},{24,16},{28,20},{1,9},{5... | collective-permute-start | bytes 393224 | tf_op jit(solution)/shard_map/ppermute | solution.py:312
  13.7 8.3 %collective-permute-start.9 = (bf16[32,2048]{1,0:T(8,128)(2,1)S(1)}, bf16[32,2048]{1,0:T(8,128)(2,1)S(1)}, u32[]{:S(2)}, u32[]{:S(2)}) collective-permute-start(bf16[32,2048]{1,0:T(8,128)(2,1)S(1)} %collective-permute-done.6.refs_0_), channel_id=1, source_target_pairs={{0,12},{4,8},{8,4},{12,0},{16,28},{20,24},{24,20},{28,16},{1,13},{... | collective-permute-start | bytes 393224 | tf_op jit(solution)/shard_map/ppermute | solution.py:312
  16.8 10.3 %collective-permute-start.3 = (bf16[32,2176]{1,0:T(8,128)(2,1)S(1)}, bf16[32,2176]{1,0:T(8,128)(2,1)S(1)}, u32[]{:S(2)}, u32[]{:S(2)}) collective-permute-start(bf16[32,2176]{1,0:T(8,128)(2,1)S(1)} %get-tuple-element.24), channel_id=1, source_target_pairs={{0,4},{4,0},{8,12},{12,8},{16,20},{20,16},{24,28},{28,24},{1,5},{5... | collective-permute-start | bytes 417800 | tf_op jit(solution)/shard_map/ppermute | solution.py:312
  20.5 8.1 %collective-permute-start.4 = (bf16[32,2176]{1,0:T(8,128)(2,1)S(1)}, bf16[32,2176]{1,0:T(8,128)(2,1)S(1)}, u32[]{:S(2)}, u32[]{:S(2)}) collective-permute-start(bf16[32,2176]{1,0:T(8,128)(2,1)S(1)} %get-tuple-element.25), channel_id=1, source_target_pairs={{0,8},{4,12},{8,0},{12,4},{16,24},{20,28},{24,16},{28,20},{1,9},{5... | collective-permute-start | bytes 417800 | tf_op jit(solution)/shard_map/ppermute | solution.py:312
  20.5 30.1 %copy-start = (bf16[2048,1024]{1,0:T(8,128)(2,1)S(1)}, bf16[2048,1024]{1,0:T(8,128)(2,1)}, u32[]{:S(2)}) copy-start(bf16[2048,1024]{1,0:T(8,128)(2,1)} %refs_4_.3) | copy-start | bytes 12582916
  20.5 8.0 %collective-permute-start.5 = (bf16[32,2176]{1,0:T(8,128)(2,1)S(1)}, bf16[32,2176]{1,0:T(8,128)(2,1)S(1)}, u32[]{:S(2)}, u32[]{:S(2)}) collective-permute-start(bf16[32,2176]{1,0:T(8,128)(2,1)S(1)} %get-tuple-element.26), channel_id=1, source_target_pairs={{0,12},{4,8},{8,4},{12,0},{16,28},{20,24},{24,20},{28,16},{1,13},{... | collective-permute-start | bytes 417800 | tf_op jit(solution)/shard_map/ppermute | solution.py:312
  22.7 8.4 %collective-permute-start.10 = (bf16[32,2176]{1,0:T(8,128)(2,1)S(1)}, bf16[32,2176]{1,0:T(8,128)(2,1)S(1)}, u32[]{:S(2)}, u32[]{:S(2)}) collective-permute-start(bf16[32,2176]{1,0:T(8,128)(2,1)S(1)} %get-tuple-element.28), channel_id=1, source_target_pairs={{0,4},{4,0},{8,12},{12,8},{16,20},{20,16},{24,28},{28,24},{1,5},{5... | collective-permute-start | bytes 417800 | tf_op jit(solution)/shard_map/ppermute | solution.py:312
  27.0 6.1 %collective-permute-start.11 = (bf16[32,2176]{1,0:T(8,128)(2,1)S(1)}, bf16[32,2176]{1,0:T(8,128)(2,1)S(1)}, u32[]{:S(2)}, u32[]{:S(2)}) collective-permute-start(bf16[32,2176]{1,0:T(8,128)(2,1)S(1)} %get-tuple-element.29), channel_id=1, source_target_pairs={{0,8},{4,12},{8,0},{12,4},{16,24},{20,28},{24,16},{28,20},{1,9},{5... | collective-permute-start | bytes 417800 | tf_op jit(solution)/shard_map/ppermute | solution.py:312
  27.0 7.5 %collective-permute-start.12 = (bf16[32,2176]{1,0:T(8,128)(2,1)S(1)}, bf16[32,2176]{1,0:T(8,128)(2,1)S(1)}, u32[]{:S(2)}, u32[]{:S(2)}) collective-permute-start(bf16[32,2176]{1,0:T(8,128)(2,1)S(1)} %get-tuple-element.30), channel_id=1, source_target_pairs={{0,12},{4,8},{8,4},{12,0},{16,28},{20,24},{24,20},{28,16},{1,13},{... | collective-permute-start | bytes 417800 | tf_op jit(solution)/shard_map/ppermute | solution.py:312
  29.0 10.4 %collective-permute-start.18 = (bf16[32,2176]{1,0:T(8,128)(2,1)S(1)}, bf16[32,2176]{1,0:T(8,128)(2,1)S(1)}, u32[]{:S(2)}, u32[]{:S(2)}) collective-permute-start(bf16[32,2176]{1,0:T(8,128)(2,1)S(1)} %shard_map.75.near), channel_id=1, source_target_pairs={{0,16},{4,20},{8,24},{12,28},{16,0},{20,4},{24,8},{28,12},{1,17},{... | collective-permute-start | bytes 417800 | tf_op jit(solution)/shard_map/ppermute | solution.py:312
  35.0 8.3 %collective-permute-start.13 = (bf16[32,2176]{1,0:T(8,128)(2,1)S(1)}, bf16[32,2176]{1,0:T(8,128)(2,1)S(1)}, u32[]{:S(2)}, u32[]{:S(2)}) collective-permute-start(bf16[32,2176]{1,0:T(8,128)(2,1)S(1)} %shard_map.77.near), channel_id=1, source_target_pairs={{0,16},{4,20},{8,24},{12,28},{16,0},{20,4},{24,8},{28,12},{1,17},{... | collective-permute-start | bytes 417800 | tf_op jit(solution)/shard_map/ppermute | solution.py:312
  39.7 7.2 %collective-permute-start.19 = (bf16[32,2048]{1,0:T(8,128)(2,1)S(1)}, bf16[32,2048]{1,0:T(8,128)(2,1)S(1)}, u32[]{:S(2)}, u32[]{:S(2)}) collective-permute-start(bf16[32,2048]{1,0:T(8,128)(2,1)S(1)} %shard_map.80.refs_0_), channel_id=1, source_target_pairs={{0,4},{4,0},{8,12},{12,8},{16,20},{20,16},{24,28},{28,24},{1,5},{5... | collective-permute-start | bytes 393224 | tf_op jit(solution)/shard_map/ppermute | solution.py:312
  41.4 6.3 %collective-permute-start.20 = (bf16[32,2048]{1,0:T(8,128)(2,1)S(1)}, bf16[32,2048]{1,0:T(8,128)(2,1)S(1)}, u32[]{:S(2)}, u32[]{:S(2)}) collective-permute-start(bf16[32,2048]{1,0:T(8,128)(2,1)S(1)} %shard_map.80.refs_0_), channel_id=1, source_target_pairs={{0,8},{4,12},{8,0},{12,4},{16,24},{20,28},{24,16},{28,20},{1,9},{5... | collective-permute-start | bytes 393224 | tf_op jit(solution)/shard_map/ppermute | solution.py:312
  41.4 9.2 %collective-permute-start.21 = (bf16[32,2048]{1,0:T(8,128)(2,1)S(1)}, bf16[32,2048]{1,0:T(8,128)(2,1)S(1)}, u32[]{:S(2)}, u32[]{:S(2)}) collective-permute-start(bf16[32,2048]{1,0:T(8,128)(2,1)S(1)} %shard_map.80.refs_0_), channel_id=1, source_target_pairs={{0,12},{4,8},{8,4},{12,0},{16,28},{20,24},{24,20},{28,16},{1,13},{... | collective-permute-start | bytes 393224 | tf_op jit(solution)/shard_map/ppermute | solution.py:312
  43.6 7.9 %collective-permute-start.14 = (bf16[32,2048]{1,0:T(8,128)(2,1)S(1)}, bf16[32,2048]{1,0:T(8,128)(2,1)S(1)}, u32[]{:S(2)}, u32[]{:S(2)}) collective-permute-start(bf16[32,2048]{1,0:T(8,128)(2,1)S(1)} %shard_map.78.refs_0_), channel_id=1, source_target_pairs={{0,4},{4,0},{8,12},{12,8},{16,20},{20,16},{24,28},{28,24},{1,5},{5... | collective-permute-start | bytes 393224 | tf_op jit(solution)/shard_map/ppermute | solution.py:312
  45.7 5.8 %collective-permute-start.15 = (bf16[32,2048]{1,0:T(8,128)(2,1)S(1)}, bf16[32,2048]{1,0:T(8,128)(2,1)S(1)}, u32[]{:S(2)}, u32[]{:S(2)}) collective-permute-start(bf16[32,2048]{1,0:T(8,128)(2,1)S(1)} %shard_map.78.refs_0_), channel_id=1, source_target_pairs={{0,8},{4,12},{8,0},{12,4},{16,24},{20,28},{24,16},{28,20},{1,9},{5... | collective-permute-start | bytes 393224 | tf_op jit(solution)/shard_map/ppermute | solution.py:312
  46.9 6.8 %collective-permute-start.16 = (bf16[32,2048]{1,0:T(8,128)(2,1)S(1)}, bf16[32,2048]{1,0:T(8,128)(2,1)S(1)}, u32[]{:S(2)}, u32[]{:S(2)}) collective-permute-start(bf16[32,2048]{1,0:T(8,128)(2,1)S(1)} %shard_map.78.refs_0_), channel_id=1, source_target_pairs={{0,12},{4,8},{8,4},{12,0},{16,28},{20,24},{24,20},{28,16},{1,13},{... | collective-permute-start | bytes 393224 | tf_op jit(solution)/shard_map/ppermute | solution.py:312
  51.4 3.3 %collective-permute-start.22 = (bf16[64,1024]{1,0:T(8,128)(2,1)S(1)}, bf16[64,1024]{1,0:T(8,128)(2,1)S(1)}, u32[]{:S(2)}, u32[]{:S(2)}) collective-permute-start(bf16[64,1024]{1,0:T(8,128)(2,1)S(1)} %get-tuple-element.34), channel_id=1, source_target_pairs={{0,1},{1,0},{2,3},{3,2},{4,5},{5,4},{6,7},{7,6},{8,9},{9,8},{10,11... | collective-permute-start | bytes 393224 | tf_op jit(solution)/shard_map/ppermute | solution.py:312
  54.5 1.4 %collective-permute-start.17 = (bf16[64,1024]{1,0:T(8,128)(2,1)S(1)}, bf16[64,1024]{1,0:T(8,128)(2,1)S(1)}, u32[]{:S(2)}, u32[]{:S(2)}) collective-permute-start(bf16[64,1024]{1,0:T(8,128)(2,1)S(1)} %get-tuple-element.32), channel_id=1, source_target_pairs={{0,1},{1,0},{2,3},{3,2},{4,5},{5,4},{6,7},{7,6},{8,9},{9,8},{10,11... | collective-permute-start | bytes 393224 | tf_op jit(solution)/shard_map/ppermute | solution.py:312
  56.0 5.6 %collective-permute-start.23 = (bf16[64,1024]{1,0:T(8,128)(2,1)S(1)}, bf16[64,1024]{1,0:T(8,128)(2,1)S(1)}, u32[]{:S(2)}, u32[]{:S(2)}) collective-permute-start(bf16[64,1024]{1,0:T(8,128)(2,1)S(1)} %select_convert_fusion), channel_id=1, source_target_pairs={{0,2},{1,3},{2,0},{3,1},{4,6},{5,7},{6,4},{7,5},{8,10},{9,11},{10,... | collective-permute-start | bytes 393224 | tf_op jit(solution)/shard_map/ppermute | solution.py:312

commit v10 on v9

--- a/solution.py
+++ b/solution.py
@@ -326,7 +326,7 @@
     for lb, rows in enumerate((queries, far)):
         chunks = spread(rows, plan)
         outs = attend(plan, heads, lb, pages, [chunks[k] for k in range(plan.group)])
-        near.append(merge(heads, outs[0], *(swap(outs[k], "pages", k) for k in others(plan))))
+        near.append(merge(heads, *(swap(outs[k], "pages", k) for k in reversed(others(plan))), outs[0]))
     across = [swap(x, "pages", plan.cross) for x in near]
     sums = [None, None]
     for lb in (1, 0):

time: 62.3 us -> 64.2 us (1.030)
  Pallas kernels: 6.65 us -> 12.1 us
  starting transfers between devices: 32.8 us -> 27.7 us
  waiting for transfers between devices: 22 us -> 23.4 us
    ppermute x24, starting transfers between devices: 32.8 us -> 27.7 us  [swap(): return lax.ppermute(x, axis, [(i, i ^ distance) for i in range(n)])]
    pallas_call x2, Pallas kernels: 1.29 us -> 5.87 us  [attend(): pl.pallas_call(functools.partial(attend_kernel, plan, heads, lb), out_sha...]
    ppermute x24, waiting for transfers between devices: 22 us -> 23.4 us  [swap(): return lax.ppermute(x, axis, [(i, i ^ distance) for i in range(n)])]
    pallas_call x1, Pallas kernels: 2.19 us -> 3 us  [fetch(): pl.pallas_call(functools.partial(fetch_kernel, plan, pages_dev), out_shap...]
  transfers between devices with their start and end apart: 24 -> 24, of which waited for: 12 -> 13; matrix products, arithmetic and copies ran while one was open for 0% -> 0% of each run, Pallas kernels for 11% -> 19%
where the time goes in v10:
time: 64.2 us; the launch traced here: 64 us
  starting transfers between devices  27.7 us (43%)
  waiting for transfers between devices  23.4 us (36%)
  Pallas kernels  12.1 us (19%)
  other arithmetic  0.78 us (1%)
    ppermute x24, starting transfers between devices, swap(): return lax.ppermute(x, axis, [(i, i ^ distance) for i in range(n)])  27.7 us
    ppermute x24, waiting for transfers between devices, swap(): return lax.ppermute(x, axis, [(i, i ^ distance) for i in range(n)])  23.4 us
    pallas_call x2, Pallas kernels, attend(): pl.pallas_call(functools.partial(attend_kernel, plan, heads, lb), out_sha...  5.87 us
    pallas_call x1, Pallas kernels, fetch(): pl.pallas_call(functools.partial(fetch_kernel, plan, pages_dev), out_shap...  3 us
    pallas_call x2, Pallas kernels, project(): pl.pallas_call(functools.partial(project_kernel, plan, lb), out_shape=(ja...  1.57 us
  transfers between devices with their start and end apart: 24, of which 13 were waited for; matrix products, arithmetic and copies ran while one was open for 0% of the time, Pallas kernels for 19%

profile of v10, /device:TPU:0, one launch (start us, length us, event | category | flops | bytes accessed | tf_op | source)
XLA Modules:
  0.0 64.0 jit_solution(1918157181438533122)
XLA Ops:
  0.0 4.0 %collective-permute-start.6 = (bf16[32,2048]{1,0:T(8,128)(2,1)}, bf16[32,2048]{1,0:T(8,128)(2,1)S(1)}, u32[]{:S(2)}, u32[]{:S(2)}) collective-permute-start(bf16[32,2048]{1,0:T(8,128)(2,1)} %refs_0_.1), channel_id=1, source_target_pairs={{0,16},{4,20},{8,24},{12,28},{16,0},{20,4},{24,8},{28,12},{1,17},{... | collective-permute-start | bytes 393224 | tf_op jit(solution)/shard_map/ppermute | solution.py:312
  4.0 1.5 %collective-permute-start = (bf16[32,2048]{1,0:T(8,128)(2,1)}, bf16[32,2048]{1,0:T(8,128)(2,1)S(1)}, u32[]{:S(2)}, u32[]{:S(2)}) collective-permute-start(bf16[32,2048]{1,0:T(8,128)(2,1)} %refs_0_.1), channel_id=1, source_target_pairs={{0,4},{4,0},{8,12},{12,8},{16,20},{20,16},{24,28},{28,24},{1,5},{5... | collective-permute-start | bytes 393224 | tf_op jit(solution)/shard_map/ppermute | solution.py:312
  5.5 1.6 %collective-permute-start.1 = (bf16[32,2048]{1,0:T(8,128)(2,1)}, bf16[32,2048]{1,0:T(8,128)(2,1)S(1)}, u32[]{:S(2)}, u32[]{:S(2)}) collective-permute-start(bf16[32,2048]{1,0:T(8,128)(2,1)} %refs_0_.1), channel_id=1, source_target_pairs={{0,8},{4,12},{8,0},{12,4},{16,24},{20,28},{24,16},{28,20},{1,9},{5... | collective-permute-start | bytes 393224 | tf_op jit(solution)/shard_map/ppermute | solution.py:312
  7.1 0.4 collective-permute-start.2
  7.5 3.0 %shard_map.73 = (bf16[2,2,768,128]{3,2,1,0:T(8,128)(2,1)S(1)}, bf16[2,2,768,256]{3,2,1,0:T(8,128)(2,1)S(1)}, s32[2,3]{1,0:T(2,128)S(1)}) custom-call(s32[2,24]{1,0:T(2,128)} %select_hbm.1, s32[128]{0:T(128)} %table_hbm.1, s32[2]{0:T(128)} %stands_hbm.1, bf16[16,256,128]{2,1,0:T(8,128)(2,1)} %bitcast.2, bf16[16,256,128]{2,1,0:T(8,128)(2,1)} %bitcast.3), custom_call_target="tpu_custom_call" | custom-call | flops 2000000000 | bytes 8388608 | tf_op jit(solution)/shard_map/pallas_call | solution.py:118
  10.5 0.2 collective-permute-done.6.refs_0_
  10.7 1.5 %collective-permute-start.7 = (bf16[32,2048]{1,0:T(8,128)(2,1)S(1)}, bf16[32,2048]{1,0:T(8,128)(2,1)S(1)}, u32[]{:S(2)}, u32[]{:S(2)}) collective-permute-start(bf16[32,2048]{1,0:T(8,128)(2,1)S(1)} %collective-permute-done.6.refs_0_), channel_id=1, source_target_pairs={{0,4},{4,0},{8,12},{12,8},{16,20},{20,16},{24,28},{28,24},{1,5},{5... | collective-permute-start | bytes 393224 | tf_op jit(solution)/shard_map/ppermute | solution.py:312
  12.2 0.7 %collective-permute-start.8 = (bf16[32,2048]{1,0:T(8,128)(2,1)S(1)}, bf16[32,2048]{1,0:T(8,128)(2,1)S(1)}, u32[]{:S(2)}, u32[]{:S(2)}) collective-permute-start(bf16[32,2048]{1,0:T(8,128)(2,1)S(1)} %collective-permute-done.6.refs_0_), channel_id=1, source_target_pairs={{0,8},{4,12},{8,0},{12,4},{16,24},{20,28},{24,16},{28,20},{1,9},{5... | collective-permute-start | bytes 393224 | tf_op jit(solution)/shard_map/ppermute | solution.py:312
  12.9 1.3 %collective-permute-start.9 = (bf16[32,2048]{1,0:T(8,128)(2,1)S(1)}, bf16[32,2048]{1,0:T(8,128)(2,1)S(1)}, u32[]{:S(2)}, u32[]{:S(2)}) collective-permute-start(bf16[32,2048]{1,0:T(8,128)(2,1)S(1)} %collective-permute-done.6.refs_0_), channel_id=1, source_target_pairs={{0,12},{4,8},{8,4},{12,0},{16,28},{20,24},{24,20},{28,16},{1,13},{... | collective-permute-start | bytes 393224 | tf_op jit(solution)/shard_map/ppermute | solution.py:312
  14.2 1.9 %collective-permute-done.2.refs_3_ = bf16[32,2048]{1,0:T(8,128)(2,1)S(1)} collective-permute-done((bf16[32,2048]{1,0:T(8,128)(2,1)}, bf16[32,2048]{1,0:T(8,128)(2,1)S(1)}, u32[]{:S(2)}, u32[]{:S(2)}) %collective-permute-start.2) | collective-permute-done | bytes 131104 | tf_op jit(solution)/shard_map/ppermute | solution.py:312
  16.1 2.9 %shard_map.74 = (bf16[32,2176]{1,0:T(8,128)(2,1)S(1)}, bf16[32,2176]{1,0:T(8,128)(2,1)S(1)}, bf16[32,2176]{1,0:T(8,128)(2,1)S(1)}, bf16[32,2176]{1,0:T(8,128)(2,1)S(1)}) custom-call(s32[2,3]{1,0:T(2,128)S(1)} %get-tuple-element.20.info, bf16[32,2048]{1,0:T(8,128)(2,1)S(1)} %copy-done.1, bf16[32,2048]{1,0:T(8,128)(2,1)S(1)} %collective-permute-done.refs_1_, ...), custom_call_target="tpu_custom_call" | custom-call | flops 2000000000 | bytes 4194304 | tf_op jit(solution)/shard_map/pallas_call | solution.py:216
  19.1 0.1 collective-permute-start.3
  19.1 2.8 %collective-permute-start.4 = (bf16[32,2176]{1,0:T(8,128)(2,1)S(1)}, bf16[32,2176]{1,0:T(8,128)(2,1)S(1)}, u32[]{:S(2)}, u32[]{:S(2)}) collective-permute-start(bf16[32,2176]{1,0:T(8,128)(2,1)S(1)} %get-tuple-element.24), channel_id=1, source_target_pairs={{0,8},{4,12},{8,0},{12,4},{16,24},{20,28},{24,16},{28,20},{1,9},{5... | collective-permute-start | bytes 417800 | tf_op jit(solution)/shard_map/ppermute | solution.py:312
  21.9 0.0 collective-permute-done.7.refs_1_
  21.9 0.7 %collective-permute-start.5 = (bf16[32,2176]{1,0:T(8,128)(2,1)S(1)}, bf16[32,2176]{1,0:T(8,128)(2,1)S(1)}, u32[]{:S(2)}, u32[]{:S(2)}) collective-permute-start(bf16[32,2176]{1,0:T(8,128)(2,1)S(1)} %get-tuple-element.25), channel_id=1, source_target_pairs={{0,4},{4,0},{8,12},{12,8},{16,20},{20,16},{24,28},{28,24},{1,5},{5... | collective-permute-start | bytes 417800 | tf_op jit(solution)/shard_map/ppermute | solution.py:312
  22.6 0.0 collective-permute-done.9.refs_3_
  22.6 2.9 %shard_map.76 = (bf16[32,2176]{1,0:T(8,128)(2,1)S(1)}, bf16[32,2176]{1,0:T(8,128)(2,1)S(1)}, bf16[32,2176]{1,0:T(8,128)(2,1)S(1)}, bf16[32,2176]{1,0:T(8,128)(2,1)S(1)}) custom-call(s32[2,3]{1,0:T(2,128)S(1)} %get-tuple-element.20.info, bf16[32,2048]{1,0:T(8,128)(2,1)S(1)} %collective-permute-done.6.refs_0_, ...), custom_call_target="tpu_custom_call" | custom-call | flops 2000000000 | bytes 4194304 | tf_op jit(solution)/shard_map/pallas_call | solution.py:216
  25.6 0.1 collective-permute-start.10
  25.6 2.8 %collective-permute-start.11 = (bf16[32,2176]{1,0:T(8,128)(2,1)S(1)}, bf16[32,2176]{1,0:T(8,128)(2,1)S(1)}, u32[]{:S(2)}, u32[]{:S(2)}) collective-permute-start(bf16[32,2176]{1,0:T(8,128)(2,1)S(1)} %get-tuple-element.28), channel_id=1, source_target_pairs={{0,8},{4,12},{8,0},{12,4},{16,24},{20,28},{24,16},{28,20},{1,9},{5... | collective-permute-start | bytes 417800 | tf_op jit(solution)/shard_map/ppermute | solution.py:312
  28.4 0.7 %collective-permute-start.12 = (bf16[32,2176]{1,0:T(8,128)(2,1)S(1)}, bf16[32,2176]{1,0:T(8,128)(2,1)S(1)}, u32[]{:S(2)}, u32[]{:S(2)}) collective-permute-start(bf16[32,2176]{1,0:T(8,128)(2,1)S(1)} %get-tuple-element.29), channel_id=1, source_target_pairs={{0,4},{4,0},{8,12},{12,8},{16,20},{20,16},{24,28},{28,24},{1,5},{5... | collective-permute-start | bytes 417800 | tf_op jit(solution)/shard_map/ppermute | solution.py:312
  29.1 0.5 shard_map.75.near
  29.6 0.5 collective-permute-start.18
  30.1 3.1 %collective-permute-done.10.refs_0_ = bf16[32,2176]{1,0:T(8,128)(2,1)S(1)} collective-permute-done((bf16[32,2176]{1,0:T(8,128)(2,1)S(1)}, bf16[32,2176]{1,0:T(8,128)(2,1)S(1)}, u32[]{:S(2)}, u32[]{:S(2)}) %collective-permute-start.10) | collective-permute-done | bytes 139296 | tf_op jit(solution)/shard_map/ppermute | solution.py:312
  33.2 0.8 %collective-permute-done.11.refs_1_ = bf16[32,2176]{1,0:T(8,128)(2,1)S(1)} collective-permute-done((bf16[32,2176]{1,0:T(8,128)(2,1)S(1)}, bf16[32,2176]{1,0:T(8,128)(2,1)S(1)}, u32[]{:S(2)}, u32[]{:S(2)}) %collective-permute-start.11) | collective-permute-done | bytes 139296 | tf_op jit(solution)/shard_map/ppermute | solution.py:312
  34.0 0.6 collective-permute-done.12.refs_2_
  34.6 0.5 shard_map.77.near
  35.0 1.4 %collective-permute-start.13 = (bf16[32,2176]{1,0:T(8,128)(2,1)S(1)}, bf16[32,2176]{1,0:T(8,128)(2,1)S(1)}, u32[]{:S(2)}, u32[]{:S(2)}) collective-permute-start(bf16[32,2176]{1,0:T(8,128)(2,1)S(1)} %shard_map.77.near), channel_id=1, source_target_pairs={{0,16},{4,20},{8,24},{12,28},{16,0},{20,4},{24,8},{28,12},{1,17},{... | collective-permute-start | bytes 417800 | tf_op jit(solution)/shard_map/ppermute | solution.py:312
  36.4 5.3 %collective-permute-done.18.far = bf16[32,2176]{1,0:T(8,128)(2,1)S(1)} collective-permute-done((bf16[32,2176]{1,0:T(8,128)(2,1)S(1)}, bf16[32,2176]{1,0:T(8,128)(2,1)S(1)}, u32[]{:S(2)}, u32[]{:S(2)}) %collective-permute-start.18) | collective-permute-done | bytes 139296 | tf_op jit(solution)/shard_map/ppermute | solution.py:312
  41.7 0.3 shard_map.80.refs_0_
  42.0 1.6 %collective-permute-start.19 = (bf16[32,2048]{1,0:T(8,128)(2,1)S(1)}, bf16[32,2048]{1,0:T(8,128)(2,1)S(1)}, u32[]{:S(2)}, u32[]{:S(2)}) collective-permute-start(bf16[32,2048]{1,0:T(8,128)(2,1)S(1)} %shard_map.80.refs_0_), channel_id=1, source_target_pairs={{0,4},{4,0},{8,12},{12,8},{16,20},{20,16},{24,28},{28,24},{1,5},{5... | collective-permute-start | bytes 393224 | tf_op jit(solution)/shard_map/ppermute | solution.py:312
  43.7 1.9 %collective-permute-start.21 = (bf16[32,2048]{1,0:T(8,128)(2,1)S(1)}, bf16[32,2048]{1,0:T(8,128)(2,1)S(1)}, u32[]{:S(2)}, u32[]{:S(2)}) collective-permute-start(bf16[32,2048]{1,0:T(8,128)(2,1)S(1)} %shard_map.80.refs_0_), channel_id=1, source_target_pairs={{0,12},{4,8},{8,4},{12,0},{16,28},{20,24},{24,20},{28,16},{1,13},{... | collective-permute-start | bytes 393224 | tf_op jit(solution)/shard_map/ppermute | solution.py:312
  45.6 0.3 shard_map.78.refs_0_
  45.9 1.7 %collective-permute-start.14 = (bf16[32,2048]{1,0:T(8,128)(2,1)S(1)}, bf16[32,2048]{1,0:T(8,128)(2,1)S(1)}, u32[]{:S(2)}, u32[]{:S(2)}) collective-permute-start(bf16[32,2048]{1,0:T(8,128)(2,1)S(1)} %shard_map.78.refs_0_), channel_id=1, source_target_pairs={{0,4},{4,0},{8,12},{12,8},{16,20},{20,16},{24,28},{28,24},{1,5},{5... | collective-permute-start | bytes 393224 | tf_op jit(solution)/shard_map/ppermute | solution.py:312
  47.6 1.1 %collective-permute-done.19.refs_1_ = bf16[32,2048]{1,0:T(8,128)(2,1)S(1)} collective-permute-done((bf16[32,2048]{1,0:T(8,128)(2,1)S(1)}, bf16[32,2048]{1,0:T(8,128)(2,1)S(1)}, u32[]{:S(2)}, u32[]{:S(2)}) %collective-permute-start.19) | collective-permute-done | bytes 131104 | tf_op jit(solution)/shard_map/ppermute | solution.py:312
  48.7 0.8 %collective-permute-start.16 = (bf16[32,2048]{1,0:T(8,128)(2,1)S(1)}, bf16[32,2048]{1,0:T(8,128)(2,1)S(1)}, u32[]{:S(2)}, u32[]{:S(2)}) collective-permute-start(bf16[32,2048]{1,0:T(8,128)(2,1)S(1)} %shard_map.78.refs_0_), channel_id=1, source_target_pairs={{0,12},{4,8},{8,4},{12,0},{16,28},{20,24},{24,20},{28,16},{1,13},{... | collective-permute-start | bytes 393224 | tf_op jit(solution)/shard_map/ppermute | solution.py:312
  49.5 0.6 collective-permute-done.20.refs_2_
  50.1 2.6 %collective-permute-done.21.refs_3_ = bf16[32,2048]{1,0:T(8,128)(2,1)S(1)} collective-permute-done((bf16[32,2048]{1,0:T(8,128)(2,1)S(1)}, bf16[32,2048]{1,0:T(8,128)(2,1)S(1)}, u32[]{:S(2)}, u32[]{:S(2)}) %collective-permute-start.21) | collective-permute-done | bytes 131104 | tf_op jit(solution)/shard_map/ppermute | solution.py:312
  52.7 0.8 %shard_map.81 = (f32[64,1024]{1,0:T(8,128)S(1)}, bf16[64,1024]{1,0:T(8,128)(2,1)S(1)}) custom-call(bf16[32,2048]{1,0:T(8,128)(2,1)S(1)} %shard_map.80.refs_0_, bf16[32,2048]{1,0:T(8,128)(2,1)S(1)} %collective-permute-done.19.refs_1_, bf16[32,2048]{1,0:T(8,128)(2,1)S(1)} %collective-permute-done.20.refs_2_, ...), custom_call_target="tpu_custom_call" | custom-call | tf_op jit(solution)/shard_map/pallas_call | solution.py:300
  53.5 0.1 collective-permute-start.22
  53.6 0.2 collective-permute-done.14.refs_1_
  53.8 1.7 %collective-permute-done.16.refs_3_ = bf16[32,2048]{1,0:T(8,128)(2,1)S(1)} collective-permute-done((bf16[32,2048]{1,0:T(8,128)(2,1)S(1)}, bf16[32,2048]{1,0:T(8,128)(2,1)S(1)}, u32[]{:S(2)}, u32[]{:S(2)}) %collective-permute-start.16) | collective-permute-done | bytes 131104 | tf_op jit(solution)/shard_map/ppermute | solution.py:312
  55.4 0.8 %shard_map.79 = (f32[64,1024]{1,0:T(8,128)S(1)}, bf16[64,1024]{1,0:T(8,128)(2,1)S(1)}) custom-call(bf16[32,2048]{1,0:T(8,128)(2,1)S(1)} %shard_map.78.refs_0_, bf16[32,2048]{1,0:T(8,128)(2,1)S(1)} %collective-permute-done.14.refs_1_, bf16[32,2048]{1,0:T(8,128)(2,1)S(1)} %collective-permute-done.15.refs_2_, ...), custom_call_target="tpu_custom_call" | custom-call | tf_op jit(solution)/shard_map/pallas_call | solution.py:300
  56.2 0.1 collective-permute-start.17
  56.3 1.3 %collective-permute-done.17 = bf16[64,1024]{1,0:T(8,128)(2,1)S(1)} collective-permute-done((bf16[64,1024]{1,0:T(8,128)(2,1)S(1)}, bf16[64,1024]{1,0:T(8,128)(2,1)S(1)}, u32[]{:S(2)}, u32[]{:S(2)}) %collective-permute-start.17) | collective-permute-done | bytes 131104 | tf_op jit(solution)/shard_map/ppermute | solution.py:312
  57.6 0.1 select_convert_fusion
  57.7 1.6 %collective-permute-start.23 = (bf16[64,1024]{1,0:T(8,128)(2,1)S(1)}, bf16[64,1024]{1,0:T(8,128)(2,1)S(1)}, u32[]{:S(2)}, u32[]{:S(2)}) collective-permute-start(bf16[64,1024]{1,0:T(8,128)(2,1)S(1)} %select_convert_fusion), channel_id=1, source_target_pairs={{0,2},{1,3},{2,0},{3,1},{4,6},{5,7},{6,4},{7,5},{8,10},{9,11},{10,... | collective-permute-start | bytes 393224 | tf_op jit(solution)/shard_map/ppermute | solution.py:312
  59.3 4.0 %collective-permute-done.23 = bf16[64,1024]{1,0:T(8,128)(2,1)S(1)} collective-permute-done((bf16[64,1024]{1,0:T(8,128)(2,1)S(1)}, bf16[64,1024]{1,0:T(8,128)(2,1)S(1)}, u32[]{:S(2)}, u32[]{:S(2)}) %collective-permute-start.23) | collective-permute-done | bytes 131104 | tf_op jit(solution)/shard_map/ppermute | solution.py:312
  63.3 0.7 %add_convert_fusion = bf16[64,1024]{1,0:T(8,128)(2,1)} fusion(bf16[64,1024]{1,0:T(8,128)(2,1)S(1)} %collective-permute-done.23, f32[64,1024]{1,0:T(8,128)S(1)} %get-tuple-element.31, bf16[64,1024]{1,0:T(8,128)(2,1)S(1)} %collective-permute-done.17, f32[64,1024]{1,0:T(8,128)S(1)} %get-tuple-element.33, bf16[64,1024]{1,0:T(8,128)(2,1)S(1)} %collective-permute-done.22, ...), kind=kLoop, calls=%fused_computation | loop fusion | flops 524288 | bytes 1048577 | tf_op jit(solution)/shard_map/convert_element_type | solution.py:339
  (15 shorter events, 0.0 us)
Async XLA Ops:
  0.0 16.1 %copy-start.1 = (bf16[32,2048]{1,0:T(8,128)(2,1)S(1)}, bf16[32,2048]{1,0:T(8,128)(2,1)}, u32[]{:S(2)}) copy-start(bf16[32,2048]{1,0:T(8,128)(2,1)} %refs_0_.1) | copy-start | bytes 393220
  0.0 10.7 %collective-permute-start.6 = (bf16[32,2048]{1,0:T(8,128)(2,1)}, bf16[32,2048]{1,0:T(8,128)(2,1)S(1)}, u32[]{:S(2)}, u32[]{:S(2)}) collective-permute-start(bf16[32,2048]{1,0:T(8,128)(2,1)} %refs_0_.1), channel_id=1, source_target_pairs={{0,16},{4,20},{8,24},{12,28},{16,0},{20,4},{24,8},{28,12},{1,17},{... | collective-permute-start | bytes 393224 | tf_op jit(solution)/shard_map/ppermute | solution.py:312
  4.0 8.9 %collective-permute-start = (bf16[32,2048]{1,0:T(8,128)(2,1)}, bf16[32,2048]{1,0:T(8,128)(2,1)S(1)}, u32[]{:S(2)}, u32[]{:S(2)}) collective-permute-start(bf16[32,2048]{1,0:T(8,128)(2,1)} %refs_0_.1), channel_id=1, source_target_pairs={{0,4},{4,0},{8,12},{12,8},{16,20},{20,16},{24,28},{28,24},{1,5},{5... | collective-permute-start | bytes 393224 | tf_op jit(solution)/shard_map/ppermute | solution.py:312
  5.5 8.7 %collective-permute-start.1 = (bf16[32,2048]{1,0:T(8,128)(2,1)}, bf16[32,2048]{1,0:T(8,128)(2,1)S(1)}, u32[]{:S(2)}, u32[]{:S(2)}) collective-permute-start(bf16[32,2048]{1,0:T(8,128)(2,1)} %refs_0_.1), channel_id=1, source_target_pairs={{0,8},{4,12},{8,0},{12,4},{16,24},{20,28},{24,16},{28,20},{1,9},{5... | collective-permute-start | bytes 393224 | tf_op jit(solution)/shard_map/ppermute | solution.py:312
  7.1 9.0 %collective-permute-start.2 = (bf16[32,2048]{1,0:T(8,128)(2,1)}, bf16[32,2048]{1,0:T(8,128)(2,1)S(1)}, u32[]{:S(2)}, u32[]{:S(2)}) collective-permute-start(bf16[32,2048]{1,0:T(8,128)(2,1)} %refs_0_.1), channel_id=1, source_target_pairs={{0,12},{4,8},{8,4},{12,0},{16,28},{20,24},{24,20},{28,16},{1,13},{... | collective-permute-start | bytes 393224 | tf_op jit(solution)/shard_map/ppermute | solution.py:312
  10.7 11.2 %collective-permute-start.7 = (bf16[32,2048]{1,0:T(8,128)(2,1)S(1)}, bf16[32,2048]{1,0:T(8,128)(2,1)S(1)}, u32[]{:S(2)}, u32[]{:S(2)}) collective-permute-start(bf16[32,2048]{1,0:T(8,128)(2,1)S(1)} %collective-permute-done.6.refs_0_), channel_id=1, source_target_pairs={{0,4},{4,0},{8,12},{12,8},{16,20},{20,16},{24,28},{28,24},{1,5},{5... | collective-permute-start | bytes 393224 | tf_op jit(solution)/shard_map/ppermute | solution.py:312
  12.2 10.4 %collective-permute-start.8 = (bf16[32,2048]{1,0:T(8,128)(2,1)S(1)}, bf16[32,2048]{1,0:T(8,128)(2,1)S(1)}, u32[]{:S(2)}, u32[]{:S(2)}) collective-permute-start(bf16[32,2048]{1,0:T(8,128)(2,1)S(1)} %collective-permute-done.6.refs_0_), channel_id=1, source_target_pairs={{0,8},{4,12},{8,0},{12,4},{16,24},{20,28},{24,16},{28,20},{1,9},{5... | collective-permute-start | bytes 393224 | tf_op jit(solution)/shard_map/ppermute | solution.py:312
  12.9 9.7 %collective-permute-start.9 = (bf16[32,2048]{1,0:T(8,128)(2,1)S(1)}, bf16[32,2048]{1,0:T(8,128)(2,1)S(1)}, u32[]{:S(2)}, u32[]{:S(2)}) collective-permute-start(bf16[32,2048]{1,0:T(8,128)(2,1)S(1)} %collective-permute-done.6.refs_0_), channel_id=1, source_target_pairs={{0,12},{4,8},{8,4},{12,0},{16,28},{20,24},{24,20},{28,16},{1,13},{... | collective-permute-start | bytes 393224 | tf_op jit(solution)/shard_map/ppermute | solution.py:312
  19.1 9.4 %collective-permute-start.3 = (bf16[32,2176]{1,0:T(8,128)(2,1)S(1)}, bf16[32,2176]{1,0:T(8,128)(2,1)S(1)}, u32[]{:S(2)}, u32[]{:S(2)}) collective-permute-start(bf16[32,2176]{1,0:T(8,128)(2,1)S(1)} %get-tuple-element.23), channel_id=1, source_target_pairs={{0,12},{4,8},{8,4},{12,0},{16,28},{20,24},{24,20},{28,16},{1,13},{... | collective-permute-start | bytes 417800 | tf_op jit(solution)/shard_map/ppermute | solution.py:312
  19.1 10.0 %collective-permute-start.4 = (bf16[32,2176]{1,0:T(8,128)(2,1)S(1)}, bf16[32,2176]{1,0:T(8,128)(2,1)S(1)}, u32[]{:S(2)}, u32[]{:S(2)}) collective-permute-start(bf16[32,2176]{1,0:T(8,128)(2,1)S(1)} %get-tuple-element.24), channel_id=1, source_target_pairs={{0,8},{4,12},{8,0},{12,4},{16,24},{20,28},{24,16},{28,20},{1,9},{5... | collective-permute-start | bytes 417800 | tf_op jit(solution)/shard_map/ppermute | solution.py:312
  21.9 30.8 %copy-start = (bf16[2048,1024]{1,0:T(8,128)(2,1)S(1)}, bf16[2048,1024]{1,0:T(8,128)(2,1)}, u32[]{:S(2)}) copy-start(bf16[2048,1024]{1,0:T(8,128)(2,1)} %refs_4_.3) | copy-start | bytes 12582916
  21.9 7.2 %collective-permute-start.5 = (bf16[32,2176]{1,0:T(8,128)(2,1)S(1)}, bf16[32,2176]{1,0:T(8,128)(2,1)S(1)}, u32[]{:S(2)}, u32[]{:S(2)}) collective-permute-start(bf16[32,2176]{1,0:T(8,128)(2,1)S(1)} %get-tuple-element.25), channel_id=1, source_target_pairs={{0,4},{4,0},{8,12},{12,8},{16,20},{20,16},{24,28},{28,24},{1,5},{5... | collective-permute-start | bytes 417800 | tf_op jit(solution)/shard_map/ppermute | solution.py:312
  25.6 7.6 %collective-permute-start.10 = (bf16[32,2176]{1,0:T(8,128)(2,1)S(1)}, bf16[32,2176]{1,0:T(8,128)(2,1)S(1)}, u32[]{:S(2)}, u32[]{:S(2)}) collective-permute-start(bf16[32,2176]{1,0:T(8,128)(2,1)S(1)} %get-tuple-element.27), channel_id=1, source_target_pairs={{0,12},{4,8},{8,4},{12,0},{16,28},{20,24},{24,20},{28,16},{1,13},{... | collective-permute-start | bytes 417800 | tf_op jit(solution)/shard_map/ppermute | solution.py:312
  25.6 8.3 %collective-permute-start.11 = (bf16[32,2176]{1,0:T(8,128)(2,1)S(1)}, bf16[32,2176]{1,0:T(8,128)(2,1)S(1)}, u32[]{:S(2)}, u32[]{:S(2)}) collective-permute-start(bf16[32,2176]{1,0:T(8,128)(2,1)S(1)} %get-tuple-element.28), channel_id=1, source_target_pairs={{0,8},{4,12},{8,0},{12,4},{16,24},{20,28},{24,16},{28,20},{1,9},{5... | collective-permute-start | bytes 417800 | tf_op jit(solution)/shard_map/ppermute | solution.py:312
  28.4 6.1 %collective-permute-start.12 = (bf16[32,2176]{1,0:T(8,128)(2,1)S(1)}, bf16[32,2176]{1,0:T(8,128)(2,1)S(1)}, u32[]{:S(2)}, u32[]{:S(2)}) collective-permute-start(bf16[32,2176]{1,0:T(8,128)(2,1)S(1)} %get-tuple-element.29), channel_id=1, source_target_pairs={{0,4},{4,0},{8,12},{12,8},{16,20},{20,16},{24,28},{28,24},{1,5},{5... | collective-permute-start | bytes 417800 | tf_op jit(solution)/shard_map/ppermute | solution.py:312
  29.6 12.1 %collective-permute-start.18 = (bf16[32,2176]{1,0:T(8,128)(2,1)S(1)}, bf16[32,2176]{1,0:T(8,128)(2,1)S(1)}, u32[]{:S(2)}, u32[]{:S(2)}) collective-permute-start(bf16[32,2176]{1,0:T(8,128)(2,1)S(1)} %shard_map.75.near), channel_id=1, source_target_pairs={{0,16},{4,20},{8,24},{12,28},{16,0},{20,4},{24,8},{28,12},{1,17},{... | collective-permute-start | bytes 417800 | tf_op jit(solution)/shard_map/ppermute | solution.py:312
  35.0 10.5 %collective-permute-start.13 = (bf16[32,2176]{1,0:T(8,128)(2,1)S(1)}, bf16[32,2176]{1,0:T(8,128)(2,1)S(1)}, u32[]{:S(2)}, u32[]{:S(2)}) collective-permute-start(bf16[32,2176]{1,0:T(8,128)(2,1)S(1)} %shard_map.77.near), channel_id=1, source_target_pairs={{0,16},{4,20},{8,24},{12,28},{16,0},{20,4},{24,8},{28,12},{1,17},{... | collective-permute-start | bytes 417800 | tf_op jit(solution)/shard_map/ppermute | solution.py:312
  42.0 6.7 %collective-permute-start.19 = (bf16[32,2048]{1,0:T(8,128)(2,1)S(1)}, bf16[32,2048]{1,0:T(8,128)(2,1)S(1)}, u32[]{:S(2)}, u32[]{:S(2)}) collective-permute-start(bf16[32,2048]{1,0:T(8,128)(2,1)S(1)} %shard_map.80.refs_0_), channel_id=1, source_target_pairs={{0,4},{4,0},{8,12},{12,8},{16,20},{20,16},{24,28},{28,24},{1,5},{5... | collective-permute-start | bytes 393224 | tf_op jit(solution)/shard_map/ppermute | solution.py:312
  43.7 6.4 %collective-permute-start.20 = (bf16[32,2048]{1,0:T(8,128)(2,1)S(1)}, bf16[32,2048]{1,0:T(8,128)(2,1)S(1)}, u32[]{:S(2)}, u32[]{:S(2)}) collective-permute-start(bf16[32,2048]{1,0:T(8,128)(2,1)S(1)} %shard_map.80.refs_0_), channel_id=1, source_target_pairs={{0,8},{4,12},{8,0},{12,4},{16,24},{20,28},{24,16},{28,20},{1,9},{5... | collective-permute-start | bytes 393224 | tf_op jit(solution)/shard_map/ppermute | solution.py:312
  43.7 9.0 %collective-permute-start.21 = (bf16[32,2048]{1,0:T(8,128)(2,1)S(1)}, bf16[32,2048]{1,0:T(8,128)(2,1)S(1)}, u32[]{:S(2)}, u32[]{:S(2)}) collective-permute-start(bf16[32,2048]{1,0:T(8,128)(2,1)S(1)} %shard_map.80.refs_0_), channel_id=1, source_target_pairs={{0,12},{4,8},{8,4},{12,0},{16,28},{20,24},{24,20},{28,16},{1,13},{... | collective-permute-start | bytes 393224 | tf_op jit(solution)/shard_map/ppermute | solution.py:312
  45.9 7.8 %collective-permute-start.14 = (bf16[32,2048]{1,0:T(8,128)(2,1)S(1)}, bf16[32,2048]{1,0:T(8,128)(2,1)S(1)}, u32[]{:S(2)}, u32[]{:S(2)}) collective-permute-start(bf16[32,2048]{1,0:T(8,128)(2,1)S(1)} %shard_map.78.refs_0_), channel_id=1, source_target_pairs={{0,4},{4,0},{8,12},{12,8},{16,20},{20,16},{24,28},{28,24},{1,5},{5... | collective-permute-start | bytes 393224 | tf_op jit(solution)/shard_map/ppermute | solution.py:312
  47.6 6.2 %collective-permute-start.15 = (bf16[32,2048]{1,0:T(8,128)(2,1)S(1)}, bf16[32,2048]{1,0:T(8,128)(2,1)S(1)}, u32[]{:S(2)}, u32[]{:S(2)}) collective-permute-start(bf16[32,2048]{1,0:T(8,128)(2,1)S(1)} %shard_map.78.refs_0_), channel_id=1, source_target_pairs={{0,8},{4,12},{8,0},{12,4},{16,24},{20,28},{24,16},{28,20},{1,9},{5... | collective-permute-start | bytes 393224 | tf_op jit(solution)/shard_map/ppermute | solution.py:312
  48.7 6.7 %collective-permute-start.16 = (bf16[32,2048]{1,0:T(8,128)(2,1)S(1)}, bf16[32,2048]{1,0:T(8,128)(2,1)S(1)}, u32[]{:S(2)}, u32[]{:S(2)}) collective-permute-start(bf16[32,2048]{1,0:T(8,128)(2,1)S(1)} %shard_map.78.refs_0_), channel_id=1, source_target_pairs={{0,12},{4,8},{8,4},{12,0},{16,28},{20,24},{24,20},{28,16},{1,13},{... | collective-permute-start | bytes 393224 | tf_op jit(solution)/shard_map/ppermute | solution.py:312
  53.5 2.9 %collective-permute-start.22 = (bf16[64,1024]{1,0:T(8,128)(2,1)S(1)}, bf16[64,1024]{1,0:T(8,128)(2,1)S(1)}, u32[]{:S(2)}, u32[]{:S(2)}) collective-permute-start(bf16[64,1024]{1,0:T(8,128)(2,1)S(1)} %get-tuple-element.34), channel_id=1, source_target_pairs={{0,1},{1,0},{2,3},{3,2},{4,5},{5,4},{6,7},{7,6},{8,9},{9,8},{10,11... | collective-permute-start | bytes 393224 | tf_op jit(solution)/shard_map/ppermute | solution.py:312
  56.2 1.4 %collective-permute-start.17 = (bf16[64,1024]{1,0:T(8,128)(2,1)S(1)}, bf16[64,1024]{1,0:T(8,128)(2,1)S(1)}, u32[]{:S(2)}, u32[]{:S(2)}) collective-permute-start(bf16[64,1024]{1,0:T(8,128)(2,1)S(1)} %get-tuple-element.32), channel_id=1, source_target_pairs={{0,1},{1,0},{2,3},{3,2},{4,5},{5,4},{6,7},{7,6},{8,9},{9,8},{10,11... | collective-permute-start | bytes 393224 | tf_op jit(solution)/shard_map/ppermute | solution.py:312
  57.7 5.6 %collective-permute-start.23 = (bf16[64,1024]{1,0:T(8,128)(2,1)S(1)}, bf16[64,1024]{1,0:T(8,128)(2,1)S(1)}, u32[]{:S(2)}, u32[]{:S(2)}) collective-permute-start(bf16[64,1024]{1,0:T(8,128)(2,1)S(1)} %select_convert_fusion), channel_id=1, source_target_pairs={{0,2},{1,3},{2,0},{3,1},{4,6},{5,7},{6,4},{7,5},{8,10},{9,11},{10,... | collective-permute-start | bytes 393224 | tf_op jit(solution)/shard_map/ppermute | solution.py:312

commit v11 on v9

--- a/solution.py
+++ b/solution.py
@@ -36,7 +36,7 @@
         self.n, self.rows, self.blocks, self.page = n, rows, blocks, page
         self.group = n // blocks
         self.halves = blocks == 2 and n == 8 and ways == 4 and rows * self.group == page
-        self.cross = n // 2
+        self.cross = n * 3 // 4
         self.chunks = self.group if self.halves else 1
 
     def block(self, me, lb):
@@ -159,7 +159,7 @@
 def attend_kernel(plan, heads, lb, info, *refs):
     me = lax.axis_index("pages")
     chunks, page = plan.chunks, plan.page
-    queries, (k_ref, v_ref), outs = refs[:chunks], refs[chunks : chunks + 2], refs[chunks + 2 :]
+    queries, (k_ref, v_ref), outs = refs[:chunks][::-1], refs[chunks : chunks + 2], refs[chunks + 2 :]
     kv_heads, size = k_ref.shape[1], k_ref.shape[3]
     repeat = heads // kv_heads
     width = heads * size
@@ -220,7 +220,7 @@
         out_specs=(in_vmem(),) * plan.chunks,
         compiler_params=params(32),
         cost_estimate=pl.CostEstimate(flops=2 * 10**9, bytes_accessed=4 * 2**20, transcendentals=10**6),
-    )(info, *queries, keys, values)
+    )(info, *queries[::-1], keys, values)
 
 
 def merged(parts, stats):

time: 62.3 us -> 60.7 us (0.974)
  waiting for transfers between devices: 22 us -> 16.1 us
  Pallas kernels: 6.65 us -> 12 us
  starting transfers between devices: 32.8 us -> 31.4 us
    ppermute x24, waiting for transfers between devices: 22 us -> 16.1 us  [swap(): return lax.ppermute(x, axis, [(i, i ^ distance) for i in range(n)])]
    pallas_call x2, Pallas kernels: 1.29 us -> 5.87 us  [attend(): pl.pallas_call(functools.partial(attend_kernel, plan, heads, lb), out_sha...]
    ppermute x24, starting transfers between devices: 32.8 us -> 31.4 us  [swap(): return lax.ppermute(x, axis, [(i, i ^ distance) for i in range(n)])]
    pallas_call x1, Pallas kernels: 2.19 us -> 3.01 us  [fetch(): pl.pallas_call(functools.partial(fetch_kernel, plan, pages_dev), out_shap...]
  transfers between devices with their start and end apart: 24 -> 24, of which waited for: 12 -> 12; matrix products, arithmetic and copies ran while one was open for 0% -> 0% of each run, Pallas kernels for 11% -> 20%
where the time goes in v11:
time: 60.7 us; the launch traced here: 60.6 us
  starting transfers between devices  31.4 us (52%)
  waiting for transfers between devices  16.1 us (27%)
  Pallas kernels  12 us (20%)
  other arithmetic  0.78 us (1%)
    ppermute x24, starting transfers between devices, swap(): return lax.ppermute(x, axis, [(i, i ^ distance) for i in range(n)])  31.4 us
    ppermute x24, waiting for transfers between devices, swap(): return lax.ppermute(x, axis, [(i, i ^ distance) for i in range(n)])  16.1 us
    pallas_call x2, Pallas kernels, attend(): pl.pallas_call(functools.partial(attend_kernel, plan, heads, lb), out_sha...  5.87 us
    pallas_call x1, Pallas kernels, fetch(): pl.pallas_call(functools.partial(fetch_kernel, plan, pages_dev), out_shap...  3.01 us
    pallas_call x2, Pallas kernels, project(): pl.pallas_call(functools.partial(project_kernel, plan, lb), out_shape=(ja...  1.57 us
  transfers between devices with their start and end apart: 24, of which 12 were waited for; matrix products, arithmetic and copies ran while one was open for 0% of the time, Pallas kernels for 20%

profile of v11, /device:TPU:0, one launch (start us, length us, event | category | flops | bytes accessed | tf_op | source)
XLA Modules:
  0.0 60.6 jit_solution(14101994904073387293)
XLA Ops:
  0.0 5.0 %collective-permute-start.6 = (bf16[32,2048]{1,0:T(8,128)(2,1)}, bf16[32,2048]{1,0:T(8,128)(2,1)S(1)}, u32[]{:S(2)}, u32[]{:S(2)}) collective-permute-start(bf16[32,2048]{1,0:T(8,128)(2,1)} %refs_3_.1), channel_id=1, source_target_pairs={{0,24},{4,28},{8,16},{12,20},{16,8},{20,12},{24,0},{28,4},{1,25},{... | collective-permute-start | bytes 393224 | tf_op jit(solution)/shard_map/ppermute | solution.py:312
  5.1 0.5 collective-permute-start
  5.5 2.5 %collective-permute-start.1 = (bf16[32,2048]{1,0:T(8,128)(2,1)}, bf16[32,2048]{1,0:T(8,128)(2,1)S(1)}, u32[]{:S(2)}, u32[]{:S(2)}) collective-permute-start(bf16[32,2048]{1,0:T(8,128)(2,1)} %refs_3_.1), channel_id=1, source_target_pairs={{0,8},{4,12},{8,0},{12,4},{16,24},{20,28},{24,16},{28,20},{1,9},{5... | collective-permute-start | bytes 393224 | tf_op jit(solution)/shard_map/ppermute | solution.py:312
  8.0 0.5 collective-permute-start.2
  8.5 3.0 %shard_map.73 = (bf16[2,2,768,128]{3,2,1,0:T(8,128)(2,1)S(1)}, bf16[2,2,768,256]{3,2,1,0:T(8,128)(2,1)S(1)}, s32[2,3]{1,0:T(2,128)S(1)}) custom-call(s32[2,24]{1,0:T(2,128)} %select_hbm.1, s32[128]{0:T(128)} %table_hbm.1, s32[2]{0:T(128)} %stands_hbm.1, bf16[16,256,128]{2,1,0:T(8,128)(2,1)} %bitcast.2, bf16[16,256,128]{2,1,0:T(8,128)(2,1)} %bitcast.3), custom_call_target="tpu_custom_call" | custom-call | flops 2000000000 | bytes 8388608 | tf_op jit(solution)/shard_map/pallas_call | solution.py:118
  11.6 0.0 collective-permute-done.6.refs_3_
  11.6 1.0 %collective-permute-start.7 = (bf16[32,2048]{1,0:T(8,128)(2,1)S(1)}, bf16[32,2048]{1,0:T(8,128)(2,1)S(1)}, u32[]{:S(2)}, u32[]{:S(2)}) collective-permute-start(bf16[32,2048]{1,0:T(8,128)(2,1)S(1)} %collective-permute-done.6.refs_3_), channel_id=1, source_target_pairs={{0,12},{4,8},{8,4},{12,0},{16,28},{20,24},{24,20},{28,16},{1,13},{... | collective-permute-start | bytes 393224 | tf_op jit(solution)/shard_map/ppermute | solution.py:312
  12.6 1.2 %collective-permute-start.8 = (bf16[32,2048]{1,0:T(8,128)(2,1)S(1)}, bf16[32,2048]{1,0:T(8,128)(2,1)S(1)}, u32[]{:S(2)}, u32[]{:S(2)}) collective-permute-start(bf16[32,2048]{1,0:T(8,128)(2,1)S(1)} %collective-permute-done.6.refs_3_), channel_id=1, source_target_pairs={{0,8},{4,12},{8,0},{12,4},{16,24},{20,28},{24,16},{28,20},{1,9},{5... | collective-permute-start | bytes 393224 | tf_op jit(solution)/shard_map/ppermute | solution.py:312
  13.8 1.4 %collective-permute-start.9 = (bf16[32,2048]{1,0:T(8,128)(2,1)S(1)}, bf16[32,2048]{1,0:T(8,128)(2,1)S(1)}, u32[]{:S(2)}, u32[]{:S(2)}) collective-permute-start(bf16[32,2048]{1,0:T(8,128)(2,1)S(1)} %collective-permute-done.6.refs_3_), channel_id=1, source_target_pairs={{0,4},{4,0},{8,12},{12,8},{16,20},{20,16},{24,28},{28,24},{1,5},{5... | collective-permute-start | bytes 393224 | tf_op jit(solution)/shard_map/ppermute | solution.py:312
  15.1 0.3 collective-permute-done.1.refs_1_
  15.5 0.0 collective-permute-done.2.refs_2_
  15.5 2.9 %shard_map.74 = (bf16[32,2176]{1,0:T(8,128)(2,1)S(1)}, bf16[32,2176]{1,0:T(8,128)(2,1)S(1)}, bf16[32,2176]{1,0:T(8,128)(2,1)S(1)}, bf16[32,2176]{1,0:T(8,128)(2,1)S(1)}) custom-call(s32[2,3]{1,0:T(2,128)S(1)} %get-tuple-element.20.info, bf16[32,2048]{1,0:T(8,128)(2,1)S(1)} %collective-permute-done.refs_0_, ...), custom_call_target="tpu_custom_call" | custom-call | flops 2000000000 | bytes 4194304 | tf_op jit(solution)/shard_map/pallas_call | solution.py:216
  18.4 0.1 collective-permute-start.3
  18.5 3.3 %collective-permute-start.4 = (bf16[32,2176]{1,0:T(8,128)(2,1)S(1)}, bf16[32,2176]{1,0:T(8,128)(2,1)S(1)}, u32[]{:S(2)}, u32[]{:S(2)}) collective-permute-start(bf16[32,2176]{1,0:T(8,128)(2,1)S(1)} %get-tuple-element.25), channel_id=1, source_target_pairs={{0,8},{4,12},{8,0},{12,4},{16,24},{20,28},{24,16},{28,20},{1,9},{5... | collective-permute-start | bytes 417800 | tf_op jit(solution)/shard_map/ppermute | solution.py:312
  21.8 0.2 collective-permute-start.5
  22.0 2.9 %shard_map.76 = (bf16[32,2176]{1,0:T(8,128)(2,1)S(1)}, bf16[32,2176]{1,0:T(8,128)(2,1)S(1)}, bf16[32,2176]{1,0:T(8,128)(2,1)S(1)}, bf16[32,2176]{1,0:T(8,128)(2,1)S(1)}) custom-call(s32[2,3]{1,0:T(2,128)S(1)} %get-tuple-element.20.info, bf16[32,2048]{1,0:T(8,128)(2,1)S(1)} %collective-permute-done.7.refs_0_, ...), custom_call_target="tpu_custom_call" | custom-call | flops 2000000000 | bytes 4194304 | tf_op jit(solution)/shard_map/pallas_call | solution.py:216
  24.9 0.1 collective-permute-start.10
  25.0 3.3 %collective-permute-start.11 = (bf16[32,2176]{1,0:T(8,128)(2,1)S(1)}, bf16[32,2176]{1,0:T(8,128)(2,1)S(1)}, u32[]{:S(2)}, u32[]{:S(2)}) collective-permute-start(bf16[32,2176]{1,0:T(8,128)(2,1)S(1)} %get-tuple-element.29), channel_id=1, source_target_pairs={{0,8},{4,12},{8,0},{12,4},{16,24},{20,28},{24,16},{28,20},{1,9},{5... | collective-permute-start | bytes 417800 | tf_op jit(solution)/shard_map/ppermute | solution.py:312
  28.3 0.2 collective-permute-start.12
  28.5 0.1 collective-permute-done.5.refs_3_
  28.6 0.5 shard_map.75.near
  29.1 1.3 %collective-permute-start.18 = (bf16[32,2176]{1,0:T(8,128)(2,1)S(1)}, bf16[32,2176]{1,0:T(8,128)(2,1)S(1)}, u32[]{:S(2)}, u32[]{:S(2)}) collective-permute-start(bf16[32,2176]{1,0:T(8,128)(2,1)S(1)} %shard_map.75.near), channel_id=1, source_target_pairs={{0,24},{4,28},{8,16},{12,20},{16,8},{20,12},{24,0},{28,4},{1,25},{... | collective-permute-start | bytes 417800 | tf_op jit(solution)/shard_map/ppermute | solution.py:312
  30.4 1.3 %collective-permute-done.10.refs_1_ = bf16[32,2176]{1,0:T(8,128)(2,1)S(1)} collective-permute-done((bf16[32,2176]{1,0:T(8,128)(2,1)S(1)}, bf16[32,2176]{1,0:T(8,128)(2,1)S(1)}, u32[]{:S(2)}, u32[]{:S(2)}) %collective-permute-start.10) | collective-permute-done | bytes 139296 | tf_op jit(solution)/shard_map/ppermute | solution.py:312
  31.7 0.2 collective-permute-done.11.refs_2_
  31.9 3.3 %collective-permute-done.12.refs_3_ = bf16[32,2176]{1,0:T(8,128)(2,1)S(1)} collective-permute-done((bf16[32,2176]{1,0:T(8,128)(2,1)S(1)}, bf16[32,2176]{1,0:T(8,128)(2,1)S(1)}, u32[]{:S(2)}, u32[]{:S(2)}) %collective-permute-start.12) | collective-permute-done | bytes 139296 | tf_op jit(solution)/shard_map/ppermute | solution.py:312
  35.2 0.5 shard_map.77.near
  35.7 0.4 collective-permute-start.13
  36.1 1.1 %collective-permute-done.18.far = bf16[32,2176]{1,0:T(8,128)(2,1)S(1)} collective-permute-done((bf16[32,2176]{1,0:T(8,128)(2,1)S(1)}, bf16[32,2176]{1,0:T(8,128)(2,1)S(1)}, u32[]{:S(2)}, u32[]{:S(2)}) %collective-permute-start.18) | collective-permute-done | bytes 139296 | tf_op jit(solution)/shard_map/ppermute | solution.py:312
  37.2 0.3 shard_map.80.refs_0_
  37.6 1.8 %collective-permute-start.19 = (bf16[32,2048]{1,0:T(8,128)(2,1)S(1)}, bf16[32,2048]{1,0:T(8,128)(2,1)S(1)}, u32[]{:S(2)}, u32[]{:S(2)}) collective-permute-start(bf16[32,2048]{1,0:T(8,128)(2,1)S(1)} %shard_map.80.refs_0_), channel_id=1, source_target_pairs={{0,4},{4,0},{8,12},{12,8},{16,20},{20,16},{24,28},{28,24},{1,5},{5... | collective-permute-start | bytes 393224 | tf_op jit(solution)/shard_map/ppermute | solution.py:312
  39.3 2.9 %collective-permute-start.20 = (bf16[32,2048]{1,0:T(8,128)(2,1)S(1)}, bf16[32,2048]{1,0:T(8,128)(2,1)S(1)}, u32[]{:S(2)}, u32[]{:S(2)}) collective-permute-start(bf16[32,2048]{1,0:T(8,128)(2,1)S(1)} %shard_map.80.refs_0_), channel_id=1, source_target_pairs={{0,8},{4,12},{8,0},{12,4},{16,24},{20,28},{24,16},{28,20},{1,9},{5... | collective-permute-start | bytes 393224 | tf_op jit(solution)/shard_map/ppermute | solution.py:312
  42.2 0.5 collective-permute-done.13.far
  42.7 0.3 shard_map.78.refs_0_
  43.0 1.3 %collective-permute-start.14 = (bf16[32,2048]{1,0:T(8,128)(2,1)S(1)}, bf16[32,2048]{1,0:T(8,128)(2,1)S(1)}, u32[]{:S(2)}, u32[]{:S(2)}) collective-permute-start(bf16[32,2048]{1,0:T(8,128)(2,1)S(1)} %shard_map.78.refs_0_), channel_id=1, source_target_pairs={{0,4},{4,0},{8,12},{12,8},{16,20},{20,16},{24,28},{28,24},{1,5},{5... | collective-permute-start | bytes 393224 | tf_op jit(solution)/shard_map/ppermute | solution.py:312
  44.3 1.8 %collective-permute-start.15 = (bf16[32,2048]{1,0:T(8,128)(2,1)S(1)}, bf16[32,2048]{1,0:T(8,128)(2,1)S(1)}, u32[]{:S(2)}, u32[]{:S(2)}) collective-permute-start(bf16[32,2048]{1,0:T(8,128)(2,1)S(1)} %shard_map.78.refs_0_), channel_id=1, source_target_pairs={{0,8},{4,12},{8,0},{12,4},{16,24},{20,28},{24,16},{28,20},{1,9},{5... | collective-permute-start | bytes 393224 | tf_op jit(solution)/shard_map/ppermute | solution.py:312
  46.1 1.0 %collective-permute-start.16 = (bf16[32,2048]{1,0:T(8,128)(2,1)S(1)}, bf16[32,2048]{1,0:T(8,128)(2,1)S(1)}, u32[]{:S(2)}, u32[]{:S(2)}) collective-permute-start(bf16[32,2048]{1,0:T(8,128)(2,1)S(1)} %shard_map.78.refs_0_), channel_id=1, source_target_pairs={{0,12},{4,8},{8,4},{12,0},{16,28},{20,24},{24,20},{28,16},{1,13},{... | collective-permute-start | bytes 393224 | tf_op jit(solution)/shard_map/ppermute | solution.py:312
  47.1 1.9 %collective-permute-done.21.refs_3_ = bf16[32,2048]{1,0:T(8,128)(2,1)S(1)} collective-permute-done((bf16[32,2048]{1,0:T(8,128)(2,1)S(1)}, bf16[32,2048]{1,0:T(8,128)(2,1)S(1)}, u32[]{:S(2)}, u32[]{:S(2)}) %collective-permute-start.21) | collective-permute-done | bytes 131104 | tf_op jit(solution)/shard_map/ppermute | solution.py:312
  49.0 0.8 %shard_map.81 = (f32[64,1024]{1,0:T(8,128)S(1)}, bf16[64,1024]{1,0:T(8,128)(2,1)S(1)}) custom-call(bf16[32,2048]{1,0:T(8,128)(2,1)S(1)} %shard_map.80.refs_0_, bf16[32,2048]{1,0:T(8,128)(2,1)S(1)} %collective-permute-done.19.refs_1_, bf16[32,2048]{1,0:T(8,128)(2,1)S(1)} %collective-permute-done.20.refs_2_, ...), custom_call_target="tpu_custom_call" | custom-call | tf_op jit(solution)/shard_map/pallas_call | solution.py:300
  49.8 0.1 collective-permute-start.22
  49.9 0.4 collective-permute-done.14.refs_1_
  50.3 1.6 %collective-permute-done.16.refs_3_ = bf16[32,2048]{1,0:T(8,128)(2,1)S(1)} collective-permute-done((bf16[32,2048]{1,0:T(8,128)(2,1)S(1)}, bf16[32,2048]{1,0:T(8,128)(2,1)S(1)}, u32[]{:S(2)}, u32[]{:S(2)}) %collective-permute-start.16) | collective-permute-done | bytes 131104 | tf_op jit(solution)/shard_map/ppermute | solution.py:312
  51.9 0.8 %shard_map.79 = (f32[64,1024]{1,0:T(8,128)S(1)}, bf16[64,1024]{1,0:T(8,128)(2,1)S(1)}) custom-call(bf16[32,2048]{1,0:T(8,128)(2,1)S(1)} %shard_map.78.refs_0_, bf16[32,2048]{1,0:T(8,128)(2,1)S(1)} %collective-permute-done.14.refs_1_, bf16[32,2048]{1,0:T(8,128)(2,1)S(1)} %collective-permute-done.15.refs_2_, ...), custom_call_target="tpu_custom_call" | custom-call | tf_op jit(solution)/shard_map/pallas_call | solution.py:300
  52.7 0.1 collective-permute-start.17
  52.9 1.3 %collective-permute-done.17 = bf16[64,1024]{1,0:T(8,128)(2,1)S(1)} collective-permute-done((bf16[64,1024]{1,0:T(8,128)(2,1)S(1)}, bf16[64,1024]{1,0:T(8,128)(2,1)S(1)}, u32[]{:S(2)}, u32[]{:S(2)}) %collective-permute-start.17) | collective-permute-done | bytes 131104 | tf_op jit(solution)/shard_map/ppermute | solution.py:312
  54.2 0.1 select_convert_fusion
  54.2 1.6 %collective-permute-start.23 = (bf16[64,1024]{1,0:T(8,128)(2,1)S(1)}, bf16[64,1024]{1,0:T(8,128)(2,1)S(1)}, u32[]{:S(2)}, u32[]{:S(2)}) collective-permute-start(bf16[64,1024]{1,0:T(8,128)(2,1)S(1)} %select_convert_fusion), channel_id=1, source_target_pairs={{0,2},{1,3},{2,0},{3,1},{4,6},{5,7},{6,4},{7,5},{8,10},{9,11},{10,... | collective-permute-start | bytes 393224 | tf_op jit(solution)/shard_map/ppermute | solution.py:312
  55.8 4.0 %collective-permute-done.23 = bf16[64,1024]{1,0:T(8,128)(2,1)S(1)} collective-permute-done((bf16[64,1024]{1,0:T(8,128)(2,1)S(1)}, bf16[64,1024]{1,0:T(8,128)(2,1)S(1)}, u32[]{:S(2)}, u32[]{:S(2)}) %collective-permute-start.23) | collective-permute-done | bytes 131104 | tf_op jit(solution)/shard_map/ppermute | solution.py:312
  59.8 0.7 %add_convert_fusion = bf16[64,1024]{1,0:T(8,128)(2,1)} fusion(bf16[64,1024]{1,0:T(8,128)(2,1)S(1)} %collective-permute-done.23, f32[64,1024]{1,0:T(8,128)S(1)} %get-tuple-element.31, bf16[64,1024]{1,0:T(8,128)(2,1)S(1)} %collective-permute-done.17, f32[64,1024]{1,0:T(8,128)S(1)} %get-tuple-element.33, bf16[64,1024]{1,0:T(8,128)(2,1)S(1)} %collective-permute-done.22, ...), kind=kLoop, calls=%fused_computation | loop fusion | flops 524288 | bytes 1048577 | tf_op jit(solution)/shard_map/convert_element_type | solution.py:339
  (15 shorter events, 0.0 us)
Async XLA Ops:
  0.0 15.5 %copy-start.1 = (bf16[32,2048]{1,0:T(8,128)(2,1)S(1)}, bf16[32,2048]{1,0:T(8,128)(2,1)}, u32[]{:S(2)}) copy-start(bf16[32,2048]{1,0:T(8,128)(2,1)} %refs_3_.1) | copy-start | bytes 393220
  0.0 11.6 %collective-permute-start.6 = (bf16[32,2048]{1,0:T(8,128)(2,1)}, bf16[32,2048]{1,0:T(8,128)(2,1)S(1)}, u32[]{:S(2)}, u32[]{:S(2)}) collective-permute-start(bf16[32,2048]{1,0:T(8,128)(2,1)} %refs_3_.1), channel_id=1, source_target_pairs={{0,24},{4,28},{8,16},{12,20},{16,8},{20,12},{24,0},{28,4},{1,25},{... | collective-permute-start | bytes 393224 | tf_op jit(solution)/shard_map/ppermute | solution.py:312
  5.1 8.7 %collective-permute-start = (bf16[32,2048]{1,0:T(8,128)(2,1)}, bf16[32,2048]{1,0:T(8,128)(2,1)S(1)}, u32[]{:S(2)}, u32[]{:S(2)}) collective-permute-start(bf16[32,2048]{1,0:T(8,128)(2,1)} %refs_3_.1), channel_id=1, source_target_pairs={{0,12},{4,8},{8,4},{12,0},{16,28},{20,24},{24,20},{28,16},{1,13},{... | collective-permute-start | bytes 393224 | tf_op jit(solution)/shard_map/ppermute | solution.py:312
  5.5 9.9 %collective-permute-start.1 = (bf16[32,2048]{1,0:T(8,128)(2,1)}, bf16[32,2048]{1,0:T(8,128)(2,1)S(1)}, u32[]{:S(2)}, u32[]{:S(2)}) collective-permute-start(bf16[32,2048]{1,0:T(8,128)(2,1)} %refs_3_.1), channel_id=1, source_target_pairs={{0,8},{4,12},{8,0},{12,4},{16,24},{20,28},{24,16},{28,20},{1,9},{5... | collective-permute-start | bytes 393224 | tf_op jit(solution)/shard_map/ppermute | solution.py:312
  8.0 7.5 %collective-permute-start.2 = (bf16[32,2048]{1,0:T(8,128)(2,1)}, bf16[32,2048]{1,0:T(8,128)(2,1)S(1)}, u32[]{:S(2)}, u32[]{:S(2)}) collective-permute-start(bf16[32,2048]{1,0:T(8,128)(2,1)} %refs_3_.1), channel_id=1, source_target_pairs={{0,4},{4,0},{8,12},{12,8},{16,20},{20,16},{24,28},{28,24},{1,5},{5... | collective-permute-start | bytes 393224 | tf_op jit(solution)/shard_map/ppermute | solution.py:312
  11.6 10.2 %collective-permute-start.7 = (bf16[32,2048]{1,0:T(8,128)(2,1)S(1)}, bf16[32,2048]{1,0:T(8,128)(2,1)S(1)}, u32[]{:S(2)}, u32[]{:S(2)}) collective-permute-start(bf16[32,2048]{1,0:T(8,128)(2,1)S(1)} %collective-permute-done.6.refs_3_), channel_id=1, source_target_pairs={{0,12},{4,8},{8,4},{12,0},{16,28},{20,24},{24,20},{28,16},{1,13},{... | collective-permute-start | bytes 393224 | tf_op jit(solution)/shard_map/ppermute | solution.py:312
  12.6 9.4 %collective-permute-start.8 = (bf16[32,2048]{1,0:T(8,128)(2,1)S(1)}, bf16[32,2048]{1,0:T(8,128)(2,1)S(1)}, u32[]{:S(2)}, u32[]{:S(2)}) collective-permute-start(bf16[32,2048]{1,0:T(8,128)(2,1)S(1)} %collective-permute-done.6.refs_3_), channel_id=1, source_target_pairs={{0,8},{4,12},{8,0},{12,4},{16,24},{20,28},{24,16},{28,20},{1,9},{5... | collective-permute-start | bytes 393224 | tf_op jit(solution)/shard_map/ppermute | solution.py:312
  13.8 8.2 %collective-permute-start.9 = (bf16[32,2048]{1,0:T(8,128)(2,1)S(1)}, bf16[32,2048]{1,0:T(8,128)(2,1)S(1)}, u32[]{:S(2)}, u32[]{:S(2)}) collective-permute-start(bf16[32,2048]{1,0:T(8,128)(2,1)S(1)} %collective-permute-done.6.refs_3_), channel_id=1, source_target_pairs={{0,4},{4,0},{8,12},{12,8},{16,20},{20,16},{24,28},{28,24},{1,5},{5... | collective-permute-start | bytes 393224 | tf_op jit(solution)/shard_map/ppermute | solution.py:312
  18.4 9.9 %collective-permute-start.3 = (bf16[32,2176]{1,0:T(8,128)(2,1)S(1)}, bf16[32,2176]{1,0:T(8,128)(2,1)S(1)}, u32[]{:S(2)}, u32[]{:S(2)}) collective-permute-start(bf16[32,2176]{1,0:T(8,128)(2,1)S(1)} %get-tuple-element.24), channel_id=1, source_target_pairs={{0,4},{4,0},{8,12},{12,8},{16,20},{20,16},{24,28},{28,24},{1,5},{5... | collective-permute-start | bytes 417800 | tf_op jit(solution)/shard_map/ppermute | solution.py:312
  18.5 10.0 %collective-permute-start.4 = (bf16[32,2176]{1,0:T(8,128)(2,1)S(1)}, bf16[32,2176]{1,0:T(8,128)(2,1)S(1)}, u32[]{:S(2)}, u32[]{:S(2)}) collective-permute-start(bf16[32,2176]{1,0:T(8,128)(2,1)S(1)} %get-tuple-element.25), channel_id=1, source_target_pairs={{0,8},{4,12},{8,0},{12,4},{16,24},{20,28},{24,16},{28,20},{1,9},{5... | collective-permute-start | bytes 417800 | tf_op jit(solution)/shard_map/ppermute | solution.py:312
  21.8 27.2 %copy-start = (bf16[2048,1024]{1,0:T(8,128)(2,1)S(1)}, bf16[2048,1024]{1,0:T(8,128)(2,1)}, u32[]{:S(2)}) copy-start(bf16[2048,1024]{1,0:T(8,128)(2,1)} %refs_4_.3) | copy-start | bytes 12582916
  21.8 6.8 %collective-permute-start.5 = (bf16[32,2176]{1,0:T(8,128)(2,1)S(1)}, bf16[32,2176]{1,0:T(8,128)(2,1)S(1)}, u32[]{:S(2)}, u32[]{:S(2)}) collective-permute-start(bf16[32,2176]{1,0:T(8,128)(2,1)S(1)} %get-tuple-element.26), channel_id=1, source_target_pairs={{0,12},{4,8},{8,4},{12,0},{16,28},{20,24},{24,20},{28,16},{1,13},{... | collective-permute-start | bytes 417800 | tf_op jit(solution)/shard_map/ppermute | solution.py:312
  24.9 6.8 %collective-permute-start.10 = (bf16[32,2176]{1,0:T(8,128)(2,1)S(1)}, bf16[32,2176]{1,0:T(8,128)(2,1)S(1)}, u32[]{:S(2)}, u32[]{:S(2)}) collective-permute-start(bf16[32,2176]{1,0:T(8,128)(2,1)S(1)} %get-tuple-element.28), channel_id=1, source_target_pairs={{0,4},{4,0},{8,12},{12,8},{16,20},{20,16},{24,28},{28,24},{1,5},{5... | collective-permute-start | bytes 417800 | tf_op jit(solution)/shard_map/ppermute | solution.py:312
  25.0 6.9 %collective-permute-start.11 = (bf16[32,2176]{1,0:T(8,128)(2,1)S(1)}, bf16[32,2176]{1,0:T(8,128)(2,1)S(1)}, u32[]{:S(2)}, u32[]{:S(2)}) collective-permute-start(bf16[32,2176]{1,0:T(8,128)(2,1)S(1)} %get-tuple-element.29), channel_id=1, source_target_pairs={{0,8},{4,12},{8,0},{12,4},{16,24},{20,28},{24,16},{28,20},{1,9},{5... | collective-permute-start | bytes 417800 | tf_op jit(solution)/shard_map/ppermute | solution.py:312
  28.3 6.9 %collective-permute-start.12 = (bf16[32,2176]{1,0:T(8,128)(2,1)S(1)}, bf16[32,2176]{1,0:T(8,128)(2,1)S(1)}, u32[]{:S(2)}, u32[]{:S(2)}) collective-permute-start(bf16[32,2176]{1,0:T(8,128)(2,1)S(1)} %get-tuple-element.30), channel_id=1, source_target_pairs={{0,12},{4,8},{8,4},{12,0},{16,28},{20,24},{24,20},{28,16},{1,13},{... | collective-permute-start | bytes 417800 | tf_op jit(solution)/shard_map/ppermute | solution.py:312
  29.1 8.2 %collective-permute-start.18 = (bf16[32,2176]{1,0:T(8,128)(2,1)S(1)}, bf16[32,2176]{1,0:T(8,128)(2,1)S(1)}, u32[]{:S(2)}, u32[]{:S(2)}) collective-permute-start(bf16[32,2176]{1,0:T(8,128)(2,1)S(1)} %shard_map.75.near), channel_id=1, source_target_pairs={{0,24},{4,28},{8,16},{12,20},{16,8},{20,12},{24,0},{28,4},{1,25},{... | collective-permute-start | bytes 417800 | tf_op jit(solution)/shard_map/ppermute | solution.py:312
  35.7 7.0 %collective-permute-start.13 = (bf16[32,2176]{1,0:T(8,128)(2,1)S(1)}, bf16[32,2176]{1,0:T(8,128)(2,1)S(1)}, u32[]{:S(2)}, u32[]{:S(2)}) collective-permute-start(bf16[32,2176]{1,0:T(8,128)(2,1)S(1)} %shard_map.77.near), channel_id=1, source_target_pairs={{0,24},{4,28},{8,16},{12,20},{16,8},{20,12},{24,0},{28,4},{1,25},{... | collective-permute-start | bytes 417800 | tf_op jit(solution)/shard_map/ppermute | solution.py:312
  37.6 8.5 %collective-permute-start.19 = (bf16[32,2048]{1,0:T(8,128)(2,1)S(1)}, bf16[32,2048]{1,0:T(8,128)(2,1)S(1)}, u32[]{:S(2)}, u32[]{:S(2)}) collective-permute-start(bf16[32,2048]{1,0:T(8,128)(2,1)S(1)} %shard_map.80.refs_0_), channel_id=1, source_target_pairs={{0,4},{4,0},{8,12},{12,8},{16,20},{20,16},{24,28},{28,24},{1,5},{5... | collective-permute-start | bytes 393224 | tf_op jit(solution)/shard_map/ppermute | solution.py:312
  39.3 7.8 %collective-permute-start.20 = (bf16[32,2048]{1,0:T(8,128)(2,1)S(1)}, bf16[32,2048]{1,0:T(8,128)(2,1)S(1)}, u32[]{:S(2)}, u32[]{:S(2)}) collective-permute-start(bf16[32,2048]{1,0:T(8,128)(2,1)S(1)} %shard_map.80.refs_0_), channel_id=1, source_target_pairs={{0,8},{4,12},{8,0},{12,4},{16,24},{20,28},{24,16},{28,20},{1,9},{5... | collective-permute-start | bytes 393224 | tf_op jit(solution)/shard_map/ppermute | solution.py:312
  42.2 6.8 %collective-permute-start.21 = (bf16[32,2048]{1,0:T(8,128)(2,1)S(1)}, bf16[32,2048]{1,0:T(8,128)(2,1)S(1)}, u32[]{:S(2)}, u32[]{:S(2)}) collective-permute-start(bf16[32,2048]{1,0:T(8,128)(2,1)S(1)} %shard_map.80.refs_0_), channel_id=1, source_target_pairs={{0,12},{4,8},{8,4},{12,0},{16,28},{20,24},{24,20},{28,16},{1,13},{... | collective-permute-start | bytes 393224 | tf_op jit(solution)/shard_map/ppermute | solution.py:312
  43.0 7.3 %collective-permute-start.14 = (bf16[32,2048]{1,0:T(8,128)(2,1)S(1)}, bf16[32,2048]{1,0:T(8,128)(2,1)S(1)}, u32[]{:S(2)}, u32[]{:S(2)}) collective-permute-start(bf16[32,2048]{1,0:T(8,128)(2,1)S(1)} %shard_map.78.refs_0_), channel_id=1, source_target_pairs={{0,4},{4,0},{8,12},{12,8},{16,20},{20,16},{24,28},{28,24},{1,5},{5... | collective-permute-start | bytes 393224 | tf_op jit(solution)/shard_map/ppermute | solution.py:312
  44.3 6.0 %collective-permute-start.15 = (bf16[32,2048]{1,0:T(8,128)(2,1)S(1)}, bf16[32,2048]{1,0:T(8,128)(2,1)S(1)}, u32[]{:S(2)}, u32[]{:S(2)}) collective-permute-start(bf16[32,2048]{1,0:T(8,128)(2,1)S(1)} %shard_map.78.refs_0_), channel_id=1, source_target_pairs={{0,8},{4,12},{8,0},{12,4},{16,24},{20,28},{24,16},{28,20},{1,9},{5... | collective-permute-start | bytes 393224 | tf_op jit(solution)/shard_map/ppermute | solution.py:312
  46.1 5.9 %collective-permute-start.16 = (bf16[32,2048]{1,0:T(8,128)(2,1)S(1)}, bf16[32,2048]{1,0:T(8,128)(2,1)S(1)}, u32[]{:S(2)}, u32[]{:S(2)}) collective-permute-start(bf16[32,2048]{1,0:T(8,128)(2,1)S(1)} %shard_map.78.refs_0_), channel_id=1, source_target_pairs={{0,12},{4,8},{8,4},{12,0},{16,28},{20,24},{24,20},{28,16},{1,13},{... | collective-permute-start | bytes 393224 | tf_op jit(solution)/shard_map/ppermute | solution.py:312
  49.8 3.0 %collective-permute-start.22 = (bf16[64,1024]{1,0:T(8,128)(2,1)S(1)}, bf16[64,1024]{1,0:T(8,128)(2,1)S(1)}, u32[]{:S(2)}, u32[]{:S(2)}) collective-permute-start(bf16[64,1024]{1,0:T(8,128)(2,1)S(1)} %get-tuple-element.34), channel_id=1, source_target_pairs={{0,1},{1,0},{2,3},{3,2},{4,5},{5,4},{6,7},{7,6},{8,9},{9,8},{10,11... | collective-permute-start | bytes 393224 | tf_op jit(solution)/shard_map/ppermute | solution.py:312
  52.7 1.4 %collective-permute-start.17 = (bf16[64,1024]{1,0:T(8,128)(2,1)S(1)}, bf16[64,1024]{1,0:T(8,128)(2,1)S(1)}, u32[]{:S(2)}, u32[]{:S(2)}) collective-permute-start(bf16[64,1024]{1,0:T(8,128)(2,1)S(1)} %get-tuple-element.32), channel_id=1, source_target_pairs={{0,1},{1,0},{2,3},{3,2},{4,5},{5,4},{6,7},{7,6},{8,9},{9,8},{10,11... | collective-permute-start | bytes 393224 | tf_op jit(solution)/shard_map/ppermute | solution.py:312
  54.2 5.6 %collective-permute-start.23 = (bf16[64,1024]{1,0:T(8,128)(2,1)S(1)}, bf16[64,1024]{1,0:T(8,128)(2,1)S(1)}, u32[]{:S(2)}, u32[]{:S(2)}) collective-permute-start(bf16[64,1024]{1,0:T(8,128)(2,1)S(1)} %select_convert_fusion), channel_id=1, source_target_pairs={{0,2},{1,3},{2,0},{3,1},{4,6},{5,7},{6,4},{7,5},{8,10},{9,11},{10,... | collective-permute-start | bytes 393224 | tf_op jit(solution)/shard_map/ppermute | solution.py:312

commit v12 on v11

--- a/solution.py
+++ b/solution.py
@@ -326,7 +326,8 @@
     for lb, rows in enumerate((queries, far)):
         chunks = spread(rows, plan)
         outs = attend(plan, heads, lb, pages, [chunks[k] for k in range(plan.group)])
-        near.append(merge(heads, outs[0], *(swap(outs[k], "pages", k) for k in others(plan))))
+        order = reversed(others(plan)) if lb else others(plan)
+        near.append(merge(heads, outs[0], *(swap(outs[k], "pages", k) for k in order)))
     across = [swap(x, "pages", plan.cross) for x in near]
     sums = [None, None]
     for lb in (1, 0):

time: 60.7 us -> 60.7 us (level)
  starting transfers between devices: 31.4 us -> 34.5 us
  waiting for transfers between devices: 16.1 us -> 13.1 us
    ppermute x24, starting transfers between devices: 31.4 us -> 34.5 us  [swap(): return lax.ppermute(x, axis, [(i, i ^ distance) for i in range(n)])]
    ppermute x24, waiting for transfers between devices: 16.1 us -> 13.1 us  [swap(): return lax.ppermute(x, axis, [(i, i ^ distance) for i in range(n)])]
  transfers between devices with their start and end apart: 24 -> 24, of which waited for: 12 -> 10; matrix products, arithmetic and copies ran while one was open for 0% -> 0% of each run, Pallas kernels for 20% -> 20%
where the time goes in v12:
time: 60.7 us; the launch traced here: 60.6 us
  starting transfers between devices  34.5 us (57%)
  waiting for transfers between devices  13.1 us (22%)
  Pallas kernels  12 us (20%)
  other arithmetic  0.78 us (1%)
    ppermute x24, starting transfers between devices, swap(): return lax.ppermute(x, axis, [(i, i ^ distance) for i in range(n)])  34.5 us
    ppermute x24, waiting for transfers between devices, swap(): return lax.ppermute(x, axis, [(i, i ^ distance) for i in range(n)])  13.1 us
    pallas_call x2, Pallas kernels, attend(): pl.pallas_call(functools.partial(attend_kernel, plan, heads, lb), out_sha...  5.87 us
    pallas_call x1, Pallas kernels, fetch(): pl.pallas_call(functools.partial(fetch_kernel, plan, pages_dev), out_shap...  3.01 us
    pallas_call x2, Pallas kernels, project(): pl.pallas_call(functools.partial(project_kernel, plan, lb), out_shape=(ja...  1.57 us
  transfers between devices with their start and end apart: 24, of which 10 were waited for; matrix products, arithmetic and copies ran while one was open for 0% of the time, Pallas kernels for 20%

profile of v12, /device:TPU:0, one launch (start us, length us, event | category | flops | bytes accessed | tf_op | source)
XLA Modules:
  0.0 60.6 jit_solution(10602207093488580133)
XLA Ops:
  0.0 5.0 %collective-permute-start.6 = (bf16[32,2048]{1,0:T(8,128)(2,1)}, bf16[32,2048]{1,0:T(8,128)(2,1)S(1)}, u32[]{:S(2)}, u32[]{:S(2)}) collective-permute-start(bf16[32,2048]{1,0:T(8,128)(2,1)} %refs_3_.1), channel_id=1, source_target_pairs={{0,24},{4,28},{8,16},{12,20},{16,8},{20,12},{24,0},{28,4},{1,25},{... | collective-permute-start | bytes 393224 | tf_op jit(solution)/shard_map/ppermute | solution.py:312
  5.1 0.5 collective-permute-start
  5.5 2.5 %collective-permute-start.1 = (bf16[32,2048]{1,0:T(8,128)(2,1)}, bf16[32,2048]{1,0:T(8,128)(2,1)S(1)}, u32[]{:S(2)}, u32[]{:S(2)}) collective-permute-start(bf16[32,2048]{1,0:T(8,128)(2,1)} %refs_3_.1), channel_id=1, source_target_pairs={{0,8},{4,12},{8,0},{12,4},{16,24},{20,28},{24,16},{28,20},{1,9},{5... | collective-permute-start | bytes 393224 | tf_op jit(solution)/shard_map/ppermute | solution.py:312
  8.0 0.5 collective-permute-start.2
  8.5 3.0 %shard_map.73 = (bf16[2,2,768,128]{3,2,1,0:T(8,128)(2,1)S(1)}, bf16[2,2,768,256]{3,2,1,0:T(8,128)(2,1)S(1)}, s32[2,3]{1,0:T(2,128)S(1)}) custom-call(s32[2,24]{1,0:T(2,128)} %select_hbm.1, s32[128]{0:T(128)} %table_hbm.1, s32[2]{0:T(128)} %stands_hbm.1, bf16[16,256,128]{2,1,0:T(8,128)(2,1)} %bitcast.2, bf16[16,256,128]{2,1,0:T(8,128)(2,1)} %bitcast.3), custom_call_target="tpu_custom_call" | custom-call | flops 2000000000 | bytes 8388608 | tf_op jit(solution)/shard_map/pallas_call | solution.py:118
  11.6 0.0 collective-permute-done.6.refs_3_
  11.6 0.6 %collective-permute-start.7 = (bf16[32,2048]{1,0:T(8,128)(2,1)S(1)}, bf16[32,2048]{1,0:T(8,128)(2,1)S(1)}, u32[]{:S(2)}, u32[]{:S(2)}) collective-permute-start(bf16[32,2048]{1,0:T(8,128)(2,1)S(1)} %collective-permute-done.6.refs_3_), channel_id=1, source_target_pairs={{0,12},{4,8},{8,4},{12,0},{16,28},{20,24},{24,20},{28,16},{1,13},{... | collective-permute-start | bytes 393224 | tf_op jit(solution)/shard_map/ppermute | solution.py:312
  12.2 1.6 %collective-permute-start.8 = (bf16[32,2048]{1,0:T(8,128)(2,1)S(1)}, bf16[32,2048]{1,0:T(8,128)(2,1)S(1)}, u32[]{:S(2)}, u32[]{:S(2)}) collective-permute-start(bf16[32,2048]{1,0:T(8,128)(2,1)S(1)} %collective-permute-done.6.refs_3_), channel_id=1, source_target_pairs={{0,8},{4,12},{8,0},{12,4},{16,24},{20,28},{24,16},{28,20},{1,9},{5... | collective-permute-start | bytes 393224 | tf_op jit(solution)/shard_map/ppermute | solution.py:312
  13.8 0.0 collective-permute-done.refs_0_
  13.8 1.4 %collective-permute-start.9 = (bf16[32,2048]{1,0:T(8,128)(2,1)S(1)}, bf16[32,2048]{1,0:T(8,128)(2,1)S(1)}, u32[]{:S(2)}, u32[]{:S(2)}) collective-permute-start(bf16[32,2048]{1,0:T(8,128)(2,1)S(1)} %collective-permute-done.6.refs_3_), channel_id=1, source_target_pairs={{0,4},{4,0},{8,12},{12,8},{16,20},{20,16},{24,28},{28,24},{1,5},{5... | collective-permute-start | bytes 393224 | tf_op jit(solution)/shard_map/ppermute | solution.py:312
  15.1 0.3 collective-permute-done.1.refs_1_
  15.5 0.0 collective-permute-done.2.refs_2_
  15.5 2.9 %shard_map.74 = (bf16[32,2176]{1,0:T(8,128)(2,1)S(1)}, bf16[32,2176]{1,0:T(8,128)(2,1)S(1)}, bf16[32,2176]{1,0:T(8,128)(2,1)S(1)}, bf16[32,2176]{1,0:T(8,128)(2,1)S(1)}) custom-call(s32[2,3]{1,0:T(2,128)S(1)} %get-tuple-element.20.info, bf16[32,2048]{1,0:T(8,128)(2,1)S(1)} %collective-permute-done.refs_0_, ...), custom_call_target="tpu_custom_call" | custom-call | flops 2000000000 | bytes 4194304 | tf_op jit(solution)/shard_map/pallas_call | solution.py:216
  18.4 0.1 collective-permute-start.3
  18.5 1.9 %collective-permute-start.4 = (bf16[32,2176]{1,0:T(8,128)(2,1)S(1)}, bf16[32,2176]{1,0:T(8,128)(2,1)S(1)}, u32[]{:S(2)}, u32[]{:S(2)}) collective-permute-start(bf16[32,2176]{1,0:T(8,128)(2,1)S(1)} %get-tuple-element.25), channel_id=1, source_target_pairs={{0,8},{4,12},{8,0},{12,4},{16,24},{20,28},{24,16},{28,20},{1,9},{5... | collective-permute-start | bytes 417800 | tf_op jit(solution)/shard_map/ppermute | solution.py:312
  20.4 1.6 %collective-permute-start.5 = (bf16[32,2176]{1,0:T(8,128)(2,1)S(1)}, bf16[32,2176]{1,0:T(8,128)(2,1)S(1)}, u32[]{:S(2)}, u32[]{:S(2)}) collective-permute-start(bf16[32,2176]{1,0:T(8,128)(2,1)S(1)} %get-tuple-element.26), channel_id=1, source_target_pairs={{0,12},{4,8},{8,4},{12,0},{16,28},{20,24},{24,20},{28,16},{1,13},{... | collective-permute-start | bytes 417800 | tf_op jit(solution)/shard_map/ppermute | solution.py:312
  22.0 2.9 %shard_map.76 = (bf16[32,2176]{1,0:T(8,128)(2,1)S(1)}, bf16[32,2176]{1,0:T(8,128)(2,1)S(1)}, bf16[32,2176]{1,0:T(8,128)(2,1)S(1)}, bf16[32,2176]{1,0:T(8,128)(2,1)S(1)}) custom-call(s32[2,3]{1,0:T(2,128)S(1)} %get-tuple-element.20.info, bf16[32,2048]{1,0:T(8,128)(2,1)S(1)} %collective-permute-done.7.refs_0_, ...), custom_call_target="tpu_custom_call" | custom-call | flops 2000000000 | bytes 4194304 | tf_op jit(solution)/shard_map/pallas_call | solution.py:216
  24.9 0.1 collective-permute-start.10
  25.0 1.9 %collective-permute-start.11 = (bf16[32,2176]{1,0:T(8,128)(2,1)S(1)}, bf16[32,2176]{1,0:T(8,128)(2,1)S(1)}, u32[]{:S(2)}, u32[]{:S(2)}) collective-permute-start(bf16[32,2176]{1,0:T(8,128)(2,1)S(1)} %get-tuple-element.29), channel_id=1, source_target_pairs={{0,8},{4,12},{8,0},{12,4},{16,24},{20,28},{24,16},{28,20},{1,9},{5... | collective-permute-start | bytes 417800 | tf_op jit(solution)/shard_map/ppermute | solution.py:312
  26.9 0.0 collective-permute-done.3.refs_1_
  26.9 1.6 %collective-permute-start.12 = (bf16[32,2176]{1,0:T(8,128)(2,1)S(1)}, bf16[32,2176]{1,0:T(8,128)(2,1)S(1)}, u32[]{:S(2)}, u32[]{:S(2)}) collective-permute-start(bf16[32,2176]{1,0:T(8,128)(2,1)S(1)} %get-tuple-element.30), channel_id=1, source_target_pairs={{0,4},{4,0},{8,12},{12,8},{16,20},{20,16},{24,28},{28,24},{1,5},{5... | collective-permute-start | bytes 417800 | tf_op jit(solution)/shard_map/ppermute | solution.py:312
  28.5 0.5 shard_map.75.near
  29.0 2.7 %collective-permute-start.18 = (bf16[32,2176]{1,0:T(8,128)(2,1)S(1)}, bf16[32,2176]{1,0:T(8,128)(2,1)S(1)}, u32[]{:S(2)}, u32[]{:S(2)}) collective-permute-start(bf16[32,2176]{1,0:T(8,128)(2,1)S(1)} %shard_map.75.near), channel_id=1, source_target_pairs={{0,24},{4,28},{8,16},{12,20},{16,8},{20,12},{24,0},{28,4},{1,25},{... | collective-permute-start | bytes 417800 | tf_op jit(solution)/shard_map/ppermute | solution.py:312
  31.6 1.3 %collective-permute-done.10.refs_1_ = bf16[32,2176]{1,0:T(8,128)(2,1)S(1)} collective-permute-done((bf16[32,2176]{1,0:T(8,128)(2,1)S(1)}, bf16[32,2176]{1,0:T(8,128)(2,1)S(1)}, u32[]{:S(2)}, u32[]{:S(2)}) %collective-permute-start.10) | collective-permute-done | bytes 139296 | tf_op jit(solution)/shard_map/ppermute | solution.py:312
  33.0 0.2 collective-permute-done.11.refs_2_
  33.2 0.5 shard_map.77.near
  33.7 2.3 %collective-permute-start.13 = (bf16[32,2176]{1,0:T(8,128)(2,1)S(1)}, bf16[32,2176]{1,0:T(8,128)(2,1)S(1)}, u32[]{:S(2)}, u32[]{:S(2)}) collective-permute-start(bf16[32,2176]{1,0:T(8,128)(2,1)S(1)} %shard_map.77.near), channel_id=1, source_target_pairs={{0,24},{4,28},{8,16},{12,20},{16,8},{20,12},{24,0},{28,4},{1,25},{... | collective-permute-start | bytes 417800 | tf_op jit(solution)/shard_map/ppermute | solution.py:312
  36.0 0.5 collective-permute-done.18.far
  36.5 0.3 shard_map.80.refs_0_
  36.9 0.8 %collective-permute-start.19 = (bf16[32,2048]{1,0:T(8,128)(2,1)S(1)}, bf16[32,2048]{1,0:T(8,128)(2,1)S(1)}, u32[]{:S(2)}, u32[]{:S(2)}) collective-permute-start(bf16[32,2048]{1,0:T(8,128)(2,1)S(1)} %shard_map.80.refs_0_), channel_id=1, source_target_pairs={{0,4},{4,0},{8,12},{12,8},{16,20},{20,16},{24,28},{28,24},{1,5},{5... | collective-permute-start | bytes 393224 | tf_op jit(solution)/shard_map/ppermute | solution.py:312
  37.7 2.9 %collective-permute-start.20 = (bf16[32,2048]{1,0:T(8,128)(2,1)S(1)}, bf16[32,2048]{1,0:T(8,128)(2,1)S(1)}, u32[]{:S(2)}, u32[]{:S(2)}) collective-permute-start(bf16[32,2048]{1,0:T(8,128)(2,1)S(1)} %shard_map.80.refs_0_), channel_id=1, source_target_pairs={{0,8},{4,12},{8,0},{12,4},{16,24},{20,28},{24,16},{28,20},{1,9},{5... | collective-permute-start | bytes 393224 | tf_op jit(solution)/shard_map/ppermute | solution.py:312
  40.5 1.4 %collective-permute-start.21 = (bf16[32,2048]{1,0:T(8,128)(2,1)S(1)}, bf16[32,2048]{1,0:T(8,128)(2,1)S(1)}, u32[]{:S(2)}, u32[]{:S(2)}) collective-permute-start(bf16[32,2048]{1,0:T(8,128)(2,1)S(1)} %shard_map.80.refs_0_), channel_id=1, source_target_pairs={{0,12},{4,8},{8,4},{12,0},{16,28},{20,24},{24,20},{28,16},{1,13},{... | collective-permute-start | bytes 393224 | tf_op jit(solution)/shard_map/ppermute | solution.py:312
  41.9 0.3 shard_map.78.refs_0_
  42.3 2.2 %collective-permute-start.14 = (bf16[32,2048]{1,0:T(8,128)(2,1)S(1)}, bf16[32,2048]{1,0:T(8,128)(2,1)S(1)}, u32[]{:S(2)}, u32[]{:S(2)}) collective-permute-start(bf16[32,2048]{1,0:T(8,128)(2,1)S(1)} %shard_map.78.refs_0_), channel_id=1, source_target_pairs={{0,4},{4,0},{8,12},{12,8},{16,20},{20,16},{24,28},{28,24},{1,5},{5... | collective-permute-start | bytes 393224 | tf_op jit(solution)/shard_map/ppermute | solution.py:312
  44.5 1.5 %collective-permute-start.16 = (bf16[32,2048]{1,0:T(8,128)(2,1)S(1)}, bf16[32,2048]{1,0:T(8,128)(2,1)S(1)}, u32[]{:S(2)}, u32[]{:S(2)}) collective-permute-start(bf16[32,2048]{1,0:T(8,128)(2,1)S(1)} %shard_map.78.refs_0_), channel_id=1, source_target_pairs={{0,12},{4,8},{8,4},{12,0},{16,28},{20,24},{24,20},{28,16},{1,13},{... | collective-permute-start | bytes 393224 | tf_op jit(solution)/shard_map/ppermute | solution.py:312
  46.0 1.4 %collective-permute-done.21.refs_3_ = bf16[32,2048]{1,0:T(8,128)(2,1)S(1)} collective-permute-done((bf16[32,2048]{1,0:T(8,128)(2,1)S(1)}, bf16[32,2048]{1,0:T(8,128)(2,1)S(1)}, u32[]{:S(2)}, u32[]{:S(2)}) %collective-permute-start.21) | collective-permute-done | bytes 131104 | tf_op jit(solution)/shard_map/ppermute | solution.py:312
  47.5 0.8 %shard_map.81 = (f32[64,1024]{1,0:T(8,128)S(1)}, bf16[64,1024]{1,0:T(8,128)(2,1)S(1)}) custom-call(bf16[32,2048]{1,0:T(8,128)(2,1)S(1)} %shard_map.80.refs_0_, bf16[32,2048]{1,0:T(8,128)(2,1)S(1)} %collective-permute-done.19.refs_1_, bf16[32,2048]{1,0:T(8,128)(2,1)S(1)} %collective-permute-done.20.refs_2_, ...), custom_call_target="tpu_custom_call" | custom-call | tf_op jit(solution)/shard_map/pallas_call | solution.py:300
  48.3 0.1 collective-permute-start.22
  48.3 0.6 collective-permute-done.14.refs_1_
  48.9 1.0 %collective-permute-done.15.refs_2_ = bf16[32,2048]{1,0:T(8,128)(2,1)S(1)} collective-permute-done((bf16[32,2048]{1,0:T(8,128)(2,1)S(1)}, bf16[32,2048]{1,0:T(8,128)(2,1)S(1)}, u32[]{:S(2)}, u32[]{:S(2)}) %collective-permute-start.15) | collective-permute-done | bytes 131104 | tf_op jit(solution)/shard_map/ppermute | solution.py:312
  49.9 2.1 %collective-permute-done.16.refs_3_ = bf16[32,2048]{1,0:T(8,128)(2,1)S(1)} collective-permute-done((bf16[32,2048]{1,0:T(8,128)(2,1)S(1)}, bf16[32,2048]{1,0:T(8,128)(2,1)S(1)}, u32[]{:S(2)}, u32[]{:S(2)}) %collective-permute-start.16) | collective-permute-done | bytes 131104 | tf_op jit(solution)/shard_map/ppermute | solution.py:312
  52.0 0.8 %shard_map.79 = (f32[64,1024]{1,0:T(8,128)S(1)}, bf16[64,1024]{1,0:T(8,128)(2,1)S(1)}) custom-call(bf16[32,2048]{1,0:T(8,128)(2,1)S(1)} %shard_map.78.refs_0_, bf16[32,2048]{1,0:T(8,128)(2,1)S(1)} %collective-permute-done.14.refs_1_, bf16[32,2048]{1,0:T(8,128)(2,1)S(1)} %collective-permute-done.15.refs_2_, ...), custom_call_target="tpu_custom_call" | custom-call | tf_op jit(solution)/shard_map/pallas_call | solution.py:300
  52.8 0.1 collective-permute-start.17
  52.9 1.3 %collective-permute-done.17 = bf16[64,1024]{1,0:T(8,128)(2,1)S(1)} collective-permute-done((bf16[64,1024]{1,0:T(8,128)(2,1)S(1)}, bf16[64,1024]{1,0:T(8,128)(2,1)S(1)}, u32[]{:S(2)}, u32[]{:S(2)}) %collective-permute-start.17) | collective-permute-done | bytes 131104 | tf_op jit(solution)/shard_map/ppermute | solution.py:312
  54.2 0.1 select_convert_fusion
  54.3 1.4 %collective-permute-start.23 = (bf16[64,1024]{1,0:T(8,128)(2,1)S(1)}, bf16[64,1024]{1,0:T(8,128)(2,1)S(1)}, u32[]{:S(2)}, u32[]{:S(2)}) collective-permute-start(bf16[64,1024]{1,0:T(8,128)(2,1)S(1)} %select_convert_fusion), channel_id=1, source_target_pairs={{0,2},{1,3},{2,0},{3,1},{4,6},{5,7},{6,4},{7,5},{8,10},{9,11},{10,... | collective-permute-start | bytes 393224 | tf_op jit(solution)/shard_map/ppermute | solution.py:312
  55.7 4.2 %collective-permute-done.23 = bf16[64,1024]{1,0:T(8,128)(2,1)S(1)} collective-permute-done((bf16[64,1024]{1,0:T(8,128)(2,1)S(1)}, bf16[64,1024]{1,0:T(8,128)(2,1)S(1)}, u32[]{:S(2)}, u32[]{:S(2)}) %collective-permute-start.23) | collective-permute-done | bytes 131104 | tf_op jit(solution)/shard_map/ppermute | solution.py:312
  59.9 0.7 %add_convert_fusion = bf16[64,1024]{1,0:T(8,128)(2,1)} fusion(bf16[64,1024]{1,0:T(8,128)(2,1)S(1)} %collective-permute-done.23, f32[64,1024]{1,0:T(8,128)S(1)} %get-tuple-element.31, bf16[64,1024]{1,0:T(8,128)(2,1)S(1)} %collective-permute-done.17, f32[64,1024]{1,0:T(8,128)S(1)} %get-tuple-element.33, bf16[64,1024]{1,0:T(8,128)(2,1)S(1)} %collective-permute-done.22, ...), kind=kLoop, calls=%fused_computation | loop fusion | flops 524288 | bytes 1048577 | tf_op jit(solution)/shard_map/convert_element_type | solution.py:340
  (15 shorter events, 0.0 us)
Async XLA Ops:
  0.0 15.5 %copy-start.1 = (bf16[32,2048]{1,0:T(8,128)(2,1)S(1)}, bf16[32,2048]{1,0:T(8,128)(2,1)}, u32[]{:S(2)}) copy-start(bf16[32,2048]{1,0:T(8,128)(2,1)} %refs_3_.1) | copy-start | bytes 393220
  0.0 11.6 %collective-permute-start.6 = (bf16[32,2048]{1,0:T(8,128)(2,1)}, bf16[32,2048]{1,0:T(8,128)(2,1)S(1)}, u32[]{:S(2)}, u32[]{:S(2)}) collective-permute-start(bf16[32,2048]{1,0:T(8,128)(2,1)} %refs_3_.1), channel_id=1, source_target_pairs={{0,24},{4,28},{8,16},{12,20},{16,8},{20,12},{24,0},{28,4},{1,25},{... | collective-permute-start | bytes 393224 | tf_op jit(solution)/shard_map/ppermute | solution.py:312
  5.1 8.7 %collective-permute-start = (bf16[32,2048]{1,0:T(8,128)(2,1)}, bf16[32,2048]{1,0:T(8,128)(2,1)S(1)}, u32[]{:S(2)}, u32[]{:S(2)}) collective-permute-start(bf16[32,2048]{1,0:T(8,128)(2,1)} %refs_3_.1), channel_id=1, source_target_pairs={{0,12},{4,8},{8,4},{12,0},{16,28},{20,24},{24,20},{28,16},{1,13},{... | collective-permute-start | bytes 393224 | tf_op jit(solution)/shard_map/ppermute | solution.py:312
  5.5 9.9 %collective-permute-start.1 = (bf16[32,2048]{1,0:T(8,128)(2,1)}, bf16[32,2048]{1,0:T(8,128)(2,1)S(1)}, u32[]{:S(2)}, u32[]{:S(2)}) collective-permute-start(bf16[32,2048]{1,0:T(8,128)(2,1)} %refs_3_.1), channel_id=1, source_target_pairs={{0,8},{4,12},{8,0},{12,4},{16,24},{20,28},{24,16},{28,20},{1,9},{5... | collective-permute-start | bytes 393224 | tf_op jit(solution)/shard_map/ppermute | solution.py:312
  8.0 7.5 %collective-permute-start.2 = (bf16[32,2048]{1,0:T(8,128)(2,1)}, bf16[32,2048]{1,0:T(8,128)(2,1)S(1)}, u32[]{:S(2)}, u32[]{:S(2)}) collective-permute-start(bf16[32,2048]{1,0:T(8,128)(2,1)} %refs_3_.1), channel_id=1, source_target_pairs={{0,4},{4,0},{8,12},{12,8},{16,20},{20,16},{24,28},{28,24},{1,5},{5... | collective-permute-start | bytes 393224 | tf_op jit(solution)/shard_map/ppermute | solution.py:312
  11.6 8.8 %collective-permute-start.7 = (bf16[32,2048]{1,0:T(8,128)(2,1)S(1)}, bf16[32,2048]{1,0:T(8,128)(2,1)S(1)}, u32[]{:S(2)}, u32[]{:S(2)}) collective-permute-start(bf16[32,2048]{1,0:T(8,128)(2,1)S(1)} %collective-permute-done.6.refs_3_), channel_id=1, source_target_pairs={{0,12},{4,8},{8,4},{12,0},{16,28},{20,24},{24,20},{28,16},{1,13},{... | collective-permute-start | bytes 393224 | tf_op jit(solution)/shard_map/ppermute | solution.py:312
  12.2 9.8 %collective-permute-start.8 = (bf16[32,2048]{1,0:T(8,128)(2,1)S(1)}, bf16[32,2048]{1,0:T(8,128)(2,1)S(1)}, u32[]{:S(2)}, u32[]{:S(2)}) collective-permute-start(bf16[32,2048]{1,0:T(8,128)(2,1)S(1)} %collective-permute-done.6.refs_3_), channel_id=1, source_target_pairs={{0,8},{4,12},{8,0},{12,4},{16,24},{20,28},{24,16},{28,20},{1,9},{5... | collective-permute-start | bytes 393224 | tf_op jit(solution)/shard_map/ppermute | solution.py:312
  13.8 8.2 %collective-permute-start.9 = (bf16[32,2048]{1,0:T(8,128)(2,1)S(1)}, bf16[32,2048]{1,0:T(8,128)(2,1)S(1)}, u32[]{:S(2)}, u32[]{:S(2)}) collective-permute-start(bf16[32,2048]{1,0:T(8,128)(2,1)S(1)} %collective-permute-done.6.refs_3_), channel_id=1, source_target_pairs={{0,4},{4,0},{8,12},{12,8},{16,20},{20,16},{24,28},{28,24},{1,5},{5... | collective-permute-start | bytes 393224 | tf_op jit(solution)/shard_map/ppermute | solution.py:312
  18.4 8.5 %collective-permute-start.3 = (bf16[32,2176]{1,0:T(8,128)(2,1)S(1)}, bf16[32,2176]{1,0:T(8,128)(2,1)S(1)}, u32[]{:S(2)}, u32[]{:S(2)}) collective-permute-start(bf16[32,2176]{1,0:T(8,128)(2,1)S(1)} %get-tuple-element.24), channel_id=1, source_target_pairs={{0,4},{4,0},{8,12},{12,8},{16,20},{20,16},{24,28},{28,24},{1,5},{5... | collective-permute-start | bytes 417800 | tf_op jit(solution)/shard_map/ppermute | solution.py:312
  18.5 10.0 %collective-permute-start.4 = (bf16[32,2176]{1,0:T(8,128)(2,1)S(1)}, bf16[32,2176]{1,0:T(8,128)(2,1)S(1)}, u32[]{:S(2)}, u32[]{:S(2)}) collective-permute-start(bf16[32,2176]{1,0:T(8,128)(2,1)S(1)} %get-tuple-element.25), channel_id=1, source_target_pairs={{0,8},{4,12},{8,0},{12,4},{16,24},{20,28},{24,16},{28,20},{1,9},{5... | collective-permute-start | bytes 417800 | tf_op jit(solution)/shard_map/ppermute | solution.py:312
  20.4 27.1 %copy-start = (bf16[2048,1024]{1,0:T(8,128)(2,1)S(1)}, bf16[2048,1024]{1,0:T(8,128)(2,1)}, u32[]{:S(2)}) copy-start(bf16[2048,1024]{1,0:T(8,128)(2,1)} %refs_4_.3) | copy-start | bytes 12582916
  20.4 8.1 %collective-permute-start.5 = (bf16[32,2176]{1,0:T(8,128)(2,1)S(1)}, bf16[32,2176]{1,0:T(8,128)(2,1)S(1)}, u32[]{:S(2)}, u32[]{:S(2)}) collective-permute-start(bf16[32,2176]{1,0:T(8,128)(2,1)S(1)} %get-tuple-element.26), channel_id=1, source_target_pairs={{0,12},{4,8},{8,4},{12,0},{16,28},{20,24},{24,20},{28,16},{1,13},{... | collective-permute-start | bytes 417800 | tf_op jit(solution)/shard_map/ppermute | solution.py:312
  24.9 8.0 %collective-permute-start.10 = (bf16[32,2176]{1,0:T(8,128)(2,1)S(1)}, bf16[32,2176]{1,0:T(8,128)(2,1)S(1)}, u32[]{:S(2)}, u32[]{:S(2)}) collective-permute-start(bf16[32,2176]{1,0:T(8,128)(2,1)S(1)} %get-tuple-element.28), channel_id=1, source_target_pairs={{0,12},{4,8},{8,4},{12,0},{16,28},{20,24},{24,20},{28,16},{1,13},{... | collective-permute-start | bytes 417800 | tf_op jit(solution)/shard_map/ppermute | solution.py:312
  25.0 8.2 %collective-permute-start.11 = (bf16[32,2176]{1,0:T(8,128)(2,1)S(1)}, bf16[32,2176]{1,0:T(8,128)(2,1)S(1)}, u32[]{:S(2)}, u32[]{:S(2)}) collective-permute-start(bf16[32,2176]{1,0:T(8,128)(2,1)S(1)} %get-tuple-element.29), channel_id=1, source_target_pairs={{0,8},{4,12},{8,0},{12,4},{16,24},{20,28},{24,16},{28,20},{1,9},{5... | collective-permute-start | bytes 417800 | tf_op jit(solution)/shard_map/ppermute | solution.py:312
  26.9 6.3 %collective-permute-start.12 = (bf16[32,2176]{1,0:T(8,128)(2,1)S(1)}, bf16[32,2176]{1,0:T(8,128)(2,1)S(1)}, u32[]{:S(2)}, u32[]{:S(2)}) collective-permute-start(bf16[32,2176]{1,0:T(8,128)(2,1)S(1)} %get-tuple-element.30), channel_id=1, source_target_pairs={{0,4},{4,0},{8,12},{12,8},{16,20},{20,16},{24,28},{28,24},{1,5},{5... | collective-permute-start | bytes 417800 | tf_op jit(solution)/shard_map/ppermute | solution.py:312
  29.0 7.6 %collective-permute-start.18 = (bf16[32,2176]{1,0:T(8,128)(2,1)S(1)}, bf16[32,2176]{1,0:T(8,128)(2,1)S(1)}, u32[]{:S(2)}, u32[]{:S(2)}) collective-permute-start(bf16[32,2176]{1,0:T(8,128)(2,1)S(1)} %shard_map.75.near), channel_id=1, source_target_pairs={{0,24},{4,28},{8,16},{12,20},{16,8},{20,12},{24,0},{28,4},{1,25},{... | collective-permute-start | bytes 417800 | tf_op jit(solution)/shard_map/ppermute | solution.py:312
  33.7 8.3 %collective-permute-start.13 = (bf16[32,2176]{1,0:T(8,128)(2,1)S(1)}, bf16[32,2176]{1,0:T(8,128)(2,1)S(1)}, u32[]{:S(2)}, u32[]{:S(2)}) collective-permute-start(bf16[32,2176]{1,0:T(8,128)(2,1)S(1)} %shard_map.77.near), channel_id=1, source_target_pairs={{0,24},{4,28},{8,16},{12,20},{16,8},{20,12},{24,0},{28,4},{1,25},{... | collective-permute-start | bytes 417800 | tf_op jit(solution)/shard_map/ppermute | solution.py:312
  36.9 7.6 %collective-permute-start.19 = (bf16[32,2048]{1,0:T(8,128)(2,1)S(1)}, bf16[32,2048]{1,0:T(8,128)(2,1)S(1)}, u32[]{:S(2)}, u32[]{:S(2)}) collective-permute-start(bf16[32,2048]{1,0:T(8,128)(2,1)S(1)} %shard_map.80.refs_0_), channel_id=1, source_target_pairs={{0,4},{4,0},{8,12},{12,8},{16,20},{20,16},{24,28},{28,24},{1,5},{5... | collective-permute-start | bytes 393224 | tf_op jit(solution)/shard_map/ppermute | solution.py:312
  37.7 8.3 %collective-permute-start.20 = (bf16[32,2048]{1,0:T(8,128)(2,1)S(1)}, bf16[32,2048]{1,0:T(8,128)(2,1)S(1)}, u32[]{:S(2)}, u32[]{:S(2)}) collective-permute-start(bf16[32,2048]{1,0:T(8,128)(2,1)S(1)} %shard_map.80.refs_0_), channel_id=1, source_target_pairs={{0,8},{4,12},{8,0},{12,4},{16,24},{20,28},{24,16},{28,20},{1,9},{5... | collective-permute-start | bytes 393224 | tf_op jit(solution)/shard_map/ppermute | solution.py:312
  40.5 6.9 %collective-permute-start.21 = (bf16[32,2048]{1,0:T(8,128)(2,1)S(1)}, bf16[32,2048]{1,0:T(8,128)(2,1)S(1)}, u32[]{:S(2)}, u32[]{:S(2)}) collective-permute-start(bf16[32,2048]{1,0:T(8,128)(2,1)S(1)} %shard_map.80.refs_0_), channel_id=1, source_target_pairs={{0,12},{4,8},{8,4},{12,0},{16,28},{20,24},{24,20},{28,16},{1,13},{... | collective-permute-start | bytes 393224 | tf_op jit(solution)/shard_map/ppermute | solution.py:312
  42.3 6.7 %collective-permute-start.14 = (bf16[32,2048]{1,0:T(8,128)(2,1)S(1)}, bf16[32,2048]{1,0:T(8,128)(2,1)S(1)}, u32[]{:S(2)}, u32[]{:S(2)}) collective-permute-start(bf16[32,2048]{1,0:T(8,128)(2,1)S(1)} %shard_map.78.refs_0_), channel_id=1, source_target_pairs={{0,4},{4,0},{8,12},{12,8},{16,20},{20,16},{24,28},{28,24},{1,5},{5... | collective-permute-start | bytes 393224 | tf_op jit(solution)/shard_map/ppermute | solution.py:312
  44.5 5.5 %collective-permute-start.15 = (bf16[32,2048]{1,0:T(8,128)(2,1)S(1)}, bf16[32,2048]{1,0:T(8,128)(2,1)S(1)}, u32[]{:S(2)}, u32[]{:S(2)}) collective-permute-start(bf16[32,2048]{1,0:T(8,128)(2,1)S(1)} %shard_map.78.refs_0_), channel_id=1, source_target_pairs={{0,8},{4,12},{8,0},{12,4},{16,24},{20,28},{24,16},{28,20},{1,9},{5... | collective-permute-start | bytes 393224 | tf_op jit(solution)/shard_map/ppermute | solution.py:312
  44.5 7.5 %collective-permute-start.16 = (bf16[32,2048]{1,0:T(8,128)(2,1)S(1)}, bf16[32,2048]{1,0:T(8,128)(2,1)S(1)}, u32[]{:S(2)}, u32[]{:S(2)}) collective-permute-start(bf16[32,2048]{1,0:T(8,128)(2,1)S(1)} %shard_map.78.refs_0_), channel_id=1, source_target_pairs={{0,12},{4,8},{8,4},{12,0},{16,28},{20,24},{24,20},{28,16},{1,13},{... | collective-permute-start | bytes 393224 | tf_op jit(solution)/shard_map/ppermute | solution.py:312
  48.3 4.7 %collective-permute-start.22 = (bf16[64,1024]{1,0:T(8,128)(2,1)S(1)}, bf16[64,1024]{1,0:T(8,128)(2,1)S(1)}, u32[]{:S(2)}, u32[]{:S(2)}) collective-permute-start(bf16[64,1024]{1,0:T(8,128)(2,1)S(1)} %get-tuple-element.34), channel_id=1, source_target_pairs={{0,1},{1,0},{2,3},{3,2},{4,5},{5,4},{6,7},{7,6},{8,9},{9,8},{10,11... | collective-permute-start | bytes 393224 | tf_op jit(solution)/shard_map/ppermute | solution.py:312
  52.8 1.4 %collective-permute-start.17 = (bf16[64,1024]{1,0:T(8,128)(2,1)S(1)}, bf16[64,1024]{1,0:T(8,128)(2,1)S(1)}, u32[]{:S(2)}, u32[]{:S(2)}) collective-permute-start(bf16[64,1024]{1,0:T(8,128)(2,1)S(1)} %get-tuple-element.32), channel_id=1, source_target_pairs={{0,1},{1,0},{2,3},{3,2},{4,5},{5,4},{6,7},{7,6},{8,9},{9,8},{10,11... | collective-permute-start | bytes 393224 | tf_op jit(solution)/shard_map/ppermute | solution.py:312
  54.3 5.6 %collective-permute-start.23 = (bf16[64,1024]{1,0:T(8,128)(2,1)S(1)}, bf16[64,1024]{1,0:T(8,128)(2,1)S(1)}, u32[]{:S(2)}, u32[]{:S(2)}) collective-permute-start(bf16[64,1024]{1,0:T(8,128)(2,1)S(1)} %select_convert_fusion), channel_id=1, source_target_pairs={{0,2},{1,3},{2,0},{3,1},{4,6},{5,7},{6,4},{7,5},{8,10},{9,11},{10,... | collective-permute-start | bytes 393224 | tf_op jit(solution)/shard_map/ppermute | solution.py:312

commit v13 on v7

--- a/solution.py
+++ b/solution.py
@@ -159,7 +159,7 @@
 def attend_kernel(plan, heads, lb, info, *refs):
     me = lax.axis_index("pages")
     chunks, page = plan.chunks, plan.page
-    queries, (k_ref, v_ref), outs = refs[:chunks], refs[chunks : chunks + 2], refs[chunks + 2 :]
+    queries, (k_ref, v_ref), outs = refs[:chunks][::-1], refs[chunks : chunks + 2], refs[chunks + 2 :]
     kv_heads, size = k_ref.shape[1], k_ref.shape[3]
     repeat = heads // kv_heads
     width = heads * size
@@ -220,7 +220,7 @@
         out_specs=(in_vmem(),) * plan.chunks,
         compiler_params=params(32),
         cost_estimate=pl.CostEstimate(flops=2 * 10**9, bytes_accessed=4 * 2**20, transcendentals=10**6),
-    )(info, *queries, keys, values)
+    )(info, *queries[::-1], keys, values)
 
 
 def merged(parts, stats):
@@ -280,7 +280,7 @@
 
 
 def sources_of(plan, lb):
-    return range(plan.group) if lb else reversed(range(plan.group))
+    return range(plan.group) if lb else [0, *middle_first(plan)]
 
 
 def project_kernel(plan, lb, *refs):
@@ -320,6 +320,10 @@
     return range(1, plan.group)
 
 
+def middle_first(plan):
+    return [*range(plan.group // 2, plan.group), *range(1, plan.group // 2)]
+
+
 def spread(x, plan):
     return {0: x} | {k: swap(x, "pages", k) for k in others(plan)}
 
@@ -330,7 +334,7 @@
     for lb, rows in enumerate((queries, far)):
         chunks = spread(rows, plan)
         outs = attend(plan, heads, lb, pages, [chunks[k] for k in range(plan.group)])
-        near.append(merge(heads, *(swap(outs[k], "pages", k) for k in reversed(others(plan))), outs[0]))
+        near.append(merge(heads, outs[0], *(swap(outs[k], "pages", k) for k in middle_first(plan))))
     across = [swap(x, "pages", plan.cross) for x in near]
     sums = [None, None]
     for lb in (1, 0):

time: 62.1 us -> 60.9 us (0.981)
  starting transfers between devices: 41 us -> 32.8 us
  Pallas kernels: 6.65 us -> 12 us
  waiting for transfers between devices: 13.4 us -> 15.4 us
    ppermute x24, starting transfers between devices: 41 us -> 32.8 us  [swap(): return lax.ppermute(x, axis, [(i, i ^ distance) for i in range(n)])]
    pallas_call x2, Pallas kernels: 1.29 us -> 5.87 us  [attend(): pl.pallas_call(functools.partial(attend_kernel, plan, heads, lb), out_sha...]
    ppermute x24, waiting for transfers between devices: 13.4 us -> 15.4 us  [swap(): return lax.ppermute(x, axis, [(i, i ^ distance) for i in range(n)])]
    pallas_call x1, Pallas kernels: 2.19 us -> 3.01 us  [fetch(): pl.pallas_call(functools.partial(fetch_kernel, plan, pages_dev), out_shap...]
  transfers between devices with their start and end apart: 24 -> 24, of which waited for: 10 -> 9; matrix products, arithmetic and copies ran while one was open for 0% -> 0% of each run, Pallas kernels for 11% -> 20%
where the time goes in v13:
time: 60.9 us; the launch traced here: 61.2 us
  starting transfers between devices  32.8 us (54%)
  waiting for transfers between devices  15.4 us (25%)
  Pallas kernels  12 us (20%)
  other arithmetic  0.78 us (1%)
    ppermute x24, starting transfers between devices, swap(): return lax.ppermute(x, axis, [(i, i ^ distance) for i in range(n)])  32.8 us
    ppermute x24, waiting for transfers between devices, swap(): return lax.ppermute(x, axis, [(i, i ^ distance) for i in range(n)])  15.4 us
    pallas_call x2, Pallas kernels, attend(): pl.pallas_call(functools.partial(attend_kernel, plan, heads, lb), out_sha...  5.87 us
    pallas_call x1, Pallas kernels, fetch(): pl.pallas_call(functools.partial(fetch_kernel, plan, pages_dev), out_shap...  3.01 us
    pallas_call x2, Pallas kernels, project(): pl.pallas_call(functools.partial(project_kernel, plan, lb), out_shape=(ja...  1.57 us
  transfers between devices with their start and end apart: 24, of which 9 were waited for; matrix products, arithmetic and copies ran while one was open for 0% of the time, Pallas kernels for 20%

profile of v13, /device:TPU:0, one launch (start us, length us, event | category | flops | bytes accessed | tf_op | source)
XLA Modules:
  0.0 61.2 jit_solution(12934022256088382016)
XLA Ops:
  0.0 5.0 %collective-permute-start.6 = (bf16[32,2048]{1,0:T(8,128)(2,1)}, bf16[32,2048]{1,0:T(8,128)(2,1)S(1)}, u32[]{:S(2)}, u32[]{:S(2)}) collective-permute-start(bf16[32,2048]{1,0:T(8,128)(2,1)} %refs_3_.1), channel_id=1, source_target_pairs={{0,24},{4,28},{8,16},{12,20},{16,8},{20,12},{24,0},{28,4},{1,25},{... | collective-permute-start | bytes 393224 | tf_op jit(solution)/shard_map/ppermute | solution.py:316
  5.1 0.5 collective-permute-start
  5.5 2.5 %collective-permute-start.1 = (bf16[32,2048]{1,0:T(8,128)(2,1)}, bf16[32,2048]{1,0:T(8,128)(2,1)S(1)}, u32[]{:S(2)}, u32[]{:S(2)}) collective-permute-start(bf16[32,2048]{1,0:T(8,128)(2,1)} %refs_3_.1), channel_id=1, source_target_pairs={{0,8},{4,12},{8,0},{12,4},{16,24},{20,28},{24,16},{28,20},{1,9},{5... | collective-permute-start | bytes 393224 | tf_op jit(solution)/shard_map/ppermute | solution.py:316
  8.0 0.5 collective-permute-start.2
  8.5 3.0 %shard_map.73 = (bf16[2,2,768,128]{3,2,1,0:T(8,128)(2,1)S(1)}, bf16[2,2,768,256]{3,2,1,0:T(8,128)(2,1)S(1)}, s32[2,3]{1,0:T(2,128)S(1)}) custom-call(s32[2,24]{1,0:T(2,128)} %select_hbm.1, s32[128]{0:T(128)} %table_hbm.1, s32[2]{0:T(128)} %stands_hbm.1, bf16[16,256,128]{2,1,0:T(8,128)(2,1)} %bitcast.2, bf16[16,256,128]{2,1,0:T(8,128)(2,1)} %bitcast.3), custom_call_target="tpu_custom_call" | custom-call | flops 2000000000 | bytes 8388608 | tf_op jit(solution)/shard_map/pallas_call | solution.py:118
  11.6 1.0 %collective-permute-start.7 = (bf16[32,2048]{1,0:T(8,128)(2,1)S(1)}, bf16[32,2048]{1,0:T(8,128)(2,1)S(1)}, u32[]{:S(2)}, u32[]{:S(2)}) collective-permute-start(bf16[32,2048]{1,0:T(8,128)(2,1)S(1)} %collective-permute-done.6.refs_3_), channel_id=1, source_target_pairs={{0,12},{4,8},{8,4},{12,0},{16,28},{20,24},{24,20},{28,16},{1,13},{... | collective-permute-start | bytes 393224 | tf_op jit(solution)/shard_map/ppermute | solution.py:316
  12.6 1.2 %collective-permute-start.8 = (bf16[32,2048]{1,0:T(8,128)(2,1)S(1)}, bf16[32,2048]{1,0:T(8,128)(2,1)S(1)}, u32[]{:S(2)}, u32[]{:S(2)}) collective-permute-start(bf16[32,2048]{1,0:T(8,128)(2,1)S(1)} %collective-permute-done.6.refs_3_), channel_id=1, source_target_pairs={{0,8},{4,12},{8,0},{12,4},{16,24},{20,28},{24,16},{28,20},{1,9},{5... | collective-permute-start | bytes 393224 | tf_op jit(solution)/shard_map/ppermute | solution.py:316
  13.8 0.0 collective-permute-done.refs_0_
  13.8 1.4 %collective-permute-start.9 = (bf16[32,2048]{1,0:T(8,128)(2,1)S(1)}, bf16[32,2048]{1,0:T(8,128)(2,1)S(1)}, u32[]{:S(2)}, u32[]{:S(2)}) collective-permute-start(bf16[32,2048]{1,0:T(8,128)(2,1)S(1)} %collective-permute-done.6.refs_3_), channel_id=1, source_target_pairs={{0,4},{4,0},{8,12},{12,8},{16,20},{20,16},{24,28},{28,24},{1,5},{5... | collective-permute-start | bytes 393224 | tf_op jit(solution)/shard_map/ppermute | solution.py:316
  15.1 0.3 collective-permute-done.1.refs_1_
  15.5 0.0 collective-permute-done.2.refs_2_
  15.5 2.9 %shard_map.74 = (bf16[32,2176]{1,0:T(8,128)(2,1)S(1)}, bf16[32,2176]{1,0:T(8,128)(2,1)S(1)}, bf16[32,2176]{1,0:T(8,128)(2,1)S(1)}, bf16[32,2176]{1,0:T(8,128)(2,1)S(1)}) custom-call(s32[2,3]{1,0:T(2,128)S(1)} %get-tuple-element.20.info, bf16[32,2048]{1,0:T(8,128)(2,1)S(1)} %collective-permute-done.refs_0_, ...), custom_call_target="tpu_custom_call" | custom-call | flops 2000000000 | bytes 4194304 | tf_op jit(solution)/shard_map/pallas_call | solution.py:216
  18.4 0.1 collective-permute-start.3
  18.5 2.8 %collective-permute-start.4 = (bf16[32,2176]{1,0:T(8,128)(2,1)S(1)}, bf16[32,2176]{1,0:T(8,128)(2,1)S(1)}, u32[]{:S(2)}, u32[]{:S(2)}) collective-permute-start(bf16[32,2176]{1,0:T(8,128)(2,1)S(1)} %get-tuple-element.25), channel_id=1, source_target_pairs={{0,12},{4,8},{8,4},{12,0},{16,28},{20,24},{24,20},{28,16},{1,13},{... | collective-permute-start | bytes 417800 | tf_op jit(solution)/shard_map/ppermute | solution.py:316
  21.3 0.0 collective-permute-done.7.refs_0_
  21.3 0.7 %collective-permute-start.5 = (bf16[32,2176]{1,0:T(8,128)(2,1)S(1)}, bf16[32,2176]{1,0:T(8,128)(2,1)S(1)}, u32[]{:S(2)}, u32[]{:S(2)}) collective-permute-start(bf16[32,2176]{1,0:T(8,128)(2,1)S(1)} %get-tuple-element.26), channel_id=1, source_target_pairs={{0,4},{4,0},{8,12},{12,8},{16,20},{20,16},{24,28},{28,24},{1,5},{5... | collective-permute-start | bytes 417800 | tf_op jit(solution)/shard_map/ppermute | solution.py:316
  22.0 0.0 collective-permute-done.8.refs_1_
  22.0 2.9 %shard_map.76 = (bf16[32,2176]{1,0:T(8,128)(2,1)S(1)}, bf16[32,2176]{1,0:T(8,128)(2,1)S(1)}, bf16[32,2176]{1,0:T(8,128)(2,1)S(1)}, bf16[32,2176]{1,0:T(8,128)(2,1)S(1)}) custom-call(s32[2,3]{1,0:T(2,128)S(1)} %get-tuple-element.20.info, bf16[32,2048]{1,0:T(8,128)(2,1)S(1)} %collective-permute-done.7.refs_0_, ...), custom_call_target="tpu_custom_call" | custom-call | flops 2000000000 | bytes 4194304 | tf_op jit(solution)/shard_map/pallas_call | solution.py:216
  24.9 0.1 collective-permute-start.10
  25.0 2.8 %collective-permute-start.11 = (bf16[32,2176]{1,0:T(8,128)(2,1)S(1)}, bf16[32,2176]{1,0:T(8,128)(2,1)S(1)}, u32[]{:S(2)}, u32[]{:S(2)}) collective-permute-start(bf16[32,2176]{1,0:T(8,128)(2,1)S(1)} %get-tuple-element.29), channel_id=1, source_target_pairs={{0,12},{4,8},{8,4},{12,0},{16,28},{20,24},{24,20},{28,16},{1,13},{... | collective-permute-start | bytes 417800 | tf_op jit(solution)/shard_map/ppermute | solution.py:316
  27.8 0.7 %collective-permute-start.12 = (bf16[32,2176]{1,0:T(8,128)(2,1)S(1)}, bf16[32,2176]{1,0:T(8,128)(2,1)S(1)}, u32[]{:S(2)}, u32[]{:S(2)}) collective-permute-start(bf16[32,2176]{1,0:T(8,128)(2,1)S(1)} %get-tuple-element.30), channel_id=1, source_target_pairs={{0,4},{4,0},{8,12},{12,8},{16,20},{20,16},{24,28},{28,24},{1,5},{5... | collective-permute-start | bytes 417800 | tf_op jit(solution)/shard_map/ppermute | solution.py:316
  28.5 0.1 collective-permute-done.4.refs_2_
  28.6 0.5 shard_map.75.near
  29.1 2.1 %collective-permute-start.18 = (bf16[32,2176]{1,0:T(8,128)(2,1)S(1)}, bf16[32,2176]{1,0:T(8,128)(2,1)S(1)}, u32[]{:S(2)}, u32[]{:S(2)}) collective-permute-start(bf16[32,2176]{1,0:T(8,128)(2,1)S(1)} %shard_map.75.near), channel_id=1, source_target_pairs={{0,24},{4,28},{8,16},{12,20},{16,8},{20,12},{24,0},{28,4},{1,25},{... | collective-permute-start | bytes 417800 | tf_op jit(solution)/shard_map/ppermute | solution.py:316
  31.2 3.5 %collective-permute-done.11.refs_2_ = bf16[32,2176]{1,0:T(8,128)(2,1)S(1)} collective-permute-done((bf16[32,2176]{1,0:T(8,128)(2,1)S(1)}, bf16[32,2176]{1,0:T(8,128)(2,1)S(1)}, u32[]{:S(2)}, u32[]{:S(2)}) %collective-permute-start.11) | collective-permute-done | bytes 139296 | tf_op jit(solution)/shard_map/ppermute | solution.py:316
  34.6 0.5 shard_map.77.near
  35.1 1.6 %collective-permute-start.13 = (bf16[32,2176]{1,0:T(8,128)(2,1)S(1)}, bf16[32,2176]{1,0:T(8,128)(2,1)S(1)}, u32[]{:S(2)}, u32[]{:S(2)}) collective-permute-start(bf16[32,2176]{1,0:T(8,128)(2,1)S(1)} %shard_map.77.near), channel_id=1, source_target_pairs={{0,24},{4,28},{8,16},{12,20},{16,8},{20,12},{24,0},{28,4},{1,25},{... | collective-permute-start | bytes 417800 | tf_op jit(solution)/shard_map/ppermute | solution.py:316
  36.7 0.3 shard_map.80.refs_0_
  37.0 1.2 %collective-permute-start.19 = (bf16[32,2048]{1,0:T(8,128)(2,1)S(1)}, bf16[32,2048]{1,0:T(8,128)(2,1)S(1)}, u32[]{:S(2)}, u32[]{:S(2)}) collective-permute-start(bf16[32,2048]{1,0:T(8,128)(2,1)S(1)} %shard_map.80.refs_0_), channel_id=1, source_target_pairs={{0,4},{4,0},{8,12},{12,8},{16,20},{20,16},{24,28},{28,24},{1,5},{5... | collective-permute-start | bytes 393224 | tf_op jit(solution)/shard_map/ppermute | solution.py:316
  38.2 3.5 %collective-permute-start.20 = (bf16[32,2048]{1,0:T(8,128)(2,1)S(1)}, bf16[32,2048]{1,0:T(8,128)(2,1)S(1)}, u32[]{:S(2)}, u32[]{:S(2)}) collective-permute-start(bf16[32,2048]{1,0:T(8,128)(2,1)S(1)} %shard_map.80.refs_0_), channel_id=1, source_target_pairs={{0,8},{4,12},{8,0},{12,4},{16,24},{20,28},{24,16},{28,20},{1,9},{5... | collective-permute-start | bytes 393224 | tf_op jit(solution)/shard_map/ppermute | solution.py:316
  41.7 1.0 %collective-permute-done.13.far = bf16[32,2176]{1,0:T(8,128)(2,1)S(1)} collective-permute-done((bf16[32,2176]{1,0:T(8,128)(2,1)S(1)}, bf16[32,2176]{1,0:T(8,128)(2,1)S(1)}, u32[]{:S(2)}, u32[]{:S(2)}) %collective-permute-start.13) | collective-permute-done | bytes 139296 | tf_op jit(solution)/shard_map/ppermute | solution.py:316
  42.7 0.3 shard_map.78.refs_0_
  43.0 0.8 %collective-permute-start.14 = (bf16[32,2048]{1,0:T(8,128)(2,1)S(1)}, bf16[32,2048]{1,0:T(8,128)(2,1)S(1)}, u32[]{:S(2)}, u32[]{:S(2)}) collective-permute-start(bf16[32,2048]{1,0:T(8,128)(2,1)S(1)} %shard_map.78.refs_0_), channel_id=1, source_target_pairs={{0,8},{4,12},{8,0},{12,4},{16,24},{20,28},{24,16},{28,20},{1,9},{5... | collective-permute-start | bytes 393224 | tf_op jit(solution)/shard_map/ppermute | solution.py:316
  43.8 2.2 %collective-permute-start.15 = (bf16[32,2048]{1,0:T(8,128)(2,1)S(1)}, bf16[32,2048]{1,0:T(8,128)(2,1)S(1)}, u32[]{:S(2)}, u32[]{:S(2)}) collective-permute-start(bf16[32,2048]{1,0:T(8,128)(2,1)S(1)} %shard_map.78.refs_0_), channel_id=1, source_target_pairs={{0,12},{4,8},{8,4},{12,0},{16,28},{20,24},{24,20},{28,16},{1,13},{... | collective-permute-start | bytes 393224 | tf_op jit(solution)/shard_map/ppermute | solution.py:316
  45.9 0.6 collective-permute-start.16
  46.6 2.3 %collective-permute-done.21.refs_3_ = bf16[32,2048]{1,0:T(8,128)(2,1)S(1)} collective-permute-done((bf16[32,2048]{1,0:T(8,128)(2,1)S(1)}, bf16[32,2048]{1,0:T(8,128)(2,1)S(1)}, u32[]{:S(2)}, u32[]{:S(2)}) %collective-permute-start.21) | collective-permute-done | bytes 131104 | tf_op jit(solution)/shard_map/ppermute | solution.py:316
  48.9 0.8 %shard_map.81 = (f32[64,1024]{1,0:T(8,128)S(1)}, bf16[64,1024]{1,0:T(8,128)(2,1)S(1)}) custom-call(bf16[32,2048]{1,0:T(8,128)(2,1)S(1)} %shard_map.80.refs_0_, bf16[32,2048]{1,0:T(8,128)(2,1)S(1)} %collective-permute-done.19.refs_1_, bf16[32,2048]{1,0:T(8,128)(2,1)S(1)} %collective-permute-done.20.refs_2_, ...), custom_call_target="tpu_custom_call" | custom-call | tf_op jit(solution)/shard_map/pallas_call | solution.py:304
  49.6 0.1 collective-permute-start.22
  49.7 0.0 collective-permute-done.14.refs_1_
  49.7 2.0 %collective-permute-done.15.refs_2_ = bf16[32,2048]{1,0:T(8,128)(2,1)S(1)} collective-permute-done((bf16[32,2048]{1,0:T(8,128)(2,1)S(1)}, bf16[32,2048]{1,0:T(8,128)(2,1)S(1)}, u32[]{:S(2)}, u32[]{:S(2)}) %collective-permute-start.15) | collective-permute-done | bytes 131104 | tf_op jit(solution)/shard_map/ppermute | solution.py:316
  51.7 0.8 %collective-permute-done.16.refs_3_ = bf16[32,2048]{1,0:T(8,128)(2,1)S(1)} collective-permute-done((bf16[32,2048]{1,0:T(8,128)(2,1)S(1)}, bf16[32,2048]{1,0:T(8,128)(2,1)S(1)}, u32[]{:S(2)}, u32[]{:S(2)}) %collective-permute-start.16) | collective-permute-done | bytes 131104 | tf_op jit(solution)/shard_map/ppermute | solution.py:316
  52.5 0.8 %shard_map.79 = (f32[64,1024]{1,0:T(8,128)S(1)}, bf16[64,1024]{1,0:T(8,128)(2,1)S(1)}) custom-call(bf16[32,2048]{1,0:T(8,128)(2,1)S(1)} %shard_map.78.refs_0_, bf16[32,2048]{1,0:T(8,128)(2,1)S(1)} %collective-permute-done.14.refs_1_, bf16[32,2048]{1,0:T(8,128)(2,1)S(1)} %collective-permute-done.15.refs_2_, ...), custom_call_target="tpu_custom_call" | custom-call | tf_op jit(solution)/shard_map/pallas_call | solution.py:304
  53.3 0.1 collective-permute-start.17
  53.5 1.3 %collective-permute-done.17 = bf16[64,1024]{1,0:T(8,128)(2,1)S(1)} collective-permute-done((bf16[64,1024]{1,0:T(8,128)(2,1)S(1)}, bf16[64,1024]{1,0:T(8,128)(2,1)S(1)}, u32[]{:S(2)}, u32[]{:S(2)}) %collective-permute-start.17) | collective-permute-done | bytes 131104 | tf_op jit(solution)/shard_map/ppermute | solution.py:316
  54.8 0.1 select_convert_fusion
  54.8 1.6 %collective-permute-start.23 = (bf16[64,1024]{1,0:T(8,128)(2,1)S(1)}, bf16[64,1024]{1,0:T(8,128)(2,1)S(1)}, u32[]{:S(2)}, u32[]{:S(2)}) collective-permute-start(bf16[64,1024]{1,0:T(8,128)(2,1)S(1)} %select_convert_fusion), channel_id=1, source_target_pairs={{0,2},{1,3},{2,0},{3,1},{4,6},{5,7},{6,4},{7,5},{8,10},{9,11},{10,... | collective-permute-start | bytes 393224 | tf_op jit(solution)/shard_map/ppermute | solution.py:316
  56.4 4.0 %collective-permute-done.23 = bf16[64,1024]{1,0:T(8,128)(2,1)S(1)} collective-permute-done((bf16[64,1024]{1,0:T(8,128)(2,1)S(1)}, bf16[64,1024]{1,0:T(8,128)(2,1)S(1)}, u32[]{:S(2)}, u32[]{:S(2)}) %collective-permute-start.23) | collective-permute-done | bytes 131104 | tf_op jit(solution)/shard_map/ppermute | solution.py:316
  60.4 0.7 %add_convert_fusion = bf16[64,1024]{1,0:T(8,128)(2,1)} fusion(bf16[64,1024]{1,0:T(8,128)(2,1)S(1)} %collective-permute-done.23, f32[64,1024]{1,0:T(8,128)S(1)} %get-tuple-element.31, bf16[64,1024]{1,0:T(8,128)(2,1)S(1)} %collective-permute-done.17, f32[64,1024]{1,0:T(8,128)S(1)} %get-tuple-element.33, bf16[64,1024]{1,0:T(8,128)(2,1)S(1)} %collective-permute-done.22, ...), kind=kLoop, calls=%fused_computation | loop fusion | flops 524288 | bytes 1048577 | tf_op jit(solution)/shard_map/convert_element_type | solution.py:347
  (15 shorter events, 0.0 us)
Async XLA Ops:
  0.0 15.5 %copy-start.1 = (bf16[32,2048]{1,0:T(8,128)(2,1)S(1)}, bf16[32,2048]{1,0:T(8,128)(2,1)}, u32[]{:S(2)}) copy-start(bf16[32,2048]{1,0:T(8,128)(2,1)} %refs_3_.1) | copy-start | bytes 393220
  0.0 11.6 %collective-permute-start.6 = (bf16[32,2048]{1,0:T(8,128)(2,1)}, bf16[32,2048]{1,0:T(8,128)(2,1)S(1)}, u32[]{:S(2)}, u32[]{:S(2)}) collective-permute-start(bf16[32,2048]{1,0:T(8,128)(2,1)} %refs_3_.1), channel_id=1, source_target_pairs={{0,24},{4,28},{8,16},{12,20},{16,8},{20,12},{24,0},{28,4},{1,25},{... | collective-permute-start | bytes 393224 | tf_op jit(solution)/shard_map/ppermute | solution.py:316
  5.1 8.7 %collective-permute-start = (bf16[32,2048]{1,0:T(8,128)(2,1)}, bf16[32,2048]{1,0:T(8,128)(2,1)S(1)}, u32[]{:S(2)}, u32[]{:S(2)}) collective-permute-start(bf16[32,2048]{1,0:T(8,128)(2,1)} %refs_3_.1), channel_id=1, source_target_pairs={{0,12},{4,8},{8,4},{12,0},{16,28},{20,24},{24,20},{28,16},{1,13},{... | collective-permute-start | bytes 393224 | tf_op jit(solution)/shard_map/ppermute | solution.py:316
  5.5 9.9 %collective-permute-start.1 = (bf16[32,2048]{1,0:T(8,128)(2,1)}, bf16[32,2048]{1,0:T(8,128)(2,1)S(1)}, u32[]{:S(2)}, u32[]{:S(2)}) collective-permute-start(bf16[32,2048]{1,0:T(8,128)(2,1)} %refs_3_.1), channel_id=1, source_target_pairs={{0,8},{4,12},{8,0},{12,4},{16,24},{20,28},{24,16},{28,20},{1,9},{5... | collective-permute-start | bytes 393224 | tf_op jit(solution)/shard_map/ppermute | solution.py:316
  8.0 7.5 %collective-permute-start.2 = (bf16[32,2048]{1,0:T(8,128)(2,1)}, bf16[32,2048]{1,0:T(8,128)(2,1)S(1)}, u32[]{:S(2)}, u32[]{:S(2)}) collective-permute-start(bf16[32,2048]{1,0:T(8,128)(2,1)} %refs_3_.1), channel_id=1, source_target_pairs={{0,4},{4,0},{8,12},{12,8},{16,20},{20,16},{24,28},{28,24},{1,5},{5... | collective-permute-start | bytes 393224 | tf_op jit(solution)/shard_map/ppermute | solution.py:316
  11.6 9.7 %collective-permute-start.7 = (bf16[32,2048]{1,0:T(8,128)(2,1)S(1)}, bf16[32,2048]{1,0:T(8,128)(2,1)S(1)}, u32[]{:S(2)}, u32[]{:S(2)}) collective-permute-start(bf16[32,2048]{1,0:T(8,128)(2,1)S(1)} %collective-permute-done.6.refs_3_), channel_id=1, source_target_pairs={{0,12},{4,8},{8,4},{12,0},{16,28},{20,24},{24,20},{28,16},{1,13},{... | collective-permute-start | bytes 393224 | tf_op jit(solution)/shard_map/ppermute | solution.py:316
  12.6 9.4 %collective-permute-start.8 = (bf16[32,2048]{1,0:T(8,128)(2,1)S(1)}, bf16[32,2048]{1,0:T(8,128)(2,1)S(1)}, u32[]{:S(2)}, u32[]{:S(2)}) collective-permute-start(bf16[32,2048]{1,0:T(8,128)(2,1)S(1)} %collective-permute-done.6.refs_3_), channel_id=1, source_target_pairs={{0,8},{4,12},{8,0},{12,4},{16,24},{20,28},{24,16},{28,20},{1,9},{5... | collective-permute-start | bytes 393224 | tf_op jit(solution)/shard_map/ppermute | solution.py:316
  13.8 8.2 %collective-permute-start.9 = (bf16[32,2048]{1,0:T(8,128)(2,1)S(1)}, bf16[32,2048]{1,0:T(8,128)(2,1)S(1)}, u32[]{:S(2)}, u32[]{:S(2)}) collective-permute-start(bf16[32,2048]{1,0:T(8,128)(2,1)S(1)} %collective-permute-done.6.refs_3_), channel_id=1, source_target_pairs={{0,4},{4,0},{8,12},{12,8},{16,20},{20,16},{24,28},{28,24},{1,5},{5... | collective-permute-start | bytes 393224 | tf_op jit(solution)/shard_map/ppermute | solution.py:316
  18.4 9.4 %collective-permute-start.3 = (bf16[32,2176]{1,0:T(8,128)(2,1)S(1)}, bf16[32,2176]{1,0:T(8,128)(2,1)S(1)}, u32[]{:S(2)}, u32[]{:S(2)}) collective-permute-start(bf16[32,2176]{1,0:T(8,128)(2,1)S(1)} %get-tuple-element.24), channel_id=1, source_target_pairs={{0,8},{4,12},{8,0},{12,4},{16,24},{20,28},{24,16},{28,20},{1,9},{5... | collective-permute-start | bytes 417800 | tf_op jit(solution)/shard_map/ppermute | solution.py:316
  18.5 10.1 %collective-permute-start.4 = (bf16[32,2176]{1,0:T(8,128)(2,1)S(1)}, bf16[32,2176]{1,0:T(8,128)(2,1)S(1)}, u32[]{:S(2)}, u32[]{:S(2)}) collective-permute-start(bf16[32,2176]{1,0:T(8,128)(2,1)S(1)} %get-tuple-element.25), channel_id=1, source_target_pairs={{0,12},{4,8},{8,4},{12,0},{16,28},{20,24},{24,20},{28,16},{1,13},{... | collective-permute-start | bytes 417800 | tf_op jit(solution)/shard_map/ppermute | solution.py:316
  21.3 27.6 %copy-start = (bf16[2048,1024]{1,0:T(8,128)(2,1)S(1)}, bf16[2048,1024]{1,0:T(8,128)(2,1)}, u32[]{:S(2)}) copy-start(bf16[2048,1024]{1,0:T(8,128)(2,1)} %refs_4_.3) | copy-start | bytes 12582916
  21.3 7.3 %collective-permute-start.5 = (bf16[32,2176]{1,0:T(8,128)(2,1)S(1)}, bf16[32,2176]{1,0:T(8,128)(2,1)S(1)}, u32[]{:S(2)}, u32[]{:S(2)}) collective-permute-start(bf16[32,2176]{1,0:T(8,128)(2,1)S(1)} %get-tuple-element.26), channel_id=1, source_target_pairs={{0,4},{4,0},{8,12},{12,8},{16,20},{20,16},{24,28},{28,24},{1,5},{5... | collective-permute-start | bytes 417800 | tf_op jit(solution)/shard_map/ppermute | solution.py:316
  24.9 6.2 %collective-permute-start.10 = (bf16[32,2176]{1,0:T(8,128)(2,1)S(1)}, bf16[32,2176]{1,0:T(8,128)(2,1)S(1)}, u32[]{:S(2)}, u32[]{:S(2)}) collective-permute-start(bf16[32,2176]{1,0:T(8,128)(2,1)S(1)} %get-tuple-element.28), channel_id=1, source_target_pairs={{0,8},{4,12},{8,0},{12,4},{16,24},{20,28},{24,16},{28,20},{1,9},{5... | collective-permute-start | bytes 417800 | tf_op jit(solution)/shard_map/ppermute | solution.py:316
  25.0 9.6 %collective-permute-start.11 = (bf16[32,2176]{1,0:T(8,128)(2,1)S(1)}, bf16[32,2176]{1,0:T(8,128)(2,1)S(1)}, u32[]{:S(2)}, u32[]{:S(2)}) collective-permute-start(bf16[32,2176]{1,0:T(8,128)(2,1)S(1)} %get-tuple-element.29), channel_id=1, source_target_pairs={{0,12},{4,8},{8,4},{12,0},{16,28},{20,24},{24,20},{28,16},{1,13},{... | collective-permute-start | bytes 417800 | tf_op jit(solution)/shard_map/ppermute | solution.py:316
  27.8 6.8 %collective-permute-start.12 = (bf16[32,2176]{1,0:T(8,128)(2,1)S(1)}, bf16[32,2176]{1,0:T(8,128)(2,1)S(1)}, u32[]{:S(2)}, u32[]{:S(2)}) collective-permute-start(bf16[32,2176]{1,0:T(8,128)(2,1)S(1)} %get-tuple-element.30), channel_id=1, source_target_pairs={{0,4},{4,0},{8,12},{12,8},{16,20},{20,16},{24,28},{28,24},{1,5},{5... | collective-permute-start | bytes 417800 | tf_op jit(solution)/shard_map/ppermute | solution.py:316
  29.1 7.6 %collective-permute-start.18 = (bf16[32,2176]{1,0:T(8,128)(2,1)S(1)}, bf16[32,2176]{1,0:T(8,128)(2,1)S(1)}, u32[]{:S(2)}, u32[]{:S(2)}) collective-permute-start(bf16[32,2176]{1,0:T(8,128)(2,1)S(1)} %shard_map.75.near), channel_id=1, source_target_pairs={{0,24},{4,28},{8,16},{12,20},{16,8},{20,12},{24,0},{28,4},{1,25},{... | collective-permute-start | bytes 417800 | tf_op jit(solution)/shard_map/ppermute | solution.py:316
  35.1 7.6 %collective-permute-start.13 = (bf16[32,2176]{1,0:T(8,128)(2,1)S(1)}, bf16[32,2176]{1,0:T(8,128)(2,1)S(1)}, u32[]{:S(2)}, u32[]{:S(2)}) collective-permute-start(bf16[32,2176]{1,0:T(8,128)(2,1)S(1)} %shard_map.77.near), channel_id=1, source_target_pairs={{0,24},{4,28},{8,16},{12,20},{16,8},{20,12},{24,0},{28,4},{1,25},{... | collective-permute-start | bytes 417800 | tf_op jit(solution)/shard_map/ppermute | solution.py:316
  37.0 8.9 %collective-permute-start.19 = (bf16[32,2048]{1,0:T(8,128)(2,1)S(1)}, bf16[32,2048]{1,0:T(8,128)(2,1)S(1)}, u32[]{:S(2)}, u32[]{:S(2)}) collective-permute-start(bf16[32,2048]{1,0:T(8,128)(2,1)S(1)} %shard_map.80.refs_0_), channel_id=1, source_target_pairs={{0,4},{4,0},{8,12},{12,8},{16,20},{20,16},{24,28},{28,24},{1,5},{5... | collective-permute-start | bytes 393224 | tf_op jit(solution)/shard_map/ppermute | solution.py:316
  38.2 8.3 %collective-permute-start.20 = (bf16[32,2048]{1,0:T(8,128)(2,1)S(1)}, bf16[32,2048]{1,0:T(8,128)(2,1)S(1)}, u32[]{:S(2)}, u32[]{:S(2)}) collective-permute-start(bf16[32,2048]{1,0:T(8,128)(2,1)S(1)} %shard_map.80.refs_0_), channel_id=1, source_target_pairs={{0,8},{4,12},{8,0},{12,4},{16,24},{20,28},{24,16},{28,20},{1,9},{5... | collective-permute-start | bytes 393224 | tf_op jit(solution)/shard_map/ppermute | solution.py:316
  41.7 7.2 %collective-permute-start.21 = (bf16[32,2048]{1,0:T(8,128)(2,1)S(1)}, bf16[32,2048]{1,0:T(8,128)(2,1)S(1)}, u32[]{:S(2)}, u32[]{:S(2)}) collective-permute-start(bf16[32,2048]{1,0:T(8,128)(2,1)S(1)} %shard_map.80.refs_0_), channel_id=1, source_target_pairs={{0,12},{4,8},{8,4},{12,0},{16,28},{20,24},{24,20},{28,16},{1,13},{... | collective-permute-start | bytes 393224 | tf_op jit(solution)/shard_map/ppermute | solution.py:316
  43.0 6.7 %collective-permute-start.14 = (bf16[32,2048]{1,0:T(8,128)(2,1)S(1)}, bf16[32,2048]{1,0:T(8,128)(2,1)S(1)}, u32[]{:S(2)}, u32[]{:S(2)}) collective-permute-start(bf16[32,2048]{1,0:T(8,128)(2,1)S(1)} %shard_map.78.refs_0_), channel_id=1, source_target_pairs={{0,8},{4,12},{8,0},{12,4},{16,24},{20,28},{24,16},{28,20},{1,9},{5... | collective-permute-start | bytes 393224 | tf_op jit(solution)/shard_map/ppermute | solution.py:316
  43.8 7.9 %collective-permute-start.15 = (bf16[32,2048]{1,0:T(8,128)(2,1)S(1)}, bf16[32,2048]{1,0:T(8,128)(2,1)S(1)}, u32[]{:S(2)}, u32[]{:S(2)}) collective-permute-start(bf16[32,2048]{1,0:T(8,128)(2,1)S(1)} %shard_map.78.refs_0_), channel_id=1, source_target_pairs={{0,12},{4,8},{8,4},{12,0},{16,28},{20,24},{24,20},{28,16},{1,13},{... | collective-permute-start | bytes 393224 | tf_op jit(solution)/shard_map/ppermute | solution.py:316
  45.9 6.6 %collective-permute-start.16 = (bf16[32,2048]{1,0:T(8,128)(2,1)S(1)}, bf16[32,2048]{1,0:T(8,128)(2,1)S(1)}, u32[]{:S(2)}, u32[]{:S(2)}) collective-permute-start(bf16[32,2048]{1,0:T(8,128)(2,1)S(1)} %shard_map.78.refs_0_), channel_id=1, source_target_pairs={{0,4},{4,0},{8,12},{12,8},{16,20},{20,16},{24,28},{28,24},{1,5},{5... | collective-permute-start | bytes 393224 | tf_op jit(solution)/shard_map/ppermute | solution.py:316
  49.6 3.8 %collective-permute-start.22 = (bf16[64,1024]{1,0:T(8,128)(2,1)S(1)}, bf16[64,1024]{1,0:T(8,128)(2,1)S(1)}, u32[]{:S(2)}, u32[]{:S(2)}) collective-permute-start(bf16[64,1024]{1,0:T(8,128)(2,1)S(1)} %get-tuple-element.34), channel_id=1, source_target_pairs={{0,1},{1,0},{2,3},{3,2},{4,5},{5,4},{6,7},{7,6},{8,9},{9,8},{10,11... | collective-permute-start | bytes 393224 | tf_op jit(solution)/shard_map/ppermute | solution.py:316
  53.3 1.4 %collective-permute-start.17 = (bf16[64,1024]{1,0:T(8,128)(2,1)S(1)}, bf16[64,1024]{1,0:T(8,128)(2,1)S(1)}, u32[]{:S(2)}, u32[]{:S(2)}) collective-permute-start(bf16[64,1024]{1,0:T(8,128)(2,1)S(1)} %get-tuple-element.32), channel_id=1, source_target_pairs={{0,1},{1,0},{2,3},{3,2},{4,5},{5,4},{6,7},{7,6},{8,9},{9,8},{10,11... | collective-permute-start | bytes 393224 | tf_op jit(solution)/shard_map/ppermute | solution.py:316
  54.8 5.6 %collective-permute-start.23 = (bf16[64,1024]{1,0:T(8,128)(2,1)S(1)}, bf16[64,1024]{1,0:T(8,128)(2,1)S(1)}, u32[]{:S(2)}, u32[]{:S(2)}) collective-permute-start(bf16[64,1024]{1,0:T(8,128)(2,1)S(1)} %select_convert_fusion), channel_id=1, source_target_pairs={{0,2},{1,3},{2,0},{3,1},{4,6},{5,7},{6,4},{7,5},{8,10},{9,11},{10,... | collective-permute-start | bytes 393224 | tf_op jit(solution)/shard_map/ppermute | solution.py:316

commit v14 on v13

--- a/solution.py
+++ b/solution.py
@@ -334,7 +334,8 @@
     for lb, rows in enumerate((queries, far)):
         chunks = spread(rows, plan)
         outs = attend(plan, heads, lb, pages, [chunks[k] for k in range(plan.group)])
-        near.append(merge(heads, outs[0], *(swap(outs[k], "pages", k) for k in middle_first(plan))))
+        order = reversed(others(plan)) if lb else others(plan)
+        near.append(merge(heads, outs[0], *(swap(outs[k], "pages", k) for k in order)))
     across = [swap(x, "pages", plan.cross) for x in near]
     sums = [None, None]
     for lb in (1, 0):

time: 60.9 us -> 60.8 us (level)
  Pallas kernels: 12 us -> 6.65 us
  starting transfers between devices: 32.8 us -> 36 us
  waiting for transfers between devices: 15.4 us -> 17.2 us
    pallas_call x2, Pallas kernels: 5.87 us -> 1.29 us  [attend(): pl.pallas_call(functools.partial(attend_kernel, plan, heads, lb), out_sha...]
    ppermute x24, starting transfers between devices: 32.8 us -> 36 us  [swap(): return lax.ppermute(x, axis, [(i, i ^ distance) for i in range(n)])]
    ppermute x24, waiting for transfers between devices: 15.4 us -> 17.2 us  [swap(): return lax.ppermute(x, axis, [(i, i ^ distance) for i in range(n)])]
    pallas_call x1, Pallas kernels: 3.01 us -> 2.19 us  [fetch(): pl.pallas_call(functools.partial(fetch_kernel, plan, pages_dev), out_shap...]
  transfers between devices with their start and end apart: 24 -> 24, of which waited for: 9 -> 12; matrix products, arithmetic and copies ran while one was open for 0% -> 0% of each run, Pallas kernels for 20% -> 11%
where the time goes in v14:
time: 60.8 us
  starting transfers between devices  36 us (59%)
  waiting for transfers between devices  17.2 us (28%)
  Pallas kernels  6.65 us (11%)
  other arithmetic  0.78 us (1%)
    ppermute x24, starting transfers between devices, swap(): return lax.ppermute(x, axis, [(i, i ^ distance) for i in range(n)])  36 us
    ppermute x24, waiting for transfers between devices, swap(): return lax.ppermute(x, axis, [(i, i ^ distance) for i in range(n)])  17.2 us
    pallas_call x1, Pallas kernels, fetch(): pl.pallas_call(functools.partial(fetch_kernel, plan, pages_dev), out_shap...  2.19 us
    pallas_call x2, Pallas kernels, project(): pl.pallas_call(functools.partial(project_kernel, plan, lb), out_shape=(ja...  1.57 us
    pallas_call x2, Pallas kernels, attend(): pl.pallas_call(functools.partial(attend_kernel, plan, heads, lb), out_sha...  1.29 us
  transfers between devices with their start and end apart: 24, of which 12 were waited for; matrix products, arithmetic and copies ran while one was open for 0% of the time, Pallas kernels for 11%

profile of v14, /device:TPU:0, one launch (start us, length us, event | category | flops | bytes accessed | tf_op | source)
XLA Modules:
  0.0 60.8 jit_solution(193231523512269397)
XLA Ops:
  0.0 5.0 %collective-permute-start.6 = (bf16[32,2048]{1,0:T(8,128)(2,1)}, bf16[32,2048]{1,0:T(8,128)(2,1)S(1)}, u32[]{:S(2)}, u32[]{:S(2)}) collective-permute-start(bf16[32,2048]{1,0:T(8,128)(2,1)} %refs_3_.1), channel_id=1, source_target_pairs={{0,24},{4,28},{8,16},{12,20},{16,8},{20,12},{24,0},{28,4},{1,25},{... | collective-permute-start | bytes 393224 | tf_op jit(solution)/shard_map/ppermute | solution.py:316
  5.1 0.5 collective-permute-start
  5.5 2.5 %collective-permute-start.1 = (bf16[32,2048]{1,0:T(8,128)(2,1)}, bf16[32,2048]{1,0:T(8,128)(2,1)S(1)}, u32[]{:S(2)}, u32[]{:S(2)}) collective-permute-start(bf16[32,2048]{1,0:T(8,128)(2,1)} %refs_3_.1), channel_id=1, source_target_pairs={{0,8},{4,12},{8,0},{12,4},{16,24},{20,28},{24,16},{28,20},{1,9},{5... | collective-permute-start | bytes 393224 | tf_op jit(solution)/shard_map/ppermute | solution.py:316
  8.0 0.5 collective-permute-start.2
  8.5 2.2 %shard_map.73 = (bf16[2,2,768,128]{3,2,1,0:T(8,128)(2,1)S(1)}, bf16[2,2,768,256]{3,2,1,0:T(8,128)(2,1)S(1)}, s32[2,3]{1,0:T(2,128)S(1)}) custom-call(s32[2,24]{1,0:T(2,128)} %select_hbm.1, s32[128]{0:T(128)} %table_hbm.1, s32[2]{0:T(128)} %stands_hbm.1, bf16[16,256,128]{2,1,0:T(8,128)(2,1)} %bitcast.2, bf16[16,256,128]{2,1,0:T(8,128)(2,1)} %bitcast.3), custom_call_target="tpu_custom_call" | custom-call | flops 2000000000 | bytes 8388608 | tf_op jit(solution)/shard_map/pallas_call | solution.py:118
  10.8 1.5 %collective-permute-start.7 = (bf16[32,2048]{1,0:T(8,128)(2,1)S(1)}, bf16[32,2048]{1,0:T(8,128)(2,1)S(1)}, u32[]{:S(2)}, u32[]{:S(2)}) collective-permute-start(bf16[32,2048]{1,0:T(8,128)(2,1)S(1)} %collective-permute-done.6.refs_3_), channel_id=1, source_target_pairs={{0,12},{4,8},{8,4},{12,0},{16,28},{20,24},{24,20},{28,16},{1,13},{... | collective-permute-start | bytes 393224 | tf_op jit(solution)/shard_map/ppermute | solution.py:316
  12.2 2.4 %collective-permute-start.8 = (bf16[32,2048]{1,0:T(8,128)(2,1)S(1)}, bf16[32,2048]{1,0:T(8,128)(2,1)S(1)}, u32[]{:S(2)}, u32[]{:S(2)}) collective-permute-start(bf16[32,2048]{1,0:T(8,128)(2,1)S(1)} %collective-permute-done.6.refs_3_), channel_id=1, source_target_pairs={{0,8},{4,12},{8,0},{12,4},{16,24},{20,28},{24,16},{28,20},{1,9},{5... | collective-permute-start | bytes 393224 | tf_op jit(solution)/shard_map/ppermute | solution.py:316
  14.6 0.0 collective-permute-done.refs_0_
  14.6 0.0 collective-permute-start.9
  14.6 0.9 %collective-permute-done.1.refs_1_ = bf16[32,2048]{1,0:T(8,128)(2,1)S(1)} collective-permute-done((bf16[32,2048]{1,0:T(8,128)(2,1)}, bf16[32,2048]{1,0:T(8,128)(2,1)S(1)}, u32[]{:S(2)}, u32[]{:S(2)}) %collective-permute-start.1) | collective-permute-done | bytes 131104 | tf_op jit(solution)/shard_map/ppermute | solution.py:316
  15.5 0.6 %shard_map.74 = (bf16[32,2176]{1,0:T(8,128)(2,1)S(1)}, bf16[32,2176]{1,0:T(8,128)(2,1)S(1)}, bf16[32,2176]{1,0:T(8,128)(2,1)S(1)}, bf16[32,2176]{1,0:T(8,128)(2,1)S(1)}) custom-call(s32[2,3]{1,0:T(2,128)S(1)} %get-tuple-element.20.info, bf16[32,2048]{1,0:T(8,128)(2,1)S(1)} %collective-permute-done.refs_0_, ...), custom_call_target="tpu_custom_call" | custom-call | flops 2000000000 | bytes 4194304 | tf_op jit(solution)/shard_map/pallas_call | solution.py:216
  16.1 3.5 %collective-permute-start.3 = (bf16[32,2176]{1,0:T(8,128)(2,1)S(1)}, bf16[32,2176]{1,0:T(8,128)(2,1)S(1)}, u32[]{:S(2)}, u32[]{:S(2)}) collective-permute-start(bf16[32,2176]{1,0:T(8,128)(2,1)S(1)} %get-tuple-element.24), channel_id=1, source_target_pairs={{0,4},{4,0},{8,12},{12,8},{16,20},{20,16},{24,28},{28,24},{1,5},{5... | collective-permute-start | bytes 417800 | tf_op jit(solution)/shard_map/ppermute | solution.py:316
  19.6 0.7 %collective-permute-start.4 = (bf16[32,2176]{1,0:T(8,128)(2,1)S(1)}, bf16[32,2176]{1,0:T(8,128)(2,1)S(1)}, u32[]{:S(2)}, u32[]{:S(2)}) collective-permute-start(bf16[32,2176]{1,0:T(8,128)(2,1)S(1)} %get-tuple-element.25), channel_id=1, source_target_pairs={{0,8},{4,12},{8,0},{12,4},{16,24},{20,28},{24,16},{28,20},{1,9},{5... | collective-permute-start | bytes 417800 | tf_op jit(solution)/shard_map/ppermute | solution.py:316
  20.4 1.5 %collective-permute-start.5 = (bf16[32,2176]{1,0:T(8,128)(2,1)S(1)}, bf16[32,2176]{1,0:T(8,128)(2,1)S(1)}, u32[]{:S(2)}, u32[]{:S(2)}) collective-permute-start(bf16[32,2176]{1,0:T(8,128)(2,1)S(1)} %get-tuple-element.26), channel_id=1, source_target_pairs={{0,12},{4,8},{8,4},{12,0},{16,28},{20,24},{24,20},{28,16},{1,13},{... | collective-permute-start | bytes 417800 | tf_op jit(solution)/shard_map/ppermute | solution.py:316
  21.8 0.6 %shard_map.76 = (bf16[32,2176]{1,0:T(8,128)(2,1)S(1)}, bf16[32,2176]{1,0:T(8,128)(2,1)S(1)}, bf16[32,2176]{1,0:T(8,128)(2,1)S(1)}, bf16[32,2176]{1,0:T(8,128)(2,1)S(1)}) custom-call(s32[2,3]{1,0:T(2,128)S(1)} %get-tuple-element.20.info, bf16[32,2048]{1,0:T(8,128)(2,1)S(1)} %collective-permute-done.7.refs_0_, ...), custom_call_target="tpu_custom_call" | custom-call | flops 2000000000 | bytes 4194304 | tf_op jit(solution)/shard_map/pallas_call | solution.py:216
  22.5 1.6 %collective-permute-start.10 = (bf16[32,2176]{1,0:T(8,128)(2,1)S(1)}, bf16[32,2176]{1,0:T(8,128)(2,1)S(1)}, u32[]{:S(2)}, u32[]{:S(2)}) collective-permute-start(bf16[32,2176]{1,0:T(8,128)(2,1)S(1)} %get-tuple-element.28), channel_id=1, source_target_pairs={{0,12},{4,8},{8,4},{12,0},{16,28},{20,24},{24,20},{28,16},{1,13},{... | collective-permute-start | bytes 417800 | tf_op jit(solution)/shard_map/ppermute | solution.py:316
  24.1 3.5 %collective-permute-start.11 = (bf16[32,2176]{1,0:T(8,128)(2,1)S(1)}, bf16[32,2176]{1,0:T(8,128)(2,1)S(1)}, u32[]{:S(2)}, u32[]{:S(2)}) collective-permute-start(bf16[32,2176]{1,0:T(8,128)(2,1)S(1)} %get-tuple-element.29), channel_id=1, source_target_pairs={{0,8},{4,12},{8,0},{12,4},{16,24},{20,28},{24,16},{28,20},{1,9},{5... | collective-permute-start | bytes 417800 | tf_op jit(solution)/shard_map/ppermute | solution.py:316
  27.6 0.6 %collective-permute-start.12 = (bf16[32,2176]{1,0:T(8,128)(2,1)S(1)}, bf16[32,2176]{1,0:T(8,128)(2,1)S(1)}, u32[]{:S(2)}, u32[]{:S(2)}) collective-permute-start(bf16[32,2176]{1,0:T(8,128)(2,1)S(1)} %get-tuple-element.30), channel_id=1, source_target_pairs={{0,4},{4,0},{8,12},{12,8},{16,20},{20,16},{24,28},{28,24},{1,5},{5... | collective-permute-start | bytes 417800 | tf_op jit(solution)/shard_map/ppermute | solution.py:316
  28.3 1.0 %collective-permute-done.5.refs_3_ = bf16[32,2176]{1,0:T(8,128)(2,1)S(1)} collective-permute-done((bf16[32,2176]{1,0:T(8,128)(2,1)S(1)}, bf16[32,2176]{1,0:T(8,128)(2,1)S(1)}, u32[]{:S(2)}, u32[]{:S(2)}) %collective-permute-start.5) | collective-permute-done | bytes 139296 | tf_op jit(solution)/shard_map/ppermute | solution.py:316
  29.3 0.5 shard_map.75.near
  29.8 1.8 %collective-permute-start.18 = (bf16[32,2176]{1,0:T(8,128)(2,1)S(1)}, bf16[32,2176]{1,0:T(8,128)(2,1)S(1)}, u32[]{:S(2)}, u32[]{:S(2)}) collective-permute-start(bf16[32,2176]{1,0:T(8,128)(2,1)S(1)} %shard_map.75.near), channel_id=1, source_target_pairs={{0,24},{4,28},{8,16},{12,20},{16,8},{20,12},{24,0},{28,4},{1,25},{... | collective-permute-start | bytes 417800 | tf_op jit(solution)/shard_map/ppermute | solution.py:316
  31.6 0.1 collective-permute-done.10.refs_1_
  31.7 2.8 %collective-permute-done.11.refs_2_ = bf16[32,2176]{1,0:T(8,128)(2,1)S(1)} collective-permute-done((bf16[32,2176]{1,0:T(8,128)(2,1)S(1)}, bf16[32,2176]{1,0:T(8,128)(2,1)S(1)}, u32[]{:S(2)}, u32[]{:S(2)}) %collective-permute-start.11) | collective-permute-done | bytes 139296 | tf_op jit(solution)/shard_map/ppermute | solution.py:316
  34.5 0.5 shard_map.77.near
  35.0 1.5 %collective-permute-start.13 = (bf16[32,2176]{1,0:T(8,128)(2,1)S(1)}, bf16[32,2176]{1,0:T(8,128)(2,1)S(1)}, u32[]{:S(2)}, u32[]{:S(2)}) collective-permute-start(bf16[32,2176]{1,0:T(8,128)(2,1)S(1)} %shard_map.77.near), channel_id=1, source_target_pairs={{0,24},{4,28},{8,16},{12,20},{16,8},{20,12},{24,0},{28,4},{1,25},{... | collective-permute-start | bytes 417800 | tf_op jit(solution)/shard_map/ppermute | solution.py:316
  36.6 1.0 %collective-permute-done.18.far = bf16[32,2176]{1,0:T(8,128)(2,1)S(1)} collective-permute-done((bf16[32,2176]{1,0:T(8,128)(2,1)S(1)}, bf16[32,2176]{1,0:T(8,128)(2,1)S(1)}, u32[]{:S(2)}, u32[]{:S(2)}) %collective-permute-start.18) | collective-permute-done | bytes 139296 | tf_op jit(solution)/shard_map/ppermute | solution.py:316
  37.5 0.3 shard_map.80.refs_0_
  37.9 0.1 collective-permute-start.19
  37.9 3.4 %collective-permute-start.20 = (bf16[32,2048]{1,0:T(8,128)(2,1)S(1)}, bf16[32,2048]{1,0:T(8,128)(2,1)S(1)}, u32[]{:S(2)}, u32[]{:S(2)}) collective-permute-start(bf16[32,2048]{1,0:T(8,128)(2,1)S(1)} %shard_map.80.refs_0_), channel_id=1, source_target_pairs={{0,8},{4,12},{8,0},{12,4},{16,24},{20,28},{24,16},{28,20},{1,9},{5... | collective-permute-start | bytes 393224 | tf_op jit(solution)/shard_map/ppermute | solution.py:316
  41.4 0.1 collective-permute-start.21
  41.4 1.5 %collective-permute-done.13.far = bf16[32,2176]{1,0:T(8,128)(2,1)S(1)} collective-permute-done((bf16[32,2176]{1,0:T(8,128)(2,1)S(1)}, bf16[32,2176]{1,0:T(8,128)(2,1)S(1)}, u32[]{:S(2)}, u32[]{:S(2)}) %collective-permute-start.13) | collective-permute-done | bytes 139296 | tf_op jit(solution)/shard_map/ppermute | solution.py:316
  42.9 0.3 shard_map.78.refs_0_
  43.2 0.5 collective-permute-start.14
  43.8 2.0 %collective-permute-start.15 = (bf16[32,2048]{1,0:T(8,128)(2,1)S(1)}, bf16[32,2048]{1,0:T(8,128)(2,1)S(1)}, u32[]{:S(2)}, u32[]{:S(2)}) collective-permute-start(bf16[32,2048]{1,0:T(8,128)(2,1)S(1)} %shard_map.78.refs_0_), channel_id=1, source_target_pairs={{0,12},{4,8},{8,4},{12,0},{16,28},{20,24},{24,20},{28,16},{1,13},{... | collective-permute-start | bytes 393224 | tf_op jit(solution)/shard_map/ppermute | solution.py:316
  45.8 1.0 %collective-permute-start.16 = (bf16[32,2048]{1,0:T(8,128)(2,1)S(1)}, bf16[32,2048]{1,0:T(8,128)(2,1)S(1)}, u32[]{:S(2)}, u32[]{:S(2)}) collective-permute-start(bf16[32,2048]{1,0:T(8,128)(2,1)S(1)} %shard_map.78.refs_0_), channel_id=1, source_target_pairs={{0,4},{4,0},{8,12},{12,8},{16,20},{20,16},{24,28},{28,24},{1,5},{5... | collective-permute-start | bytes 393224 | tf_op jit(solution)/shard_map/ppermute | solution.py:316
  46.8 2.0 %collective-permute-done.21.refs_3_ = bf16[32,2048]{1,0:T(8,128)(2,1)S(1)} collective-permute-done((bf16[32,2048]{1,0:T(8,128)(2,1)S(1)}, bf16[32,2048]{1,0:T(8,128)(2,1)S(1)}, u32[]{:S(2)}, u32[]{:S(2)}) %collective-permute-start.21) | collective-permute-done | bytes 131104 | tf_op jit(solution)/shard_map/ppermute | solution.py:316
  48.8 0.8 %shard_map.81 = (f32[64,1024]{1,0:T(8,128)S(1)}, bf16[64,1024]{1,0:T(8,128)(2,1)S(1)}) custom-call(bf16[32,2048]{1,0:T(8,128)(2,1)S(1)} %shard_map.80.refs_0_, bf16[32,2048]{1,0:T(8,128)(2,1)S(1)} %collective-permute-done.19.refs_1_, bf16[32,2048]{1,0:T(8,128)(2,1)S(1)} %collective-permute-done.20.refs_2_, ...), custom_call_target="tpu_custom_call" | custom-call | tf_op jit(solution)/shard_map/pallas_call | solution.py:304
  49.6 0.1 collective-permute-start.22
  49.7 0.3 collective-permute-done.14.refs_1_
  50.0 1.8 %collective-permute-done.15.refs_2_ = bf16[32,2048]{1,0:T(8,128)(2,1)S(1)} collective-permute-done((bf16[32,2048]{1,0:T(8,128)(2,1)S(1)}, bf16[32,2048]{1,0:T(8,128)(2,1)S(1)}, u32[]{:S(2)}, u32[]{:S(2)}) %collective-permute-start.15) | collective-permute-done | bytes 131104 | tf_op jit(solution)/shard_map/ppermute | solution.py:316
  51.8 0.3 collective-permute-done.16.refs_3_
  52.2 0.8 %shard_map.79 = (f32[64,1024]{1,0:T(8,128)S(1)}, bf16[64,1024]{1,0:T(8,128)(2,1)S(1)}) custom-call(bf16[32,2048]{1,0:T(8,128)(2,1)S(1)} %shard_map.78.refs_0_, bf16[32,2048]{1,0:T(8,128)(2,1)S(1)} %collective-permute-done.14.refs_1_, bf16[32,2048]{1,0:T(8,128)(2,1)S(1)} %collective-permute-done.15.refs_2_, ...), custom_call_target="tpu_custom_call" | custom-call | tf_op jit(solution)/shard_map/pallas_call | solution.py:304
  52.9 0.1 collective-permute-start.17
  53.1 1.3 %collective-permute-done.17 = bf16[64,1024]{1,0:T(8,128)(2,1)S(1)} collective-permute-done((bf16[64,1024]{1,0:T(8,128)(2,1)S(1)}, bf16[64,1024]{1,0:T(8,128)(2,1)S(1)}, u32[]{:S(2)}, u32[]{:S(2)}) %collective-permute-start.17) | collective-permute-done | bytes 131104 | tf_op jit(solution)/shard_map/ppermute | solution.py:316
  54.4 0.1 select_convert_fusion
  54.4 1.6 %collective-permute-start.23 = (bf16[64,1024]{1,0:T(8,128)(2,1)S(1)}, bf16[64,1024]{1,0:T(8,128)(2,1)S(1)}, u32[]{:S(2)}, u32[]{:S(2)}) collective-permute-start(bf16[64,1024]{1,0:T(8,128)(2,1)S(1)} %select_convert_fusion), channel_id=1, source_target_pairs={{0,2},{1,3},{2,0},{3,1},{4,6},{5,7},{6,4},{7,5},{8,10},{9,11},{10,... | collective-permute-start | bytes 393224 | tf_op jit(solution)/shard_map/ppermute | solution.py:316
  56.0 4.0 %collective-permute-done.23 = bf16[64,1024]{1,0:T(8,128)(2,1)S(1)} collective-permute-done((bf16[64,1024]{1,0:T(8,128)(2,1)S(1)}, bf16[64,1024]{1,0:T(8,128)(2,1)S(1)}, u32[]{:S(2)}, u32[]{:S(2)}) %collective-permute-start.23) | collective-permute-done | bytes 131104 | tf_op jit(solution)/shard_map/ppermute | solution.py:316
  60.0 0.7 %add_convert_fusion = bf16[64,1024]{1,0:T(8,128)(2,1)} fusion(bf16[64,1024]{1,0:T(8,128)(2,1)S(1)} %collective-permute-done.23, f32[64,1024]{1,0:T(8,128)S(1)} %get-tuple-element.31, bf16[64,1024]{1,0:T(8,128)(2,1)S(1)} %collective-permute-done.17, f32[64,1024]{1,0:T(8,128)S(1)} %get-tuple-element.33, bf16[64,1024]{1,0:T(8,128)(2,1)S(1)} %collective-permute-done.22, ...), kind=kLoop, calls=%fused_computation | loop fusion | flops 524288 | bytes 1048577 | tf_op jit(solution)/shard_map/convert_element_type | solution.py:348
  (15 shorter events, 0.0 us)
Async XLA Ops:
  0.0 15.5 %copy-start.1 = (bf16[32,2048]{1,0:T(8,128)(2,1)S(1)}, bf16[32,2048]{1,0:T(8,128)(2,1)}, u32[]{:S(2)}) copy-start(bf16[32,2048]{1,0:T(8,128)(2,1)} %refs_3_.1) | copy-start | bytes 393220
  0.0 10.7 %collective-permute-start.6 = (bf16[32,2048]{1,0:T(8,128)(2,1)}, bf16[32,2048]{1,0:T(8,128)(2,1)S(1)}, u32[]{:S(2)}, u32[]{:S(2)}) collective-permute-start(bf16[32,2048]{1,0:T(8,128)(2,1)} %refs_3_.1), channel_id=1, source_target_pairs={{0,24},{4,28},{8,16},{12,20},{16,8},{20,12},{24,0},{28,4},{1,25},{... | collective-permute-start | bytes 393224 | tf_op jit(solution)/shard_map/ppermute | solution.py:316
  5.1 9.5 %collective-permute-start = (bf16[32,2048]{1,0:T(8,128)(2,1)}, bf16[32,2048]{1,0:T(8,128)(2,1)S(1)}, u32[]{:S(2)}, u32[]{:S(2)}) collective-permute-start(bf16[32,2048]{1,0:T(8,128)(2,1)} %refs_3_.1), channel_id=1, source_target_pairs={{0,12},{4,8},{8,4},{12,0},{16,28},{20,24},{24,20},{28,16},{1,13},{... | collective-permute-start | bytes 393224 | tf_op jit(solution)/shard_map/ppermute | solution.py:316
  5.5 9.9 %collective-permute-start.1 = (bf16[32,2048]{1,0:T(8,128)(2,1)}, bf16[32,2048]{1,0:T(8,128)(2,1)S(1)}, u32[]{:S(2)}, u32[]{:S(2)}) collective-permute-start(bf16[32,2048]{1,0:T(8,128)(2,1)} %refs_3_.1), channel_id=1, source_target_pairs={{0,8},{4,12},{8,0},{12,4},{16,24},{20,28},{24,16},{28,20},{1,9},{5... | collective-permute-start | bytes 393224 | tf_op jit(solution)/shard_map/ppermute | solution.py:316
  8.0 7.5 %collective-permute-start.2 = (bf16[32,2048]{1,0:T(8,128)(2,1)}, bf16[32,2048]{1,0:T(8,128)(2,1)S(1)}, u32[]{:S(2)}, u32[]{:S(2)}) collective-permute-start(bf16[32,2048]{1,0:T(8,128)(2,1)} %refs_3_.1), channel_id=1, source_target_pairs={{0,4},{4,0},{8,12},{12,8},{16,20},{20,16},{24,28},{28,24},{1,5},{5... | collective-permute-start | bytes 393224 | tf_op jit(solution)/shard_map/ppermute | solution.py:316
  10.8 9.6 %collective-permute-start.7 = (bf16[32,2048]{1,0:T(8,128)(2,1)S(1)}, bf16[32,2048]{1,0:T(8,128)(2,1)S(1)}, u32[]{:S(2)}, u32[]{:S(2)}) collective-permute-start(bf16[32,2048]{1,0:T(8,128)(2,1)S(1)} %collective-permute-done.6.refs_3_), channel_id=1, source_target_pairs={{0,12},{4,8},{8,4},{12,0},{16,28},{20,24},{24,20},{28,16},{1,13},{... | collective-permute-start | bytes 393224 | tf_op jit(solution)/shard_map/ppermute | solution.py:316
  12.2 9.6 %collective-permute-start.8 = (bf16[32,2048]{1,0:T(8,128)(2,1)S(1)}, bf16[32,2048]{1,0:T(8,128)(2,1)S(1)}, u32[]{:S(2)}, u32[]{:S(2)}) collective-permute-start(bf16[32,2048]{1,0:T(8,128)(2,1)S(1)} %collective-permute-done.6.refs_3_), channel_id=1, source_target_pairs={{0,8},{4,12},{8,0},{12,4},{16,24},{20,28},{24,16},{28,20},{1,9},{5... | collective-permute-start | bytes 393224 | tf_op jit(solution)/shard_map/ppermute | solution.py:316
  14.6 7.2 %collective-permute-start.9 = (bf16[32,2048]{1,0:T(8,128)(2,1)S(1)}, bf16[32,2048]{1,0:T(8,128)(2,1)S(1)}, u32[]{:S(2)}, u32[]{:S(2)}) collective-permute-start(bf16[32,2048]{1,0:T(8,128)(2,1)S(1)} %collective-permute-done.6.refs_3_), channel_id=1, source_target_pairs={{0,4},{4,0},{8,12},{12,8},{16,20},{20,16},{24,28},{28,24},{1,5},{5... | collective-permute-start | bytes 393224 | tf_op jit(solution)/shard_map/ppermute | solution.py:316
  16.1 11.5 %collective-permute-start.3 = (bf16[32,2176]{1,0:T(8,128)(2,1)S(1)}, bf16[32,2176]{1,0:T(8,128)(2,1)S(1)}, u32[]{:S(2)}, u32[]{:S(2)}) collective-permute-start(bf16[32,2176]{1,0:T(8,128)(2,1)S(1)} %get-tuple-element.24), channel_id=1, source_target_pairs={{0,4},{4,0},{8,12},{12,8},{16,20},{20,16},{24,28},{28,24},{1,5},{5... | collective-permute-start | bytes 417800 | tf_op jit(solution)/shard_map/ppermute | solution.py:316
  19.6 8.6 %collective-permute-start.4 = (bf16[32,2176]{1,0:T(8,128)(2,1)S(1)}, bf16[32,2176]{1,0:T(8,128)(2,1)S(1)}, u32[]{:S(2)}, u32[]{:S(2)}) collective-permute-start(bf16[32,2176]{1,0:T(8,128)(2,1)S(1)} %get-tuple-element.25), channel_id=1, source_target_pairs={{0,8},{4,12},{8,0},{12,4},{16,24},{20,28},{24,16},{28,20},{1,9},{5... | collective-permute-start | bytes 417800 | tf_op jit(solution)/shard_map/ppermute | solution.py:316
  20.4 28.4 %copy-start = (bf16[2048,1024]{1,0:T(8,128)(2,1)S(1)}, bf16[2048,1024]{1,0:T(8,128)(2,1)}, u32[]{:S(2)}) copy-start(bf16[2048,1024]{1,0:T(8,128)(2,1)} %refs_4_.3) | copy-start | bytes 12582916
  20.4 8.9 %collective-permute-start.5 = (bf16[32,2176]{1,0:T(8,128)(2,1)S(1)}, bf16[32,2176]{1,0:T(8,128)(2,1)S(1)}, u32[]{:S(2)}, u32[]{:S(2)}) collective-permute-start(bf16[32,2176]{1,0:T(8,128)(2,1)S(1)} %get-tuple-element.26), channel_id=1, source_target_pairs={{0,12},{4,8},{8,4},{12,0},{16,28},{20,24},{24,20},{28,16},{1,13},{... | collective-permute-start | bytes 417800 | tf_op jit(solution)/shard_map/ppermute | solution.py:316
  22.5 9.2 %collective-permute-start.10 = (bf16[32,2176]{1,0:T(8,128)(2,1)S(1)}, bf16[32,2176]{1,0:T(8,128)(2,1)S(1)}, u32[]{:S(2)}, u32[]{:S(2)}) collective-permute-start(bf16[32,2176]{1,0:T(8,128)(2,1)S(1)} %get-tuple-element.28), channel_id=1, source_target_pairs={{0,12},{4,8},{8,4},{12,0},{16,28},{20,24},{24,20},{28,16},{1,13},{... | collective-permute-start | bytes 417800 | tf_op jit(solution)/shard_map/ppermute | solution.py:316
  24.1 10.4 %collective-permute-start.11 = (bf16[32,2176]{1,0:T(8,128)(2,1)S(1)}, bf16[32,2176]{1,0:T(8,128)(2,1)S(1)}, u32[]{:S(2)}, u32[]{:S(2)}) collective-permute-start(bf16[32,2176]{1,0:T(8,128)(2,1)S(1)} %get-tuple-element.29), channel_id=1, source_target_pairs={{0,8},{4,12},{8,0},{12,4},{16,24},{20,28},{24,16},{28,20},{1,9},{5... | collective-permute-start | bytes 417800 | tf_op jit(solution)/shard_map/ppermute | solution.py:316
  27.6 6.9 %collective-permute-start.12 = (bf16[32,2176]{1,0:T(8,128)(2,1)S(1)}, bf16[32,2176]{1,0:T(8,128)(2,1)S(1)}, u32[]{:S(2)}, u32[]{:S(2)}) collective-permute-start(bf16[32,2176]{1,0:T(8,128)(2,1)S(1)} %get-tuple-element.30), channel_id=1, source_target_pairs={{0,4},{4,0},{8,12},{12,8},{16,20},{20,16},{24,28},{28,24},{1,5},{5... | collective-permute-start | bytes 417800 | tf_op jit(solution)/shard_map/ppermute | solution.py:316
  29.8 7.7 %collective-permute-start.18 = (bf16[32,2176]{1,0:T(8,128)(2,1)S(1)}, bf16[32,2176]{1,0:T(8,128)(2,1)S(1)}, u32[]{:S(2)}, u32[]{:S(2)}) collective-permute-start(bf16[32,2176]{1,0:T(8,128)(2,1)S(1)} %shard_map.75.near), channel_id=1, source_target_pairs={{0,24},{4,28},{8,16},{12,20},{16,8},{20,12},{24,0},{28,4},{1,25},{... | collective-permute-start | bytes 417800 | tf_op jit(solution)/shard_map/ppermute | solution.py:316
  35.0 7.9 %collective-permute-start.13 = (bf16[32,2176]{1,0:T(8,128)(2,1)S(1)}, bf16[32,2176]{1,0:T(8,128)(2,1)S(1)}, u32[]{:S(2)}, u32[]{:S(2)}) collective-permute-start(bf16[32,2176]{1,0:T(8,128)(2,1)S(1)} %shard_map.77.near), channel_id=1, source_target_pairs={{0,24},{4,28},{8,16},{12,20},{16,8},{20,12},{24,0},{28,4},{1,25},{... | collective-permute-start | bytes 417800 | tf_op jit(solution)/shard_map/ppermute | solution.py:316
  37.9 7.9 %collective-permute-start.19 = (bf16[32,2048]{1,0:T(8,128)(2,1)S(1)}, bf16[32,2048]{1,0:T(8,128)(2,1)S(1)}, u32[]{:S(2)}, u32[]{:S(2)}) collective-permute-start(bf16[32,2048]{1,0:T(8,128)(2,1)S(1)} %shard_map.80.refs_0_), channel_id=1, source_target_pairs={{0,4},{4,0},{8,12},{12,8},{16,20},{20,16},{24,28},{28,24},{1,5},{5... | collective-permute-start | bytes 393224 | tf_op jit(solution)/shard_map/ppermute | solution.py:316
  37.9 8.9 %collective-permute-start.20 = (bf16[32,2048]{1,0:T(8,128)(2,1)S(1)}, bf16[32,2048]{1,0:T(8,128)(2,1)S(1)}, u32[]{:S(2)}, u32[]{:S(2)}) collective-permute-start(bf16[32,2048]{1,0:T(8,128)(2,1)S(1)} %shard_map.80.refs_0_), channel_id=1, source_target_pairs={{0,8},{4,12},{8,0},{12,4},{16,24},{20,28},{24,16},{28,20},{1,9},{5... | collective-permute-start | bytes 393224 | tf_op jit(solution)/shard_map/ppermute | solution.py:316
  41.4 7.4 %collective-permute-start.21 = (bf16[32,2048]{1,0:T(8,128)(2,1)S(1)}, bf16[32,2048]{1,0:T(8,128)(2,1)S(1)}, u32[]{:S(2)}, u32[]{:S(2)}) collective-permute-start(bf16[32,2048]{1,0:T(8,128)(2,1)S(1)} %shard_map.80.refs_0_), channel_id=1, source_target_pairs={{0,12},{4,8},{8,4},{12,0},{16,28},{20,24},{24,20},{28,16},{1,13},{... | collective-permute-start | bytes 393224 | tf_op jit(solution)/shard_map/ppermute | solution.py:316
  43.2 6.7 %collective-permute-start.14 = (bf16[32,2048]{1,0:T(8,128)(2,1)S(1)}, bf16[32,2048]{1,0:T(8,128)(2,1)S(1)}, u32[]{:S(2)}, u32[]{:S(2)}) collective-permute-start(bf16[32,2048]{1,0:T(8,128)(2,1)S(1)} %shard_map.78.refs_0_), channel_id=1, source_target_pairs={{0,8},{4,12},{8,0},{12,4},{16,24},{20,28},{24,16},{28,20},{1,9},{5... | collective-permute-start | bytes 393224 | tf_op jit(solution)/shard_map/ppermute | solution.py:316
  43.8 8.0 %collective-permute-start.15 = (bf16[32,2048]{1,0:T(8,128)(2,1)S(1)}, bf16[32,2048]{1,0:T(8,128)(2,1)S(1)}, u32[]{:S(2)}, u32[]{:S(2)}) collective-permute-start(bf16[32,2048]{1,0:T(8,128)(2,1)S(1)} %shard_map.78.refs_0_), channel_id=1, source_target_pairs={{0,12},{4,8},{8,4},{12,0},{16,28},{20,24},{24,20},{28,16},{1,13},{... | collective-permute-start | bytes 393224 | tf_op jit(solution)/shard_map/ppermute | solution.py:316
  45.8 6.4 %collective-permute-start.16 = (bf16[32,2048]{1,0:T(8,128)(2,1)S(1)}, bf16[32,2048]{1,0:T(8,128)(2,1)S(1)}, u32[]{:S(2)}, u32[]{:S(2)}) collective-permute-start(bf16[32,2048]{1,0:T(8,128)(2,1)S(1)} %shard_map.78.refs_0_), channel_id=1, source_target_pairs={{0,4},{4,0},{8,12},{12,8},{16,20},{20,16},{24,28},{28,24},{1,5},{5... | collective-permute-start | bytes 393224 | tf_op jit(solution)/shard_map/ppermute | solution.py:316
  49.6 3.5 %collective-permute-start.22 = (bf16[64,1024]{1,0:T(8,128)(2,1)S(1)}, bf16[64,1024]{1,0:T(8,128)(2,1)S(1)}, u32[]{:S(2)}, u32[]{:S(2)}) collective-permute-start(bf16[64,1024]{1,0:T(8,128)(2,1)S(1)} %get-tuple-element.34), channel_id=1, source_target_pairs={{0,1},{1,0},{2,3},{3,2},{4,5},{5,4},{6,7},{7,6},{8,9},{9,8},{10,11... | collective-permute-start | bytes 393224 | tf_op jit(solution)/shard_map/ppermute | solution.py:316
  52.9 1.4 %collective-permute-start.17 = (bf16[64,1024]{1,0:T(8,128)(2,1)S(1)}, bf16[64,1024]{1,0:T(8,128)(2,1)S(1)}, u32[]{:S(2)}, u32[]{:S(2)}) collective-permute-start(bf16[64,1024]{1,0:T(8,128)(2,1)S(1)} %get-tuple-element.32), channel_id=1, source_target_pairs={{0,1},{1,0},{2,3},{3,2},{4,5},{5,4},{6,7},{7,6},{8,9},{9,8},{10,11... | collective-permute-start | bytes 393224 | tf_op jit(solution)/shard_map/ppermute | solution.py:316
  54.4 5.6 %collective-permute-start.23 = (bf16[64,1024]{1,0:T(8,128)(2,1)S(1)}, bf16[64,1024]{1,0:T(8,128)(2,1)S(1)}, u32[]{:S(2)}, u32[]{:S(2)}) collective-permute-start(bf16[64,1024]{1,0:T(8,128)(2,1)S(1)} %select_convert_fusion), channel_id=1, source_target_pairs={{0,2},{1,3},{2,0},{3,1},{4,6},{5,7},{6,4},{7,5},{8,10},{9,11},{10,... | collective-permute-start | bytes 393224 | tf_op jit(solution)/shard_map/ppermute | solution.py:316

commit v15 on v13

--- a/solution.py
+++ b/solution.py
@@ -334,7 +334,7 @@
     for lb, rows in enumerate((queries, far)):
         chunks = spread(rows, plan)
         outs = attend(plan, heads, lb, pages, [chunks[k] for k in range(plan.group)])
-        near.append(merge(heads, outs[0], *(swap(outs[k], "pages", k) for k in middle_first(plan))))
+        near.append(merge(heads, outs[0], *(swap(outs[k], "pages", k) for k in others(plan))))
     across = [swap(x, "pages", plan.cross) for x in near]
     sums = [None, None]
     for lb in (1, 0):

time: 60.9 us -> 60.6 us (level)
  waiting for transfers between devices: 15.4 us -> 13.8 us
  starting transfers between devices: 32.8 us -> 33.7 us
    ppermute x24, waiting for transfers between devices: 15.4 us -> 13.8 us  [swap(): return lax.ppermute(x, axis, [(i, i ^ distance) for i in range(n)])]
    ppermute x24, starting transfers between devices: 32.8 us -> 33.7 us  [swap(): return lax.ppermute(x, axis, [(i, i ^ distance) for i in range(n)])]
  transfers between devices with their start and end apart: 24 -> 24, of which waited for: 9 -> 11; matrix products, arithmetic and copies ran while one was open for 0% -> 0% of each run, Pallas kernels for 20% -> 20%
where the time goes in v15:
time: 60.6 us; the launch traced here: 60.5 us
  starting transfers between devices  33.7 us (56%)
  waiting for transfers between devices  13.8 us (23%)
  Pallas kernels  12 us (20%)
  other arithmetic  0.78 us (1%)
    ppermute x24, starting transfers between devices, swap(): return lax.ppermute(x, axis, [(i, i ^ distance) for i in range(n)])  33.7 us
    ppermute x24, waiting for transfers between devices, swap(): return lax.ppermute(x, axis, [(i, i ^ distance) for i in range(n)])  13.8 us
    pallas_call x2, Pallas kernels, attend(): pl.pallas_call(functools.partial(attend_kernel, plan, heads, lb), out_sha...  5.87 us
    pallas_call x1, Pallas kernels, fetch(): pl.pallas_call(functools.partial(fetch_kernel, plan, pages_dev), out_shap...  3.01 us
    pallas_call x2, Pallas kernels, project(): pl.pallas_call(functools.partial(project_kernel, plan, lb), out_shape=(ja...  1.57 us
  transfers between devices with their start and end apart: 24, of which 11 were waited for; matrix products, arithmetic and copies ran while one was open for 0% of the time, Pallas kernels for 20%

profile of v15, /device:TPU:0, one launch (start us, length us, event | category | flops | bytes accessed | tf_op | source)
XLA Modules:
  0.0 60.5 jit_solution(15176847875561482590)
XLA Ops:
  0.0 5.0 %collective-permute-start.6 = (bf16[32,2048]{1,0:T(8,128)(2,1)}, bf16[32,2048]{1,0:T(8,128)(2,1)S(1)}, u32[]{:S(2)}, u32[]{:S(2)}) collective-permute-start(bf16[32,2048]{1,0:T(8,128)(2,1)} %refs_3_.1), channel_id=1, source_target_pairs={{0,24},{4,28},{8,16},{12,20},{16,8},{20,12},{24,0},{28,4},{1,25},{... | collective-permute-start | bytes 393224 | tf_op jit(solution)/shard_map/ppermute | solution.py:316
  5.1 0.5 collective-permute-start
  5.5 2.5 %collective-permute-start.1 = (bf16[32,2048]{1,0:T(8,128)(2,1)}, bf16[32,2048]{1,0:T(8,128)(2,1)S(1)}, u32[]{:S(2)}, u32[]{:S(2)}) collective-permute-start(bf16[32,2048]{1,0:T(8,128)(2,1)} %refs_3_.1), channel_id=1, source_target_pairs={{0,8},{4,12},{8,0},{12,4},{16,24},{20,28},{24,16},{28,20},{1,9},{5... | collective-permute-start | bytes 393224 | tf_op jit(solution)/shard_map/ppermute | solution.py:316
  8.0 0.5 collective-permute-start.2
  8.5 3.0 %shard_map.73 = (bf16[2,2,768,128]{3,2,1,0:T(8,128)(2,1)S(1)}, bf16[2,2,768,256]{3,2,1,0:T(8,128)(2,1)S(1)}, s32[2,3]{1,0:T(2,128)S(1)}) custom-call(s32[2,24]{1,0:T(2,128)} %select_hbm.1, s32[128]{0:T(128)} %table_hbm.1, s32[2]{0:T(128)} %stands_hbm.1, bf16[16,256,128]{2,1,0:T(8,128)(2,1)} %bitcast.2, bf16[16,256,128]{2,1,0:T(8,128)(2,1)} %bitcast.3), custom_call_target="tpu_custom_call" | custom-call | flops 2000000000 | bytes 8388608 | tf_op jit(solution)/shard_map/pallas_call | solution.py:118
  11.6 0.6 %collective-permute-start.7 = (bf16[32,2048]{1,0:T(8,128)(2,1)S(1)}, bf16[32,2048]{1,0:T(8,128)(2,1)S(1)}, u32[]{:S(2)}, u32[]{:S(2)}) collective-permute-start(bf16[32,2048]{1,0:T(8,128)(2,1)S(1)} %collective-permute-done.6.refs_3_), channel_id=1, source_target_pairs={{0,12},{4,8},{8,4},{12,0},{16,28},{20,24},{24,20},{28,16},{1,13},{... | collective-permute-start | bytes 393224 | tf_op jit(solution)/shard_map/ppermute | solution.py:316
  12.2 1.6 %collective-permute-start.8 = (bf16[32,2048]{1,0:T(8,128)(2,1)S(1)}, bf16[32,2048]{1,0:T(8,128)(2,1)S(1)}, u32[]{:S(2)}, u32[]{:S(2)}) collective-permute-start(bf16[32,2048]{1,0:T(8,128)(2,1)S(1)} %collective-permute-done.6.refs_3_), channel_id=1, source_target_pairs={{0,8},{4,12},{8,0},{12,4},{16,24},{20,28},{24,16},{28,20},{1,9},{5... | collective-permute-start | bytes 393224 | tf_op jit(solution)/shard_map/ppermute | solution.py:316
  13.8 1.4 %collective-permute-start.9 = (bf16[32,2048]{1,0:T(8,128)(2,1)S(1)}, bf16[32,2048]{1,0:T(8,128)(2,1)S(1)}, u32[]{:S(2)}, u32[]{:S(2)}) collective-permute-start(bf16[32,2048]{1,0:T(8,128)(2,1)S(1)} %collective-permute-done.6.refs_3_), channel_id=1, source_target_pairs={{0,4},{4,0},{8,12},{12,8},{16,20},{20,16},{24,28},{28,24},{1,5},{5... | collective-permute-start | bytes 393224 | tf_op jit(solution)/shard_map/ppermute | solution.py:316
  15.1 0.3 collective-permute-done.1.refs_1_
  15.5 2.9 %shard_map.74 = (bf16[32,2176]{1,0:T(8,128)(2,1)S(1)}, bf16[32,2176]{1,0:T(8,128)(2,1)S(1)}, bf16[32,2176]{1,0:T(8,128)(2,1)S(1)}, bf16[32,2176]{1,0:T(8,128)(2,1)S(1)}) custom-call(s32[2,3]{1,0:T(2,128)S(1)} %get-tuple-element.20.info, bf16[32,2048]{1,0:T(8,128)(2,1)S(1)} %collective-permute-done.refs_0_, ...), custom_call_target="tpu_custom_call" | custom-call | flops 2000000000 | bytes 4194304 | tf_op jit(solution)/shard_map/pallas_call | solution.py:216
  18.4 0.1 collective-permute-start.3
  18.5 1.9 %collective-permute-start.4 = (bf16[32,2176]{1,0:T(8,128)(2,1)S(1)}, bf16[32,2176]{1,0:T(8,128)(2,1)S(1)}, u32[]{:S(2)}, u32[]{:S(2)}) collective-permute-start(bf16[32,2176]{1,0:T(8,128)(2,1)S(1)} %get-tuple-element.25), channel_id=1, source_target_pairs={{0,8},{4,12},{8,0},{12,4},{16,24},{20,28},{24,16},{28,20},{1,9},{5... | collective-permute-start | bytes 417800 | tf_op jit(solution)/shard_map/ppermute | solution.py:316
  20.4 0.0 collective-permute-done.7.refs_0_
  20.4 1.6 %collective-permute-start.5 = (bf16[32,2176]{1,0:T(8,128)(2,1)S(1)}, bf16[32,2176]{1,0:T(8,128)(2,1)S(1)}, u32[]{:S(2)}, u32[]{:S(2)}) collective-permute-start(bf16[32,2176]{1,0:T(8,128)(2,1)S(1)} %get-tuple-element.26), channel_id=1, source_target_pairs={{0,12},{4,8},{8,4},{12,0},{16,28},{20,24},{24,20},{28,16},{1,13},{... | collective-permute-start | bytes 417800 | tf_op jit(solution)/shard_map/ppermute | solution.py:316
  22.0 0.0 collective-permute-done.8.refs_1_
  22.0 2.9 %shard_map.76 = (bf16[32,2176]{1,0:T(8,128)(2,1)S(1)}, bf16[32,2176]{1,0:T(8,128)(2,1)S(1)}, bf16[32,2176]{1,0:T(8,128)(2,1)S(1)}, bf16[32,2176]{1,0:T(8,128)(2,1)S(1)}) custom-call(s32[2,3]{1,0:T(2,128)S(1)} %get-tuple-element.20.info, bf16[32,2048]{1,0:T(8,128)(2,1)S(1)} %collective-permute-done.7.refs_0_, ...), custom_call_target="tpu_custom_call" | custom-call | flops 2000000000 | bytes 4194304 | tf_op jit(solution)/shard_map/pallas_call | solution.py:216
  24.9 0.1 collective-permute-start.10
  25.0 1.9 %collective-permute-start.11 = (bf16[32,2176]{1,0:T(8,128)(2,1)S(1)}, bf16[32,2176]{1,0:T(8,128)(2,1)S(1)}, u32[]{:S(2)}, u32[]{:S(2)}) collective-permute-start(bf16[32,2176]{1,0:T(8,128)(2,1)S(1)} %get-tuple-element.29), channel_id=1, source_target_pairs={{0,8},{4,12},{8,0},{12,4},{16,24},{20,28},{24,16},{28,20},{1,9},{5... | collective-permute-start | bytes 417800 | tf_op jit(solution)/shard_map/ppermute | solution.py:316
  26.9 1.6 %collective-permute-start.12 = (bf16[32,2176]{1,0:T(8,128)(2,1)S(1)}, bf16[32,2176]{1,0:T(8,128)(2,1)S(1)}, u32[]{:S(2)}, u32[]{:S(2)}) collective-permute-start(bf16[32,2176]{1,0:T(8,128)(2,1)S(1)} %get-tuple-element.30), channel_id=1, source_target_pairs={{0,12},{4,8},{8,4},{12,0},{16,28},{20,24},{24,20},{28,16},{1,13},{... | collective-permute-start | bytes 417800 | tf_op jit(solution)/shard_map/ppermute | solution.py:316
  28.5 0.5 shard_map.75.near
  29.0 2.7 %collective-permute-start.18 = (bf16[32,2176]{1,0:T(8,128)(2,1)S(1)}, bf16[32,2176]{1,0:T(8,128)(2,1)S(1)}, u32[]{:S(2)}, u32[]{:S(2)}) collective-permute-start(bf16[32,2176]{1,0:T(8,128)(2,1)S(1)} %shard_map.75.near), channel_id=1, source_target_pairs={{0,24},{4,28},{8,16},{12,20},{16,8},{20,12},{24,0},{28,4},{1,25},{... | collective-permute-start | bytes 417800 | tf_op jit(solution)/shard_map/ppermute | solution.py:316
  31.6 0.1 collective-permute-done.10.refs_1_
  31.7 3.0 %collective-permute-done.12.refs_3_ = bf16[32,2176]{1,0:T(8,128)(2,1)S(1)} collective-permute-done((bf16[32,2176]{1,0:T(8,128)(2,1)S(1)}, bf16[32,2176]{1,0:T(8,128)(2,1)S(1)}, u32[]{:S(2)}, u32[]{:S(2)}) %collective-permute-start.12) | collective-permute-done | bytes 139296 | tf_op jit(solution)/shard_map/ppermute | solution.py:316
  34.7 0.5 shard_map.77.near
  35.2 2.4 %collective-permute-start.13 = (bf16[32,2176]{1,0:T(8,128)(2,1)S(1)}, bf16[32,2176]{1,0:T(8,128)(2,1)S(1)}, u32[]{:S(2)}, u32[]{:S(2)}) collective-permute-start(bf16[32,2176]{1,0:T(8,128)(2,1)S(1)} %shard_map.77.near), channel_id=1, source_target_pairs={{0,24},{4,28},{8,16},{12,20},{16,8},{20,12},{24,0},{28,4},{1,25},{... | collective-permute-start | bytes 417800 | tf_op jit(solution)/shard_map/ppermute | solution.py:316
  37.6 0.1 collective-permute-done.18.far
  37.7 0.3 shard_map.80.refs_0_
  38.0 0.6 collective-permute-start.19
  38.6 2.2 %collective-permute-start.20 = (bf16[32,2048]{1,0:T(8,128)(2,1)S(1)}, bf16[32,2048]{1,0:T(8,128)(2,1)S(1)}, u32[]{:S(2)}, u32[]{:S(2)}) collective-permute-start(bf16[32,2048]{1,0:T(8,128)(2,1)S(1)} %shard_map.80.refs_0_), channel_id=1, source_target_pairs={{0,8},{4,12},{8,0},{12,4},{16,24},{20,28},{24,16},{28,20},{1,9},{5... | collective-permute-start | bytes 393224 | tf_op jit(solution)/shard_map/ppermute | solution.py:316
  40.8 1.4 %collective-permute-start.21 = (bf16[32,2048]{1,0:T(8,128)(2,1)S(1)}, bf16[32,2048]{1,0:T(8,128)(2,1)S(1)}, u32[]{:S(2)}, u32[]{:S(2)}) collective-permute-start(bf16[32,2048]{1,0:T(8,128)(2,1)S(1)} %shard_map.80.refs_0_), channel_id=1, source_target_pairs={{0,12},{4,8},{8,4},{12,0},{16,28},{20,24},{24,20},{28,16},{1,13},{... | collective-permute-start | bytes 393224 | tf_op jit(solution)/shard_map/ppermute | solution.py:316
  42.2 0.3 collective-permute-done.13.far
  42.5 0.3 shard_map.78.refs_0_
  42.8 1.7 %collective-permute-start.14 = (bf16[32,2048]{1,0:T(8,128)(2,1)S(1)}, bf16[32,2048]{1,0:T(8,128)(2,1)S(1)}, u32[]{:S(2)}, u32[]{:S(2)}) collective-permute-start(bf16[32,2048]{1,0:T(8,128)(2,1)S(1)} %shard_map.78.refs_0_), channel_id=1, source_target_pairs={{0,8},{4,12},{8,0},{12,4},{16,24},{20,28},{24,16},{28,20},{1,9},{5... | collective-permute-start | bytes 393224 | tf_op jit(solution)/shard_map/ppermute | solution.py:316
  44.6 0.9 %collective-permute-start.15 = (bf16[32,2048]{1,0:T(8,128)(2,1)S(1)}, bf16[32,2048]{1,0:T(8,128)(2,1)S(1)}, u32[]{:S(2)}, u32[]{:S(2)}) collective-permute-start(bf16[32,2048]{1,0:T(8,128)(2,1)S(1)} %shard_map.78.refs_0_), channel_id=1, source_target_pairs={{0,12},{4,8},{8,4},{12,0},{16,28},{20,24},{24,20},{28,16},{1,13},{... | collective-permute-start | bytes 393224 | tf_op jit(solution)/shard_map/ppermute | solution.py:316
  45.5 0.9 %collective-permute-start.16 = (bf16[32,2048]{1,0:T(8,128)(2,1)S(1)}, bf16[32,2048]{1,0:T(8,128)(2,1)S(1)}, u32[]{:S(2)}, u32[]{:S(2)}) collective-permute-start(bf16[32,2048]{1,0:T(8,128)(2,1)S(1)} %shard_map.78.refs_0_), channel_id=1, source_target_pairs={{0,4},{4,0},{8,12},{12,8},{16,20},{20,16},{24,28},{28,24},{1,5},{5... | collective-permute-start | bytes 393224 | tf_op jit(solution)/shard_map/ppermute | solution.py:316
  46.4 1.7 %collective-permute-done.21.refs_3_ = bf16[32,2048]{1,0:T(8,128)(2,1)S(1)} collective-permute-done((bf16[32,2048]{1,0:T(8,128)(2,1)S(1)}, bf16[32,2048]{1,0:T(8,128)(2,1)S(1)}, u32[]{:S(2)}, u32[]{:S(2)}) %collective-permute-start.21) | collective-permute-done | bytes 131104 | tf_op jit(solution)/shard_map/ppermute | solution.py:316
  48.1 0.8 %shard_map.81 = (f32[64,1024]{1,0:T(8,128)S(1)}, bf16[64,1024]{1,0:T(8,128)(2,1)S(1)}) custom-call(bf16[32,2048]{1,0:T(8,128)(2,1)S(1)} %shard_map.80.refs_0_, bf16[32,2048]{1,0:T(8,128)(2,1)S(1)} %collective-permute-done.19.refs_1_, bf16[32,2048]{1,0:T(8,128)(2,1)S(1)} %collective-permute-done.20.refs_2_, ...), custom_call_target="tpu_custom_call" | custom-call | tf_op jit(solution)/shard_map/pallas_call | solution.py:304
  48.9 0.1 collective-permute-start.22
  49.0 0.5 collective-permute-done.14.refs_1_
  49.5 1.5 %collective-permute-done.15.refs_2_ = bf16[32,2048]{1,0:T(8,128)(2,1)S(1)} collective-permute-done((bf16[32,2048]{1,0:T(8,128)(2,1)S(1)}, bf16[32,2048]{1,0:T(8,128)(2,1)S(1)}, u32[]{:S(2)}, u32[]{:S(2)}) %collective-permute-start.15) | collective-permute-done | bytes 131104 | tf_op jit(solution)/shard_map/ppermute | solution.py:316
  51.0 0.9 %collective-permute-done.16.refs_3_ = bf16[32,2048]{1,0:T(8,128)(2,1)S(1)} collective-permute-done((bf16[32,2048]{1,0:T(8,128)(2,1)S(1)}, bf16[32,2048]{1,0:T(8,128)(2,1)S(1)}, u32[]{:S(2)}, u32[]{:S(2)}) %collective-permute-start.16) | collective-permute-done | bytes 131104 | tf_op jit(solution)/shard_map/ppermute | solution.py:316
  51.9 0.8 %shard_map.79 = (f32[64,1024]{1,0:T(8,128)S(1)}, bf16[64,1024]{1,0:T(8,128)(2,1)S(1)}) custom-call(bf16[32,2048]{1,0:T(8,128)(2,1)S(1)} %shard_map.78.refs_0_, bf16[32,2048]{1,0:T(8,128)(2,1)S(1)} %collective-permute-done.14.refs_1_, bf16[32,2048]{1,0:T(8,128)(2,1)S(1)} %collective-permute-done.15.refs_2_, ...), custom_call_target="tpu_custom_call" | custom-call | tf_op jit(solution)/shard_map/pallas_call | solution.py:304
  52.7 0.1 collective-permute-start.17
  52.8 1.3 %collective-permute-done.17 = bf16[64,1024]{1,0:T(8,128)(2,1)S(1)} collective-permute-done((bf16[64,1024]{1,0:T(8,128)(2,1)S(1)}, bf16[64,1024]{1,0:T(8,128)(2,1)S(1)}, u32[]{:S(2)}, u32[]{:S(2)}) %collective-permute-start.17) | collective-permute-done | bytes 131104 | tf_op jit(solution)/shard_map/ppermute | solution.py:316
  54.1 0.1 select_convert_fusion
  54.1 1.6 %collective-permute-start.23 = (bf16[64,1024]{1,0:T(8,128)(2,1)S(1)}, bf16[64,1024]{1,0:T(8,128)(2,1)S(1)}, u32[]{:S(2)}, u32[]{:S(2)}) collective-permute-start(bf16[64,1024]{1,0:T(8,128)(2,1)S(1)} %select_convert_fusion), channel_id=1, source_target_pairs={{0,2},{1,3},{2,0},{3,1},{4,6},{5,7},{6,4},{7,5},{8,10},{9,11},{10,... | collective-permute-start | bytes 393224 | tf_op jit(solution)/shard_map/ppermute | solution.py:316
  55.7 4.0 %collective-permute-done.23 = bf16[64,1024]{1,0:T(8,128)(2,1)S(1)} collective-permute-done((bf16[64,1024]{1,0:T(8,128)(2,1)S(1)}, bf16[64,1024]{1,0:T(8,128)(2,1)S(1)}, u32[]{:S(2)}, u32[]{:S(2)}) %collective-permute-start.23) | collective-permute-done | bytes 131104 | tf_op jit(solution)/shard_map/ppermute | solution.py:316
  59.7 0.7 %add_convert_fusion = bf16[64,1024]{1,0:T(8,128)(2,1)} fusion(bf16[64,1024]{1,0:T(8,128)(2,1)S(1)} %collective-permute-done.23, f32[64,1024]{1,0:T(8,128)S(1)} %get-tuple-element.31, bf16[64,1024]{1,0:T(8,128)(2,1)S(1)} %collective-permute-done.17, f32[64,1024]{1,0:T(8,128)S(1)} %get-tuple-element.33, bf16[64,1024]{1,0:T(8,128)(2,1)S(1)} %collective-permute-done.22, ...), kind=kLoop, calls=%fused_computation | loop fusion | flops 524288 | bytes 1048577 | tf_op jit(solution)/shard_map/convert_element_type | solution.py:347
  (15 shorter events, 0.0 us)
Async XLA Ops:
  0.0 15.5 %copy-start.1 = (bf16[32,2048]{1,0:T(8,128)(2,1)S(1)}, bf16[32,2048]{1,0:T(8,128)(2,1)}, u32[]{:S(2)}) copy-start(bf16[32,2048]{1,0:T(8,128)(2,1)} %refs_3_.1) | copy-start | bytes 393220
  0.0 11.6 %collective-permute-start.6 = (bf16[32,2048]{1,0:T(8,128)(2,1)}, bf16[32,2048]{1,0:T(8,128)(2,1)S(1)}, u32[]{:S(2)}, u32[]{:S(2)}) collective-permute-start(bf16[32,2048]{1,0:T(8,128)(2,1)} %refs_3_.1), channel_id=1, source_target_pairs={{0,24},{4,28},{8,16},{12,20},{16,8},{20,12},{24,0},{28,4},{1,25},{... | collective-permute-start | bytes 393224 | tf_op jit(solution)/shard_map/ppermute | solution.py:316
  5.1 8.7 %collective-permute-start = (bf16[32,2048]{1,0:T(8,128)(2,1)}, bf16[32,2048]{1,0:T(8,128)(2,1)S(1)}, u32[]{:S(2)}, u32[]{:S(2)}) collective-permute-start(bf16[32,2048]{1,0:T(8,128)(2,1)} %refs_3_.1), channel_id=1, source_target_pairs={{0,12},{4,8},{8,4},{12,0},{16,28},{20,24},{24,20},{28,16},{1,13},{... | collective-permute-start | bytes 393224 | tf_op jit(solution)/shard_map/ppermute | solution.py:316
  5.5 9.9 %collective-permute-start.1 = (bf16[32,2048]{1,0:T(8,128)(2,1)}, bf16[32,2048]{1,0:T(8,128)(2,1)S(1)}, u32[]{:S(2)}, u32[]{:S(2)}) collective-permute-start(bf16[32,2048]{1,0:T(8,128)(2,1)} %refs_3_.1), channel_id=1, source_target_pairs={{0,8},{4,12},{8,0},{12,4},{16,24},{20,28},{24,16},{28,20},{1,9},{5... | collective-permute-start | bytes 393224 | tf_op jit(solution)/shard_map/ppermute | solution.py:316
  8.0 7.5 %collective-permute-start.2 = (bf16[32,2048]{1,0:T(8,128)(2,1)}, bf16[32,2048]{1,0:T(8,128)(2,1)S(1)}, u32[]{:S(2)}, u32[]{:S(2)}) collective-permute-start(bf16[32,2048]{1,0:T(8,128)(2,1)} %refs_3_.1), channel_id=1, source_target_pairs={{0,4},{4,0},{8,12},{12,8},{16,20},{20,16},{24,28},{28,24},{1,5},{5... | collective-permute-start | bytes 393224 | tf_op jit(solution)/shard_map/ppermute | solution.py:316
  11.6 8.8 %collective-permute-start.7 = (bf16[32,2048]{1,0:T(8,128)(2,1)S(1)}, bf16[32,2048]{1,0:T(8,128)(2,1)S(1)}, u32[]{:S(2)}, u32[]{:S(2)}) collective-permute-start(bf16[32,2048]{1,0:T(8,128)(2,1)S(1)} %collective-permute-done.6.refs_3_), channel_id=1, source_target_pairs={{0,12},{4,8},{8,4},{12,0},{16,28},{20,24},{24,20},{28,16},{1,13},{... | collective-permute-start | bytes 393224 | tf_op jit(solution)/shard_map/ppermute | solution.py:316
  12.2 9.8 %collective-permute-start.8 = (bf16[32,2048]{1,0:T(8,128)(2,1)S(1)}, bf16[32,2048]{1,0:T(8,128)(2,1)S(1)}, u32[]{:S(2)}, u32[]{:S(2)}) collective-permute-start(bf16[32,2048]{1,0:T(8,128)(2,1)S(1)} %collective-permute-done.6.refs_3_), channel_id=1, source_target_pairs={{0,8},{4,12},{8,0},{12,4},{16,24},{20,28},{24,16},{28,20},{1,9},{5... | collective-permute-start | bytes 393224 | tf_op jit(solution)/shard_map/ppermute | solution.py:316
  13.8 8.2 %collective-permute-start.9 = (bf16[32,2048]{1,0:T(8,128)(2,1)S(1)}, bf16[32,2048]{1,0:T(8,128)(2,1)S(1)}, u32[]{:S(2)}, u32[]{:S(2)}) collective-permute-start(bf16[32,2048]{1,0:T(8,128)(2,1)S(1)} %collective-permute-done.6.refs_3_), channel_id=1, source_target_pairs={{0,4},{4,0},{8,12},{12,8},{16,20},{20,16},{24,28},{28,24},{1,5},{5... | collective-permute-start | bytes 393224 | tf_op jit(solution)/shard_map/ppermute | solution.py:316
  18.4 8.5 %collective-permute-start.3 = (bf16[32,2176]{1,0:T(8,128)(2,1)S(1)}, bf16[32,2176]{1,0:T(8,128)(2,1)S(1)}, u32[]{:S(2)}, u32[]{:S(2)}) collective-permute-start(bf16[32,2176]{1,0:T(8,128)(2,1)S(1)} %get-tuple-element.24), channel_id=1, source_target_pairs={{0,4},{4,0},{8,12},{12,8},{16,20},{20,16},{24,28},{28,24},{1,5},{5... | collective-permute-start | bytes 417800 | tf_op jit(solution)/shard_map/ppermute | solution.py:316
  18.5 10.0 %collective-permute-start.4 = (bf16[32,2176]{1,0:T(8,128)(2,1)S(1)}, bf16[32,2176]{1,0:T(8,128)(2,1)S(1)}, u32[]{:S(2)}, u32[]{:S(2)}) collective-permute-start(bf16[32,2176]{1,0:T(8,128)(2,1)S(1)} %get-tuple-element.25), channel_id=1, source_target_pairs={{0,8},{4,12},{8,0},{12,4},{16,24},{20,28},{24,16},{28,20},{1,9},{5... | collective-permute-start | bytes 417800 | tf_op jit(solution)/shard_map/ppermute | solution.py:316
  20.4 27.7 %copy-start = (bf16[2048,1024]{1,0:T(8,128)(2,1)S(1)}, bf16[2048,1024]{1,0:T(8,128)(2,1)}, u32[]{:S(2)}) copy-start(bf16[2048,1024]{1,0:T(8,128)(2,1)} %refs_4_.3) | copy-start | bytes 12582916
  20.4 8.1 %collective-permute-start.5 = (bf16[32,2176]{1,0:T(8,128)(2,1)S(1)}, bf16[32,2176]{1,0:T(8,128)(2,1)S(1)}, u32[]{:S(2)}, u32[]{:S(2)}) collective-permute-start(bf16[32,2176]{1,0:T(8,128)(2,1)S(1)} %get-tuple-element.26), channel_id=1, source_target_pairs={{0,12},{4,8},{8,4},{12,0},{16,28},{20,24},{24,20},{28,16},{1,13},{... | collective-permute-start | bytes 417800 | tf_op jit(solution)/shard_map/ppermute | solution.py:316
  24.9 6.8 %collective-permute-start.10 = (bf16[32,2176]{1,0:T(8,128)(2,1)S(1)}, bf16[32,2176]{1,0:T(8,128)(2,1)S(1)}, u32[]{:S(2)}, u32[]{:S(2)}) collective-permute-start(bf16[32,2176]{1,0:T(8,128)(2,1)S(1)} %get-tuple-element.28), channel_id=1, source_target_pairs={{0,4},{4,0},{8,12},{12,8},{16,20},{20,16},{24,28},{28,24},{1,5},{5... | collective-permute-start | bytes 417800 | tf_op jit(solution)/shard_map/ppermute | solution.py:316
  25.0 6.7 %collective-permute-start.11 = (bf16[32,2176]{1,0:T(8,128)(2,1)S(1)}, bf16[32,2176]{1,0:T(8,128)(2,1)S(1)}, u32[]{:S(2)}, u32[]{:S(2)}) collective-permute-start(bf16[32,2176]{1,0:T(8,128)(2,1)S(1)} %get-tuple-element.29), channel_id=1, source_target_pairs={{0,8},{4,12},{8,0},{12,4},{16,24},{20,28},{24,16},{28,20},{1,9},{5... | collective-permute-start | bytes 417800 | tf_op jit(solution)/shard_map/ppermute | solution.py:316
  26.9 7.9 %collective-permute-start.12 = (bf16[32,2176]{1,0:T(8,128)(2,1)S(1)}, bf16[32,2176]{1,0:T(8,128)(2,1)S(1)}, u32[]{:S(2)}, u32[]{:S(2)}) collective-permute-start(bf16[32,2176]{1,0:T(8,128)(2,1)S(1)} %get-tuple-element.30), channel_id=1, source_target_pairs={{0,12},{4,8},{8,4},{12,0},{16,28},{20,24},{24,20},{28,16},{1,13},{... | collective-permute-start | bytes 417800 | tf_op jit(solution)/shard_map/ppermute | solution.py:316
  29.0 8.7 %collective-permute-start.18 = (bf16[32,2176]{1,0:T(8,128)(2,1)S(1)}, bf16[32,2176]{1,0:T(8,128)(2,1)S(1)}, u32[]{:S(2)}, u32[]{:S(2)}) collective-permute-start(bf16[32,2176]{1,0:T(8,128)(2,1)S(1)} %shard_map.75.near), channel_id=1, source_target_pairs={{0,24},{4,28},{8,16},{12,20},{16,8},{20,12},{24,0},{28,4},{1,25},{... | collective-permute-start | bytes 417800 | tf_op jit(solution)/shard_map/ppermute | solution.py:316
  35.2 7.3 %collective-permute-start.13 = (bf16[32,2176]{1,0:T(8,128)(2,1)S(1)}, bf16[32,2176]{1,0:T(8,128)(2,1)S(1)}, u32[]{:S(2)}, u32[]{:S(2)}) collective-permute-start(bf16[32,2176]{1,0:T(8,128)(2,1)S(1)} %shard_map.77.near), channel_id=1, source_target_pairs={{0,24},{4,28},{8,16},{12,20},{16,8},{20,12},{24,0},{28,4},{1,25},{... | collective-permute-start | bytes 417800 | tf_op jit(solution)/shard_map/ppermute | solution.py:316
  38.0 7.4 %collective-permute-start.19 = (bf16[32,2048]{1,0:T(8,128)(2,1)S(1)}, bf16[32,2048]{1,0:T(8,128)(2,1)S(1)}, u32[]{:S(2)}, u32[]{:S(2)}) collective-permute-start(bf16[32,2048]{1,0:T(8,128)(2,1)S(1)} %shard_map.80.refs_0_), channel_id=1, source_target_pairs={{0,4},{4,0},{8,12},{12,8},{16,20},{20,16},{24,28},{28,24},{1,5},{5... | collective-permute-start | bytes 393224 | tf_op jit(solution)/shard_map/ppermute | solution.py:316
  38.6 7.8 %collective-permute-start.20 = (bf16[32,2048]{1,0:T(8,128)(2,1)S(1)}, bf16[32,2048]{1,0:T(8,128)(2,1)S(1)}, u32[]{:S(2)}, u32[]{:S(2)}) collective-permute-start(bf16[32,2048]{1,0:T(8,128)(2,1)S(1)} %shard_map.80.refs_0_), channel_id=1, source_target_pairs={{0,8},{4,12},{8,0},{12,4},{16,24},{20,28},{24,16},{28,20},{1,9},{5... | collective-permute-start | bytes 393224 | tf_op jit(solution)/shard_map/ppermute | solution.py:316
  40.8 7.3 %collective-permute-start.21 = (bf16[32,2048]{1,0:T(8,128)(2,1)S(1)}, bf16[32,2048]{1,0:T(8,128)(2,1)S(1)}, u32[]{:S(2)}, u32[]{:S(2)}) collective-permute-start(bf16[32,2048]{1,0:T(8,128)(2,1)S(1)} %shard_map.80.refs_0_), channel_id=1, source_target_pairs={{0,12},{4,8},{8,4},{12,0},{16,28},{20,24},{24,20},{28,16},{1,13},{... | collective-permute-start | bytes 393224 | tf_op jit(solution)/shard_map/ppermute | solution.py:316
  42.8 6.6 %collective-permute-start.14 = (bf16[32,2048]{1,0:T(8,128)(2,1)S(1)}, bf16[32,2048]{1,0:T(8,128)(2,1)S(1)}, u32[]{:S(2)}, u32[]{:S(2)}) collective-permute-start(bf16[32,2048]{1,0:T(8,128)(2,1)S(1)} %shard_map.78.refs_0_), channel_id=1, source_target_pairs={{0,8},{4,12},{8,0},{12,4},{16,24},{20,28},{24,16},{28,20},{1,9},{5... | collective-permute-start | bytes 393224 | tf_op jit(solution)/shard_map/ppermute | solution.py:316
  44.6 6.4 %collective-permute-start.15 = (bf16[32,2048]{1,0:T(8,128)(2,1)S(1)}, bf16[32,2048]{1,0:T(8,128)(2,1)S(1)}, u32[]{:S(2)}, u32[]{:S(2)}) collective-permute-start(bf16[32,2048]{1,0:T(8,128)(2,1)S(1)} %shard_map.78.refs_0_), channel_id=1, source_target_pairs={{0,12},{4,8},{8,4},{12,0},{16,28},{20,24},{24,20},{28,16},{1,13},{... | collective-permute-start | bytes 393224 | tf_op jit(solution)/shard_map/ppermute | solution.py:316
  45.5 6.4 %collective-permute-start.16 = (bf16[32,2048]{1,0:T(8,128)(2,1)S(1)}, bf16[32,2048]{1,0:T(8,128)(2,1)S(1)}, u32[]{:S(2)}, u32[]{:S(2)}) collective-permute-start(bf16[32,2048]{1,0:T(8,128)(2,1)S(1)} %shard_map.78.refs_0_), channel_id=1, source_target_pairs={{0,4},{4,0},{8,12},{12,8},{16,20},{20,16},{24,28},{28,24},{1,5},{5... | collective-permute-start | bytes 393224 | tf_op jit(solution)/shard_map/ppermute | solution.py:316
  48.9 3.9 %collective-permute-start.22 = (bf16[64,1024]{1,0:T(8,128)(2,1)S(1)}, bf16[64,1024]{1,0:T(8,128)(2,1)S(1)}, u32[]{:S(2)}, u32[]{:S(2)}) collective-permute-start(bf16[64,1024]{1,0:T(8,128)(2,1)S(1)} %get-tuple-element.34), channel_id=1, source_target_pairs={{0,1},{1,0},{2,3},{3,2},{4,5},{5,4},{6,7},{7,6},{8,9},{9,8},{10,11... | collective-permute-start | bytes 393224 | tf_op jit(solution)/shard_map/ppermute | solution.py:316
  52.7 1.4 %collective-permute-start.17 = (bf16[64,1024]{1,0:T(8,128)(2,1)S(1)}, bf16[64,1024]{1,0:T(8,128)(2,1)S(1)}, u32[]{:S(2)}, u32[]{:S(2)}) collective-permute-start(bf16[64,1024]{1,0:T(8,128)(2,1)S(1)} %get-tuple-element.32), channel_id=1, source_target_pairs={{0,1},{1,0},{2,3},{3,2},{4,5},{5,4},{6,7},{7,6},{8,9},{9,8},{10,11... | collective-permute-start | bytes 393224 | tf_op jit(solution)/shard_map/ppermute | solution.py:316
  54.1 5.6 %collective-permute-start.23 = (bf16[64,1024]{1,0:T(8,128)(2,1)S(1)}, bf16[64,1024]{1,0:T(8,128)(2,1)S(1)}, u32[]{:S(2)}, u32[]{:S(2)}) collective-permute-start(bf16[64,1024]{1,0:T(8,128)(2,1)S(1)} %select_convert_fusion), channel_id=1, source_target_pairs={{0,2},{1,3},{2,0},{3,1},{4,6},{5,7},{6,4},{7,5},{8,10},{9,11},{10,... | collective-permute-start | bytes 393224 | tf_op jit(solution)/shard_map/ppermute | solution.py:316

commit v16 on v11

--- a/solution.py
+++ b/solution.py
@@ -156,10 +156,15 @@
     return wide + pltpu.roll(wide, LANES - heads, 1) + pltpu.roll(wide, LANES - 2 * heads, 1)
 
 
+def as_sent(chunks):
+    return [*range(chunks // 2, chunks), *range(1, chunks // 2), 0] if chunks > 1 else [0]
+
+
 def attend_kernel(plan, heads, lb, info, *refs):
     me = lax.axis_index("pages")
     chunks, page = plan.chunks, plan.page
-    queries, (k_ref, v_ref), outs = refs[:chunks][::-1], refs[chunks : chunks + 2], refs[chunks + 2 :]
+    sent, (k_ref, v_ref), outs = refs[:chunks], refs[chunks : chunks + 2], refs[chunks + 2 :]
+    queries = [sent[i] for i in sorted(range(chunks), key=as_sent(chunks).__getitem__)]
     kv_heads, size = k_ref.shape[1], k_ref.shape[3]
     repeat = heads // kv_heads
     width = heads * size
@@ -220,7 +225,7 @@
         out_specs=(in_vmem(),) * plan.chunks,
         compiler_params=params(32),
         cost_estimate=pl.CostEstimate(flops=2 * 10**9, bytes_accessed=4 * 2**20, transcendentals=10**6),
-    )(info, *queries[::-1], keys, values)
+    )(info, *(queries[k] for k in as_sent(len(queries))), keys, values)
 
 
 def merged(parts, stats):

time: 60.7 us -> 62.6 us (1.031)
  starting transfers between devices: 31.4 us -> 37.7 us
  Pallas kernels: 12 us -> 6.65 us
  waiting for transfers between devices: 16.1 us -> 17 us
    ppermute x24, starting transfers between devices: 31.4 us -> 37.7 us  [swap(): return lax.ppermute(x, axis, [(i, i ^ distance) for i in range(n)])]
    pallas_call x2, Pallas kernels: 5.87 us -> 1.29 us  [attend(): pl.pallas_call(functools.partial(attend_kernel, plan, heads, lb), out_sha...]
    ppermute x24, waiting for transfers between devices: 16.1 us -> 17 us  [swap(): return lax.ppermute(x, axis, [(i, i ^ distance) for i in range(n)])]
    pallas_call x1, Pallas kernels: 3.01 us -> 2.19 us  [fetch(): pl.pallas_call(functools.partial(fetch_kernel, plan, pages_dev), out_shap...]
  transfers between devices with their start and end apart: 24 -> 24, of which waited for: 12 -> 13; matrix products, arithmetic and copies ran while one was open for 0% -> 0% of each run, Pallas kernels for 20% -> 11%
where the time goes in v16:
time: 62.6 us; the launch traced here: 62.4 us
  starting transfers between devices  37.7 us (60%)
  waiting for transfers between devices  17 us (27%)
  Pallas kernels  6.65 us (11%)
  other arithmetic  0.78 us (1%)
    ppermute x24, starting transfers between devices, swap(): return lax.ppermute(x, axis, [(i, i ^ distance) for i in range(n)])  37.7 us
    ppermute x24, waiting for transfers between devices, swap(): return lax.ppermute(x, axis, [(i, i ^ distance) for i in range(n)])  17 us
    pallas_call x1, Pallas kernels, fetch(): pl.pallas_call(functools.partial(fetch_kernel, plan, pages_dev), out_shap...  2.19 us
    pallas_call x2, Pallas kernels, project(): pl.pallas_call(functools.partial(project_kernel, plan, lb), out_shape=(ja...  1.57 us
    pallas_call x2, Pallas kernels, attend(): pl.pallas_call(functools.partial(attend_kernel, plan, heads, lb), out_sha...  1.29 us
  transfers between devices with their start and end apart: 24, of which 13 were waited for; matrix products, arithmetic and copies ran while one was open for 0% of the time, Pallas kernels for 11%

profile of v16, /device:TPU:0, one launch (start us, length us, event | category | flops | bytes accessed | tf_op | source)
XLA Modules:
  0.0 62.4 jit_solution(9049045249974656109)
XLA Ops:
  0.0 5.0 %collective-permute-start.6 = (bf16[32,2048]{1,0:T(8,128)(2,1)}, bf16[32,2048]{1,0:T(8,128)(2,1)S(1)}, u32[]{:S(2)}, u32[]{:S(2)}) collective-permute-start(bf16[32,2048]{1,0:T(8,128)(2,1)} %refs_3_.1), channel_id=1, source_target_pairs={{0,24},{4,28},{8,16},{12,20},{16,8},{20,12},{24,0},{28,4},{1,25},{... | collective-permute-start | bytes 393224 | tf_op jit(solution)/shard_map/ppermute | solution.py:317
  5.1 3.0 %collective-permute-start.1 = (bf16[32,2048]{1,0:T(8,128)(2,1)}, bf16[32,2048]{1,0:T(8,128)(2,1)S(1)}, u32[]{:S(2)}, u32[]{:S(2)}) collective-permute-start(bf16[32,2048]{1,0:T(8,128)(2,1)} %refs_3_.1), channel_id=1, source_target_pairs={{0,12},{4,8},{8,4},{12,0},{16,28},{20,24},{24,20},{28,16},{1,13},{... | collective-permute-start | bytes 393224 | tf_op jit(solution)/shard_map/ppermute | solution.py:317
  8.0 0.5 collective-permute-start.2
  8.5 2.2 %shard_map.73 = (bf16[2,2,768,128]{3,2,1,0:T(8,128)(2,1)S(1)}, bf16[2,2,768,256]{3,2,1,0:T(8,128)(2,1)S(1)}, s32[2,3]{1,0:T(2,128)S(1)}) custom-call(s32[2,24]{1,0:T(2,128)} %select_hbm.1, s32[128]{0:T(128)} %table_hbm.1, s32[2]{0:T(128)} %stands_hbm.1, bf16[16,256,128]{2,1,0:T(8,128)(2,1)} %bitcast.2, bf16[16,256,128]{2,1,0:T(8,128)(2,1)} %bitcast.3), custom_call_target="tpu_custom_call" | custom-call | flops 2000000000 | bytes 8388608 | tf_op jit(solution)/shard_map/pallas_call | solution.py:118
  10.7 0.0 collective-permute-done.6.refs_3_
  10.8 0.5 collective-permute-start.7
  11.3 3.3 %collective-permute-start.8 = (bf16[32,2048]{1,0:T(8,128)(2,1)S(1)}, bf16[32,2048]{1,0:T(8,128)(2,1)S(1)}, u32[]{:S(2)}, u32[]{:S(2)}) collective-permute-start(bf16[32,2048]{1,0:T(8,128)(2,1)S(1)} %collective-permute-done.6.refs_3_), channel_id=1, source_target_pairs={{0,12},{4,8},{8,4},{12,0},{16,28},{20,24},{24,20},{28,16},{1,13},{... | collective-permute-start | bytes 393224 | tf_op jit(solution)/shard_map/ppermute | solution.py:317
  14.6 0.0 collective-permute-done.refs_0_
  14.6 0.0 collective-permute-start.9
  14.6 1.4 %collective-permute-done.1.refs_1_ = bf16[32,2048]{1,0:T(8,128)(2,1)S(1)} collective-permute-done((bf16[32,2048]{1,0:T(8,128)(2,1)}, bf16[32,2048]{1,0:T(8,128)(2,1)S(1)}, u32[]{:S(2)}, u32[]{:S(2)}) %collective-permute-start.1) | collective-permute-done | bytes 131104 | tf_op jit(solution)/shard_map/ppermute | solution.py:317
  16.0 0.3 collective-permute-done.2.refs_2_
  16.3 0.6 %shard_map.74 = (bf16[32,2176]{1,0:T(8,128)(2,1)S(1)}, bf16[32,2176]{1,0:T(8,128)(2,1)S(1)}, bf16[32,2176]{1,0:T(8,128)(2,1)S(1)}, bf16[32,2176]{1,0:T(8,128)(2,1)S(1)}) custom-call(s32[2,3]{1,0:T(2,128)S(1)} %get-tuple-element.20.info, bf16[32,2048]{1,0:T(8,128)(2,1)S(1)} %collective-permute-done.refs_0_, ...), custom_call_target="tpu_custom_call" | custom-call | flops 2000000000 | bytes 4194304 | tf_op jit(solution)/shard_map/pallas_call | solution.py:221
  16.9 3.0 %collective-permute-start.3 = (bf16[32,2176]{1,0:T(8,128)(2,1)S(1)}, bf16[32,2176]{1,0:T(8,128)(2,1)S(1)}, u32[]{:S(2)}, u32[]{:S(2)}) collective-permute-start(bf16[32,2176]{1,0:T(8,128)(2,1)S(1)} %get-tuple-element.24), channel_id=1, source_target_pairs={{0,4},{4,0},{8,12},{12,8},{16,20},{20,16},{24,28},{28,24},{1,5},{5... | collective-permute-start | bytes 417800 | tf_op jit(solution)/shard_map/ppermute | solution.py:317
  19.9 1.8 %collective-permute-start.4 = (bf16[32,2176]{1,0:T(8,128)(2,1)S(1)}, bf16[32,2176]{1,0:T(8,128)(2,1)S(1)}, u32[]{:S(2)}, u32[]{:S(2)}) collective-permute-start(bf16[32,2176]{1,0:T(8,128)(2,1)S(1)} %get-tuple-element.25), channel_id=1, source_target_pairs={{0,8},{4,12},{8,0},{12,4},{16,24},{20,28},{24,16},{28,20},{1,9},{5... | collective-permute-start | bytes 417800 | tf_op jit(solution)/shard_map/ppermute | solution.py:317
  21.7 0.0 collective-permute-start.5
  21.8 1.8 %collective-permute-done.9.refs_2_ = bf16[32,2048]{1,0:T(8,128)(2,1)S(1)} collective-permute-done((bf16[32,2048]{1,0:T(8,128)(2,1)S(1)}, bf16[32,2048]{1,0:T(8,128)(2,1)S(1)}, u32[]{:S(2)}, u32[]{:S(2)}) %collective-permute-start.9) | collective-permute-done | bytes 131104 | tf_op jit(solution)/shard_map/ppermute | solution.py:317
  23.6 0.6 %shard_map.76 = (bf16[32,2176]{1,0:T(8,128)(2,1)S(1)}, bf16[32,2176]{1,0:T(8,128)(2,1)S(1)}, bf16[32,2176]{1,0:T(8,128)(2,1)S(1)}, bf16[32,2176]{1,0:T(8,128)(2,1)S(1)}) custom-call(s32[2,3]{1,0:T(2,128)S(1)} %get-tuple-element.20.info, bf16[32,2048]{1,0:T(8,128)(2,1)S(1)} %collective-permute-done.7.refs_0_, ...), custom_call_target="tpu_custom_call" | custom-call | flops 2000000000 | bytes 4194304 | tf_op jit(solution)/shard_map/pallas_call | solution.py:221
  24.2 2.2 %collective-permute-start.10 = (bf16[32,2176]{1,0:T(8,128)(2,1)S(1)}, bf16[32,2176]{1,0:T(8,128)(2,1)S(1)}, u32[]{:S(2)}, u32[]{:S(2)}) collective-permute-start(bf16[32,2176]{1,0:T(8,128)(2,1)S(1)} %get-tuple-element.28), channel_id=1, source_target_pairs={{0,4},{4,0},{8,12},{12,8},{16,20},{20,16},{24,28},{28,24},{1,5},{5... | collective-permute-start | bytes 417800 | tf_op jit(solution)/shard_map/ppermute | solution.py:317
  26.4 1.8 %collective-permute-start.11 = (bf16[32,2176]{1,0:T(8,128)(2,1)S(1)}, bf16[32,2176]{1,0:T(8,128)(2,1)S(1)}, u32[]{:S(2)}, u32[]{:S(2)}) collective-permute-start(bf16[32,2176]{1,0:T(8,128)(2,1)S(1)} %get-tuple-element.29), channel_id=1, source_target_pairs={{0,8},{4,12},{8,0},{12,4},{16,24},{20,28},{24,16},{28,20},{1,9},{5... | collective-permute-start | bytes 417800 | tf_op jit(solution)/shard_map/ppermute | solution.py:317
  28.2 0.7 %collective-permute-done.3.refs_1_ = bf16[32,2176]{1,0:T(8,128)(2,1)S(1)} collective-permute-done((bf16[32,2176]{1,0:T(8,128)(2,1)S(1)}, bf16[32,2176]{1,0:T(8,128)(2,1)S(1)}, u32[]{:S(2)}, u32[]{:S(2)}) %collective-permute-start.3) | collective-permute-done | bytes 139296 | tf_op jit(solution)/shard_map/ppermute | solution.py:317
  28.9 0.5 shard_map.75.near
  29.4 3.0 %collective-permute-start.18 = (bf16[32,2176]{1,0:T(8,128)(2,1)S(1)}, bf16[32,2176]{1,0:T(8,128)(2,1)S(1)}, u32[]{:S(2)}, u32[]{:S(2)}) collective-permute-start(bf16[32,2176]{1,0:T(8,128)(2,1)S(1)} %shard_map.75.near), channel_id=1, source_target_pairs={{0,24},{4,28},{8,16},{12,20},{16,8},{20,12},{24,0},{28,4},{1,25},{... | collective-permute-start | bytes 417800 | tf_op jit(solution)/shard_map/ppermute | solution.py:317
  32.4 0.1 collective-permute-done.10.refs_1_
  32.5 0.6 %collective-permute-done.11.refs_2_ = bf16[32,2176]{1,0:T(8,128)(2,1)S(1)} collective-permute-done((bf16[32,2176]{1,0:T(8,128)(2,1)S(1)}, bf16[32,2176]{1,0:T(8,128)(2,1)S(1)}, u32[]{:S(2)}, u32[]{:S(2)}) %collective-permute-start.11) | collective-permute-done | bytes 139296 | tf_op jit(solution)/shard_map/ppermute | solution.py:317
  33.1 2.2 %collective-permute-done.12.refs_3_ = bf16[32,2176]{1,0:T(8,128)(2,1)S(1)} collective-permute-done((bf16[32,2176]{1,0:T(8,128)(2,1)S(1)}, bf16[32,2176]{1,0:T(8,128)(2,1)S(1)}, u32[]{:S(2)}, u32[]{:S(2)}) %collective-permute-start.12) | collective-permute-done | bytes 139296 | tf_op jit(solution)/shard_map/ppermute | solution.py:317
  35.4 0.5 shard_map.77.near
  35.8 2.9 %collective-permute-start.13 = (bf16[32,2176]{1,0:T(8,128)(2,1)S(1)}, bf16[32,2176]{1,0:T(8,128)(2,1)S(1)}, u32[]{:S(2)}, u32[]{:S(2)}) collective-permute-start(bf16[32,2176]{1,0:T(8,128)(2,1)S(1)} %shard_map.77.near), channel_id=1, source_target_pairs={{0,24},{4,28},{8,16},{12,20},{16,8},{20,12},{24,0},{28,4},{1,25},{... | collective-permute-start | bytes 417800 | tf_op jit(solution)/shard_map/ppermute | solution.py:317
  38.8 0.3 shard_map.80.refs_0_
  39.1 0.9 %collective-permute-start.19 = (bf16[32,2048]{1,0:T(8,128)(2,1)S(1)}, bf16[32,2048]{1,0:T(8,128)(2,1)S(1)}, u32[]{:S(2)}, u32[]{:S(2)}) collective-permute-start(bf16[32,2048]{1,0:T(8,128)(2,1)S(1)} %shard_map.80.refs_0_), channel_id=1, source_target_pairs={{0,4},{4,0},{8,12},{12,8},{16,20},{20,16},{24,28},{28,24},{1,5},{5... | collective-permute-start | bytes 393224 | tf_op jit(solution)/shard_map/ppermute | solution.py:317
  40.0 2.2 %collective-permute-start.20 = (bf16[32,2048]{1,0:T(8,128)(2,1)S(1)}, bf16[32,2048]{1,0:T(8,128)(2,1)S(1)}, u32[]{:S(2)}, u32[]{:S(2)}) collective-permute-start(bf16[32,2048]{1,0:T(8,128)(2,1)S(1)} %shard_map.80.refs_0_), channel_id=1, source_target_pairs={{0,8},{4,12},{8,0},{12,4},{16,24},{20,28},{24,16},{28,20},{1,9},{5... | collective-permute-start | bytes 393224 | tf_op jit(solution)/shard_map/ppermute | solution.py:317
  42.2 0.5 collective-permute-start.21
  42.6 1.3 %collective-permute-done.13.far = bf16[32,2176]{1,0:T(8,128)(2,1)S(1)} collective-permute-done((bf16[32,2176]{1,0:T(8,128)(2,1)S(1)}, bf16[32,2176]{1,0:T(8,128)(2,1)S(1)}, u32[]{:S(2)}, u32[]{:S(2)}) %collective-permute-start.13) | collective-permute-done | bytes 139296 | tf_op jit(solution)/shard_map/ppermute | solution.py:317
  43.9 0.3 shard_map.78.refs_0_
  44.3 0.5 collective-permute-start.14
  44.8 1.3 %collective-permute-start.15 = (bf16[32,2048]{1,0:T(8,128)(2,1)S(1)}, bf16[32,2048]{1,0:T(8,128)(2,1)S(1)}, u32[]{:S(2)}, u32[]{:S(2)}) collective-permute-start(bf16[32,2048]{1,0:T(8,128)(2,1)S(1)} %shard_map.78.refs_0_), channel_id=1, source_target_pairs={{0,8},{4,12},{8,0},{12,4},{16,24},{20,28},{24,16},{28,20},{1,9},{5... | collective-permute-start | bytes 393224 | tf_op jit(solution)/shard_map/ppermute | solution.py:317
  46.0 1.8 %collective-permute-start.16 = (bf16[32,2048]{1,0:T(8,128)(2,1)S(1)}, bf16[32,2048]{1,0:T(8,128)(2,1)S(1)}, u32[]{:S(2)}, u32[]{:S(2)}) collective-permute-start(bf16[32,2048]{1,0:T(8,128)(2,1)S(1)} %shard_map.78.refs_0_), channel_id=1, source_target_pairs={{0,12},{4,8},{8,4},{12,0},{16,28},{20,24},{24,20},{28,16},{1,13},{... | collective-permute-start | bytes 393224 | tf_op jit(solution)/shard_map/ppermute | solution.py:317
  47.8 1.7 %collective-permute-done.21.refs_3_ = bf16[32,2048]{1,0:T(8,128)(2,1)S(1)} collective-permute-done((bf16[32,2048]{1,0:T(8,128)(2,1)S(1)}, bf16[32,2048]{1,0:T(8,128)(2,1)S(1)}, u32[]{:S(2)}, u32[]{:S(2)}) %collective-permute-start.21) | collective-permute-done | bytes 131104 | tf_op jit(solution)/shard_map/ppermute | solution.py:317
  49.5 0.8 %shard_map.81 = (f32[64,1024]{1,0:T(8,128)S(1)}, bf16[64,1024]{1,0:T(8,128)(2,1)S(1)}) custom-call(bf16[32,2048]{1,0:T(8,128)(2,1)S(1)} %shard_map.80.refs_0_, bf16[32,2048]{1,0:T(8,128)(2,1)S(1)} %collective-permute-done.19.refs_1_, bf16[32,2048]{1,0:T(8,128)(2,1)S(1)} %collective-permute-done.20.refs_2_, ...), custom_call_target="tpu_custom_call" | custom-call | tf_op jit(solution)/shard_map/pallas_call | solution.py:305
  50.3 0.1 collective-permute-start.22
  50.4 0.4 collective-permute-done.14.refs_1_
  50.8 1.4 %collective-permute-done.16.refs_3_ = bf16[32,2048]{1,0:T(8,128)(2,1)S(1)} collective-permute-done((bf16[32,2048]{1,0:T(8,128)(2,1)S(1)}, bf16[32,2048]{1,0:T(8,128)(2,1)S(1)}, u32[]{:S(2)}, u32[]{:S(2)}) %collective-permute-start.16) | collective-permute-done | bytes 131104 | tf_op jit(solution)/shard_map/ppermute | solution.py:317
  52.2 0.8 %shard_map.79 = (f32[64,1024]{1,0:T(8,128)S(1)}, bf16[64,1024]{1,0:T(8,128)(2,1)S(1)}) custom-call(bf16[32,2048]{1,0:T(8,128)(2,1)S(1)} %shard_map.78.refs_0_, bf16[32,2048]{1,0:T(8,128)(2,1)S(1)} %collective-permute-done.14.refs_1_, bf16[32,2048]{1,0:T(8,128)(2,1)S(1)} %collective-permute-done.15.refs_2_, ...), custom_call_target="tpu_custom_call" | custom-call | tf_op jit(solution)/shard_map/pallas_call | solution.py:305
  53.0 0.1 collective-permute-start.17
  53.1 1.3 %collective-permute-done.17 = bf16[64,1024]{1,0:T(8,128)(2,1)S(1)} collective-permute-done((bf16[64,1024]{1,0:T(8,128)(2,1)S(1)}, bf16[64,1024]{1,0:T(8,128)(2,1)S(1)}, u32[]{:S(2)}, u32[]{:S(2)}) %collective-permute-start.17) | collective-permute-done | bytes 131104 | tf_op jit(solution)/shard_map/ppermute | solution.py:317
  54.4 0.1 select_convert_fusion
  54.5 3.4 %collective-permute-start.23 = (bf16[64,1024]{1,0:T(8,128)(2,1)S(1)}, bf16[64,1024]{1,0:T(8,128)(2,1)S(1)}, u32[]{:S(2)}, u32[]{:S(2)}) collective-permute-start(bf16[64,1024]{1,0:T(8,128)(2,1)S(1)} %select_convert_fusion), channel_id=1, source_target_pairs={{0,2},{1,3},{2,0},{3,1},{4,6},{5,7},{6,4},{7,5},{8,10},{9,11},{10,... | collective-permute-start | bytes 393224 | tf_op jit(solution)/shard_map/ppermute | solution.py:317
  57.8 3.8 %collective-permute-done.23 = bf16[64,1024]{1,0:T(8,128)(2,1)S(1)} collective-permute-done((bf16[64,1024]{1,0:T(8,128)(2,1)S(1)}, bf16[64,1024]{1,0:T(8,128)(2,1)S(1)}, u32[]{:S(2)}, u32[]{:S(2)}) %collective-permute-start.23) | collective-permute-done | bytes 131104 | tf_op jit(solution)/shard_map/ppermute | solution.py:317
  61.6 0.7 %add_convert_fusion = bf16[64,1024]{1,0:T(8,128)(2,1)} fusion(bf16[64,1024]{1,0:T(8,128)(2,1)S(1)} %collective-permute-done.23, f32[64,1024]{1,0:T(8,128)S(1)} %get-tuple-element.31, bf16[64,1024]{1,0:T(8,128)(2,1)S(1)} %collective-permute-done.17, f32[64,1024]{1,0:T(8,128)S(1)} %get-tuple-element.33, bf16[64,1024]{1,0:T(8,128)(2,1)S(1)} %collective-permute-done.22, ...), kind=kLoop, calls=%fused_computation | loop fusion | flops 524288 | bytes 1048577 | tf_op jit(solution)/shard_map/convert_element_type | solution.py:344
  (15 shorter events, 0.0 us)
Async XLA Ops:
  0.0 16.3 %copy-start.1 = (bf16[32,2048]{1,0:T(8,128)(2,1)S(1)}, bf16[32,2048]{1,0:T(8,128)(2,1)}, u32[]{:S(2)}) copy-start(bf16[32,2048]{1,0:T(8,128)(2,1)} %refs_3_.1) | copy-start | bytes 393220
  0.0 10.7 %collective-permute-start.6 = (bf16[32,2048]{1,0:T(8,128)(2,1)}, bf16[32,2048]{1,0:T(8,128)(2,1)S(1)}, u32[]{:S(2)}, u32[]{:S(2)}) collective-permute-start(bf16[32,2048]{1,0:T(8,128)(2,1)} %refs_3_.1), channel_id=1, source_target_pairs={{0,24},{4,28},{8,16},{12,20},{16,8},{20,12},{24,0},{28,4},{1,25},{... | collective-permute-start | bytes 393224 | tf_op jit(solution)/shard_map/ppermute | solution.py:317
  5.1 9.5 %collective-permute-start = (bf16[32,2048]{1,0:T(8,128)(2,1)}, bf16[32,2048]{1,0:T(8,128)(2,1)S(1)}, u32[]{:S(2)}, u32[]{:S(2)}) collective-permute-start(bf16[32,2048]{1,0:T(8,128)(2,1)} %refs_3_.1), channel_id=1, source_target_pairs={{0,8},{4,12},{8,0},{12,4},{16,24},{20,28},{24,16},{28,20},{1,9},{5... | collective-permute-start | bytes 393224 | tf_op jit(solution)/shard_map/ppermute | solution.py:317
  5.1 10.9 %collective-permute-start.1 = (bf16[32,2048]{1,0:T(8,128)(2,1)}, bf16[32,2048]{1,0:T(8,128)(2,1)S(1)}, u32[]{:S(2)}, u32[]{:S(2)}) collective-permute-start(bf16[32,2048]{1,0:T(8,128)(2,1)} %refs_3_.1), channel_id=1, source_target_pairs={{0,12},{4,8},{8,4},{12,0},{16,28},{20,24},{24,20},{28,16},{1,13},{... | collective-permute-start | bytes 393224 | tf_op jit(solution)/shard_map/ppermute | solution.py:317
  8.0 8.3 %collective-permute-start.2 = (bf16[32,2048]{1,0:T(8,128)(2,1)}, bf16[32,2048]{1,0:T(8,128)(2,1)S(1)}, u32[]{:S(2)}, u32[]{:S(2)}) collective-permute-start(bf16[32,2048]{1,0:T(8,128)(2,1)} %refs_3_.1), channel_id=1, source_target_pairs={{0,4},{4,0},{8,12},{12,8},{16,20},{20,16},{24,28},{28,24},{1,5},{5... | collective-permute-start | bytes 393224 | tf_op jit(solution)/shard_map/ppermute | solution.py:317
  10.8 11.0 %collective-permute-start.7 = (bf16[32,2048]{1,0:T(8,128)(2,1)S(1)}, bf16[32,2048]{1,0:T(8,128)(2,1)S(1)}, u32[]{:S(2)}, u32[]{:S(2)}) collective-permute-start(bf16[32,2048]{1,0:T(8,128)(2,1)S(1)} %collective-permute-done.6.refs_3_), channel_id=1, source_target_pairs={{0,8},{4,12},{8,0},{12,4},{16,24},{20,28},{24,16},{28,20},{1,9},{5... | collective-permute-start | bytes 393224 | tf_op jit(solution)/shard_map/ppermute | solution.py:317
  11.3 10.5 %collective-permute-start.8 = (bf16[32,2048]{1,0:T(8,128)(2,1)S(1)}, bf16[32,2048]{1,0:T(8,128)(2,1)S(1)}, u32[]{:S(2)}, u32[]{:S(2)}) collective-permute-start(bf16[32,2048]{1,0:T(8,128)(2,1)S(1)} %collective-permute-done.6.refs_3_), channel_id=1, source_target_pairs={{0,12},{4,8},{8,4},{12,0},{16,28},{20,24},{24,20},{28,16},{1,13},{... | collective-permute-start | bytes 393224 | tf_op jit(solution)/shard_map/ppermute | solution.py:317
  14.6 9.0 %collective-permute-start.9 = (bf16[32,2048]{1,0:T(8,128)(2,1)S(1)}, bf16[32,2048]{1,0:T(8,128)(2,1)S(1)}, u32[]{:S(2)}, u32[]{:S(2)}) collective-permute-start(bf16[32,2048]{1,0:T(8,128)(2,1)S(1)} %collective-permute-done.6.refs_3_), channel_id=1, source_target_pairs={{0,4},{4,0},{8,12},{12,8},{16,20},{20,16},{24,28},{28,24},{1,5},{5... | collective-permute-start | bytes 393224 | tf_op jit(solution)/shard_map/ppermute | solution.py:317
  16.9 12.0 %collective-permute-start.3 = (bf16[32,2176]{1,0:T(8,128)(2,1)S(1)}, bf16[32,2176]{1,0:T(8,128)(2,1)S(1)}, u32[]{:S(2)}, u32[]{:S(2)}) collective-permute-start(bf16[32,2176]{1,0:T(8,128)(2,1)S(1)} %get-tuple-element.24), channel_id=1, source_target_pairs={{0,4},{4,0},{8,12},{12,8},{16,20},{20,16},{24,28},{28,24},{1,5},{5... | collective-permute-start | bytes 417800 | tf_op jit(solution)/shard_map/ppermute | solution.py:317
  19.9 9.0 %collective-permute-start.4 = (bf16[32,2176]{1,0:T(8,128)(2,1)S(1)}, bf16[32,2176]{1,0:T(8,128)(2,1)S(1)}, u32[]{:S(2)}, u32[]{:S(2)}) collective-permute-start(bf16[32,2176]{1,0:T(8,128)(2,1)S(1)} %get-tuple-element.25), channel_id=1, source_target_pairs={{0,8},{4,12},{8,0},{12,4},{16,24},{20,28},{24,16},{28,20},{1,9},{5... | collective-permute-start | bytes 417800 | tf_op jit(solution)/shard_map/ppermute | solution.py:317
  21.7 27.8 %copy-start = (bf16[2048,1024]{1,0:T(8,128)(2,1)S(1)}, bf16[2048,1024]{1,0:T(8,128)(2,1)}, u32[]{:S(2)}) copy-start(bf16[2048,1024]{1,0:T(8,128)(2,1)} %refs_4_.3) | copy-start | bytes 12582916
  21.7 7.2 %collective-permute-start.5 = (bf16[32,2176]{1,0:T(8,128)(2,1)S(1)}, bf16[32,2176]{1,0:T(8,128)(2,1)S(1)}, u32[]{:S(2)}, u32[]{:S(2)}) collective-permute-start(bf16[32,2176]{1,0:T(8,128)(2,1)S(1)} %get-tuple-element.26), channel_id=1, source_target_pairs={{0,12},{4,8},{8,4},{12,0},{16,28},{20,24},{24,20},{28,16},{1,13},{... | collective-permute-start | bytes 417800 | tf_op jit(solution)/shard_map/ppermute | solution.py:317
  24.2 8.3 %collective-permute-start.10 = (bf16[32,2176]{1,0:T(8,128)(2,1)S(1)}, bf16[32,2176]{1,0:T(8,128)(2,1)S(1)}, u32[]{:S(2)}, u32[]{:S(2)}) collective-permute-start(bf16[32,2176]{1,0:T(8,128)(2,1)S(1)} %get-tuple-element.28), channel_id=1, source_target_pairs={{0,4},{4,0},{8,12},{12,8},{16,20},{20,16},{24,28},{28,24},{1,5},{5... | collective-permute-start | bytes 417800 | tf_op jit(solution)/shard_map/ppermute | solution.py:317
  26.4 6.7 %collective-permute-start.11 = (bf16[32,2176]{1,0:T(8,128)(2,1)S(1)}, bf16[32,2176]{1,0:T(8,128)(2,1)S(1)}, u32[]{:S(2)}, u32[]{:S(2)}) collective-permute-start(bf16[32,2176]{1,0:T(8,128)(2,1)S(1)} %get-tuple-element.29), channel_id=1, source_target_pairs={{0,8},{4,12},{8,0},{12,4},{16,24},{20,28},{24,16},{28,20},{1,9},{5... | collective-permute-start | bytes 417800 | tf_op jit(solution)/shard_map/ppermute | solution.py:317
  28.9 6.5 %collective-permute-start.12 = (bf16[32,2176]{1,0:T(8,128)(2,1)S(1)}, bf16[32,2176]{1,0:T(8,128)(2,1)S(1)}, u32[]{:S(2)}, u32[]{:S(2)}) collective-permute-start(bf16[32,2176]{1,0:T(8,128)(2,1)S(1)} %get-tuple-element.30), channel_id=1, source_target_pairs={{0,12},{4,8},{8,4},{12,0},{16,28},{20,24},{24,20},{28,16},{1,13},{... | collective-permute-start | bytes 417800 | tf_op jit(solution)/shard_map/ppermute | solution.py:317
  29.4 9.4 %collective-permute-start.18 = (bf16[32,2176]{1,0:T(8,128)(2,1)S(1)}, bf16[32,2176]{1,0:T(8,128)(2,1)S(1)}, u32[]{:S(2)}, u32[]{:S(2)}) collective-permute-start(bf16[32,2176]{1,0:T(8,128)(2,1)S(1)} %shard_map.75.near), channel_id=1, source_target_pairs={{0,24},{4,28},{8,16},{12,20},{16,8},{20,12},{24,0},{28,4},{1,25},{... | collective-permute-start | bytes 417800 | tf_op jit(solution)/shard_map/ppermute | solution.py:317
  35.8 8.1 %collective-permute-start.13 = (bf16[32,2176]{1,0:T(8,128)(2,1)S(1)}, bf16[32,2176]{1,0:T(8,128)(2,1)S(1)}, u32[]{:S(2)}, u32[]{:S(2)}) collective-permute-start(bf16[32,2176]{1,0:T(8,128)(2,1)S(1)} %shard_map.77.near), channel_id=1, source_target_pairs={{0,24},{4,28},{8,16},{12,20},{16,8},{20,12},{24,0},{28,4},{1,25},{... | collective-permute-start | bytes 417800 | tf_op jit(solution)/shard_map/ppermute | solution.py:317
  39.1 7.0 %collective-permute-start.19 = (bf16[32,2048]{1,0:T(8,128)(2,1)S(1)}, bf16[32,2048]{1,0:T(8,128)(2,1)S(1)}, u32[]{:S(2)}, u32[]{:S(2)}) collective-permute-start(bf16[32,2048]{1,0:T(8,128)(2,1)S(1)} %shard_map.80.refs_0_), channel_id=1, source_target_pairs={{0,4},{4,0},{8,12},{12,8},{16,20},{20,16},{24,28},{28,24},{1,5},{5... | collective-permute-start | bytes 393224 | tf_op jit(solution)/shard_map/ppermute | solution.py:317
  40.0 7.9 %collective-permute-start.20 = (bf16[32,2048]{1,0:T(8,128)(2,1)S(1)}, bf16[32,2048]{1,0:T(8,128)(2,1)S(1)}, u32[]{:S(2)}, u32[]{:S(2)}) collective-permute-start(bf16[32,2048]{1,0:T(8,128)(2,1)S(1)} %shard_map.80.refs_0_), channel_id=1, source_target_pairs={{0,8},{4,12},{8,0},{12,4},{16,24},{20,28},{24,16},{28,20},{1,9},{5... | collective-permute-start | bytes 393224 | tf_op jit(solution)/shard_map/ppermute | solution.py:317
  42.2 7.4 %collective-permute-start.21 = (bf16[32,2048]{1,0:T(8,128)(2,1)S(1)}, bf16[32,2048]{1,0:T(8,128)(2,1)S(1)}, u32[]{:S(2)}, u32[]{:S(2)}) collective-permute-start(bf16[32,2048]{1,0:T(8,128)(2,1)S(1)} %shard_map.80.refs_0_), channel_id=1, source_target_pairs={{0,12},{4,8},{8,4},{12,0},{16,28},{20,24},{24,20},{28,16},{1,13},{... | collective-permute-start | bytes 393224 | tf_op jit(solution)/shard_map/ppermute | solution.py:317
  44.3 6.5 %collective-permute-start.14 = (bf16[32,2048]{1,0:T(8,128)(2,1)S(1)}, bf16[32,2048]{1,0:T(8,128)(2,1)S(1)}, u32[]{:S(2)}, u32[]{:S(2)}) collective-permute-start(bf16[32,2048]{1,0:T(8,128)(2,1)S(1)} %shard_map.78.refs_0_), channel_id=1, source_target_pairs={{0,4},{4,0},{8,12},{12,8},{16,20},{20,16},{24,28},{28,24},{1,5},{5... | collective-permute-start | bytes 393224 | tf_op jit(solution)/shard_map/ppermute | solution.py:317
  44.8 6.0 %collective-permute-start.15 = (bf16[32,2048]{1,0:T(8,128)(2,1)S(1)}, bf16[32,2048]{1,0:T(8,128)(2,1)S(1)}, u32[]{:S(2)}, u32[]{:S(2)}) collective-permute-start(bf16[32,2048]{1,0:T(8,128)(2,1)S(1)} %shard_map.78.refs_0_), channel_id=1, source_target_pairs={{0,8},{4,12},{8,0},{12,4},{16,24},{20,28},{24,16},{28,20},{1,9},{5... | collective-permute-start | bytes 393224 | tf_op jit(solution)/shard_map/ppermute | solution.py:317
  46.0 6.2 %collective-permute-start.16 = (bf16[32,2048]{1,0:T(8,128)(2,1)S(1)}, bf16[32,2048]{1,0:T(8,128)(2,1)S(1)}, u32[]{:S(2)}, u32[]{:S(2)}) collective-permute-start(bf16[32,2048]{1,0:T(8,128)(2,1)S(1)} %shard_map.78.refs_0_), channel_id=1, source_target_pairs={{0,12},{4,8},{8,4},{12,0},{16,28},{20,24},{24,20},{28,16},{1,13},{... | collective-permute-start | bytes 393224 | tf_op jit(solution)/shard_map/ppermute | solution.py:317
  50.3 2.8 %collective-permute-start.22 = (bf16[64,1024]{1,0:T(8,128)(2,1)S(1)}, bf16[64,1024]{1,0:T(8,128)(2,1)S(1)}, u32[]{:S(2)}, u32[]{:S(2)}) collective-permute-start(bf16[64,1024]{1,0:T(8,128)(2,1)S(1)} %get-tuple-element.34), channel_id=1, source_target_pairs={{0,1},{1,0},{2,3},{3,2},{4,5},{5,4},{6,7},{7,6},{8,9},{9,8},{10,11... | collective-permute-start | bytes 393224 | tf_op jit(solution)/shard_map/ppermute | solution.py:317
  53.0 1.4 %collective-permute-start.17 = (bf16[64,1024]{1,0:T(8,128)(2,1)S(1)}, bf16[64,1024]{1,0:T(8,128)(2,1)S(1)}, u32[]{:S(2)}, u32[]{:S(2)}) collective-permute-start(bf16[64,1024]{1,0:T(8,128)(2,1)S(1)} %get-tuple-element.32), channel_id=1, source_target_pairs={{0,1},{1,0},{2,3},{3,2},{4,5},{5,4},{6,7},{7,6},{8,9},{9,8},{10,11... | collective-permute-start | bytes 393224 | tf_op jit(solution)/shard_map/ppermute | solution.py:317
  54.5 7.2 %collective-permute-start.23 = (bf16[64,1024]{1,0:T(8,128)(2,1)S(1)}, bf16[64,1024]{1,0:T(8,128)(2,1)S(1)}, u32[]{:S(2)}, u32[]{:S(2)}) collective-permute-start(bf16[64,1024]{1,0:T(8,128)(2,1)S(1)} %select_convert_fusion), channel_id=1, source_target_pairs={{0,2},{1,3},{2,0},{3,1},{4,6},{5,7},{6,4},{7,5},{8,10},{9,11},{10,... | collective-permute-start | bytes 393224 | tf_op jit(solution)/shard_map/ppermute | solution.py:317

commit v17 on v12

--- a/solution.py
+++ b/solution.py
@@ -326,7 +326,7 @@
     for lb, rows in enumerate((queries, far)):
         chunks = spread(rows, plan)
         outs = attend(plan, heads, lb, pages, [chunks[k] for k in range(plan.group)])
-        order = reversed(others(plan)) if lb else others(plan)
+        order = [*range(plan.group // 2, plan.group), *range(1, plan.group // 2)] if lb else others(plan)
         near.append(merge(heads, outs[0], *(swap(outs[k], "pages", k) for k in order)))
     across = [swap(x, "pages", plan.cross) for x in near]
     sums = [None, None]

time: 60.7 us -> 61.2 us (level)
  waiting for transfers between devices: 13.1 us -> 13.8 us
    ppermute x24, waiting for transfers between devices: 13.1 us -> 13.8 us  [swap(): return lax.ppermute(x, axis, [(i, i ^ distance) for i in range(n)])]
  transfers between devices with their start and end apart: 24 -> 24, of which waited for: 10 -> 9; matrix products, arithmetic and copies ran while one was open for 0% -> 0% of each run, Pallas kernels for 20% -> 20%
where the time goes in v17:
time: 61.2 us; the launch traced here: 60.9 us
  starting transfers between devices  34.2 us (56%)
  waiting for transfers between devices  13.8 us (23%)
  Pallas kernels  12 us (20%)
  other arithmetic  0.78 us (1%)
    ppermute x24, starting transfers between devices, swap(): return lax.ppermute(x, axis, [(i, i ^ distance) for i in range(n)])  34.2 us
    ppermute x24, waiting for transfers between devices, swap(): return lax.ppermute(x, axis, [(i, i ^ distance) for i in range(n)])  13.8 us
    pallas_call x2, Pallas kernels, attend(): pl.pallas_call(functools.partial(attend_kernel, plan, heads, lb), out_sha...  5.87 us
    pallas_call x1, Pallas kernels, fetch(): pl.pallas_call(functools.partial(fetch_kernel, plan, pages_dev), out_shap...  3.01 us
    pallas_call x2, Pallas kernels, project(): pl.pallas_call(functools.partial(project_kernel, plan, lb), out_shape=(ja...  1.57 us
  transfers between devices with their start and end apart: 24, of which 9 were waited for; matrix products, arithmetic and copies ran while one was open for 0% of the time, Pallas kernels for 20%

profile of v17, /device:TPU:0, one launch (start us, length us, event | category | flops | bytes accessed | tf_op | source)
XLA Modules:
  0.0 60.9 jit_solution(9280242600568467357)
XLA Ops:
  0.0 5.0 %collective-permute-start.6 = (bf16[32,2048]{1,0:T(8,128)(2,1)}, bf16[32,2048]{1,0:T(8,128)(2,1)S(1)}, u32[]{:S(2)}, u32[]{:S(2)}) collective-permute-start(bf16[32,2048]{1,0:T(8,128)(2,1)} %refs_3_.1), channel_id=1, source_target_pairs={{0,24},{4,28},{8,16},{12,20},{16,8},{20,12},{24,0},{28,4},{1,25},{... | collective-permute-start | bytes 393224 | tf_op jit(solution)/shard_map/ppermute | solution.py:312
  5.1 0.5 collective-permute-start
  5.5 2.5 %collective-permute-start.1 = (bf16[32,2048]{1,0:T(8,128)(2,1)}, bf16[32,2048]{1,0:T(8,128)(2,1)S(1)}, u32[]{:S(2)}, u32[]{:S(2)}) collective-permute-start(bf16[32,2048]{1,0:T(8,128)(2,1)} %refs_3_.1), channel_id=1, source_target_pairs={{0,8},{4,12},{8,0},{12,4},{16,24},{20,28},{24,16},{28,20},{1,9},{5... | collective-permute-start | bytes 393224 | tf_op jit(solution)/shard_map/ppermute | solution.py:312
  8.0 0.5 collective-permute-start.2
  8.5 3.0 %shard_map.73 = (bf16[2,2,768,128]{3,2,1,0:T(8,128)(2,1)S(1)}, bf16[2,2,768,256]{3,2,1,0:T(8,128)(2,1)S(1)}, s32[2,3]{1,0:T(2,128)S(1)}) custom-call(s32[2,24]{1,0:T(2,128)} %select_hbm.1, s32[128]{0:T(128)} %table_hbm.1, s32[2]{0:T(128)} %stands_hbm.1, bf16[16,256,128]{2,1,0:T(8,128)(2,1)} %bitcast.2, bf16[16,256,128]{2,1,0:T(8,128)(2,1)} %bitcast.3), custom_call_target="tpu_custom_call" | custom-call | flops 2000000000 | bytes 8388608 | tf_op jit(solution)/shard_map/pallas_call | solution.py:118
  11.6 0.0 collective-permute-done.6.refs_3_
  11.6 0.6 %collective-permute-start.7 = (bf16[32,2048]{1,0:T(8,128)(2,1)S(1)}, bf16[32,2048]{1,0:T(8,128)(2,1)S(1)}, u32[]{:S(2)}, u32[]{:S(2)}) collective-permute-start(bf16[32,2048]{1,0:T(8,128)(2,1)S(1)} %collective-permute-done.6.refs_3_), channel_id=1, source_target_pairs={{0,12},{4,8},{8,4},{12,0},{16,28},{20,24},{24,20},{28,16},{1,13},{... | collective-permute-start | bytes 393224 | tf_op jit(solution)/shard_map/ppermute | solution.py:312
  12.2 1.6 %collective-permute-start.8 = (bf16[32,2048]{1,0:T(8,128)(2,1)S(1)}, bf16[32,2048]{1,0:T(8,128)(2,1)S(1)}, u32[]{:S(2)}, u32[]{:S(2)}) collective-permute-start(bf16[32,2048]{1,0:T(8,128)(2,1)S(1)} %collective-permute-done.6.refs_3_), channel_id=1, source_target_pairs={{0,8},{4,12},{8,0},{12,4},{16,24},{20,28},{24,16},{28,20},{1,9},{5... | collective-permute-start | bytes 393224 | tf_op jit(solution)/shard_map/ppermute | solution.py:312
  13.8 0.0 collective-permute-done.refs_0_
  13.8 1.4 %collective-permute-start.9 = (bf16[32,2048]{1,0:T(8,128)(2,1)S(1)}, bf16[32,2048]{1,0:T(8,128)(2,1)S(1)}, u32[]{:S(2)}, u32[]{:S(2)}) collective-permute-start(bf16[32,2048]{1,0:T(8,128)(2,1)S(1)} %collective-permute-done.6.refs_3_), channel_id=1, source_target_pairs={{0,4},{4,0},{8,12},{12,8},{16,20},{20,16},{24,28},{28,24},{1,5},{5... | collective-permute-start | bytes 393224 | tf_op jit(solution)/shard_map/ppermute | solution.py:312
  15.1 0.3 collective-permute-done.1.refs_1_
  15.5 0.0 collective-permute-done.2.refs_2_
  15.5 2.9 %shard_map.74 = (bf16[32,2176]{1,0:T(8,128)(2,1)S(1)}, bf16[32,2176]{1,0:T(8,128)(2,1)S(1)}, bf16[32,2176]{1,0:T(8,128)(2,1)S(1)}, bf16[32,2176]{1,0:T(8,128)(2,1)S(1)}) custom-call(s32[2,3]{1,0:T(2,128)S(1)} %get-tuple-element.20.info, bf16[32,2048]{1,0:T(8,128)(2,1)S(1)} %collective-permute-done.refs_0_, ...), custom_call_target="tpu_custom_call" | custom-call | flops 2000000000 | bytes 4194304 | tf_op jit(solution)/shard_map/pallas_call | solution.py:216
  18.4 0.1 collective-permute-start.3
  18.5 1.9 %collective-permute-start.4 = (bf16[32,2176]{1,0:T(8,128)(2,1)S(1)}, bf16[32,2176]{1,0:T(8,128)(2,1)S(1)}, u32[]{:S(2)}, u32[]{:S(2)}) collective-permute-start(bf16[32,2176]{1,0:T(8,128)(2,1)S(1)} %get-tuple-element.25), channel_id=1, source_target_pairs={{0,8},{4,12},{8,0},{12,4},{16,24},{20,28},{24,16},{28,20},{1,9},{5... | collective-permute-start | bytes 417800 | tf_op jit(solution)/shard_map/ppermute | solution.py:312
  20.4 1.6 %collective-permute-start.5 = (bf16[32,2176]{1,0:T(8,128)(2,1)S(1)}, bf16[32,2176]{1,0:T(8,128)(2,1)S(1)}, u32[]{:S(2)}, u32[]{:S(2)}) collective-permute-start(bf16[32,2176]{1,0:T(8,128)(2,1)S(1)} %get-tuple-element.26), channel_id=1, source_target_pairs={{0,12},{4,8},{8,4},{12,0},{16,28},{20,24},{24,20},{28,16},{1,13},{... | collective-permute-start | bytes 417800 | tf_op jit(solution)/shard_map/ppermute | solution.py:312
  22.0 2.9 %shard_map.76 = (bf16[32,2176]{1,0:T(8,128)(2,1)S(1)}, bf16[32,2176]{1,0:T(8,128)(2,1)S(1)}, bf16[32,2176]{1,0:T(8,128)(2,1)S(1)}, bf16[32,2176]{1,0:T(8,128)(2,1)S(1)}) custom-call(s32[2,3]{1,0:T(2,128)S(1)} %get-tuple-element.20.info, bf16[32,2048]{1,0:T(8,128)(2,1)S(1)} %collective-permute-done.7.refs_0_, ...), custom_call_target="tpu_custom_call" | custom-call | flops 2000000000 | bytes 4194304 | tf_op jit(solution)/shard_map/pallas_call | solution.py:216
  24.9 1.9 %collective-permute-start.10 = (bf16[32,2176]{1,0:T(8,128)(2,1)S(1)}, bf16[32,2176]{1,0:T(8,128)(2,1)S(1)}, u32[]{:S(2)}, u32[]{:S(2)}) collective-permute-start(bf16[32,2176]{1,0:T(8,128)(2,1)S(1)} %get-tuple-element.28), channel_id=1, source_target_pairs={{0,8},{4,12},{8,0},{12,4},{16,24},{20,28},{24,16},{28,20},{1,9},{5... | collective-permute-start | bytes 417800 | tf_op jit(solution)/shard_map/ppermute | solution.py:312
  26.8 1.7 %collective-permute-start.12 = (bf16[32,2176]{1,0:T(8,128)(2,1)S(1)}, bf16[32,2176]{1,0:T(8,128)(2,1)S(1)}, u32[]{:S(2)}, u32[]{:S(2)}) collective-permute-start(bf16[32,2176]{1,0:T(8,128)(2,1)S(1)} %get-tuple-element.30), channel_id=1, source_target_pairs={{0,4},{4,0},{8,12},{12,8},{16,20},{20,16},{24,28},{28,24},{1,5},{5... | collective-permute-start | bytes 417800 | tf_op jit(solution)/shard_map/ppermute | solution.py:312
  28.5 0.0 collective-permute-done.4.refs_2_
  28.5 1.2 %collective-permute-done.5.refs_3_ = bf16[32,2176]{1,0:T(8,128)(2,1)S(1)} collective-permute-done((bf16[32,2176]{1,0:T(8,128)(2,1)S(1)}, bf16[32,2176]{1,0:T(8,128)(2,1)S(1)}, u32[]{:S(2)}, u32[]{:S(2)}) %collective-permute-start.5) | collective-permute-done | bytes 139296 | tf_op jit(solution)/shard_map/ppermute | solution.py:312
  29.6 0.5 shard_map.75.near
  30.1 2.5 %collective-permute-start.18 = (bf16[32,2176]{1,0:T(8,128)(2,1)S(1)}, bf16[32,2176]{1,0:T(8,128)(2,1)S(1)}, u32[]{:S(2)}, u32[]{:S(2)}) collective-permute-start(bf16[32,2176]{1,0:T(8,128)(2,1)S(1)} %shard_map.75.near), channel_id=1, source_target_pairs={{0,24},{4,28},{8,16},{12,20},{16,8},{20,12},{24,0},{28,4},{1,25},{... | collective-permute-start | bytes 417800 | tf_op jit(solution)/shard_map/ppermute | solution.py:312
  32.7 2.1 %collective-permute-done.11.refs_2_ = bf16[32,2176]{1,0:T(8,128)(2,1)S(1)} collective-permute-done((bf16[32,2176]{1,0:T(8,128)(2,1)S(1)}, bf16[32,2176]{1,0:T(8,128)(2,1)S(1)}, u32[]{:S(2)}, u32[]{:S(2)}) %collective-permute-start.11) | collective-permute-done | bytes 139296 | tf_op jit(solution)/shard_map/ppermute | solution.py:312
  34.7 0.0 collective-permute-done.12.refs_3_
  34.7 0.5 shard_map.77.near
  35.2 1.5 %collective-permute-start.13 = (bf16[32,2176]{1,0:T(8,128)(2,1)S(1)}, bf16[32,2176]{1,0:T(8,128)(2,1)S(1)}, u32[]{:S(2)}, u32[]{:S(2)}) collective-permute-start(bf16[32,2176]{1,0:T(8,128)(2,1)S(1)} %shard_map.77.near), channel_id=1, source_target_pairs={{0,24},{4,28},{8,16},{12,20},{16,8},{20,12},{24,0},{28,4},{1,25},{... | collective-permute-start | bytes 417800 | tf_op jit(solution)/shard_map/ppermute | solution.py:312
  36.7 0.7 %collective-permute-done.18.far = bf16[32,2176]{1,0:T(8,128)(2,1)S(1)} collective-permute-done((bf16[32,2176]{1,0:T(8,128)(2,1)S(1)}, bf16[32,2176]{1,0:T(8,128)(2,1)S(1)}, u32[]{:S(2)}, u32[]{:S(2)}) %collective-permute-start.18) | collective-permute-done | bytes 139296 | tf_op jit(solution)/shard_map/ppermute | solution.py:312
  37.4 0.3 shard_map.80.refs_0_
  37.7 0.9 %collective-permute-start.19 = (bf16[32,2048]{1,0:T(8,128)(2,1)S(1)}, bf16[32,2048]{1,0:T(8,128)(2,1)S(1)}, u32[]{:S(2)}, u32[]{:S(2)}) collective-permute-start(bf16[32,2048]{1,0:T(8,128)(2,1)S(1)} %shard_map.80.refs_0_), channel_id=1, source_target_pairs={{0,4},{4,0},{8,12},{12,8},{16,20},{20,16},{24,28},{28,24},{1,5},{5... | collective-permute-start | bytes 393224 | tf_op jit(solution)/shard_map/ppermute | solution.py:312
  38.6 3.4 %collective-permute-start.20 = (bf16[32,2048]{1,0:T(8,128)(2,1)S(1)}, bf16[32,2048]{1,0:T(8,128)(2,1)S(1)}, u32[]{:S(2)}, u32[]{:S(2)}) collective-permute-start(bf16[32,2048]{1,0:T(8,128)(2,1)S(1)} %shard_map.80.refs_0_), channel_id=1, source_target_pairs={{0,8},{4,12},{8,0},{12,4},{16,24},{20,28},{24,16},{28,20},{1,9},{5... | collective-permute-start | bytes 393224 | tf_op jit(solution)/shard_map/ppermute | solution.py:312
  42.0 1.4 %collective-permute-start.21 = (bf16[32,2048]{1,0:T(8,128)(2,1)S(1)}, bf16[32,2048]{1,0:T(8,128)(2,1)S(1)}, u32[]{:S(2)}, u32[]{:S(2)}) collective-permute-start(bf16[32,2048]{1,0:T(8,128)(2,1)S(1)} %shard_map.80.refs_0_), channel_id=1, source_target_pairs={{0,12},{4,8},{8,4},{12,0},{16,28},{20,24},{24,20},{28,16},{1,13},{... | collective-permute-start | bytes 393224 | tf_op jit(solution)/shard_map/ppermute | solution.py:312
  43.4 0.3 shard_map.78.refs_0_
  43.7 0.7 %collective-permute-start.14 = (bf16[32,2048]{1,0:T(8,128)(2,1)S(1)}, bf16[32,2048]{1,0:T(8,128)(2,1)S(1)}, u32[]{:S(2)}, u32[]{:S(2)}) collective-permute-start(bf16[32,2048]{1,0:T(8,128)(2,1)S(1)} %shard_map.78.refs_0_), channel_id=1, source_target_pairs={{0,4},{4,0},{8,12},{12,8},{16,20},{20,16},{24,28},{28,24},{1,5},{5... | collective-permute-start | bytes 393224 | tf_op jit(solution)/shard_map/ppermute | solution.py:312
  44.5 1.4 %collective-permute-start.15 = (bf16[32,2048]{1,0:T(8,128)(2,1)S(1)}, bf16[32,2048]{1,0:T(8,128)(2,1)S(1)}, u32[]{:S(2)}, u32[]{:S(2)}) collective-permute-start(bf16[32,2048]{1,0:T(8,128)(2,1)S(1)} %shard_map.78.refs_0_), channel_id=1, source_target_pairs={{0,8},{4,12},{8,0},{12,4},{16,24},{20,28},{24,16},{28,20},{1,9},{5... | collective-permute-start | bytes 393224 | tf_op jit(solution)/shard_map/ppermute | solution.py:312
  45.9 1.4 %collective-permute-start.16 = (bf16[32,2048]{1,0:T(8,128)(2,1)S(1)}, bf16[32,2048]{1,0:T(8,128)(2,1)S(1)}, u32[]{:S(2)}, u32[]{:S(2)}) collective-permute-start(bf16[32,2048]{1,0:T(8,128)(2,1)S(1)} %shard_map.78.refs_0_), channel_id=1, source_target_pairs={{0,12},{4,8},{8,4},{12,0},{16,28},{20,24},{24,20},{28,16},{1,13},{... | collective-permute-start | bytes 393224 | tf_op jit(solution)/shard_map/ppermute | solution.py:312
  47.3 2.3 %collective-permute-done.21.refs_3_ = bf16[32,2048]{1,0:T(8,128)(2,1)S(1)} collective-permute-done((bf16[32,2048]{1,0:T(8,128)(2,1)S(1)}, bf16[32,2048]{1,0:T(8,128)(2,1)S(1)}, u32[]{:S(2)}, u32[]{:S(2)}) %collective-permute-start.21) | collective-permute-done | bytes 131104 | tf_op jit(solution)/shard_map/ppermute | solution.py:312
  49.6 0.8 %shard_map.81 = (f32[64,1024]{1,0:T(8,128)S(1)}, bf16[64,1024]{1,0:T(8,128)(2,1)S(1)}) custom-call(bf16[32,2048]{1,0:T(8,128)(2,1)S(1)} %shard_map.80.refs_0_, bf16[32,2048]{1,0:T(8,128)(2,1)S(1)} %collective-permute-done.19.refs_1_, bf16[32,2048]{1,0:T(8,128)(2,1)S(1)} %collective-permute-done.20.refs_2_, ...), custom_call_target="tpu_custom_call" | custom-call | tf_op jit(solution)/shard_map/pallas_call | solution.py:300
  50.4 0.1 collective-permute-start.22
  50.5 0.2 collective-permute-done.14.refs_1_
  50.7 1.6 %collective-permute-done.16.refs_3_ = bf16[32,2048]{1,0:T(8,128)(2,1)S(1)} collective-permute-done((bf16[32,2048]{1,0:T(8,128)(2,1)S(1)}, bf16[32,2048]{1,0:T(8,128)(2,1)S(1)}, u32[]{:S(2)}, u32[]{:S(2)}) %collective-permute-start.16) | collective-permute-done | bytes 131104 | tf_op jit(solution)/shard_map/ppermute | solution.py:312
  52.3 0.8 %shard_map.79 = (f32[64,1024]{1,0:T(8,128)S(1)}, bf16[64,1024]{1,0:T(8,128)(2,1)S(1)}) custom-call(bf16[32,2048]{1,0:T(8,128)(2,1)S(1)} %shard_map.78.refs_0_, bf16[32,2048]{1,0:T(8,128)(2,1)S(1)} %collective-permute-done.14.refs_1_, bf16[32,2048]{1,0:T(8,128)(2,1)S(1)} %collective-permute-done.15.refs_2_, ...), custom_call_target="tpu_custom_call" | custom-call | tf_op jit(solution)/shard_map/pallas_call | solution.py:300
  53.1 0.1 collective-permute-start.17
  53.2 1.3 %collective-permute-done.17 = bf16[64,1024]{1,0:T(8,128)(2,1)S(1)} collective-permute-done((bf16[64,1024]{1,0:T(8,128)(2,1)S(1)}, bf16[64,1024]{1,0:T(8,128)(2,1)S(1)}, u32[]{:S(2)}, u32[]{:S(2)}) %collective-permute-start.17) | collective-permute-done | bytes 131104 | tf_op jit(solution)/shard_map/ppermute | solution.py:312
  54.5 0.1 select_convert_fusion
  54.6 1.6 %collective-permute-start.23 = (bf16[64,1024]{1,0:T(8,128)(2,1)S(1)}, bf16[64,1024]{1,0:T(8,128)(2,1)S(1)}, u32[]{:S(2)}, u32[]{:S(2)}) collective-permute-start(bf16[64,1024]{1,0:T(8,128)(2,1)S(1)} %select_convert_fusion), channel_id=1, source_target_pairs={{0,2},{1,3},{2,0},{3,1},{4,6},{5,7},{6,4},{7,5},{8,10},{9,11},{10,... | collective-permute-start | bytes 393224 | tf_op jit(solution)/shard_map/ppermute | solution.py:312
  56.2 4.0 %collective-permute-done.23 = bf16[64,1024]{1,0:T(8,128)(2,1)S(1)} collective-permute-done((bf16[64,1024]{1,0:T(8,128)(2,1)S(1)}, bf16[64,1024]{1,0:T(8,128)(2,1)S(1)}, u32[]{:S(2)}, u32[]{:S(2)}) %collective-permute-start.23) | collective-permute-done | bytes 131104 | tf_op jit(solution)/shard_map/ppermute | solution.py:312
  60.2 0.7 %add_convert_fusion = bf16[64,1024]{1,0:T(8,128)(2,1)} fusion(bf16[64,1024]{1,0:T(8,128)(2,1)S(1)} %collective-permute-done.23, f32[64,1024]{1,0:T(8,128)S(1)} %get-tuple-element.31, bf16[64,1024]{1,0:T(8,128)(2,1)S(1)} %collective-permute-done.17, f32[64,1024]{1,0:T(8,128)S(1)} %get-tuple-element.33, bf16[64,1024]{1,0:T(8,128)(2,1)S(1)} %collective-permute-done.22, ...), kind=kLoop, calls=%fused_computation | loop fusion | flops 524288 | bytes 1048577 | tf_op jit(solution)/shard_map/convert_element_type | solution.py:340
  (15 shorter events, 0.0 us)
Async XLA Ops:
  0.0 15.5 %copy-start.1 = (bf16[32,2048]{1,0:T(8,128)(2,1)S(1)}, bf16[32,2048]{1,0:T(8,128)(2,1)}, u32[]{:S(2)}) copy-start(bf16[32,2048]{1,0:T(8,128)(2,1)} %refs_3_.1) | copy-start | bytes 393220
  0.0 11.6 %collective-permute-start.6 = (bf16[32,2048]{1,0:T(8,128)(2,1)}, bf16[32,2048]{1,0:T(8,128)(2,1)S(1)}, u32[]{:S(2)}, u32[]{:S(2)}) collective-permute-start(bf16[32,2048]{1,0:T(8,128)(2,1)} %refs_3_.1), channel_id=1, source_target_pairs={{0,24},{4,28},{8,16},{12,20},{16,8},{20,12},{24,0},{28,4},{1,25},{... | collective-permute-start | bytes 393224 | tf_op jit(solution)/shard_map/ppermute | solution.py:312
  5.1 8.7 %collective-permute-start = (bf16[32,2048]{1,0:T(8,128)(2,1)}, bf16[32,2048]{1,0:T(8,128)(2,1)S(1)}, u32[]{:S(2)}, u32[]{:S(2)}) collective-permute-start(bf16[32,2048]{1,0:T(8,128)(2,1)} %refs_3_.1), channel_id=1, source_target_pairs={{0,12},{4,8},{8,4},{12,0},{16,28},{20,24},{24,20},{28,16},{1,13},{... | collective-permute-start | bytes 393224 | tf_op jit(solution)/shard_map/ppermute | solution.py:312
  5.5 9.9 %collective-permute-start.1 = (bf16[32,2048]{1,0:T(8,128)(2,1)}, bf16[32,2048]{1,0:T(8,128)(2,1)S(1)}, u32[]{:S(2)}, u32[]{:S(2)}) collective-permute-start(bf16[32,2048]{1,0:T(8,128)(2,1)} %refs_3_.1), channel_id=1, source_target_pairs={{0,8},{4,12},{8,0},{12,4},{16,24},{20,28},{24,16},{28,20},{1,9},{5... | collective-permute-start | bytes 393224 | tf_op jit(solution)/shard_map/ppermute | solution.py:312
  8.0 7.5 %collective-permute-start.2 = (bf16[32,2048]{1,0:T(8,128)(2,1)}, bf16[32,2048]{1,0:T(8,128)(2,1)S(1)}, u32[]{:S(2)}, u32[]{:S(2)}) collective-permute-start(bf16[32,2048]{1,0:T(8,128)(2,1)} %refs_3_.1), channel_id=1, source_target_pairs={{0,4},{4,0},{8,12},{12,8},{16,20},{20,16},{24,28},{28,24},{1,5},{5... | collective-permute-start | bytes 393224 | tf_op jit(solution)/shard_map/ppermute | solution.py:312
  11.6 8.8 %collective-permute-start.7 = (bf16[32,2048]{1,0:T(8,128)(2,1)S(1)}, bf16[32,2048]{1,0:T(8,128)(2,1)S(1)}, u32[]{:S(2)}, u32[]{:S(2)}) collective-permute-start(bf16[32,2048]{1,0:T(8,128)(2,1)S(1)} %collective-permute-done.6.refs_3_), channel_id=1, source_target_pairs={{0,12},{4,8},{8,4},{12,0},{16,28},{20,24},{24,20},{28,16},{1,13},{... | collective-permute-start | bytes 393224 | tf_op jit(solution)/shard_map/ppermute | solution.py:312
  12.2 9.8 %collective-permute-start.8 = (bf16[32,2048]{1,0:T(8,128)(2,1)S(1)}, bf16[32,2048]{1,0:T(8,128)(2,1)S(1)}, u32[]{:S(2)}, u32[]{:S(2)}) collective-permute-start(bf16[32,2048]{1,0:T(8,128)(2,1)S(1)} %collective-permute-done.6.refs_3_), channel_id=1, source_target_pairs={{0,8},{4,12},{8,0},{12,4},{16,24},{20,28},{24,16},{28,20},{1,9},{5... | collective-permute-start | bytes 393224 | tf_op jit(solution)/shard_map/ppermute | solution.py:312
  13.8 8.2 %collective-permute-start.9 = (bf16[32,2048]{1,0:T(8,128)(2,1)S(1)}, bf16[32,2048]{1,0:T(8,128)(2,1)S(1)}, u32[]{:S(2)}, u32[]{:S(2)}) collective-permute-start(bf16[32,2048]{1,0:T(8,128)(2,1)S(1)} %collective-permute-done.6.refs_3_), channel_id=1, source_target_pairs={{0,4},{4,0},{8,12},{12,8},{16,20},{20,16},{24,28},{28,24},{1,5},{5... | collective-permute-start | bytes 393224 | tf_op jit(solution)/shard_map/ppermute | solution.py:312
  18.4 8.4 %collective-permute-start.3 = (bf16[32,2176]{1,0:T(8,128)(2,1)S(1)}, bf16[32,2176]{1,0:T(8,128)(2,1)S(1)}, u32[]{:S(2)}, u32[]{:S(2)}) collective-permute-start(bf16[32,2176]{1,0:T(8,128)(2,1)S(1)} %get-tuple-element.24), channel_id=1, source_target_pairs={{0,4},{4,0},{8,12},{12,8},{16,20},{20,16},{24,28},{28,24},{1,5},{5... | collective-permute-start | bytes 417800 | tf_op jit(solution)/shard_map/ppermute | solution.py:312
  18.5 10.0 %collective-permute-start.4 = (bf16[32,2176]{1,0:T(8,128)(2,1)S(1)}, bf16[32,2176]{1,0:T(8,128)(2,1)S(1)}, u32[]{:S(2)}, u32[]{:S(2)}) collective-permute-start(bf16[32,2176]{1,0:T(8,128)(2,1)S(1)} %get-tuple-element.25), channel_id=1, source_target_pairs={{0,8},{4,12},{8,0},{12,4},{16,24},{20,28},{24,16},{28,20},{1,9},{5... | collective-permute-start | bytes 417800 | tf_op jit(solution)/shard_map/ppermute | solution.py:312
  20.4 29.2 %copy-start = (bf16[2048,1024]{1,0:T(8,128)(2,1)S(1)}, bf16[2048,1024]{1,0:T(8,128)(2,1)}, u32[]{:S(2)}) copy-start(bf16[2048,1024]{1,0:T(8,128)(2,1)} %refs_4_.3) | copy-start | bytes 12582916
  20.4 9.3 %collective-permute-start.5 = (bf16[32,2176]{1,0:T(8,128)(2,1)S(1)}, bf16[32,2176]{1,0:T(8,128)(2,1)S(1)}, u32[]{:S(2)}, u32[]{:S(2)}) collective-permute-start(bf16[32,2176]{1,0:T(8,128)(2,1)S(1)} %get-tuple-element.26), channel_id=1, source_target_pairs={{0,12},{4,8},{8,4},{12,0},{16,28},{20,24},{24,20},{28,16},{1,13},{... | collective-permute-start | bytes 417800 | tf_op jit(solution)/shard_map/ppermute | solution.py:312
  24.9 7.8 %collective-permute-start.10 = (bf16[32,2176]{1,0:T(8,128)(2,1)S(1)}, bf16[32,2176]{1,0:T(8,128)(2,1)S(1)}, u32[]{:S(2)}, u32[]{:S(2)}) collective-permute-start(bf16[32,2176]{1,0:T(8,128)(2,1)S(1)} %get-tuple-element.28), channel_id=1, source_target_pairs={{0,8},{4,12},{8,0},{12,4},{16,24},{20,28},{24,16},{28,20},{1,9},{5... | collective-permute-start | bytes 417800 | tf_op jit(solution)/shard_map/ppermute | solution.py:312
  26.8 7.9 %collective-permute-start.11 = (bf16[32,2176]{1,0:T(8,128)(2,1)S(1)}, bf16[32,2176]{1,0:T(8,128)(2,1)S(1)}, u32[]{:S(2)}, u32[]{:S(2)}) collective-permute-start(bf16[32,2176]{1,0:T(8,128)(2,1)S(1)} %get-tuple-element.29), channel_id=1, source_target_pairs={{0,12},{4,8},{8,4},{12,0},{16,28},{20,24},{24,20},{28,16},{1,13},{... | collective-permute-start | bytes 417800 | tf_op jit(solution)/shard_map/ppermute | solution.py:312
  26.8 7.9 %collective-permute-start.12 = (bf16[32,2176]{1,0:T(8,128)(2,1)S(1)}, bf16[32,2176]{1,0:T(8,128)(2,1)S(1)}, u32[]{:S(2)}, u32[]{:S(2)}) collective-permute-start(bf16[32,2176]{1,0:T(8,128)(2,1)S(1)} %get-tuple-element.30), channel_id=1, source_target_pairs={{0,4},{4,0},{8,12},{12,8},{16,20},{20,16},{24,28},{28,24},{1,5},{5... | collective-permute-start | bytes 417800 | tf_op jit(solution)/shard_map/ppermute | solution.py:312
  30.1 7.3 %collective-permute-start.18 = (bf16[32,2176]{1,0:T(8,128)(2,1)S(1)}, bf16[32,2176]{1,0:T(8,128)(2,1)S(1)}, u32[]{:S(2)}, u32[]{:S(2)}) collective-permute-start(bf16[32,2176]{1,0:T(8,128)(2,1)S(1)} %shard_map.75.near), channel_id=1, source_target_pairs={{0,24},{4,28},{8,16},{12,20},{16,8},{20,12},{24,0},{28,4},{1,25},{... | collective-permute-start | bytes 417800 | tf_op jit(solution)/shard_map/ppermute | solution.py:312
  35.2 8.2 %collective-permute-start.13 = (bf16[32,2176]{1,0:T(8,128)(2,1)S(1)}, bf16[32,2176]{1,0:T(8,128)(2,1)S(1)}, u32[]{:S(2)}, u32[]{:S(2)}) collective-permute-start(bf16[32,2176]{1,0:T(8,128)(2,1)S(1)} %shard_map.77.near), channel_id=1, source_target_pairs={{0,24},{4,28},{8,16},{12,20},{16,8},{20,12},{24,0},{28,4},{1,25},{... | collective-permute-start | bytes 417800 | tf_op jit(solution)/shard_map/ppermute | solution.py:312
  37.7 8.2 %collective-permute-start.19 = (bf16[32,2048]{1,0:T(8,128)(2,1)S(1)}, bf16[32,2048]{1,0:T(8,128)(2,1)S(1)}, u32[]{:S(2)}, u32[]{:S(2)}) collective-permute-start(bf16[32,2048]{1,0:T(8,128)(2,1)S(1)} %shard_map.80.refs_0_), channel_id=1, source_target_pairs={{0,4},{4,0},{8,12},{12,8},{16,20},{20,16},{24,28},{28,24},{1,5},{5... | collective-permute-start | bytes 393224 | tf_op jit(solution)/shard_map/ppermute | solution.py:312
  38.6 8.7 %collective-permute-start.20 = (bf16[32,2048]{1,0:T(8,128)(2,1)S(1)}, bf16[32,2048]{1,0:T(8,128)(2,1)S(1)}, u32[]{:S(2)}, u32[]{:S(2)}) collective-permute-start(bf16[32,2048]{1,0:T(8,128)(2,1)S(1)} %shard_map.80.refs_0_), channel_id=1, source_target_pairs={{0,8},{4,12},{8,0},{12,4},{16,24},{20,28},{24,16},{28,20},{1,9},{5... | collective-permute-start | bytes 393224 | tf_op jit(solution)/shard_map/ppermute | solution.py:312
  42.0 7.6 %collective-permute-start.21 = (bf16[32,2048]{1,0:T(8,128)(2,1)S(1)}, bf16[32,2048]{1,0:T(8,128)(2,1)S(1)}, u32[]{:S(2)}, u32[]{:S(2)}) collective-permute-start(bf16[32,2048]{1,0:T(8,128)(2,1)S(1)} %shard_map.80.refs_0_), channel_id=1, source_target_pairs={{0,12},{4,8},{8,4},{12,0},{16,28},{20,24},{24,20},{28,16},{1,13},{... | collective-permute-start | bytes 393224 | tf_op jit(solution)/shard_map/ppermute | solution.py:312
  43.7 7.0 %collective-permute-start.14 = (bf16[32,2048]{1,0:T(8,128)(2,1)S(1)}, bf16[32,2048]{1,0:T(8,128)(2,1)S(1)}, u32[]{:S(2)}, u32[]{:S(2)}) collective-permute-start(bf16[32,2048]{1,0:T(8,128)(2,1)S(1)} %shard_map.78.refs_0_), channel_id=1, source_target_pairs={{0,4},{4,0},{8,12},{12,8},{16,20},{20,16},{24,28},{28,24},{1,5},{5... | collective-permute-start | bytes 393224 | tf_op jit(solution)/shard_map/ppermute | solution.py:312
  44.5 6.2 %collective-permute-start.15 = (bf16[32,2048]{1,0:T(8,128)(2,1)S(1)}, bf16[32,2048]{1,0:T(8,128)(2,1)S(1)}, u32[]{:S(2)}, u32[]{:S(2)}) collective-permute-start(bf16[32,2048]{1,0:T(8,128)(2,1)S(1)} %shard_map.78.refs_0_), channel_id=1, source_target_pairs={{0,8},{4,12},{8,0},{12,4},{16,24},{20,28},{24,16},{28,20},{1,9},{5... | collective-permute-start | bytes 393224 | tf_op jit(solution)/shard_map/ppermute | solution.py:312
  45.9 6.4 %collective-permute-start.16 = (bf16[32,2048]{1,0:T(8,128)(2,1)S(1)}, bf16[32,2048]{1,0:T(8,128)(2,1)S(1)}, u32[]{:S(2)}, u32[]{:S(2)}) collective-permute-start(bf16[32,2048]{1,0:T(8,128)(2,1)S(1)} %shard_map.78.refs_0_), channel_id=1, source_target_pairs={{0,12},{4,8},{8,4},{12,0},{16,28},{20,24},{24,20},{28,16},{1,13},{... | collective-permute-start | bytes 393224 | tf_op jit(solution)/shard_map/ppermute | solution.py:312
  50.4 2.9 %collective-permute-start.22 = (bf16[64,1024]{1,0:T(8,128)(2,1)S(1)}, bf16[64,1024]{1,0:T(8,128)(2,1)S(1)}, u32[]{:S(2)}, u32[]{:S(2)}) collective-permute-start(bf16[64,1024]{1,0:T(8,128)(2,1)S(1)} %get-tuple-element.34), channel_id=1, source_target_pairs={{0,1},{1,0},{2,3},{3,2},{4,5},{5,4},{6,7},{7,6},{8,9},{9,8},{10,11... | collective-permute-start | bytes 393224 | tf_op jit(solution)/shard_map/ppermute | solution.py:312
  53.1 1.4 %collective-permute-start.17 = (bf16[64,1024]{1,0:T(8,128)(2,1)S(1)}, bf16[64,1024]{1,0:T(8,128)(2,1)S(1)}, u32[]{:S(2)}, u32[]{:S(2)}) collective-permute-start(bf16[64,1024]{1,0:T(8,128)(2,1)S(1)} %get-tuple-element.32), channel_id=1, source_target_pairs={{0,1},{1,0},{2,3},{3,2},{4,5},{5,4},{6,7},{7,6},{8,9},{9,8},{10,11... | collective-permute-start | bytes 393224 | tf_op jit(solution)/shard_map/ppermute | solution.py:312
  54.6 5.6 %collective-permute-start.23 = (bf16[64,1024]{1,0:T(8,128)(2,1)S(1)}, bf16[64,1024]{1,0:T(8,128)(2,1)S(1)}, u32[]{:S(2)}, u32[]{:S(2)}) collective-permute-start(bf16[64,1024]{1,0:T(8,128)(2,1)S(1)} %select_convert_fusion), channel_id=1, source_target_pairs={{0,2},{1,3},{2,0},{3,1},{4,6},{5,7},{6,4},{7,5},{8,10},{9,11},{10,... | collective-permute-start | bytes 393224 | tf_op jit(solution)/shard_map/ppermute | solution.py:312
